TPU v7x, 32 devices: a whole 2x2x4 slice. The times are simulated.
32 devices in a mesh: dp: 4 (over z), seq: 4 (over x, core), index: 2 (over y).
Axes of the slice: x: 2, y: 2, z: 4, core: 2. Of those that a mesh axis runs over, the one named last changes fastest.
Arguments:
- hidden: bfloat16 [4, 1024, 2048], P('dp', 'seq'), may hold values from -32 to 32
- proj_weight: bfloat16 [4, 2048, 1536], P(None, 'dp', 'index')
- stretch_lengths: int32 [4, 32], P('dp'), may hold values from 1 to 512, 1024 in all within a row
- shard_of: int32 [4, 32, 1], P('dp', 'seq'), may hold values from 0 to 1; in each aligned block of 8 rows (0 to 7, 8 to 15, ..., all dimensions but the last counted through in order) at most 4 rows name the same one
Outputs:
- layer_out: bfloat16 [4, 1024, 2048], P('dp', 'seq', 'index')
- shelf: float32 [4, 4, 2, 4, 2048], P('dp', 'seq', 'index')
Inputs may be any that keep to these rules, and one draw needn't show every extreme that they name: `stretch_lengths`: the 32 lengths of a manual sum to 1024; the largest is 512. `shard_of`: in each aligned block of 8 rows of a manual no shard is named more than 4 times, a bound that some block reaches.
All inputs are finite; a program needn't handle non-finite values.
Results may differ from a plain program's by a relative error of at most 0.01.
Values may be sent and summed in bfloat16 or wider, within the bound.
No kernel may reach another device: no remote copies, remote signals or barrier semaphores. Data moves between devices by JAX's collectives and lax.ppermute only.
A program may use at most 64 MiB of HBM per device.

v0:
```python
import jax
import jax.numpy as jnp
from jax import lax
from jax.sharding import PartitionSpec as P

D = 2048
HD = 64
HALF_WIN = 256


def with_halo(cells, sides, width):
    for axis, dim in sides:
        count = lax.axis_size(axis)
        ends = count - 1
        head = lax.slice_in_dim(cells, 0, width, axis=dim)
        tail = lax.slice_in_dim(cells, cells.shape[dim] - width, cells.shape[dim], axis=dim)
        cells = jnp.concatenate(
            [
                lax.ppermute(tail, axis, [(i, (i + 1) % count) for i in range(ends)]),
                cells,
                lax.ppermute(head, axis, [((i + 1) % count, i) for i in range(ends)]),
            ],
            axis=dim,
        )
    return cells


def rotate(values_in, positions):
    half_dim = HD // 2
    freqs = 10000.0 ** (-2.0 * jnp.arange(half_dim, dtype=jnp.float32) / HD)
    angles = positions.astype(jnp.float32)[:, None] * freqs[None, :]
    cosine = jnp.cos(angles)[:, None, :]
    sine = jnp.sin(angles)[:, None, :]
    first = values_in[..., :half_dim]
    second = values_in[..., half_dim:]
    return jnp.concatenate([first * cosine - second * sine, second * cosine + first * sine], -1)


def window_heads(queries, key_rows, value_rows, visible):
    scale = HD ** (-0.5)

    def one_head(items):
        query_head, key_head, value_head = items
        scores = jnp.dot(query_head, key_head.T, preferred_element_type=jnp.float32) * scale
        scores = jnp.where(visible, scores, -1e30)
        maxima = jnp.max(scores, -1, keepdims=True)
        expo = jnp.exp(scores - maxima)
        weights = (expo / jnp.sum(expo, -1, keepdims=True)).astype(jnp.bfloat16)
        return jnp.dot(weights, value_head, preferred_element_type=jnp.float32).astype(jnp.bfloat16)

    context = lax.map(
        one_head,
        (jnp.moveaxis(queries, 1, 0), jnp.moveaxis(key_rows, 1, 0), jnp.moveaxis(value_rows, 1, 0)),
    )
    return jnp.moveaxis(context, 0, 1)


def body(hidden, proj_weight, stretch_lengths, shard_of):
    states = hidden[0]
    tokens_here = states.shape[0]
    width = proj_weight.shape[2]
    heads_here = width // HD
    seq_index = lax.axis_index("seq")
    group_index = lax.axis_index("index")
    seq_count = lax.axis_size("seq")
    index_count = lax.axis_size("index")
    total_length = tokens_here * seq_count
    positions = seq_index * tokens_here + jnp.arange(tokens_here, dtype=jnp.int32)
    projected = jnp.einsum(
        "td,jdc->jtc",
        states,
        lax.all_gather(proj_weight[:3], "dp", axis=1, tiled=True),
        preferred_element_type=jnp.float32,
    )
    queries = rotate(projected[0].reshape(tokens_here, heads_here, HD), positions).astype(
        jnp.bfloat16
    )
    key_rows = rotate(projected[1].reshape(tokens_here, heads_here, HD), positions).astype(
        jnp.bfloat16
    )
    value_rows = projected[2].astype(jnp.bfloat16)
    stacked = jnp.stack([key_rows.reshape(tokens_here, width), value_rows])
    padded = with_halo(stacked, (("seq", 1),), HALF_WIN)
    span = tokens_here + 2 * HALF_WIN
    key_part = padded[0, 0:span].reshape(span, heads_here, HD)
    value_part = padded[1, 0:span].reshape(span, heads_here, HD)
    key_pos = seq_index * tokens_here + 0 - HALF_WIN + jnp.arange(span, dtype=jnp.int32)
    visible = (
        (jnp.abs(key_pos[None, :] - positions[:, None]) <= HALF_WIN)
        & (key_pos[None, :] >= 0)
        & (key_pos[None, :] < total_length)
    )
    context_parts = window_heads(queries, key_part, value_part, visible).reshape(tokens_here, width)
    partial_value = lax.dot_general(
        context_parts,
        lax.all_gather(proj_weight[3], "dp", axis=0, tiled=True),
        (((1,), (1,)), ((), ())),
        preferred_element_type=jnp.float32,
    )
    lengths = stretch_lengths[0]
    stretch_count = lengths.shape[0]
    per_block = stretch_count // seq_count
    ends = jnp.cumsum(lengths, dtype=jnp.int32)
    starts = ends - lengths
    row_ids = jnp.arange(stretch_count, dtype=jnp.int32)
    order = row_ids % per_block * seq_count + row_ids // per_block
    row_starts = starts[order]
    row_ends = ends[order]
    member = (
        (positions[None, :] >= row_starts[:, None]) & (positions[None, :] < row_ends[:, None])
    ).astype(jnp.bfloat16)
    shard_ids = shard_of[0, :, 0]
    local_rows = jnp.arange(per_block, dtype=jnp.int32)
    earlier = (shard_ids[:, None] == shard_ids[None, :]) & (
        local_rows[None, :] < local_rows[:, None]
    )
    slot_rank = jnp.sum(earlier.astype(jnp.int32), 1)
    capacity = per_block // 2
    slot_ids = jnp.arange(capacity, dtype=jnp.int32)
    quarter = D // index_count
    summed = lax.psum_scatter(
        partial_value.astype(jnp.bfloat16), "index", scatter_dimension=1, tiled=True
    ).astype(jnp.float32)
    own_states = lax.dynamic_slice_in_dim(states, group_index * quarter, quarter, 1)
    layer = (own_states.astype(jnp.float32) + summed).astype(jnp.bfloat16)
    partial_pool = jnp.dot(member, layer, preferred_element_type=jnp.float32)
    pooled = lax.psum_scatter(
        partial_pool.astype(jnp.bfloat16), "seq", scatter_dimension=0, tiled=True
    ).astype(jnp.float32)
    shard_range = jnp.arange(index_count, dtype=jnp.int32)
    routing = (
        (shard_ids[None, None, :] == shard_range[:, None, None])
        & (slot_rank[None, None, :] == slot_ids[None, :, None])
    ).astype(jnp.float32)
    outgoing = jnp.einsum("rkc,cf->rkf", routing, pooled, precision=lax.Precision.HIGHEST)
    arrived = lax.all_to_all(outgoing, "index", split_axis=0, concat_axis=2, tiled=True)[0]
    shelf_rows = arrived * lax.rsqrt(jnp.mean(arrived * arrived, -1, keepdims=True) + 1e-06)
    return (layer[None], shelf_rows[None, None, None])


def solution(mesh):
    in_specs = (P("dp", "seq", None), P(None, "dp", "index"), P("dp", None), P("dp", "seq", None))
    out_specs = (P("dp", "seq", "index"), P("dp", "seq", "index", None, None))
    return jax.shard_map(body, mesh=mesh, in_specs=in_specs, out_specs=out_specs, check_vma=False)
```

profile of v0, /device:TPU:0, one launch (start us, length us, event | category | flops | bytes accessed | tf_op | source)
XLA Modules:
  0.0 336.3 jit_solution(11386084631640545128)
XLA Ops:
  7.2 1.6 slice-done
  8.8 2.4 copy.33
  11.4 1.2 multiply_cosine_fusion
  12.6 168.3 %all-gather.4.cloned.1.call-done = bf16[3,2048,768]{1,2,0:T(8,128)(2,1)} async-done(((bf16[3,512,768]{1,2,0:T(8,128)(2,1)}), bf16[3,2048,768]{1,2,0:T(8,128)(2,1)}) %all-gather.4.cloned.1.call-update) | async-done | bytes 9437200 | tf_op jit(solution)/shard_map/all_gather | solution.py:72
  180.9 5.2 %convolution_bitcast_fusion = f32[3,256,768]{1,2,0:T(8,128)S(1)} fusion(bf16[3,2048,768]{1,2,0:T(8,128)(2,1)} %all-gather.4.cloned.1.call-done, bf16[1,256,2048]{2,1,0:T(8,128)(2,1)S(1)} %copy-done.1), kind=kOutput, calls=%fused_computation.26 | convolution fusion | flops 2415919104 | bytes 12845056 | tf_op jit(solution)/shard_map/td,jdc->jtc/dot_general | solution.py:69
  186.2 1.0 fusion.47
  187.2 0.8 fusion.49
  188.0 0.5 copy.34
  188.5 1.5 copy.35
  190.0 2.1 fusion.48
  192.0 2.6 copy.36
  194.7 2.6 copy.37
  197.3 2.8 subtract_convert_fusion
  200.1 2.0 maximum_bitcast_fusion
  202.1 2.1 copy.29
  204.2 2.0 pad_maximum_fusion.2
  206.2 2.9 collective-permute-start
  209.1 1.3 collective-permute-start.1
  210.4 0.9 slice.44
  211.5 2.3 collective-permute-done.1
  213.7 1.6 pad_maximum_fusion
  215.5 2.4 copy.31
  218.0 1.3 copy.30
  219.2 43.0 %while.11 = (s32[]{:T(128)}, bf16[12,256,64]{1,2,0:T(8,128)(2,1)}, bf16[12,256,64]{2,1,0:T(8,128)(2,1)}, bf16[12,768,64]{2,1,0:T(8,128)(2,1)S(1)}, bf16[12,768,6...) while((s32[]{:T(128)}, bf16[12,256,64]{1,2,0:T(8,128)(2,1)}, ...), condition=%wide.region_3.4_spmd.clone, body=%wide.region_0.3_spmd.clone.sunk | while | flops 52903424 | bytes 2865253 | solution.py:51
  219.3 1.4 fusion.57
  220.6 0.3 fusion.58
  220.9 2.0 fusion.59
  222.8 1.4 fusion.57
  224.2 0.3 fusion.58
  224.5 1.9 fusion.59
  226.4 1.3 fusion.57
  227.8 0.3 fusion.58
  228.1 2.0 fusion.59
  230.0 1.3 fusion.57
  231.4 0.3 fusion.58
  231.6 2.0 fusion.59
  233.6 1.3 fusion.57
  235.2 2.0 fusion.59
  237.2 1.3 fusion.57
  238.8 1.9 fusion.59
  240.8 1.3 fusion.57
  242.4 2.0 fusion.59
  244.3 1.3 fusion.57
  246.0 2.0 fusion.59
  247.9 1.3 fusion.57
  249.5 2.0 fusion.59
  251.5 1.3 fusion.57
  253.1 2.0 fusion.59
  255.1 1.3 fusion.57
  256.7 1.9 fusion.59
  258.7 1.3 fusion.57
  260.3 2.0 fusion.59
  262.2 12.4 %all-gather.6.cloned.1.call-done = bf16[1,2048,768]{2,1,0:T(8,128)(2,1)} async-done(((bf16[1,512,768]{2,1,0:T(8,128)(2,1)}), bf16[1,2048,768]{2,1,0:T(8,128)(2,1)}) %all-gather.6.cloned.1.call-update) | async-done | bytes 3145744 | tf_op jit(solution)/shard_map/all_gather | solution.py:96
  274.6 4.1 %fusion.18 = bf16[256,2048]{1,0:T(8,128)(2,1)} fusion(bf16[256,768]{0,1:T(8,128)(2,1)} %bitcast.87, bf16[1,2048,768]{2,1,0:T(8,128)(2,1)} %all-gather.6.cloned.1.call-done), kind=kOutput, calls=%fused_computation.24 | convolution fusion | flops 805830656 | bytes 4587520 | tf_op jit(solution)/shard_map/dot_general | solution.py:94
  279.1 0.7 gather_fusion.1
  279.8 0.7 gather_fusion
  280.7 17.1 %reduce-scatter.3.cloned.1.call-done = bf16[256,1024]{1,0:T(8,128)(2,1)} async-done(((bf16[256,2048]{1,0:T(8,128)(2,1)}), bf16[256,1024]{1,0:T(8,128)(2,1)}) %reduce-scatter.3.cloned.1.call-update) | async-done | bytes 524304 | tf_op jit(solution)/shard_map/reduce_scatter | solution.py:121
  297.9 1.9 convolution_convert_fusion.1
  299.8 20.4 %reduce-scatter.5.cloned.1.call-done = bf16[8,1024]{1,0:T(8,128)(2,1)} async-done(((bf16[32,1024]{1,0:T(8,128)(2,1)}), bf16[8,1024]{1,0:T(8,128)(2,1)}) %reduce-scatter.5.cloned.1.call-update) | async-done | bytes 16400 | tf_op jit(solution)/shard_map/reduce_scatter | solution.py:127
  320.3 1.5 fusion.29
  321.8 3.3 all-to-all-start
  325.0 2.0 fusion.24
  327.1 1.9 all-to-all-done
  329.1 0.7 broadcast_multiply_fusion
  (47 shorter events, 3.3 us)
Async XLA Ops:
  7.2 1.7 slice-start
  7.2 173.8 %all-gather.4.cloned.1.call-start = ((), (), s32[]{:S(2)}) async-start(), calls=%async_computation.3 | async-start | bytes 11796480 | tf_op jit(solution)/shard_map/all_gather | solution.py:72
  11.3 169.7 %copy-start.1 = (bf16[1,256,2048]{2,1,0:T(8,128)(2,1)S(1)}, bf16[1,256,2048]{2,1,0:T(8,128)(2,1)}, u32[]{:S(2)}) copy-start(bf16[1,256,2048]{2,1,0:T(8,128)(2,1)} %param.6) | copy-start | bytes 3145732
  11.3 263.3 %all-gather.6.cloned.1.call-start = ((), (), s32[]{:S(2)}) async-start(), calls=%async_computation.6 | async-start | bytes 3932160 | tf_op jit(solution)/shard_map/all_gather | solution.py:96
  200.0 10.3 %copy-start = (bf16[4,512,768]{2,1,0:T(8,128)(2,1)S(1)}, bf16[4,512,768]{2,1,0:T(8,128)(2,1)}, u32[]{:S(2)}) copy-start(bf16[4,512,768]{2,1,0:T(8,128)(2,1)} %param.7) | copy-start | bytes 9437188
  206.2 5.2 %collective-permute-start = (bf16[2,256,768]{1,2,0:T(8,128)(2,1)}, bf16[2,256,768]{1,2,0:T(8,128)(2,1)}, u32[]{:S(2)}, u32[]{:S(2)}) collective-permute-start(bf16[2,256,768]{1,2,0:T(8,128)(2,1)} %pad_maximum_fusion.2), channel_id=1, source_target_pairs={{0,2},{2,4},{4,6},{1,3},{3,5},{5,7},{8,10},{10,12},{12,14},{9,11},... | collective-permute-start | bytes 2359304 | tf_op jit(solution)/shard_map/ppermute | solution.py:19
  209.1 4.7 %collective-permute-start.1 = (bf16[2,256,768]{1,2,0:T(8,128)(2,1)}, bf16[2,256,768]{1,2,0:T(8,128)(2,1)}, u32[]{:S(2)}, u32[]{:S(2)}) collective-permute-start(bf16[2,256,768]{1,2,0:T(8,128)(2,1)} %pad_maximum_fusion.2), channel_id=1, source_target_pairs={{2,0},{4,2},{6,4},{3,1},{5,3},{7,5},{10,8},{12,10},{14,12},{11,9},... | collective-permute-start | bytes 2359304 | tf_op jit(solution)/shard_map/ppermute | solution.py:21
  211.3 86.5 %reduce-scatter.3.cloned.1.call-start = ((), (), s32[]{:S(2)}) async-start(), calls=%async_computation.4 | async-start | bytes 1572864 | tf_op jit(solution)/shard_map/reduce_scatter | solution.py:121
  274.6 4.2 %copy-start.3 = (s32[1,32]{1,0:T(1,128)S(1)}, s32[1,32]{1,0:T(1,128)}, u32[]{:S(2)}) copy-start(s32[1,32]{1,0:T(1,128)} %param.8) | copy-start | bytes 388
  274.6 5.9 %copy-start.4 = (s32[1,8,1]{1,2,0:T(1,128)S(1)}, s32[1,8,1]{1,2,0:T(1,128)}, u32[]{:S(2)}) copy-start(s32[1,8,1]{1,2,0:T(1,128)} %param.9) | copy-start | bytes 100
  274.6 23.3 %copy-start.2 = (bf16[1,256,2048]{2,1,0:T(8,128)(2,1)S(1)}, bf16[1,256,2048]{2,1,0:T(8,128)(2,1)}, u32[]{:S(2)}) copy-start(bf16[1,256,2048]{2,1,0:T(8,128)(2,1)} %param.6) | copy-start | bytes 3145732
  278.8 41.5 %reduce-scatter.5.cloned.1.call-start = ((), (), s32[]{:S(2)}) async-start(), calls=%async_computation.5 | async-start | bytes 81920 | tf_op jit(solution)/shard_map/reduce_scatter | solution.py:127
  321.8 7.2 %all-to-all-start = ((f32[2,4,1024]{2,1,0:T(4,128)}), f32[2,4,1024]{2,1,0:T(4,128)S(1)}, u32[]{:S(2)}, u32[]{:S(2)}) async-start(f32[2,4,1024]{2,1,0:T(4,128)} %fusion.29), calls=%async_computation.2 | async-start | bytes 65536 | tf_op jit(solution)/shard_map/all_to_all | solution.py:136
Sparse Core Ops, SparseCore 0:
  11.4 169.4 all-gather.3
  211.5 63.1 all-gather.5
  278.9 18.9 reduce-scatter.2
  300.9 19.3 reduce-scatter.4
where the time goes:
time: 338 us; the launch traced here: 336 us
  waiting for transfers between devices  223 us (66%)
  matrix products  52.4 us (16%)
  local copies, waits for them, and re-layouts  23.6 us (7%)
  other arithmetic  16.3 us (5%)
  between operations  14 us (4%)
  starting transfers between devices  7.56 us (2%)
    all_gather x1, waiting for transfers between devices, body(): lax.all_gather(proj_weight[:3], 'dp', axis=1, tiled=True)  168 us
    dot_general x12, matrix products, one_head(): jnp.dot(weights, value_head, preferred_element_type=jnp.float32)  23.4 us
    reduce_scatter x1, waiting for transfers between devices, body(): lax.psum_scatter(partial_pool.astype(jnp.bfloat16), 'seq', scatter_dimens...  20.4 us
    reduce_scatter x1, waiting for transfers between devices, body(): lax.psum_scatter(partial_value.astype(jnp.bfloat16), 'index', scatter_dim...  17.1 us
    dot_general x12, matrix products, one_head(): jnp.dot(query_head, key_head.T, preferred_element_type=jnp.float32) * scale  16.2 us
    all_gather x1, waiting for transfers between devices, body(): lax.all_gather(proj_weight[3], 'dp', axis=0, tiled=True)  12.4 us
    unnamed x15, local copies, waits for them, and re-layouts  9.62 us
  transfers between devices with their start and end apart: 7, of which 6 were waited for; matrix products, arithmetic and copies ran while one was open for 16% of the time, Pallas kernels for 0%

commit v1 on v0

--- a/solution.py
+++ b/solution.py
@@ -1,6 +1,10 @@
+import functools
+
 import jax
 import jax.numpy as jnp
 from jax import lax
+from jax.experimental import pallas as pl
+from jax.experimental.pallas import tpu as pltpu
 from jax.sharding import PartitionSpec as P
 
 D = 2048
@@ -138,7 +142,331 @@
     return (layer[None], shelf_rows[None, None, None])
 
 
+def lanes(shape):
+    return lax.broadcasted_iota(jnp.int32, shape, 1)
+
+
+def rotary(tile, cosine, sine):
+    first = lanes(tile.shape) % HD < HD // 2
+    partner = jnp.where(first, pltpu.roll(tile, 128 - HD // 2, 1), pltpu.roll(tile, HD // 2, 1))
+    return tile * cosine + partner * sine
+
+
+def attend_kernel(folded, pieces, *refs):
+    where, h_refs, (cos_ref, sin_ref, member_ref) = refs[0], refs[1:5], refs[5:8]
+    w_refs = refs[8 : 8 + pieces]
+    out_refs = refs[8 + pieces : 12 + pieces]
+    q_s, k_s, v_s, c_s = refs[12 + pieces :]
+    s, d = where[0], where[1]
+    rows = h_refs[0].shape[0]
+    total = 4 * rows
+    shard = h_refs[0].shape[1] // 4
+    half = shard // 2
+
+    for j in range(4):
+        block = jnp.bitwise_xor(s, j)
+        at = pl.ds(pl.multiple_of(block * rows, rows), rows)
+        if folded:
+            top = jnp.zeros((rows, 256), jnp.float32)
+            bottom = jnp.zeros((rows, 256), jnp.float32)
+            for k in range(4):
+                column = lax.rem(d - k + 4, 4) * shard
+                w = w_refs[k]
+                h_top = h_refs[j][:, pl.ds(pl.multiple_of(column, half), half)]
+                h_bottom = h_refs[j][:, pl.ds(pl.multiple_of(column + half, half), half)]
+                top += jnp.dot(h_top, jnp.concatenate([w[:, 0:128], w[:, 256:384]], 1), preferred_element_type=jnp.float32)
+                bottom += jnp.dot(h_bottom, w[:, 128:384], preferred_element_type=jnp.float32)
+            qk = rotary(top[:, :128] + bottom[:, :128], cos_ref[at, :], sin_ref[at, :])
+            low = lanes(qk.shape) < HD
+            q_s[at, :] = jnp.where(low, qk * HD**-0.5, 0.0).astype(jnp.bfloat16)
+            k_s[at, :] = pltpu.roll(qk, HD, 1).astype(jnp.bfloat16)
+            v = top[:, 128:] + pltpu.roll(bottom[:, 128:], HD, 1)
+            v_s[at, :] = jnp.where(low, v, 1.0).astype(jnp.bfloat16)
+        else:
+            acc = jnp.zeros((rows, 384), jnp.float32)
+            for k in range(4):
+                for p in range(2):
+                    column = lax.rem(d - k + 4, 4) * shard + p * half
+                    h_part = h_refs[j][:, pl.ds(pl.multiple_of(column, half), half)]
+                    acc += jnp.dot(h_part, w_refs[2 * k + p][...], preferred_element_type=jnp.float32)
+            q_s[at, :] = (rotary(acc[:, :128], cos_ref[at, :], sin_ref[at, :]) * HD**-0.5).astype(jnp.bfloat16)
+            k_s[at, :] = rotary(acc[:, 128:256], cos_ref[at, :], sin_ref[at, :]).astype(jnp.bfloat16)
+            v_s[at, 0:128] = acc[:, 256:].astype(jnp.bfloat16)
+            v_s[at, 128:256] = jnp.ones((rows, 128), jnp.bfloat16)
+
+    step = 128
+    for r in range(total // step):
+        start, end = max(0, r * step - HALF_WIN), min(total, (r + 1) * step + HALF_WIN)
+        q_tile = q_s[r * step : (r + 1) * step, :]
+        k_tile = k_s[start:end, :]
+        v_tile = v_s[start:end, :]
+        ahead = lax.broadcasted_iota(jnp.int32, (step, step), 1) - lax.broadcasted_iota(jnp.int32, (step, step), 0)
+        low = lanes(q_tile.shape) < HD
+        heads = []
+        for head in range(1 if folded else 2):
+            q = q_tile if folded else jnp.where(low if head == 0 else ~low, q_tile, jnp.zeros_like(q_tile))
+            scores = lax.dot_general(q, k_tile, (((1,), (1,)), ((), ())), preferred_element_type=jnp.float32)
+            parts = [scores]
+            if start == r * step - HALF_WIN:
+                parts = [jnp.where(ahead >= 0, scores[:, :step], -1e30), scores[:, step:]]
+            if end == (r + 1) * step + HALF_WIN:
+                last = parts.pop()
+                parts += [last[:, :-step], jnp.where(ahead <= 0, last[:, -step:], -1e30)]
+            scores = jnp.concatenate(parts, 1)
+            expo = jnp.exp(scores - jnp.max(scores, 1, keepdims=True)).astype(jnp.bfloat16)
+            o = jnp.dot(expo, v_tile, preferred_element_type=jnp.float32)
+            if folded:
+                heads.append(o / pltpu.roll(o, HD, 1))
+            else:
+                heads.append(o[:, :128] / o[:, 128:])
+        context = heads[0] if folded else jnp.where(low, heads[0], heads[1])
+        c_s[r * step : (r + 1) * step, :] = context.astype(jnp.bfloat16)
+
+    pooled = jnp.dot(member_ref[...], c_s[...], preferred_element_type=jnp.float32)
+    high = pooled.astype(jnp.bfloat16)
+    rest = (pooled - high.astype(jnp.float32)).astype(jnp.bfloat16)
+    per_block = pooled.shape[0] // 4
+    for j in range(4):
+        block = jnp.bitwise_xor(s, j)
+        both = jnp.zeros((2 * per_block, 128), jnp.bfloat16)
+        for b in range(4):
+            cut = slice(b * per_block, (b + 1) * per_block)
+            both = jnp.where(block == b, jnp.concatenate([high[cut], rest[cut]], 0), both)
+        out = out_refs[j]
+        if folded:
+            lo = c_s[pl.ds(pl.multiple_of(block * rows, rows), rows // 2), :].astype(jnp.float32)
+            hi = c_s[pl.ds(pl.multiple_of(block * rows + rows // 2, rows // 2), rows // 2), :].astype(jnp.float32)
+            low = lanes(lo.shape) < HD
+            out[0 : rows // 2, :] = jnp.where(low, lo, pltpu.roll(hi, HD, 1)).astype(jnp.bfloat16)
+            out[rows // 2 :, :] = both
+        else:
+            out[0:rows, :] = c_s[pl.ds(pl.multiple_of(block * rows, rows), rows), :]
+            out[rows:, :] = both
+
+
+def attend(where, blocks, tables, pieces, folded):
+    rows = blocks[0].shape[0]
+    total = 4 * rows
+    width = 128 if folded else 256
+    out_rows = (rows // 2 if folded else rows) + 2 * tables[2].shape[0] // 4
+    vmem = pl.BlockSpec(memory_space=pltpu.VMEM)
+    return pl.pallas_call(
+        functools.partial(attend_kernel, folded, len(pieces)),
+        out_shape=[jax.ShapeDtypeStruct((out_rows, 128), jnp.bfloat16)] * 4,
+        in_specs=[pl.BlockSpec(memory_space=pltpu.SMEM)] + [vmem] * (7 + len(pieces)),
+        out_specs=[vmem] * 4,
+        scratch_shapes=[
+            pltpu.VMEM((total, 128), jnp.bfloat16),
+            pltpu.VMEM((total, 128), jnp.bfloat16),
+            pltpu.VMEM((total, width), jnp.bfloat16),
+            pltpu.VMEM((total, 128), jnp.bfloat16),
+        ],
+        compiler_params=pltpu.CompilerParams(vmem_limit_bytes=40 * 2**20),
+        name="attend_folded" if folded else "attend_tile",
+    )(where, *blocks, *tables, *pieces)
+
+
+def project_kernel(where, h_ref, pool_ref, route_ref, *refs):
+    a_refs, b_refs, w_refs = refs[0:5], refs[5:10], refs[10:16]
+    layer_ref, keep_ref, send_ref, c_s, o_s = refs[16:]
+    s, d, g = where[0], where[1], where[2]
+    rows = h_ref.shape[0]
+    extra = a_refs[0].shape[0] - rows
+    width = c_s.shape[1] // 2
+    other = 1 - g
+    odd = jnp.bitwise_and(s, 1) == 1
+    group_of = (g, other)
+
+    for t in range(2):
+        base = group_of[t] * width
+        a_parts = [r[...] for r in a_refs[0:4]] if t == 0 else [a_refs[4][j] for j in range(4)]
+        b_parts = [r[...] for r in b_refs[0:4]] if t == 0 else [b_refs[4][j] for j in range(4)]
+        for j in range(4):
+            tile = jnp.bitwise_xor(s, j)
+            c_s[:, pl.ds(pl.multiple_of(base + tile * 128, 128), 128)] = a_parts[j]
+        for pair in range(2):
+            tile = 4 + jnp.bitwise_xor(s // 2, pair)
+            one, two = b_parts[2 * pair].astype(jnp.float32), b_parts[2 * pair + 1].astype(jnp.float32)
+            left, right = jnp.where(odd, two, one), jnp.where(odd, one, two)
+            low = lanes(left.shape) < HD
+            first = jnp.where(low, left, pltpu.roll(right, HD, 1)).astype(jnp.bfloat16)
+            second = jnp.where(low, pltpu.roll(left, HD, 1), right).astype(jnp.bfloat16)
+            at = pl.ds(pl.multiple_of(base + tile * 128, 128), 128)
+            c_s[0 : rows // 2, at] = first[0 : rows // 2]
+            c_s[rows // 2 : rows, at] = second[0 : rows // 2]
+            c_s[rows:, at] = first[rows // 2 :]
+
+    feats = w_refs[0].shape[1]
+    per_shard = 4 * feats
+    for p in range(2):
+        shard = lax.rem(d - p + 4, 4)
+        in_half = lax.rem(shard, 2)
+        for j in range(4):
+            source = (w_refs[p], w_refs[4 + p], w_refs[2 + p], w_refs[4 + p])[j]
+            quarter = jnp.bitwise_xor(s, j)
+            total = jnp.zeros((rows + extra, feats), jnp.float32)
+            for t in range(2):
+                if j == 0 or j == 2:
+                    w = source[t]
+                else:
+                    w = source[2 * (j // 2) + t]
+                c = c_s[:, pl.ds(pl.multiple_of(group_of[t] * width, 128), width)]
+                total += lax.dot_general(c, w, (((1,), (1,)), ((), ())), preferred_element_type=jnp.float32)
+            column = pl.multiple_of(in_half * per_shard + quarter * feats, 128)
+            o_s[:, pl.ds(column, feats)] = total[rows:]
+            mine = h_ref[:, pl.ds(pl.multiple_of(g * 2 * per_shard + column, 128), feats)]
+            layer_ref[:, pl.ds(column, feats)] = (mine.astype(jnp.float32) + total[:rows]).astype(jnp.bfloat16)
+
+    half = extra // 2
+    pooled = pool_ref[...] + o_s[0:half] + o_s[half:]
+    routed = jnp.dot(route_ref[...], pooled, precision=lax.Precision.HIGHEST, preferred_element_type=jnp.float32)
+    cut = routed.shape[0] // 2
+    keep_ref[...] = jnp.where(g == 0, routed[:cut], routed[cut:])
+    send_ref[...] = jnp.where(g == 0, routed[cut:], routed[:cut])
+
+
+def project(where, h, pool, route, a_parts, b_parts, w_parts):
+    rows, d_model = h.shape
+    feats = d_model // 2
+    extra = a_parts[0].shape[0] - rows
+    vmem = pl.BlockSpec(memory_space=pltpu.VMEM)
+    slots = route.shape[0] // 2
+    return pl.pallas_call(
+        project_kernel,
+        out_shape=[
+            jax.ShapeDtypeStruct((rows, feats), jnp.bfloat16),
+            jax.ShapeDtypeStruct((slots, feats), jnp.float32),
+            jax.ShapeDtypeStruct((slots, feats), jnp.float32),
+        ],
+        in_specs=[pl.BlockSpec(memory_space=pltpu.SMEM)] + [vmem] * 19,
+        out_specs=[vmem] * 3,
+        scratch_shapes=[
+            pltpu.VMEM((rows + extra, 2 * w_parts[0].shape[2]), jnp.bfloat16),
+            pltpu.VMEM((extra, feats), jnp.float32),
+        ],
+        compiler_params=pltpu.CompilerParams(vmem_limit_bytes=40 * 2**20),
+        name="project",
+    )(where, h, pool, route, *a_parts, *b_parts, *w_parts)
+
+
+def xor_send(value, axis, j):
+    return lax.ppermute(value, axis, [(i, i ^ j) for i in range(lax.axis_size(axis))])
+
+
+def ring_send(value):
+    count = lax.axis_size("dp")
+    return lax.ppermute(value, "dp", [(i, (i + 1) % count) for i in range(count)])
+
+
+def after(value, *earlier):
+    return lax.optimization_barrier((value, *earlier))[0]
+
+
+def body_by_heads(hidden, proj_weight, stretch_lengths, shard_of):
+    h = hidden[0]
+    rows = h.shape[0]
+    shard = proj_weight.shape[1]
+    s, d, g = lax.axis_index("seq"), lax.axis_index("dp"), lax.axis_index("index")
+    where = jnp.stack([s, d, g]).astype(jnp.int32)
+    total = 4 * rows
+
+    mine = lax.dynamic_slice_in_dim(proj_weight[:3], s * 128, 128, 2)
+    tile = jnp.concatenate([mine[0], mine[1], mine[2]], 1)
+    a_ring = [[tile[: shard // 2], tile[shard // 2 :]]]
+    pair = lax.dynamic_slice_in_dim(proj_weight[:3], (4 + s // 2) * 128, 128, 2)
+    one = jnp.where(s % 2 == 1, pair[:, :, HD:], pair[:, :, :HD])
+    top, bottom = one[:, : shard // 2], one[:, shard // 2 :]
+    b_ring = [jnp.concatenate([top[0], top[1], bottom[0], bottom[1], top[2], bottom[2]], 1)]
+    o_ring = [lax.dynamic_slice_in_dim(proj_weight[3], s * (shard // 4), shard // 4, 0)]
+
+    h_cross = xor_send(h, "seq", 2)
+    h_core = xor_send(h, "seq", 1)
+
+    for step in range(3):
+        a_ring.append([ring_send(a_ring[-1][0]), ring_send(a_ring[-1][1])])
+    h_far = xor_send(h_cross, "seq", 1)
+    blocks = [h, h_core, h_cross, h_far]
+
+    for step in range(3):
+        o_ring.append(ring_send(o_ring[-1]))
+        b_ring.append(ring_send(b_ring[-1]))
+
+    freqs = 10000.0 ** (-2.0 * jnp.arange(HD // 2, dtype=jnp.float32) / HD)
+    angles = jnp.arange(total, dtype=jnp.float32)[:, None] * freqs[None, :]
+    cosine, sine = jnp.cos(angles), jnp.sin(angles)
+    cos_table = jnp.concatenate([cosine] * 4, 1)
+    sin_table = jnp.concatenate([-sine, sine] * 2, 1)
+    lengths = stretch_lengths[0]
+    count = lengths.shape[0]
+    per_block = count // 4
+    ends = jnp.cumsum(lengths, dtype=jnp.int32)
+    row_ids = jnp.arange(count, dtype=jnp.int32)
+    order = row_ids % per_block * 4 + row_ids // per_block
+    row_ends = ends[order]
+    row_starts = row_ends - lengths[order]
+    positions = jnp.arange(total, dtype=jnp.int32)
+    member = (positions[None, :] >= row_starts[:, None]) & (positions[None, :] < row_ends[:, None])
+    member = member.astype(jnp.bfloat16)
+    tables = (cos_table, sin_table, member)
+
+    own_member = lax.dynamic_slice_in_dim(member, s * per_block, per_block, 0)
+    feats = h.shape[1] // 2
+    pool = jnp.zeros((per_block, feats), jnp.float32)
+    for j in range(4):
+        part = lax.dynamic_slice_in_dim(blocks[j], g * feats, feats, 1)
+        rows_of = lax.dynamic_slice_in_dim(own_member, (s ^ j) * rows, rows, 1)
+        pool += jnp.dot(rows_of, part, preferred_element_type=jnp.float32)
+
+    shard_ids = shard_of[0, :, 0]
+    local = jnp.arange(per_block, dtype=jnp.int32)
+    earlier = (shard_ids[:, None] == shard_ids[None, :]) & (local[None, :] < local[:, None])
+    rank = jnp.sum(earlier.astype(jnp.int32), 1)
+    capacity = per_block // 2
+    slot = jnp.arange(2 * capacity, dtype=jnp.int32)
+    route = (shard_ids * capacity + rank)[None, :] == slot[:, None]
+    route = route.astype(jnp.float32)
+
+    a_out = attend(where, blocks, tables, [piece for step in a_ring for piece in step], False)
+    a_parts = [a_out[0]] + [xor_send(a_out[j], "seq", j) for j in (1, 2, 3)]
+    a_parts.append(xor_send(jnp.stack(a_parts), "index", 1))
+
+    own, cross, near = [], [], []
+    for p in range(2):
+        first_mine = (d - p) % 4 // 2 == g
+        keep = jnp.where(first_mine, o_ring[p], o_ring[p + 2])
+        send = jnp.where(first_mine, o_ring[p + 2], o_ring[p])
+        both = jnp.stack([keep, xor_send(send, "index", 1)])
+        over = xor_send(both, "seq", 2)
+        own.append(both)
+        cross.append(over)
+        near.append(xor_send(jnp.concatenate([both, over]), "seq", 1))
+
+    b_out = attend(where, blocks, tables, b_ring, True)
+    b_parts = [b_out[0]] + [xor_send(b_out[j], "seq", j) for j in (1, 2, 3)]
+    b_parts.append(xor_send(jnp.stack(b_parts), "index", 1))
+
+    layer, keep, send = project(where, h, pool, route, a_parts, b_parts, own + cross + near)
+    arrived = xor_send(send, "index", 1)
+    square = (jnp.sum(keep * keep, -1, keepdims=True) + jnp.sum(arrived * arrived, -1, keepdims=True)) / (2 * feats)
+    scale = lax.rsqrt(square + 1e-06)
+    shelf = jnp.concatenate([jnp.where(g == 0, keep, arrived), jnp.where(g == 0, arrived, keep)], 1) * scale
+    return (layer[None], shelf[None, None, None])
+
+
 def solution(mesh):
     in_specs = (P("dp", "seq", None), P(None, "dp", "index"), P("dp", None), P("dp", "seq", None))
     out_specs = (P("dp", "seq", "index"), P("dp", "seq", "index", None, None))
-    return jax.shard_map(body, mesh=mesh, in_specs=in_specs, out_specs=out_specs, check_vma=False)
+
+    def whole(hidden, proj_weight, stretch_lengths, shard_of):
+        heads = proj_weight.shape[2] // HD // mesh.shape["index"]
+        rows = hidden.shape[1] // mesh.shape["seq"]
+        by_heads = (mesh.shape["dp"], mesh.shape["seq"], mesh.shape["index"], heads, rows) == (4, 4, 2, 12, 256)
+        return jax.shard_map(
+            body_by_heads if by_heads else body,
+            mesh=mesh,
+            in_specs=in_specs,
+            out_specs=out_specs,
+            check_vma=False,
+        )(hidden, proj_weight, stretch_lengths, shard_of)
+
+    return whole

time: 338 us -> 117 us (0.35)
  waiting for transfers between devices: 223 us -> 44.9 us
  matrix products: 52.4 us -> 4.61 us
  Pallas kernels: 0 us -> 16.2 us
  starting transfers between devices: 7.56 us -> 21.5 us
  local copies, waits for them, and re-layouts: 23.6 us -> 10.4 us
  between operations: 14 us -> 0.91 us
    all_gather x2 -> x0, waiting for transfers between devices: 181 us -> none  [the longest x1 168 us: body(): lax.all_gather(proj_weight[:3], 'dp', axis=1, tiled=True)]
    dot_general x28 -> x4, matrix products: 52.4 us -> 4.61 us  [body_by_heads(): pool += jnp.dot(rows_of, part, preferred_element_type=jnp.float32)]
    ppermute x2 -> x30, waiting for transfers between devices: 2.28 us -> 44.9 us  [the longest x12 30.8 us: ring_send(): lax.ppermute(value, 'dp', [(i, (i + 1) % count) for i in range(count)])]
    reduce_scatter x2 -> x0, waiting for transfers between devices: 37.6 us -> none  [the longest x1 20.4 us: body(): lax.psum_scatter(partial_pool.astype(jnp.bfloat16), 'seq', scatter_dimens...]
    ppermute x2 -> x30, starting transfers between devices: 4.14 us -> 21.5 us  [the longest x18 14.9 us: xor_send(): lax.ppermute(value, axis, [(i, i ^ j) for i in range(lax.axis_size(axis))])]
    pallas_call x0 -> x3, Pallas kernels: none -> 16.2 us  [the longest x2 12 us: attend(): pl.pallas_call(functools.partial(attend_kernel, folded, len(pieces)), out...]
    unnamed x15 -> x24, local copies, waits for them, and re-layouts: 9.62 us -> 0.05 us
    concatenate x1 -> x5, other arithmetic: 1.64 us -> 5.68 us  [the longest x1 3.23 us: body_by_heads(): cos_table = jnp.concatenate([cosine] * 4, 1)]
  transfers between devices with their start and end apart: 7 -> 30, of which waited for: 6 -> 15; matrix products, arithmetic and copies ran while one was open for 16% -> 28% of each run, Pallas kernels for 0% -> 10%
where the time goes in v1:
time: 117 us
  waiting for transfers between devices  44.9 us (38%)
  starting transfers between devices  21.5 us (18%)
  other arithmetic  18.4 us (16%)
  Pallas kernels  16.2 us (14%)
  local copies, waits for them, and re-layouts  10.4 us (9%)
  matrix products  4.61 us (4%)
    ppermute x12, waiting for transfers between devices, ring_send(): lax.ppermute(value, 'dp', [(i, (i + 1) % count) for i in range(count)])  30.8 us
    ppermute x18, starting transfers between devices, xor_send(): lax.ppermute(value, axis, [(i, i ^ j) for i in range(lax.axis_size(axis))])  14.9 us
    ppermute x18, waiting for transfers between devices, xor_send(): lax.ppermute(value, axis, [(i, i ^ j) for i in range(lax.axis_size(axis))])  14.1 us
    pallas_call x2, Pallas kernels, attend(): pl.pallas_call(functools.partial(attend_kernel, folded, len(pieces)), out...  12 us
    ppermute x12, starting transfers between devices, ring_send(): lax.ppermute(value, 'dp', [(i, (i + 1) % count) for i in range(count)])  6.63 us
    another operation x4, other arithmetic, body_by_heads(): both = jnp.stack([keep, xor_send(send, 'index', 1)])  6.35 us
    dot_general x4, matrix products, body_by_heads(): pool += jnp.dot(rows_of, part, preferred_element_type=jnp.float32)  4.61 us
    pallas_call x1, Pallas kernels, project(): pl.pallas_call(project_kernel, out_shape=[jax.ShapeDtypeStruct((rows, fea...  4.2 us
  transfers between devices with their start and end apart: 30, of which 15 were waited for; matrix products, arithmetic and copies ran while one was open for 28% of the time, Pallas kernels for 10%

profile of v1, /device:TPU:0, one launch (start us, length us, event | category | flops | bytes accessed | tf_op | source)
XLA Modules:
  0.0 116.9 jit_solution(15707229679617954071)
XLA Ops:
  0.6 0.5 collective-permute-start
  1.1 2.6 %collective-permute-start.1 = (bf16[256,2048]{1,0:T(8,128)(2,1)}, bf16[256,2048]{1,0:T(8,128)(2,1)S(1)}, u32[]{:S(2)}, u32[]{:S(2)}) collective-permute-start(bf16[256,2048]{1,0:T(8,128)(2,1)} %bitcast.55), channel_id=1, source_target_pairs={{0,4},{2,6},{4,0},{6,2},{1,5},{3,7},{5,1},{7,3},{8,12},{10,14},{12... | collective-permute-start | bytes 3145736 | tf_op jit(solution)/shard_map/ppermute | solution.py:353
  3.7 3.2 %slice.54 = bf16[3,512,768]{2,1,0:T(8,128)(2,1)} slice(bf16[4,512,768]{2,1,0:T(8,128)(2,1)} %param.5), slice={[0:3], [0:512], [0:768]} | slice | bytes 4718592 | tf_op jit(solution)/shard_map/slice | solution.py:373
  7.0 1.1 dynamic-slice_bitcast_fusion.3
  8.2 1.6 %collective-permute-start.3 = (bf16[256,384]{1,0:T(8,128)(2,1)S(1)}, bf16[256,384]{1,0:T(8,128)(2,1)}, u32[]{:S(2)}, u32[]{:S(2)}) collective-permute-start(bf16[256,384]{1,0:T(8,128)(2,1)S(1)} %get-tuple-element.38.refs_8_), channel_id=1, source_target_pairs={{0,8},{8,16},{16,24},{24,0},{1,9},{9,17},{17,25},{25,1},{2,10},{10... | collective-permute-start | bytes 589832 | tf_op jit(solution)/shard_map/ppermute | solution.py:358
  9.8 1.6 %collective-permute-start.4 = (bf16[256,384]{1,0:T(8,128)(2,1)S(1)}, bf16[256,384]{1,0:T(8,128)(2,1)}, u32[]{:S(2)}, u32[]{:S(2)}) collective-permute-start(bf16[256,384]{1,0:T(8,128)(2,1)S(1)} %get-tuple-element.37.refs_9_), channel_id=1, source_target_pairs={{0,8},{8,16},{16,24},{24,0},{1,9},{9,17},{17,25},{25,1},{2,10},{10... | collective-permute-start | bytes 589832 | tf_op jit(solution)/shard_map/ppermute | solution.py:358
  11.4 1.2 %slice.68 = bf16[1,512,768]{2,1,0:T(8,128)(2,1)S(1)} slice(bf16[4,512,768]{2,1,0:T(8,128)(2,1)} %param.5), slice={[3:4], [0:512], [0:768]} | slice | bytes 1572864 | tf_op jit(solution)/shard_map/slice | solution.py:380
  12.6 0.8 dynamic-slice_bitcast_fusion
  13.4 1.6 %collective-permute-start.20 = (bf16[128,768]{1,0:T(8,128)(2,1)}, bf16[128,768]{1,0:T(8,128)(2,1)}, u32[]{:S(2)}, u32[]{:S(2)}) collective-permute-start(bf16[128,768]{1,0:T(8,128)(2,1)} %dynamic-slice_bitcast_fusion), channel_id=1, source_target_pairs={{0,8},{8,16},{16,24},{24,0},{1,9},{9,17},{17,25},{25,1},{2,10},{10... | collective-permute-start | bytes 589832 | tf_op jit(solution)/shard_map/ppermute | solution.py:358
  15.3 0.7 gather_fusion
  16.0 0.7 gather_fusion.1
  16.7 2.9 %fusion.8 = (f32[1024,32]{1,0:T(8,128)}, f32[1024,32]{1,0:T(8,128)}, f32[1024,32]{1,0:T(8,128)}) fusion(f32[32]{0:T(128)S(1)} %multiply_power_fusion), kind=kLoop, calls=%fused_computation.23 | loop fusion | flops 65536 | bytes 393344 | tf_op jit(solution)/shard_map/neg | solution.py:398
  19.6 1.5 %dynamic-slice_select_fusion = bf16[3,512,64]{2,1,0:T(8,128)(2,1)S(1)} fusion(bf16[3,512,768]{2,1,0:T(8,128)(2,1)} %slice.54, s32[]{:T(128)S(6)} %select_n.167, s32[]{:T(128)S(6)} %add.162, pred[]{:T(512)S(6)} %eq.48), kind=kLoop, calls=%fused_computation.18 | loop fusion | flops 98304 | bytes 589833 | tf_op jit(solution)/shard_map/jit(_where)/select_n | solution.py:377
  21.1 0.7 slice_bitcast_fusion
  21.8 0.7 fusion.23
  22.6 0.2 convert_reduce_fusion
  22.8 2.8 %collective-permute-done.20 = bf16[128,768]{1,0:T(8,128)(2,1)} collective-permute-done((bf16[128,768]{1,0:T(8,128)(2,1)}, bf16[128,768]{1,0:T(8,128)(2,1)}, u32[]{:S(2)}, u32[]{:S(2)}) %collective-permute-start.20) | collective-permute-done | bytes 196640 | tf_op jit(solution)/shard_map/ppermute | solution.py:358
  25.6 8.2 %collective-permute-done.21 = bf16[128,768]{1,0:T(8,128)(2,1)S(1)} collective-permute-done((bf16[128,768]{1,0:T(8,128)(2,1)}, bf16[128,768]{1,0:T(8,128)(2,1)S(1)}, u32[]{:S(2)}, u32[]{:S(2)}) %collective-permute-start.21) | collective-permute-done | bytes 196640 | tf_op jit(solution)/shard_map/ppermute | solution.py:358
  33.8 1.7 %select_bitcast_fusion.1 = (bf16[1,128,768]{2,1,0:T(8,128)(2,1)}, bf16[128,768]{1,0:T(8,128)(2,1)}) fusion(bf16[128,768]{1,0:T(8,128)(2,1)S(1)} %collective-permute-done.21, pred[]{:T(512)S(6)} %eq.49, bf16[1,512,768]{2,1,0:T(8,128)(2,1)} %copy-done.7, s32[]{:T(128)S(6)} %select_n.172), kind=kLoop, calls=%fused_computation.25 | loop fusion | flops 196608 | bytes 786437 | tf_op jit(solution)/shard_map/stack | solution.py:438
  35.5 5.7 %collective-permute-done.23 = bf16[128,768]{1,0:T(8,128)(2,1)S(1)} collective-permute-done((bf16[128,768]{1,0:T(8,128)(2,1)S(1)}, bf16[128,768]{1,0:T(8,128)(2,1)S(1)}, u32[]{:S(2)}, u32[]{:S(2)}) %collective-permute-start.23) | collective-permute-done | bytes 196640 | tf_op jit(solution)/shard_map/ppermute | solution.py:358
  41.3 1.5 %collective-permute-start.22 = (bf16[128,768]{1,0:T(8,128)(2,1)}, bf16[128,768]{1,0:T(8,128)(2,1)}, u32[]{:S(2)}, u32[]{:S(2)}) collective-permute-start(bf16[128,768]{1,0:T(8,128)(2,1)} %get-tuple-element.30), channel_id=1, source_target_pairs={{0,1},{1,0},{2,3},{3,2},{4,5},{5,4},{6,7},{7,6},{8,9},{9,8},{10,11... | collective-permute-start | bytes 589832 | tf_op jit(solution)/shard_map/ppermute | solution.py:353
  42.8 1.7 %select_bitcast_fusion = (bf16[1,128,768]{2,1,0:T(8,128)(2,1)}, bf16[128,768]{1,0:T(8,128)(2,1)}) fusion(bf16[128,768]{1,0:T(8,128)(2,1)} %collective-permute-done.20, bf16[128,768]{1,0:T(8,128)(2,1)S(1)} %collective-permute-done.23, pred[]{:T(512)S(6)} %eq.50), kind=kLoop, calls=%fused_computation.24 | loop fusion | flops 196608 | bytes 786433 | tf_op jit(solution)/shard_map/stack | solution.py:438
  44.5 0.5 collective-permute-start.24
  45.0 1.8 %concatenate.37.refs_8_ = bf16[256,384]{1,0:T(8,128)(2,1)} concatenate(bf16[256,64]{1,0:T(8,128)(2,1)} %get-tuple-element.36, bf16[256,64]{1,0:T(8,128)(2,1)} %get-tuple-element.35, bf16[256,64]{1,0:T(8,128)(2,1)} %get-tuple-element.34, bf16[256,64]{1,0:T(8,128)(2,1)} %get-tuple-element.33, bf16[256,64]{1,0:T(8,128)(2,1)} %get-tuple-element.32, bf16[256,64]{1,0:T(8,128)(2,1)} %get-tuple-element.31), dimensions={1} | concatenate | bytes 393216 | tf_op jit(solution)/shard_map/concatenate | solution.py:379
  46.9 1.8 %collective-permute-done.22 = bf16[128,768]{1,0:T(8,128)(2,1)} collective-permute-done((bf16[128,768]{1,0:T(8,128)(2,1)}, bf16[128,768]{1,0:T(8,128)(2,1)}, u32[]{:S(2)}, u32[]{:S(2)}) %collective-permute-start.22) | collective-permute-done | bytes 196640 | tf_op jit(solution)/shard_map/ppermute | solution.py:353
  48.7 1.1 pad_maximum_fusion.5.refs_10_
  49.8 1.0 collective-permute-done.24
  50.8 0.5 collective-permute-start.25
  51.4 1.8 %pad_maximum_fusion.6.refs_11_ = bf16[2,128,768]{2,1,0:T(8,128)(2,1)} fusion(bf16[1,128,768]{2,1,0:T(8,128)(2,1)} %bitcast.30, bf16[1,128,768]{2,1,0:T(8,128)(2,1)} %get-tuple-element.27), kind=kLoop, calls=%fused_computation.21 | loop fusion | flops 196608 | bytes 786432 | tf_op jit(solution)/shard_map/stack | solution.py:438
  53.2 1.5 %collective-permute-done.13.refs_9_ = bf16[256,384]{1,0:T(8,128)(2,1)} collective-permute-done((bf16[256,384]{1,0:T(8,128)(2,1)}, bf16[256,384]{1,0:T(8,128)(2,1)}, u32[]{:S(2)}, u32[]{:S(2)}) %collective-permute-start.13) | collective-permute-done | bytes 196640 | tf_op jit(solution)/shard_map/ppermute | solution.py:358
  54.7 2.1 %collective-permute-done.5.refs_12_ = bf16[256,384]{1,0:T(8,128)(2,1)} collective-permute-done((bf16[256,384]{1,0:T(8,128)(2,1)}, bf16[256,384]{1,0:T(8,128)(2,1)}, u32[]{:S(2)}, u32[]{:S(2)}) %collective-permute-start.5) | collective-permute-done | bytes 196640 | tf_op jit(solution)/shard_map/ppermute | solution.py:358
  56.8 1.1 collective-permute-start.26
  57.9 1.5 %fusion = f32[8,1024]{1,0:T(8,128)} fusion(bf16[1,256,2048]{2,1,0:T(8,128)(2,1)S(1)} %copy-done, s32[]{:T(128)S(6)} %select_n.156, pred[32,1024]{1,0:T(8,128)(4,1)} %get-tuple-element.44, s32[]{:T(128)S(6)} %select_n.153, s32[]{:T(128)S(6)} %select_n.155), kind=kOutput, calls=%fused_computation.9 | convolution fusion | flops 4194304 | bytes 559116 | tf_op jit(solution)/shard_map/dot_general | solution.py:418
  59.4 3.2 %pad_maximum_fusion.2 = (f32[1024,128]{1,0:T(8,128)S(1)}, f32[1024,128]{1,0:T(8,128)S(1)}) fusion(f32[1024,32]{1,0:T(8,128)} %get-tuple-element.47, f32[1024,32]{1,0:T(8,128)} %get-tuple-element.46, f32[1024,32]{1,0:T(8,128)} %get-tuple-element.45), kind=kLoop, calls=%fused_computation.7 | loop fusion | flops 786432 | bytes 1441792 | tf_op jit(solution)/shard_map/concatenate | solution.py:397
  62.8 0.2 collective-permute-done.25.refs_12_
  63.0 0.6 collective-permute-start.7
  63.6 1.1 pad_maximum_fusion
  64.7 5.7 %collective-permute-done.14.refs_10_ = bf16[256,384]{1,0:T(8,128)(2,1)S(1)} collective-permute-done((bf16[256,384]{1,0:T(8,128)(2,1)}, bf16[256,384]{1,0:T(8,128)(2,1)S(1)}, u32[]{:S(2)}, u32[]{:S(2)}) %collective-permute-start.14) | collective-permute-done | bytes 196640 | tf_op jit(solution)/shard_map/ppermute | solution.py:358
  70.4 0.4 collective-permute-start.8
  70.8 0.8 collective-permute-start.15
  71.5 1.1 pad_maximum_fusion.1
  72.7 1.7 %collective-permute-done.7.refs_14_ = bf16[256,384]{1,0:T(8,128)(2,1)S(1)} collective-permute-done((bf16[256,384]{1,0:T(8,128)(2,1)}, bf16[256,384]{1,0:T(8,128)(2,1)S(1)}, u32[]{:S(2)}, u32[]{:S(2)}) %collective-permute-start.7) | collective-permute-done | bytes 196640 | tf_op jit(solution)/shard_map/ppermute | solution.py:358
  74.4 0.5 collective-permute-start.28
  74.9 0.9 convolution_add_fusion.2
  75.8 3.0 %collective-permute-done.8.refs_15_ = bf16[256,384]{1,0:T(8,128)(2,1)S(1)} collective-permute-done((bf16[256,384]{1,0:T(8,128)(2,1)}, bf16[256,384]{1,0:T(8,128)(2,1)S(1)}, u32[]{:S(2)}, u32[]{:S(2)}) %collective-permute-start.8) | collective-permute-done | bytes 196640 | tf_op jit(solution)/shard_map/ppermute | solution.py:358
  78.8 6.5 %attend_tile.1 = (bf16[272,128]{1,0:T(8,128)(2,1)S(1)}, bf16[272,128]{1,0:T(8,128)(2,1)S(1)}, bf16[272,128]{1,0:T(8,128)(2,1)S(1)}, bf16[272,128]{1,0:T(8,128)(2,1)S(1)}) custom-call(s32[3]{0:T(128)S(1)} %pad_add_fusion.refs_0_.where, bf16[256,2048]{1,0:T(8,128)(2,1)S(1)} %bitcast.56, bf16[256,2048]{1,0:T(8,128)(2,1)S(1)} %collective-permute-done.refs_2_, ...), custom_call_target="tpu_custom_call" | custom-call | tf_op jit(solution)/shard_map/attend_tile/pallas_call | solution.py:253
  85.4 1.5 %collective-permute-start.10 = (bf16[272,128]{1,0:T(8,128)(2,1)S(1)}, bf16[272,128]{1,0:T(8,128)(2,1)S(1)}, u32[]{:S(2)}, u32[]{:S(2)}) collective-permute-start(bf16[272,128]{1,0:T(8,128)(2,1)S(1)} %get-tuple-element.15), channel_id=1, source_target_pairs={{0,4},{2,6},{4,0},{6,2},{1,5},{3,7},{5,1},{7,3},{8,12},{10,14},{12... | collective-permute-start | bytes 208904 | tf_op jit(solution)/shard_map/ppermute | solution.py:353
  86.8 0.4 collective-permute-start.11
  87.3 0.9 convolution_add_fusion.1
  88.2 5.5 %attend_folded.1 = (bf16[144,128]{1,0:T(8,128)(2,1)S(1)}, bf16[144,128]{1,0:T(8,128)(2,1)S(1)}, bf16[144,128]{1,0:T(8,128)(2,1)S(1)}, bf16[144,128]{1,0:T(8,128)(2,1)S(1)}) custom-call(s32[3]{0:T(128)S(1)} %pad_add_fusion.refs_0_.where, bf16[256,2048]{1,0:T(8,128)(2,1)S(1)} %bitcast.57, bf16[256,2048]{1,0:T(8,128)(2,1)S(1)} %collective-permute-done.refs_2_, ...), custom_call_target="tpu_custom_call" | custom-call | tf_op jit(solution)/shard_map/attend_folded/pallas_call | solution.py:253
  93.7 0.4 collective-permute-start.16
  94.1 1.4 %collective-permute-start.17 = (bf16[144,128]{1,0:T(8,128)(2,1)S(1)}, bf16[144,128]{1,0:T(8,128)(2,1)S(1)}, u32[]{:S(2)}, u32[]{:S(2)}) collective-permute-start(bf16[144,128]{1,0:T(8,128)(2,1)S(1)} %get-tuple-element.19), channel_id=1, source_target_pairs={{0,4},{2,6},{4,0},{6,2},{1,5},{3,7},{5,1},{7,3},{8,12},{10,14},{12... | collective-permute-start | bytes 110600 | tf_op jit(solution)/shard_map/ppermute | solution.py:353
  95.5 0.1 collective-permute-start.18
  95.6 1.3 %collective-permute-start.12 = (bf16[4,272,128]{2,1,0:T(8,128)(2,1)S(1)}, bf16[4,272,128]{2,1,0:T(8,128)(2,1)S(1)}, u32[]{:S(2)}, u32[]{:S(2)}) collective-permute-start(bf16[4,272,128]{2,1,0:T(8,128)(2,1)S(1)} %pad_maximum_fusion.7), channel_id=1, source_target_pairs={{0,1},{1,0},{2,3},{3,2},{4,5},{5,4},{6,7},{7,6},{8,9},{9,8},{10,11... | collective-permute-start | bytes 835592 | tf_op jit(solution)/shard_map/ppermute | solution.py:353
  97.0 1.0 collective-permute-done.17.refs_7_
  98.0 1.1 collective-permute-done.18.refs_8_
  99.2 1.2 collective-permute-start.19
  100.3 1.3 %convolution_add_fusion.pool_ref = f32[8,1024]{1,0:T(8,128)S(1)} fusion(f32[8,1024]{1,0:T(8,128)S(1)} %convolution_add_fusion.1, bf16[256,2048]{1,0:T(8,128)(2,1)} %collective-permute-done.2.refs_4_, s32[]{:T(128)S(6)} %select_n.156, pred[32,1024]{1,0:T(8,128)(4,1)} %get-tuple-element.44, s32[]{:T(128)S(6)} %select_n.153, s32[]{:T(128)S(6)} %select_n.162), kind=kOutput, calls=%fused_computation.2 | convolution fusion | flops 4202496 | bytes 591884 | tf_op jit(solution)/shard_map/dot_general | solution.py:418
  101.6 6.4 %collective-permute-done.19.refs_9_ = bf16[4,144,128]{2,1,0:T(8,128)(2,1)S(1)} collective-permute-done((bf16[4,144,128]{2,1,0:T(8,128)(2,1)S(1)}, bf16[4,144,128]{2,1,0:T(8,128)(2,1)S(1)}, u32[]{:S(2)}, u32[]{:S(2)}) %collective-permute-start.19) | collective-permute-done | bytes 147488 | tf_op jit(solution)/shard_map/ppermute | solution.py:353
  108.0 4.2 %project.1 = (bf16[256,1024]{1,0:T(8,128)(2,1)}, f32[4,1024]{1,0:T(4,128)S(1)}, f32[4,1024]{1,0:T(4,128)S(1)}) custom-call(s32[3]{0:T(128)S(1)} %pad_add_fusion.refs_0_.where, bf16[256,2048]{1,0:T(8,128)(2,1)S(1)} %bitcast.58, f32[8,1024]{1,0:T(8,128)S(1)} %convolution_add_fusion.pool_ref, f32[8,8]{1,0:T(8,128)S(1)} %fusion.15.route_ref, ...), custom_call_target="tpu_custom_call" | custom-call | tf_op jit(solution)/shard_map/project/pallas_call | solution.py:334
  112.2 1.3 %collective-permute-start.29 = (f32[4,1024]{1,0:T(4,128)S(1)}, f32[4,1024]{1,0:T(4,128)S(1)}, u32[]{:S(2)}, u32[]{:S(2)}) collective-permute-start(f32[4,1024]{1,0:T(4,128)S(1)} %get-tuple-element.23), channel_id=1, source_target_pairs={{0,1},{1,0},{2,3},{3,2},{4,5},{5,4},{6,7},{7,6},{8,9},{9,8},{10,11... | collective-permute-start | bytes 49160 | tf_op jit(solution)/shard_map/ppermute | solution.py:353
  113.5 2.5 %collective-permute-done.29 = f32[4,1024]{1,0:T(4,128)S(1)} collective-permute-done((f32[4,1024]{1,0:T(4,128)S(1)}, f32[4,1024]{1,0:T(4,128)S(1)}, u32[]{:S(2)}, u32[]{:S(2)}) %collective-permute-start.29) | collective-permute-done | bytes 16416 | tf_op jit(solution)/shard_map/ppermute | solution.py:353
  116.0 0.2 select_bitcast_fusion.3
  116.2 0.7 maximum_multiply_fusion
  (63 shorter events, 0.8 us)
Async XLA Ops:
  0.6 73.8 %collective-permute-start = (bf16[256,2048]{1,0:T(8,128)(2,1)}, bf16[256,2048]{1,0:T(8,128)(2,1)S(1)}, u32[]{:S(2)}, u32[]{:S(2)}) collective-permute-start(bf16[256,2048]{1,0:T(8,128)(2,1)} %bitcast.54), channel_id=1, source_target_pairs={{0,2},{2,0},{4,6},{6,4},{1,3},{3,1},{5,7},{7,5},{8,10},{10,8},{12,... | collective-permute-start | bytes 3145736 | tf_op jit(solution)/shard_map/ppermute | solution.py:353
  1.1 47.6 %collective-permute-start.1 = (bf16[256,2048]{1,0:T(8,128)(2,1)}, bf16[256,2048]{1,0:T(8,128)(2,1)S(1)}, u32[]{:S(2)}, u32[]{:S(2)}) collective-permute-start(bf16[256,2048]{1,0:T(8,128)(2,1)} %bitcast.55), channel_id=1, source_target_pairs={{0,4},{2,6},{4,0},{6,2},{1,5},{3,7},{5,1},{7,3},{8,12},{10,14},{12... | collective-permute-start | bytes 3145736 | tf_op jit(solution)/shard_map/ppermute | solution.py:353
  6.9 8.0 %copy-start.6 = (s32[1,32]{1,0:T(1,128)S(1)}, s32[1,32]{1,0:T(1,128)}, u32[]{:S(2)}) copy-start(s32[1,32]{1,0:T(1,128)} %param.6) | copy-start | bytes 388
  8.1 11.5 %copy-start.1 = (bf16[256,384]{1,0:T(8,128)(2,1)}, bf16[256,384]{1,0:T(8,128)(2,1)S(1)}, u32[]{:S(2)}) copy-start(bf16[256,384]{1,0:T(8,128)(2,1)S(1)} %get-tuple-element.37.refs_9_) | copy-start | bytes 589828
  8.2 11.4 %copy-start.3 = (bf16[256,384]{1,0:T(8,128)(2,1)}, bf16[256,384]{1,0:T(8,128)(2,1)S(1)}, u32[]{:S(2)}) copy-start(bf16[256,384]{1,0:T(8,128)(2,1)S(1)} %get-tuple-element.38.refs_8_) | copy-start | bytes 589828
  8.2 36.4 %collective-permute-start.3 = (bf16[256,384]{1,0:T(8,128)(2,1)S(1)}, bf16[256,384]{1,0:T(8,128)(2,1)}, u32[]{:S(2)}, u32[]{:S(2)}) collective-permute-start(bf16[256,384]{1,0:T(8,128)(2,1)S(1)} %get-tuple-element.38.refs_8_), channel_id=1, source_target_pairs={{0,8},{8,16},{16,24},{24,0},{1,9},{9,17},{17,25},{25,1},{2,10},{10... | collective-permute-start | bytes 589832 | tf_op jit(solution)/shard_map/ppermute | solution.py:358
  9.8 37.1 %collective-permute-start.4 = (bf16[256,384]{1,0:T(8,128)(2,1)S(1)}, bf16[256,384]{1,0:T(8,128)(2,1)}, u32[]{:S(2)}, u32[]{:S(2)}) collective-permute-start(bf16[256,384]{1,0:T(8,128)(2,1)S(1)} %get-tuple-element.37.refs_9_), channel_id=1, source_target_pairs={{0,8},{8,16},{16,24},{24,0},{1,9},{9,17},{17,25},{25,1},{2,10},{10... | collective-permute-start | bytes 589832 | tf_op jit(solution)/shard_map/ppermute | solution.py:358
  12.6 2.5 %copy-start.7 = (bf16[1,512,768]{2,1,0:T(8,128)(2,1)}, bf16[1,512,768]{2,1,0:T(8,128)(2,1)S(1)}, u32[]{:S(2)}) copy-start(bf16[1,512,768]{2,1,0:T(8,128)(2,1)S(1)} %slice.68) | copy-start | bytes 2359300
  13.4 12.2 %collective-permute-start.20 = (bf16[128,768]{1,0:T(8,128)(2,1)}, bf16[128,768]{1,0:T(8,128)(2,1)}, u32[]{:S(2)}, u32[]{:S(2)}) collective-permute-start(bf16[128,768]{1,0:T(8,128)(2,1)} %dynamic-slice_bitcast_fusion), channel_id=1, source_target_pairs={{0,8},{8,16},{16,24},{24,0},{1,9},{9,17},{17,25},{25,1},{2,10},{10... | collective-permute-start | bytes 589832 | tf_op jit(solution)/shard_map/ppermute | solution.py:358
  15.2 7.3 %copy-start.11 = (s32[1,8,1]{1,2,0:T(1,128)S(1)}, s32[1,8,1]{1,2,0:T(1,128)}, u32[]{:S(2)}) copy-start(s32[1,8,1]{1,2,0:T(1,128)} %param.7) | copy-start | bytes 100
  21.1 36.8 %copy-start = (bf16[1,256,2048]{2,1,0:T(8,128)(2,1)S(1)}, bf16[1,256,2048]{2,1,0:T(8,128)(2,1)}, u32[]{:S(2)}) copy-start(bf16[1,256,2048]{2,1,0:T(8,128)(2,1)} %param.4) | copy-start | bytes 3145732
  25.6 8.2 %collective-permute-start.21 = (bf16[128,768]{1,0:T(8,128)(2,1)}, bf16[128,768]{1,0:T(8,128)(2,1)S(1)}, u32[]{:S(2)}, u32[]{:S(2)}) collective-permute-start(bf16[128,768]{1,0:T(8,128)(2,1)} %collective-permute-done.20), channel_id=1, source_target_pairs={{0,8},{8,16},{16,24},{24,0},{1,9},{9,17},{17,25},{25,1},{2,10},{10... | collective-permute-start | bytes 589832 | tf_op jit(solution)/shard_map/ppermute | solution.py:358
  33.8 7.5 %collective-permute-start.23 = (bf16[128,768]{1,0:T(8,128)(2,1)S(1)}, bf16[128,768]{1,0:T(8,128)(2,1)S(1)}, u32[]{:S(2)}, u32[]{:S(2)}) collective-permute-start(bf16[128,768]{1,0:T(8,128)(2,1)S(1)} %collective-permute-done.21), channel_id=1, source_target_pairs={{0,8},{8,16},{16,24},{24,0},{1,9},{9,17},{17,25},{25,1},{2,10},{10... | collective-permute-start | bytes 589832 | tf_op jit(solution)/shard_map/ppermute | solution.py:358
  41.3 7.4 %collective-permute-start.22 = (bf16[128,768]{1,0:T(8,128)(2,1)}, bf16[128,768]{1,0:T(8,128)(2,1)}, u32[]{:S(2)}, u32[]{:S(2)}) collective-permute-start(bf16[128,768]{1,0:T(8,128)(2,1)} %get-tuple-element.30), channel_id=1, source_target_pairs={{0,1},{1,0},{2,3},{3,2},{4,5},{5,4},{6,7},{7,6},{8,9},{9,8},{10,11... | collective-permute-start | bytes 589832 | tf_op jit(solution)/shard_map/ppermute | solution.py:353
  44.5 6.3 %collective-permute-start.24 = (bf16[128,768]{1,0:T(8,128)(2,1)}, bf16[128,768]{1,0:T(8,128)(2,1)}, u32[]{:S(2)}, u32[]{:S(2)}) collective-permute-start(bf16[128,768]{1,0:T(8,128)(2,1)} %get-tuple-element.28), channel_id=1, source_target_pairs={{0,1},{1,0},{2,3},{3,2},{4,5},{5,4},{6,7},{7,6},{8,9},{9,8},{10,11... | collective-permute-start | bytes 589832 | tf_op jit(solution)/shard_map/ppermute | solution.py:353
  46.9 7.8 %collective-permute-start.13 = (bf16[256,384]{1,0:T(8,128)(2,1)}, bf16[256,384]{1,0:T(8,128)(2,1)}, u32[]{:S(2)}, u32[]{:S(2)}) collective-permute-start(bf16[256,384]{1,0:T(8,128)(2,1)} %concatenate.37.refs_8_), channel_id=1, source_target_pairs={{0,8},{8,16},{16,24},{24,0},{1,9},{9,17},{17,25},{25,1},{2,10},{10... | collective-permute-start | bytes 589832 | tf_op jit(solution)/shard_map/ppermute | solution.py:358
  48.7 8.1 %collective-permute-start.5 = (bf16[256,384]{1,0:T(8,128)(2,1)}, bf16[256,384]{1,0:T(8,128)(2,1)}, u32[]{:S(2)}, u32[]{:S(2)}) collective-permute-start(bf16[256,384]{1,0:T(8,128)(2,1)} %collective-permute-done.3.refs_10_), channel_id=1, source_target_pairs={{0,8},{8,16},{16,24},{24,0},{1,9},{9,17},{17,25},{25,1},{2,10},{10... | collective-permute-start | bytes 589832 | tf_op jit(solution)/shard_map/ppermute | solution.py:358
  48.7 30.1 %collective-permute-start.2 = (bf16[256,2048]{1,0:T(8,128)(2,1)S(1)}, bf16[256,2048]{1,0:T(8,128)(2,1)}, u32[]{:S(2)}, u32[]{:S(2)}) collective-permute-start(bf16[256,2048]{1,0:T(8,128)(2,1)S(1)} %collective-permute-done.1.refs_3_), channel_id=1, source_target_pairs={{0,2},{2,0},{4,6},{6,4},{1,3},{3,1},{5,7},{7,5},{8,10},{10,8},{12,... | collective-permute-start | bytes 3145736 | tf_op jit(solution)/shard_map/ppermute | solution.py:353
  50.8 12.2 %collective-permute-start.25 = (bf16[2,128,768]{2,1,0:T(8,128)(2,1)S(1)}, bf16[2,128,768]{2,1,0:T(8,128)(2,1)}, u32[]{:S(2)}, u32[]{:S(2)}) collective-permute-start(bf16[2,128,768]{2,1,0:T(8,128)(2,1)S(1)} %pad_maximum_fusion.5.refs_10_), channel_id=1, source_target_pairs={{0,4},{2,6},{4,0},{6,2},{1,5},{3,7},{5,1},{7,3},{8,12},{10,14},{12... | collective-permute-start | bytes 1179656 | tf_op jit(solution)/shard_map/ppermute | solution.py:353
  54.7 8.0 %collective-permute-start.6 = (bf16[256,384]{1,0:T(8,128)(2,1)}, bf16[256,384]{1,0:T(8,128)(2,1)}, u32[]{:S(2)}, u32[]{:S(2)}) collective-permute-start(bf16[256,384]{1,0:T(8,128)(2,1)} %collective-permute-done.4.refs_11_), channel_id=1, source_target_pairs={{0,8},{8,16},{16,24},{24,0},{1,9},{9,17},{17,25},{25,1},{2,10},{10... | collective-permute-start | bytes 589832 | tf_op jit(solution)/shard_map/ppermute | solution.py:358
  56.8 14.0 %collective-permute-start.26 = (bf16[2,128,768]{2,1,0:T(8,128)(2,1)}, bf16[2,128,768]{2,1,0:T(8,128)(2,1)}, u32[]{:S(2)}, u32[]{:S(2)}) collective-permute-start(bf16[2,128,768]{2,1,0:T(8,128)(2,1)} %pad_maximum_fusion.6.refs_11_), channel_id=1, source_target_pairs={{0,4},{2,6},{4,0},{6,2},{1,5},{3,7},{5,1},{7,3},{8,12},{10,14},{12... | collective-permute-start | bytes 1179656 | tf_op jit(solution)/shard_map/ppermute | solution.py:353
  59.4 4.2 %copy-start.9 = (bf16[1,128,768]{2,1,0:T(8,128)(2,1)S(1)}, bf16[1,128,768]{2,1,0:T(8,128)(2,1)}, u32[]{:S(2)}) copy-start(bf16[1,128,768]{2,1,0:T(8,128)(2,1)} %get-tuple-element.29) | copy-start | bytes 589828
  59.4 12.2 %copy-start.8 = (bf16[1,128,768]{2,1,0:T(8,128)(2,1)S(1)}, bf16[1,128,768]{2,1,0:T(8,128)(2,1)}, u32[]{:S(2)}) copy-start(bf16[1,128,768]{2,1,0:T(8,128)(2,1)} %get-tuple-element.27) | copy-start | bytes 589828
  59.4 15.6 %copy-start.10 = (f32[8,1024]{1,0:T(8,128)S(1)}, f32[8,1024]{1,0:T(8,128)}, u32[]{:S(2)}) copy-start(f32[8,1024]{1,0:T(8,128)} %fusion) | copy-start | bytes 98308
  62.6 16.2 %copy-start.2 = (bf16[256,384]{1,0:T(8,128)(2,1)S(1)}, bf16[256,384]{1,0:T(8,128)(2,1)}, u32[]{:S(2)}) copy-start(bf16[256,384]{1,0:T(8,128)(2,1)} %copy-done.1) | copy-start | bytes 589828
  62.6 16.2 %copy-start.4 = (bf16[256,384]{1,0:T(8,128)(2,1)S(1)}, bf16[256,384]{1,0:T(8,128)(2,1)}, u32[]{:S(2)}) copy-start(bf16[256,384]{1,0:T(8,128)(2,1)} %copy-done.3) | copy-start | bytes 589828
  62.6 16.2 %copy-start.5 = (bf16[32,1024]{1,0:T(8,128)(2,1)S(1)}, bf16[32,1024]{1,0:T(8,128)(2,1)}, u32[]{:S(2)}) copy-start(bf16[32,1024]{1,0:T(8,128)(2,1)} %get-tuple-element.43.refs_7_) | copy-start | bytes 196612
  62.6 7.7 %collective-permute-start.14 = (bf16[256,384]{1,0:T(8,128)(2,1)}, bf16[256,384]{1,0:T(8,128)(2,1)S(1)}, u32[]{:S(2)}, u32[]{:S(2)}) collective-permute-start(bf16[256,384]{1,0:T(8,128)(2,1)} %collective-permute-done.13.refs_9_), channel_id=1, source_target_pairs={{0,8},{8,16},{16,24},{24,0},{1,9},{9,17},{17,25},{25,1},{2,10},{10... | collective-permute-start | bytes 589832 | tf_op jit(solution)/shard_map/ppermute | solution.py:358
  63.0 11.4 %collective-permute-start.7 = (bf16[256,384]{1,0:T(8,128)(2,1)}, bf16[256,384]{1,0:T(8,128)(2,1)S(1)}, u32[]{:S(2)}, u32[]{:S(2)}) collective-permute-start(bf16[256,384]{1,0:T(8,128)(2,1)} %collective-permute-done.5.refs_12_), channel_id=1, source_target_pairs={{0,8},{8,16},{16,24},{24,0},{1,9},{9,17},{17,25},{25,1},{2,10},{10... | collective-permute-start | bytes 589832 | tf_op jit(solution)/shard_map/ppermute | solution.py:358
  70.4 8.4 %collective-permute-start.8 = (bf16[256,384]{1,0:T(8,128)(2,1)}, bf16[256,384]{1,0:T(8,128)(2,1)S(1)}, u32[]{:S(2)}, u32[]{:S(2)}) collective-permute-start(bf16[256,384]{1,0:T(8,128)(2,1)} %collective-permute-done.6.refs_13_), channel_id=1, source_target_pairs={{0,8},{8,16},{16,24},{24,0},{1,9},{9,17},{17,25},{25,1},{2,10},{10... | collective-permute-start | bytes 589832 | tf_op jit(solution)/shard_map/ppermute | solution.py:358
  70.8 16.1 %collective-permute-start.15 = (bf16[256,384]{1,0:T(8,128)(2,1)S(1)}, bf16[256,384]{1,0:T(8,128)(2,1)S(1)}, u32[]{:S(2)}, u32[]{:S(2)}) collective-permute-start(bf16[256,384]{1,0:T(8,128)(2,1)S(1)} %collective-permute-done.14.refs_10_), channel_id=1, source_target_pairs={{0,8},{8,16},{16,24},{24,0},{1,9},{9,17},{17,25},{25,1},{2,10},{10... | collective-permute-start | bytes 589832 | tf_op jit(solution)/shard_map/ppermute | solution.py:358
  74.4 27.2 %collective-permute-start.27 = (bf16[4,128,768]{2,1,0:T(8,128)(2,1)S(1)}, bf16[4,128,768]{2,1,0:T(8,128)(2,1)S(1)}, u32[]{:S(2)}, u32[]{:S(2)}) collective-permute-start(bf16[4,128,768]{2,1,0:T(8,128)(2,1)S(1)} %pad_maximum_fusion), channel_id=1, source_target_pairs={{0,2},{2,0},{4,6},{6,4},{1,3},{3,1},{5,7},{7,5},{8,10},{10,8},{12,... | collective-permute-start | bytes 2359304 | tf_op jit(solution)/shard_map/ppermute | solution.py:353
  74.4 27.2 %collective-permute-start.28 = (bf16[4,128,768]{2,1,0:T(8,128)(2,1)S(1)}, bf16[4,128,768]{2,1,0:T(8,128)(2,1)S(1)}, u32[]{:S(2)}, u32[]{:S(2)}) collective-permute-start(bf16[4,128,768]{2,1,0:T(8,128)(2,1)S(1)} %pad_maximum_fusion.1), channel_id=1, source_target_pairs={{0,2},{2,0},{4,6},{6,4},{1,3},{3,1},{5,7},{7,5},{8,10},{10,8},{12,... | collective-permute-start | bytes 2359304 | tf_op jit(solution)/shard_map/ppermute | solution.py:353
  85.3 8.3 %collective-permute-start.9 = (bf16[272,128]{1,0:T(8,128)(2,1)S(1)}, bf16[272,128]{1,0:T(8,128)(2,1)S(1)}, u32[]{:S(2)}, u32[]{:S(2)}) collective-permute-start(bf16[272,128]{1,0:T(8,128)(2,1)S(1)} %get-tuple-element.14), channel_id=1, source_target_pairs={{0,2},{2,0},{4,6},{6,4},{1,3},{3,1},{5,7},{7,5},{8,10},{10,8},{12,... | collective-permute-start | bytes 208904 | tf_op jit(solution)/shard_map/ppermute | solution.py:353
  85.4 8.7 %collective-permute-start.10 = (bf16[272,128]{1,0:T(8,128)(2,1)S(1)}, bf16[272,128]{1,0:T(8,128)(2,1)S(1)}, u32[]{:S(2)}, u32[]{:S(2)}) collective-permute-start(bf16[272,128]{1,0:T(8,128)(2,1)S(1)} %get-tuple-element.15), channel_id=1, source_target_pairs={{0,4},{2,6},{4,0},{6,2},{1,5},{3,7},{5,1},{7,3},{8,12},{10,14},{12... | collective-permute-start | bytes 208904 | tf_op jit(solution)/shard_map/ppermute | solution.py:353
  86.8 8.6 %collective-permute-start.11 = (bf16[272,128]{1,0:T(8,128)(2,1)S(1)}, bf16[272,128]{1,0:T(8,128)(2,1)S(1)}, u32[]{:S(2)}, u32[]{:S(2)}) collective-permute-start(bf16[272,128]{1,0:T(8,128)(2,1)S(1)} %get-tuple-element.16), channel_id=1, source_target_pairs={{0,6},{2,4},{4,2},{6,0},{1,7},{3,5},{5,3},{7,1},{8,14},{10,12},{12... | collective-permute-start | bytes 208904 | tf_op jit(solution)/shard_map/ppermute | solution.py:353
  93.7 2.0 %collective-permute-start.16 = (bf16[144,128]{1,0:T(8,128)(2,1)S(1)}, bf16[144,128]{1,0:T(8,128)(2,1)S(1)}, u32[]{:S(2)}, u32[]{:S(2)}) collective-permute-start(bf16[144,128]{1,0:T(8,128)(2,1)S(1)} %get-tuple-element.18), channel_id=1, source_target_pairs={{0,2},{2,0},{4,6},{6,4},{1,3},{3,1},{5,7},{7,5},{8,10},{10,8},{12,... | collective-permute-start | bytes 110600 | tf_op jit(solution)/shard_map/ppermute | solution.py:353
  94.1 4.0 %collective-permute-start.17 = (bf16[144,128]{1,0:T(8,128)(2,1)S(1)}, bf16[144,128]{1,0:T(8,128)(2,1)S(1)}, u32[]{:S(2)}, u32[]{:S(2)}) collective-permute-start(bf16[144,128]{1,0:T(8,128)(2,1)S(1)} %get-tuple-element.19), channel_id=1, source_target_pairs={{0,4},{2,6},{4,0},{6,2},{1,5},{3,7},{5,1},{7,3},{8,12},{10,14},{12... | collective-permute-start | bytes 110600 | tf_op jit(solution)/shard_map/ppermute | solution.py:353
  95.5 3.7 %collective-permute-start.18 = (bf16[144,128]{1,0:T(8,128)(2,1)S(1)}, bf16[144,128]{1,0:T(8,128)(2,1)S(1)}, u32[]{:S(2)}, u32[]{:S(2)}) collective-permute-start(bf16[144,128]{1,0:T(8,128)(2,1)S(1)} %get-tuple-element.20), channel_id=1, source_target_pairs={{0,6},{2,4},{4,2},{6,0},{1,7},{3,5},{5,3},{7,1},{8,14},{10,12},{12... | collective-permute-start | bytes 110600 | tf_op jit(solution)/shard_map/ppermute | solution.py:353
  95.6 12.4 %collective-permute-start.12 = (bf16[4,272,128]{2,1,0:T(8,128)(2,1)S(1)}, bf16[4,272,128]{2,1,0:T(8,128)(2,1)S(1)}, u32[]{:S(2)}, u32[]{:S(2)}) collective-permute-start(bf16[4,272,128]{2,1,0:T(8,128)(2,1)S(1)} %pad_maximum_fusion.7), channel_id=1, source_target_pairs={{0,1},{1,0},{2,3},{3,2},{4,5},{5,4},{6,7},{7,6},{8,9},{9,8},{10,11... | collective-permute-start | bytes 835592 | tf_op jit(solution)/shard_map/ppermute | solution.py:353
  99.2 8.9 %collective-permute-start.19 = (bf16[4,144,128]{2,1,0:T(8,128)(2,1)S(1)}, bf16[4,144,128]{2,1,0:T(8,128)(2,1)S(1)}, u32[]{:S(2)}, u32[]{:S(2)}) collective-permute-start(bf16[4,144,128]{2,1,0:T(8,128)(2,1)S(1)} %pad_maximum_fusion.8), channel_id=1, source_target_pairs={{0,1},{1,0},{2,3},{3,2},{4,5},{5,4},{6,7},{7,6},{8,9},{9,8},{10,11... | collective-permute-start | bytes 442376 | tf_op jit(solution)/shard_map/ppermute | solution.py:353
  112.2 3.7 %collective-permute-start.29 = (f32[4,1024]{1,0:T(4,128)S(1)}, f32[4,1024]{1,0:T(4,128)S(1)}, u32[]{:S(2)}, u32[]{:S(2)}) collective-permute-start(f32[4,1024]{1,0:T(4,128)S(1)} %get-tuple-element.23), channel_id=1, source_target_pairs={{0,1},{1,0},{2,3},{3,2},{4,5},{5,4},{6,7},{7,6},{8,9},{9,8},{10,11... | collective-permute-start | bytes 49160 | tf_op jit(solution)/shard_map/ppermute | solution.py:353

commit v2 on v0

--- a/solution.py
+++ b/solution.py
@@ -1,11 +1,19 @@
+import functools
+
 import jax
 import jax.numpy as jnp
+import numpy as np
 from jax import lax
+from jax.experimental import pallas as pl
+from jax.experimental.pallas import tpu as pltpu
 from jax.sharding import PartitionSpec as P
 
 D = 2048
 HD = 64
 HALF_WIN = 256
+
+ATTEND = pl.CostEstimate(flops=4 * 10**9, bytes_accessed=1, transcendentals=0)
+SHORT = pl.CostEstimate(flops=1, bytes_accessed=1, transcendentals=0)
 
 
 def with_halo(cells, sides, width):
@@ -138,7 +146,359 @@
     return (layer[None], shelf_rows[None, None, None])
 
 
+def lanes(shape):
+    return lax.broadcasted_iota(jnp.int32, shape, 1)
+
+
+def rotary(tile, cosine, sine):
+    first = lanes(tile.shape) % HD < HD // 2
+    partner = jnp.where(first, pltpu.roll(tile, 128 - HD // 2, 1), pltpu.roll(tile, HD // 2, 1))
+    return tile * cosine + partner * sine
+
+
+def folded(columns, odd):
+    half = columns[0].shape[0] // 2
+    low = lanes((half, 128)) < HD
+    turn = lambda x: pltpu.roll(x, HD, 1)
+    q, k, v = [[c[:half].astype(jnp.float32), c[half:].astype(jnp.float32)] for c in columns]
+    parts = [jnp.where(low, jnp.where(odd, turn(q[p]), q[p]), jnp.where(odd, k[p], turn(k[p]))) for p in range(2)]
+    parts.append(jnp.where(low, jnp.where(odd, turn(v[0]), v[0]), jnp.where(odd, v[1], turn(v[1]))))
+    return jnp.concatenate(parts, 1).astype(columns[0].dtype)
+
+
+def pieces_kernel(where, w_ref, x_ref, o_ref, out_ref, first_ref, second_ref, third_ref):
+    out_ref[...] = o_ref[0]
+    first_ref[...] = folded([w_ref[j] for j in range(3)], False)
+    second_ref[...] = folded([w_ref[j] for j in range(3)], True)
+    third_ref[...] = folded([x_ref[j] for j in range(3)], lax.rem(where[0], 2) == 1)
+
+
+def pieces(where, proj_weight):
+    _, shard, width = proj_weight.shape
+    quarter = shard // 4
+    return pl.pallas_call(
+        pieces_kernel,
+        grid_spec=pltpu.PrefetchScalarGridSpec(
+            num_scalar_prefetch=1,
+            grid=(1,),
+            in_specs=[
+                pl.BlockSpec((3, shard, 128), lambda i, where: (0, 0, where[0])),
+                pl.BlockSpec((3, shard, 128), lambda i, where: (0, 0, 4 + where[0] // 2)),
+                pl.BlockSpec((1, quarter, width), lambda i, where: (3, where[0], 0)),
+            ],
+            out_specs=[pl.BlockSpec((quarter, width), lambda i, where: (0, 0))]
+            + [pl.BlockSpec((shard // 2, 384), lambda i, where: (0, 0))] * 3,
+        ),
+        out_shape=[jax.ShapeDtypeStruct((quarter, width), proj_weight.dtype)]
+        + [jax.ShapeDtypeStruct((shard // 2, 384), proj_weight.dtype)] * 3,
+        cost_estimate=SHORT,
+        name="pieces",
+    )(where, proj_weight, proj_weight, proj_weight)
+
+
+def after(value, *earlier):
+    return lax.optimization_barrier((value, *earlier))[0]
+
+
+def members(lengths, positions):
+    count = lengths.shape[1]
+    shape = (count, count)
+    row, other = lax.broadcasted_iota(jnp.int32, shape, 0), lax.broadcasted_iota(jnp.int32, shape, 1)
+    per_block = count // 4
+    stretch = lax.rem(row, per_block) * 4 + row // per_block
+    values = jnp.broadcast_to(lengths, shape)
+    ends = jnp.sum(jnp.where(other <= stretch, values, 0), 1, keepdims=True)
+    starts = jnp.sum(jnp.where(other < stretch, values, 0), 1, keepdims=True)
+    position = lax.broadcasted_iota(jnp.int32, (count, positions), 1)
+    return jnp.where((position >= starts) & (position < ends), 1.0, 0.0).astype(jnp.bfloat16)
+
+
+def attend_kernel(pools, *refs):
+    where, h_refs, (cos_ref, sin_ref, lengths_ref), w_refs = refs[0], refs[1:5], refs[5:8], refs[8:12]
+    out_refs = refs[12:16]
+    q_s, k_s, v_s, c_s, member_s = refs[-5:]
+    s, d, g = where[0], where[1], where[2]
+    rows, d_model = h_refs[0].shape
+    total = 4 * rows
+    shard = d_model // 4
+    half = shard // 2
+    per_block = lengths_ref.shape[1] // 4
+    member_s[...] = members(lengths_ref[...], total)
+
+    for j in range(4):
+        block = jnp.bitwise_xor(s, j)
+        at = pl.ds(pl.multiple_of(block * rows, rows), rows)
+        top = jnp.zeros((rows, 256), jnp.float32)
+        bottom = jnp.zeros((rows, 256), jnp.float32)
+        for k in range(4):
+            column = lax.rem(d - k + 4, 4) * shard
+            w = w_refs[k]
+            h_top = h_refs[j][:, pl.ds(pl.multiple_of(column, half), half)]
+            h_bottom = h_refs[j][:, pl.ds(pl.multiple_of(column + half, half), half)]
+            top += jnp.dot(h_top, jnp.concatenate([w[:, 0:128], w[:, 256:384]], 1), preferred_element_type=jnp.float32)
+            bottom += jnp.dot(h_bottom, w[:, 128:384], preferred_element_type=jnp.float32)
+        qk = rotary(top[:, :128] + bottom[:, :128], cos_ref[at, :], sin_ref[at, :])
+        low = lanes(qk.shape) < HD
+        q_s[at, :] = jnp.where(low, qk * HD**-0.5, 0.0).astype(jnp.bfloat16)
+        k_s[at, :] = pltpu.roll(qk, HD, 1).astype(jnp.bfloat16)
+        v = top[:, 128:] + pltpu.roll(bottom[:, 128:], HD, 1)
+        v_s[at, :] = jnp.where(low, v, 1.0).astype(jnp.bfloat16)
+
+    step = 128
+    for r in range(total // step):
+        start, end = max(0, r * step - HALF_WIN), min(total, (r + 1) * step + HALF_WIN)
+        ahead = lax.broadcasted_iota(jnp.int32, (step, step), 1) - lax.broadcasted_iota(jnp.int32, (step, step), 0)
+        scores = lax.dot_general(
+            q_s[r * step : (r + 1) * step, :], k_s[start:end, :], (((1,), (1,)), ((), ())), preferred_element_type=jnp.float32
+        )
+        parts = [scores]
+        if start == r * step - HALF_WIN:
+            parts = [jnp.where(ahead >= 0, scores[:, :step], -1e30), scores[:, step:]]
+        if end == (r + 1) * step + HALF_WIN:
+            last = parts.pop()
+            parts += [last[:, :-step], jnp.where(ahead <= 0, last[:, -step:], -1e30)]
+        scores = jnp.concatenate(parts, 1)
+        expo = jnp.exp(scores - jnp.max(scores, 1, keepdims=True)).astype(jnp.bfloat16)
+        o = jnp.dot(expo, v_s[start:end, :], preferred_element_type=jnp.float32)
+        low = lanes(o.shape) < HD
+        c_s[r * step : (r + 1) * step, :] = jnp.where(low, o / pltpu.roll(o, HD, 1), 0.0).astype(jnp.bfloat16)
+
+    pooled = jnp.dot(member_s[...], c_s[...], preferred_element_type=jnp.float32)
+    high = pooled.astype(jnp.bfloat16)
+    rest = (pooled - high.astype(jnp.float32)).astype(jnp.bfloat16)
+    for j in range(4):
+        block = jnp.bitwise_xor(s, j)
+        both = jnp.zeros((2 * per_block, 128), jnp.bfloat16)
+        for b in range(4):
+            cut = slice(b * per_block, (b + 1) * per_block)
+            both = jnp.where(block == b, jnp.concatenate([high[cut], rest[cut]], 0), both)
+        out = out_refs[j]
+        lo = c_s[pl.ds(pl.multiple_of(block * rows, rows), rows // 2), :].astype(jnp.float32)
+        hi = c_s[pl.ds(pl.multiple_of(block * rows + rows // 2, rows // 2), rows // 2), :].astype(jnp.float32)
+        out[0 : rows // 2, :] = (lo + pltpu.roll(hi, HD, 1)).astype(jnp.bfloat16)
+        out[rows // 2 :, :] = both
+
+    if pools:
+        feats = d_model // 2
+        sums = jnp.zeros((4 * per_block, feats), jnp.float32)
+        for j in range(4):
+            rows_of = member_s[:, pl.ds(pl.multiple_of(jnp.bitwise_xor(s, j) * rows, rows), rows)]
+            part = h_refs[j][:, pl.ds(pl.multiple_of(g * feats, feats), feats)]
+            sums += jnp.dot(rows_of, part, preferred_element_type=jnp.float32)
+        own = jnp.zeros((per_block, feats), jnp.float32)
+        for b in range(4):
+            own = jnp.where(s == b, sums[b * per_block : (b + 1) * per_block], own)
+        refs[16][...] = own
+
+
+def attend(where, blocks, tables, pieces, pools):
+    rows, d_model = blocks[0].shape
+    total = 4 * rows
+    count = tables[2].shape[1]
+    per_block = count // 4
+    vmem = pl.BlockSpec(memory_space=pltpu.VMEM)
+    out_shape = [jax.ShapeDtypeStruct((rows // 2 + 2 * per_block, 128), jnp.bfloat16)] * 4
+    if pools:
+        out_shape.append(jax.ShapeDtypeStruct((per_block, d_model // 2), jnp.float32))
+    return pl.pallas_call(
+        functools.partial(attend_kernel, pools),
+        out_shape=out_shape,
+        in_specs=[pl.BlockSpec(memory_space=pltpu.SMEM)] + [vmem] * 11,
+        out_specs=[vmem] * len(out_shape),
+        scratch_shapes=[pltpu.VMEM((total, 128), jnp.bfloat16)] * 4 + [pltpu.VMEM((count, total), jnp.bfloat16)],
+        compiler_params=pltpu.CompilerParams(vmem_limit_bytes=24 * 2**20),
+        cost_estimate=ATTEND,
+        name="attend_and_pool" if pools else "attend",
+    )(where, *blocks, *tables, *pieces)
+
+
+def project_kernel(where, shard_ref, h_ref, pool_ref, *refs):
+    heads = [refs[5 * i : 5 * i + 5] for i in range(3)]
+    w_refs = refs[15:17]
+    layer_ref, keep_ref, send_ref, c_s, o_s = refs[17:]
+    s, d, g = where[0], where[1], where[2]
+    rows = h_ref.shape[0]
+    extra = c_s.shape[0] - rows
+    width = c_s.shape[1] // 2
+    odd = jnp.bitwise_and(s, 1) == 1
+    group_of = (g, 1 - g)
+
+    def place(base, tile, left, right):
+        low = lanes(left.shape) < HD
+        first = jnp.where(low, left, pltpu.roll(right, HD, 1)).astype(jnp.bfloat16)
+        second = jnp.where(low, pltpu.roll(left, HD, 1), right).astype(jnp.bfloat16)
+        at = pl.ds(pl.multiple_of(base + tile * 128, 128), 128)
+        c_s[0 : rows // 2, at] = first[0 : rows // 2]
+        c_s[rows // 2 : rows, at] = second[0 : rows // 2]
+        c_s[rows:, at] = first[rows // 2 :]
+
+    for t in range(2):
+        base = group_of[t] * width
+        parts = [[(r[j][...] if t == 0 else r[4][j]).astype(jnp.float32) for j in range(4)] for r in heads]
+        for j in range(4):
+            place(base, jnp.bitwise_xor(s, j), parts[0][j], parts[1][j])
+        for pair in range(2):
+            one, two = parts[2][2 * pair], parts[2][2 * pair + 1]
+            left, right = jnp.where(odd, two, one), jnp.where(odd, one, two)
+            place(base, 4 + jnp.bitwise_xor(s // 2, pair), left, right)
+
+    feats = w_refs[0].shape[2]
+    per_shard = 4 * feats
+    for p in range(2):
+        in_half = lax.rem(lax.rem(d - p + 4, 4), 2)
+        for j in range(4):
+            source = w_refs[j % 2]
+            quarter = jnp.bitwise_xor(s, j)
+            total = jnp.zeros((rows + extra, feats), jnp.float32)
+            for t in range(2):
+                w = source[2 * (j // 2) + t, p]
+                c = c_s[:, pl.ds(pl.multiple_of(group_of[t] * width, 128), width)]
+                total += lax.dot_general(c, w, (((1,), (1,)), ((), ())), preferred_element_type=jnp.float32)
+            column = pl.multiple_of(in_half * per_shard + quarter * feats, 128)
+            o_s[:, pl.ds(column, feats)] = total[rows:]
+            mine = h_ref[:, pl.ds(pl.multiple_of(g * 2 * per_shard + column, 128), feats)]
+            layer_ref[:, pl.ds(column, feats)] = (mine.astype(jnp.float32) + total[:rows]).astype(jnp.bfloat16)
+
+    half = extra // 2
+    pooled = pool_ref[...] + o_s[0:half] + o_s[half:]
+    slots = 2 * keep_ref.shape[0]
+    slot = lax.broadcasted_iota(jnp.int32, (slots, half), 0)
+    source = lax.broadcasted_iota(jnp.int32, (slots, half), 1)
+    route = jnp.zeros((slots, half), jnp.float32)
+    ids = [shard_ref[c] for c in range(half)]
+    for c in range(half):
+        rank = sum([(ids[e] == ids[c]).astype(jnp.int32) for e in range(c)], jnp.int32(0))
+        route = jnp.where((slot == ids[c] * (slots // 2) + rank) & (source == c), 1.0, route)
+    routed = jnp.dot(route, pooled, precision=lax.Precision.HIGHEST, preferred_element_type=jnp.float32)
+    cut = routed.shape[0] // 2
+    keep_ref[...] = jnp.where(g == 0, routed[:cut], routed[cut:])
+    send_ref[...] = jnp.where(g == 0, routed[cut:], routed[:cut])
+
+
+def project(where, h, pool, shard_ids, contexts, w_parts):
+    rows, d_model = h.shape
+    feats = d_model // 2
+    extra = contexts[0].shape[0] - rows // 2
+    vmem = pl.BlockSpec(memory_space=pltpu.VMEM)
+    slots = shard_ids.shape[0] // 2
+    return pl.pallas_call(
+        project_kernel,
+        out_shape=[
+            jax.ShapeDtypeStruct((rows, feats), jnp.bfloat16),
+            jax.ShapeDtypeStruct((slots, feats), jnp.float32),
+            jax.ShapeDtypeStruct((slots, feats), jnp.float32),
+        ],
+        in_specs=[pl.BlockSpec(memory_space=pltpu.SMEM)] * 2 + [vmem] * 19,
+        out_specs=[vmem] * 3,
+        scratch_shapes=[
+            pltpu.VMEM((rows + extra, 2 * w_parts[0].shape[3]), jnp.bfloat16),
+            pltpu.VMEM((extra, feats), jnp.float32),
+        ],
+        compiler_params=pltpu.CompilerParams(vmem_limit_bytes=24 * 2**20),
+        cost_estimate=SHORT,
+        name="project",
+    )(where, shard_ids, h, pool, *contexts, *w_parts)
+
+
+def xor_send(name, value, axis, j):
+    with jax.named_scope(name):
+        return lax.ppermute(value, axis, [(i, i ^ j) for i in range(lax.axis_size(axis))])
+
+
+def ring_send(name, value):
+    count = lax.axis_size("dp")
+    with jax.named_scope(name):
+        return lax.ppermute(value, "dp", [(i, (i + 1) % count) for i in range(count)])
+
+
+def rotary_tables(total):
+    freqs = np.float32(10000.0) ** (np.float32(-2.0) * np.arange(HD // 2, dtype=np.float32) / np.float32(HD))
+    angles = (np.arange(total, dtype=np.float32)[:, None] * freqs[None, :]).astype(np.float64)
+    cosine, sine = np.cos(angles).astype(np.float32), np.sin(angles).astype(np.float32)
+    return jnp.asarray(np.concatenate([cosine] * 4, 1)), jnp.asarray(np.concatenate([-sine, sine] * 2, 1))
+
+
+def body_by_heads(hidden, proj_weight, stretch_lengths, shard_of):
+    h = hidden[0]
+    rows = h.shape[0]
+    s, d, g = lax.axis_index("seq"), lax.axis_index("dp"), lax.axis_index("index")
+    where = jnp.stack([s, d, g]).astype(jnp.int32)
+    total = 4 * rows
+
+    tables = (*rotary_tables(total), stretch_lengths)
+
+    def across(ring):
+        pairs = [((d - p) % 4 // 2 == g, ring[p], ring[p + 2]) for p in range(2)]
+        keep = jnp.stack([jnp.where(mine, one, two) for mine, one, two in pairs])
+        send = jnp.stack([jnp.where(mine, two, one) for mine, one, two in pairs])
+        with jax.named_scope("out_across"):
+            far = lax.ppermute(send, ("seq", "index"), [(i, i ^ 5) for i in range(8)])
+        return keep, xor_send("out_group", send, "index", 1), xor_send("out_cross", keep, "seq", 2), far
+
+    def to_seq(name, parts):
+        return [parts[0]] + [xor_send(name, parts[j], "seq", j) for j in (1, 2, 3)]
+
+    def to_other(name, parts):
+        return parts + [xor_send(name, jnp.stack(parts), "index", 1)]
+
+    h_cross = xor_send("hidden_cross", h, "seq", 2)
+    h_core = xor_send("hidden_core", h, "seq", 1)
+    o0, x0, y0, z0 = pieces(where, proj_weight)
+
+    def rings(names, starts):
+        held = [[start] for start in starts]
+        for step in range(3):
+            for ring, name in zip(held, names):
+                ring.append(ring_send(name, ring[-1]))
+        return held
+
+    out_ring, first_ring = rings(("out", "first"), (o0, x0))
+    out_ring[3], first_ring[3], h_core, h_cross, y0, z0 = lax.optimization_barrier(
+        (out_ring[3], first_ring[3], h_core, h_cross, y0, z0)
+    )
+
+    second_ring, third_ring = rings(("second", "third"), (y0, z0))
+    h_far = xor_send("hidden_far", h_cross, "seq", 1)
+    blocks = [h, h_core, h_cross, h_far]
+    four = across(out_ring)
+    first_ring[3] = after(first_ring[3], second_ring[2], third_ring[2])
+    first = attend(where, blocks, tables, first_ring, True)
+    first_parts = to_seq("context_first", first[:4])
+    second = attend(where, blocks, tables, second_ring, False)
+    third_ring[3], four, first_parts, second = lax.optimization_barrier((third_ring[3], four, first_parts, second))
+
+    four = jnp.stack(four)
+    near = xor_send("out_core", four, "seq", 1)
+    first_parts = to_other("context_first_group", first_parts)
+    second_parts = to_seq("context_second", second)
+    third = attend(where, blocks, tables, third_ring, False)
+    second_parts = to_other("context_second_group", second_parts)
+    third_parts = to_other("context_third_group", to_seq("context_third", third))
+
+    contexts = first_parts + second_parts + third_parts
+    layer, keep, send = project(where, h, first[4], shard_of[0, :, 0], contexts, [four, near])
+    arrived = xor_send("embedding_half", send, "index", 1)
+    feats = keep.shape[1]
+    square = (jnp.sum(keep * keep, -1, keepdims=True) + jnp.sum(arrived * arrived, -1, keepdims=True)) / (2 * feats)
+    scale = lax.rsqrt(square + 1e-06)
+    shelf = jnp.concatenate([jnp.where(g == 0, keep, arrived), jnp.where(g == 0, arrived, keep)], 1) * scale
+    return (layer[None], shelf[None, None, None])
+
+
 def solution(mesh):
     in_specs = (P("dp", "seq", None), P(None, "dp", "index"), P("dp", None), P("dp", "seq", None))
     out_specs = (P("dp", "seq", "index"), P("dp", "seq", "index", None, None))
-    return jax.shard_map(body, mesh=mesh, in_specs=in_specs, out_specs=out_specs, check_vma=False)
+
+    def whole(hidden, proj_weight, stretch_lengths, shard_of):
+        heads = proj_weight.shape[2] // HD // mesh.shape["index"]
+        rows = hidden.shape[1] // mesh.shape["seq"]
+        by_heads = (mesh.shape["dp"], mesh.shape["seq"], mesh.shape["index"], heads, rows) == (4, 4, 2, 12, 256)
+        return jax.shard_map(
+            body_by_heads if by_heads else body,
+            mesh=mesh,
+            in_specs=in_specs,
+            out_specs=out_specs,
+            check_vma=False,
+        )(hidden, proj_weight, stretch_lengths, shard_of)
+
+    return whole

time: 338 us -> 107 us (0.32)
  waiting for transfers between devices: 223 us -> 61.2 us
  matrix products: 52.4 us -> 0 us
  local copies, waits for them, and re-layouts: 23.6 us -> 0.77 us
  Pallas kernels: 0 us -> 20.8 us
  between operations: 14 us -> 1.03 us
  other arithmetic: 16.3 us -> 4.05 us
  starting transfers between devices: 7.56 us -> 19.3 us
    all_gather x2 -> x0, waiting for transfers between devices: 181 us -> none  [the longest x1 168 us: body(): lax.all_gather(proj_weight[:3], 'dp', axis=1, tiled=True)]
    ppermute x2 -> x32, waiting for transfers between devices: 2.28 us -> 61.2 us  [the longest x12 49 us: ring_send(): lax.ppermute(value, 'dp', [(i, (i + 1) % count) for i in range(count)])]
    dot_general x28 -> x0, matrix products: 52.4 us -> none  [the longest x12 23.4 us: one_head(): jnp.dot(weights, value_head, preferred_element_type=jnp.float32)]
    reduce_scatter x2 -> x0, waiting for transfers between devices: 37.6 us -> none  [the longest x1 20.4 us: body(): lax.psum_scatter(partial_pool.astype(jnp.bfloat16), 'seq', scatter_dimens...]
    pallas_call x0 -> x5, Pallas kernels: none -> 20.8 us  [the longest x3 14.2 us: attend(): pl.pallas_call(functools.partial(attend_kernel, pools), out_shape=out_sha...]
    ppermute x2 -> x32, starting transfers between devices: 4.14 us -> 19.3 us  [the longest x19 13.6 us: xor_send(): lax.ppermute(value, axis, [(i, i ^ j) for i in range(lax.axis_size(axis))])]
    unnamed x15 -> x28, local copies, waits for them, and re-layouts: 9.62 us -> 0.77 us
    slice x8 -> x0, local copies, waits for them, and re-layouts: 6.63 us -> none  [the longest x2 2.89 us: rotate(): second = values_in[..., half_dim:]]
  transfers between devices with their start and end apart: 7 -> 32, of which waited for: 6 -> 17; matrix products, arithmetic and copies ran while one was open for 16% -> 3% of each run, Pallas kernels for 0% -> 16%
where the time goes in v2:
time: 107 us
  waiting for transfers between devices  61.2 us (57%)
  Pallas kernels  20.8 us (19%)
  starting transfers between devices  19.3 us (18%)
  other arithmetic  4.05 us (4%)
    ppermute x12, waiting for transfers between devices, ring_send(): lax.ppermute(value, 'dp', [(i, (i + 1) % count) for i in range(count)])  49 us
    pallas_call x3, Pallas kernels, attend(): pl.pallas_call(functools.partial(attend_kernel, pools), out_shape=out_sha...  14.2 us
    ppermute x19, starting transfers between devices, xor_send(): lax.ppermute(value, axis, [(i, i ^ j) for i in range(lax.axis_size(axis))])  13.6 us
    ppermute x19, waiting for transfers between devices, xor_send(): lax.ppermute(value, axis, [(i, i ^ j) for i in range(lax.axis_size(axis))])  12.2 us
    ppermute x12, starting transfers between devices, ring_send(): lax.ppermute(value, 'dp', [(i, (i + 1) % count) for i in range(count)])  4.23 us
    pallas_call x1, Pallas kernels, project(): pl.pallas_call(project_kernel, out_shape=[jax.ShapeDtypeStruct((rows, fea...  3.66 us
    pallas_call x1, Pallas kernels, pieces(): pl.pallas_call(pieces_kernel, grid_spec=pltpu.PrefetchScalarGridSpec(num_...  2.86 us
    another operation x3, other arithmetic, across(): send = jnp.stack([jnp.where(mine, two, one) for mine, one, two in pairs])  2.29 us
  transfers between devices with their start and end apart: 32, of which 17 were waited for; matrix products, arithmetic and copies ran while one was open for 3% of the time, Pallas kernels for 16%

profile of v2, /device:TPU:0, one launch (start us, length us, event | category | flops | bytes accessed | tf_op | source)
XLA Modules:
  0.0 107.1 jit_solution(14643158530080673665)
XLA Ops:
  0.6 0.5 collective-permute-start.6
  1.1 2.6 %collective-permute-start.7 = (bf16[256,2048]{1,0:T(8,128)(2,1)}, bf16[256,2048]{1,0:T(8,128)(2,1)S(1)}, u32[]{:S(2)}, u32[]{:S(2)}) collective-permute-start(bf16[256,2048]{1,0:T(8,128)(2,1)} %bitcast.35), channel_id=1, source_target_pairs={{0,4},{2,6},{4,0},{6,2},{1,5},{3,7},{5,1},{7,3},{8,12},{10,14},{12... | collective-permute-start | bytes 3145736 | tf_op jit(solution)/shard_map/hidden_cross/ppermute | solution.py:405
  3.7 0.6 pad_add_fusion.where.refs_0_
  4.3 2.9 %pieces.1 = (bf16[128,768]{1,0:T(8,128)(2,1)}, bf16[256,384]{1,0:T(8,128)(2,1)}, bf16[256,384]{1,0:T(8,128)(2,1)}, bf16[256,384]{1,0:T(8,128)(2,1)}) custom-call(s32[3]{0:T(128)} %pad_add_fusion.where.refs_0_, bf16[4,512,768]{2,1,0:T(8,128)(2,1)} %o_ref.1, bf16[4,512,768]{2,1,0:T(8,128)(2,1)} %o_ref.1, bf16[4,512,768]{2,1,0:T(8,128)(2,1)} %o_ref.1), custom_call_target="tpu_custom_call" | custom-call | flops 1 | bytes 1 | tf_op jit(solution)/shard_map/pieces/pallas_call | solution.py:179
  7.2 1.6 %collective-permute-start = (bf16[128,768]{1,0:T(8,128)(2,1)}, bf16[128,768]{1,0:T(8,128)(2,1)S(1)}, u32[]{:S(2)}, u32[]{:S(2)}) collective-permute-start(bf16[128,768]{1,0:T(8,128)(2,1)} %get-tuple-element.42), channel_id=1, source_target_pairs={{0,8},{8,16},{16,24},{24,0},{1,9},{9,17},{17,25},{25,1},{2,10},{10... | collective-permute-start | bytes 589832 | tf_op jit(solution)/shard_map/out/ppermute | solution.py:411
  8.8 1.6 %collective-permute-start.3 = (bf16[256,384]{1,0:T(8,128)(2,1)}, bf16[256,384]{1,0:T(8,128)(2,1)S(1)}, u32[]{:S(2)}, u32[]{:S(2)}) collective-permute-start(bf16[256,384]{1,0:T(8,128)(2,1)} %get-tuple-element.43.refs_8_), channel_id=1, source_target_pairs={{0,8},{8,16},{16,24},{24,0},{1,9},{9,17},{17,25},{25,1},{2,10},{10... | collective-permute-start | bytes 589832 | tf_op jit(solution)/shard_map/first/ppermute | solution.py:411
  10.3 6.6 %collective-permute-done = bf16[128,768]{1,0:T(8,128)(2,1)S(1)} collective-permute-done((bf16[128,768]{1,0:T(8,128)(2,1)}, bf16[128,768]{1,0:T(8,128)(2,1)S(1)}, u32[]{:S(2)}, u32[]{:S(2)}) %collective-permute-start) | collective-permute-done | bytes 196640 | tf_op jit(solution)/shard_map/out/ppermute | solution.py:411
  16.9 0.0 collective-permute-start.1
  16.9 3.9 %collective-permute-done.3.refs_9_ = bf16[256,384]{1,0:T(8,128)(2,1)S(1)} collective-permute-done((bf16[256,384]{1,0:T(8,128)(2,1)}, bf16[256,384]{1,0:T(8,128)(2,1)S(1)}, u32[]{:S(2)}, u32[]{:S(2)}) %collective-permute-start.3) | collective-permute-done | bytes 196640 | tf_op jit(solution)/shard_map/first/ppermute | solution.py:411
  20.8 0.1 collective-permute-start.4
  20.9 4.1 %collective-permute-done.1 = bf16[128,768]{1,0:T(8,128)(2,1)S(1)} collective-permute-done((bf16[128,768]{1,0:T(8,128)(2,1)S(1)}, bf16[128,768]{1,0:T(8,128)(2,1)S(1)}, u32[]{:S(2)}, u32[]{:S(2)}) %collective-permute-start.1) | collective-permute-done | bytes 196640 | tf_op jit(solution)/shard_map/out/ppermute | solution.py:411
  25.0 0.1 collective-permute-start.2
  25.1 5.3 %collective-permute-done.4.refs_10_ = bf16[256,384]{1,0:T(8,128)(2,1)S(1)} collective-permute-done((bf16[256,384]{1,0:T(8,128)(2,1)S(1)}, bf16[256,384]{1,0:T(8,128)(2,1)S(1)}, u32[]{:S(2)}, u32[]{:S(2)}) %collective-permute-start.4) | collective-permute-done | bytes 196640 | tf_op jit(solution)/shard_map/first/ppermute | solution.py:411
  30.4 3.9 %collective-permute-done.2 = bf16[128,768]{1,0:T(8,128)(2,1)S(1)} collective-permute-done((bf16[128,768]{1,0:T(8,128)(2,1)S(1)}, bf16[128,768]{1,0:T(8,128)(2,1)S(1)}, u32[]{:S(2)}, u32[]{:S(2)}) %collective-permute-start.2) | collective-permute-done | bytes 196640 | tf_op jit(solution)/shard_map/out/ppermute | solution.py:411
  34.3 3.6 %collective-permute-done.5.refs_11_ = bf16[256,384]{1,0:T(8,128)(2,1)S(1)} collective-permute-done((bf16[256,384]{1,0:T(8,128)(2,1)S(1)}, bf16[256,384]{1,0:T(8,128)(2,1)S(1)}, u32[]{:S(2)}, u32[]{:S(2)}) %collective-permute-start.5) | collective-permute-done | bytes 196640 | tf_op jit(solution)/shard_map/first/ppermute | solution.py:411
  37.9 0.7 copy-done.6
  38.6 0.1 collective-permute-start.8
  38.8 0.0 copy-start
  38.8 0.0 copy-start.8
  38.8 0.0 copy-start.9
  38.8 0.0 copy-start.10
  38.8 1.2 %select_bitcast_fusion.1 = (bf16[1,128,768]{2,1,0:T(8,128)(2,1)S(1)}, bf16[1,128,768]{2,1,0:T(8,128)(2,1)S(1)}) fusion(bf16[128,768]{1,0:T(8,128)(2,1)} %copy-done.12, bf16[128,768]{1,0:T(8,128)(2,1)} %get-tuple-element.42, pred[]{:T(512)S(6)} %eq.13), kind=kLoop, calls=%fused_computation.4 | loop fusion | flops 196608 | bytes 786433 | tf_op jit(solution)/shard_map/stack | solution.py:433
  40.0 0.1 collective-permute-start.9
  40.1 0.7 collective-permute-start.11
  40.8 1.1 select_bitcast_fusion
  41.9 8.0 %collective-permute-done.9.refs_9_ = bf16[256,384]{1,0:T(8,128)(2,1)S(1)} collective-permute-done((bf16[256,384]{1,0:T(8,128)(2,1)}, bf16[256,384]{1,0:T(8,128)(2,1)S(1)}, u32[]{:S(2)}, u32[]{:S(2)}) %collective-permute-start.9) | collective-permute-done | bytes 196640 | tf_op jit(solution)/shard_map/second/ppermute | solution.py:411
  49.9 0.0 collective-permute-start.10
  49.9 3.9 %collective-permute-done.11.refs_9_ = bf16[256,384]{1,0:T(8,128)(2,1)S(1)} collective-permute-done((bf16[256,384]{1,0:T(8,128)(2,1)}, bf16[256,384]{1,0:T(8,128)(2,1)S(1)}, u32[]{:S(2)}, u32[]{:S(2)}) %collective-permute-start.11) | collective-permute-done | bytes 196640 | tf_op jit(solution)/shard_map/third/ppermute | solution.py:411
  53.7 0.0 collective-permute-start.12
  53.8 1.6 %collective-permute-start.14 = (bf16[2,128,768]{2,1,0:T(8,128)(2,1)S(1)}, bf16[2,128,768]{2,1,0:T(8,128)(2,1)S(1)}, u32[]{:S(2)}, u32[]{:S(2)}) collective-permute-start(bf16[2,128,768]{2,1,0:T(8,128)(2,1)S(1)} %pad_maximum_fusion.2), channel_id=1, source_target_pairs={{0,1},{1,0},{2,3},{3,2},{4,5},{5,4},{6,7},{7,6},{8,9},{9,8},{10,11... | collective-permute-start | bytes 1179656 | tf_op jit(solution)/shard_map/out_group/ppermute | solution.py:405
  55.4 0.6 collective-permute-start.15
  56.0 1.9 %collective-permute-done.10.refs_10_ = bf16[256,384]{1,0:T(8,128)(2,1)S(1)} collective-permute-done((bf16[256,384]{1,0:T(8,128)(2,1)S(1)}, bf16[256,384]{1,0:T(8,128)(2,1)S(1)}, u32[]{:S(2)}, u32[]{:S(2)}) %collective-permute-start.10) | collective-permute-done | bytes 196640 | tf_op jit(solution)/shard_map/second/ppermute | solution.py:411
  57.9 1.5 %collective-permute-start.16 = (bf16[2,128,768]{2,1,0:T(8,128)(2,1)S(1)}, bf16[2,128,768]{2,1,0:T(8,128)(2,1)S(1)}, u32[]{:S(2)}, u32[]{:S(2)}) collective-permute-start(bf16[2,128,768]{2,1,0:T(8,128)(2,1)S(1)} %pad_maximum_fusion.2), channel_id=1, source_target_pairs={{0,5},{1,4},{2,7},{3,6},{4,1},{5,0},{6,3},{7,2},{8,13},{9,12},{10,... | collective-permute-start | bytes 1179656 | tf_op jit(solution)/shard_map/out_across/ppermute | solution.py:435
  59.4 2.5 %collective-permute-done.12.refs_10_ = bf16[256,384]{1,0:T(8,128)(2,1)S(1)} collective-permute-done((bf16[256,384]{1,0:T(8,128)(2,1)S(1)}, bf16[256,384]{1,0:T(8,128)(2,1)S(1)}, u32[]{:S(2)}, u32[]{:S(2)}) %collective-permute-start.12) | collective-permute-done | bytes 196640 | tf_op jit(solution)/shard_map/third/ppermute | solution.py:411
  61.9 0.0 collective-permute-start.20
  62.0 5.0 %attend_and_pool.1 = (bf16[144,128]{1,0:T(8,128)(2,1)S(1)}, bf16[144,128]{1,0:T(8,128)(2,1)S(1)}, bf16[144,128]{1,0:T(8,128)(2,1)S(1)}, bf16[144,128]{1,0:T(8,128)(2,1)S(1)}, f32[8,1024]{1,0:T(8,128)S(1)}) custom-call(s32[3]{0:T(128)S(1)} %copy-done.1, bf16[256,2048]{1,0:T(8,128)(2,1)S(1)} %bitcast.36, bf16[256,2048]{1,0:T(8,128)(2,1)S(1)} %collective-permute-done.6.refs_2_, ...), custom_call_target="tpu_custom_call" | custom-call | flops 4000000000 | bytes 1 | tf_op jit(solution)/shard_map/attend_and_pool/pallas_call | solution.py:303
  67.0 0.1 collective-permute-start.17
  67.1 0.4 collective-permute-done.15
  67.5 0.5 collective-permute-start.18
  68.0 5.4 %collective-permute-done.20.refs_11_ = bf16[256,384]{1,0:T(8,128)(2,1)S(1)} collective-permute-done((bf16[256,384]{1,0:T(8,128)(2,1)S(1)}, bf16[256,384]{1,0:T(8,128)(2,1)S(1)}, u32[]{:S(2)}, u32[]{:S(2)}) %collective-permute-start.20) | collective-permute-done | bytes 196640 | tf_op jit(solution)/shard_map/second/ppermute | solution.py:411
  73.5 0.0 collective-permute-start.19
  73.5 4.6 %attend.2 = (bf16[144,128]{1,0:T(8,128)(2,1)S(1)}, bf16[144,128]{1,0:T(8,128)(2,1)S(1)}, bf16[144,128]{1,0:T(8,128)(2,1)S(1)}, bf16[144,128]{1,0:T(8,128)(2,1)S(1)}) custom-call(s32[3]{0:T(128)S(1)} %copy-done.1, bf16[256,2048]{1,0:T(8,128)(2,1)S(1)} %bitcast.37, bf16[256,2048]{1,0:T(8,128)(2,1)S(1)} %collective-permute-done.6.refs_2_, ...), custom_call_target="tpu_custom_call" | custom-call | flops 4000000000 | bytes 1 | tf_op jit(solution)/shard_map/attend/pallas_call | solution.py:303
  78.1 0.0 collective-permute-done.17.refs_1_
  78.2 0.2 pad_maximum_fusion.refs_15_
  78.4 0.5 collective-permute-start.30
  78.9 0.0 copy-start.2
  78.9 1.9 %collective-permute-start.21 = (bf16[4,144,128]{2,1,0:T(8,128)(2,1)S(1)}, bf16[4,144,128]{2,1,0:T(8,128)(2,1)S(1)}, u32[]{:S(2)}, u32[]{:S(2)}) collective-permute-start(bf16[4,144,128]{2,1,0:T(8,128)(2,1)S(1)} %pad_maximum_fusion.3), channel_id=1, source_target_pairs={{0,1},{1,0},{2,3},{3,2},{4,5},{5,4},{6,7},{7,6},{8,9},{9,8},{10,11... | collective-permute-start | bytes 442376 | tf_op jit(solution)/shard_map/context_first_group/ppermute | solution.py:405
  80.7 1.5 %collective-permute-start.23 = (bf16[144,128]{1,0:T(8,128)(2,1)S(1)}, bf16[144,128]{1,0:T(8,128)(2,1)S(1)}, u32[]{:S(2)}, u32[]{:S(2)}) collective-permute-start(bf16[144,128]{1,0:T(8,128)(2,1)S(1)} %get-tuple-element.68), channel_id=1, source_target_pairs={{0,4},{2,6},{4,0},{6,2},{1,5},{3,7},{5,1},{7,3},{8,12},{10,14},{12... | collective-permute-start | bytes 110600 | tf_op jit(solution)/shard_map/context_second/ppermute | solution.py:405
  82.2 0.4 collective-permute-start.24
  82.6 4.7 %attend.3 = (bf16[144,128]{1,0:T(8,128)(2,1)S(1)}, bf16[144,128]{1,0:T(8,128)(2,1)S(1)}, bf16[144,128]{1,0:T(8,128)(2,1)S(1)}, bf16[144,128]{1,0:T(8,128)(2,1)S(1)}) custom-call(s32[3]{0:T(128)S(1)} %copy-done.1, bf16[256,2048]{1,0:T(8,128)(2,1)S(1)} %bitcast.38, bf16[256,2048]{1,0:T(8,128)(2,1)S(1)} %collective-permute-done.6.refs_2_, ...), custom_call_target="tpu_custom_call" | custom-call | flops 4000000000 | bytes 1 | tf_op jit(solution)/shard_map/attend/pallas_call | solution.py:303
  87.3 0.3 collective-permute-start.26
  87.6 1.5 %collective-permute-start.27 = (bf16[144,128]{1,0:T(8,128)(2,1)S(1)}, bf16[144,128]{1,0:T(8,128)(2,1)S(1)}, u32[]{:S(2)}, u32[]{:S(2)}) collective-permute-start(bf16[144,128]{1,0:T(8,128)(2,1)S(1)} %get-tuple-element.73), channel_id=1, source_target_pairs={{0,4},{2,6},{4,0},{6,2},{1,5},{3,7},{5,1},{7,3},{8,12},{10,14},{12... | collective-permute-start | bytes 110600 | tf_op jit(solution)/shard_map/context_third/ppermute | solution.py:405
  89.1 0.1 collective-permute-start.28
  89.2 0.5 collective-permute-start.25
  89.7 1.8 %collective-permute-done.27.refs_12_ = bf16[144,128]{1,0:T(8,128)(2,1)S(1)} collective-permute-done((bf16[144,128]{1,0:T(8,128)(2,1)S(1)}, bf16[144,128]{1,0:T(8,128)(2,1)S(1)}, u32[]{:S(2)}, u32[]{:S(2)}) %collective-permute-start.27) | collective-permute-done | bytes 36896 | tf_op jit(solution)/shard_map/context_third/ppermute | solution.py:405
  91.6 1.2 %collective-permute-done.28.refs_13_ = bf16[144,128]{1,0:T(8,128)(2,1)S(1)} collective-permute-done((bf16[144,128]{1,0:T(8,128)(2,1)S(1)}, bf16[144,128]{1,0:T(8,128)(2,1)S(1)}, u32[]{:S(2)}, u32[]{:S(2)}) %collective-permute-start.28) | collective-permute-done | bytes 36896 | tf_op jit(solution)/shard_map/context_third/ppermute | solution.py:405
  92.8 0.6 collective-permute-start.29
  93.4 2.3 %collective-permute-done.25.refs_9_ = bf16[4,144,128]{2,1,0:T(8,128)(2,1)S(1)} collective-permute-done((bf16[4,144,128]{2,1,0:T(8,128)(2,1)S(1)}, bf16[4,144,128]{2,1,0:T(8,128)(2,1)S(1)}, u32[]{:S(2)}, u32[]{:S(2)}) %collective-permute-start.25) | collective-permute-done | bytes 147488 | tf_op jit(solution)/shard_map/context_second_group/ppermute | solution.py:405
  95.6 3.2 %collective-permute-done.29.refs_14_ = bf16[4,144,128]{2,1,0:T(8,128)(2,1)S(1)} collective-permute-done((bf16[4,144,128]{2,1,0:T(8,128)(2,1)S(1)}, bf16[4,144,128]{2,1,0:T(8,128)(2,1)S(1)}, u32[]{:S(2)}, u32[]{:S(2)}) %collective-permute-start.29) | collective-permute-done | bytes 147488 | tf_op jit(solution)/shard_map/context_third_group/ppermute | solution.py:405
  98.8 3.7 %project.1 = (bf16[256,1024]{1,0:T(8,128)(2,1)}, f32[4,1024]{1,0:T(4,128)S(1)}, f32[4,1024]{1,0:T(4,128)S(1)}) custom-call(s32[3]{0:T(128)S(1)} %copy-done.1, s32[8]{0:T(128)S(1)} %bitcast.52, bf16[256,2048]{1,0:T(8,128)(2,1)S(1)} %bitcast.39, f32[8,1024]{1,0:T(8,128)S(1)} %get-tuple-element.52.pool_ref, bf16[144,128]{1,0:T(8,128)(2,1)S(1)} %get-tuple-element.62.refs_0_, ...), custom_call_target="tpu_custom_call" | custom-call | flops 1 | bytes 1 | tf_op jit(solution)/shard_map/project/pallas_call | solution.py:384
  102.5 0.5 collective-permute-start.31
  103.0 3.2 %collective-permute-done.31 = f32[4,1024]{1,0:T(4,128)S(1)} collective-permute-done((f32[4,1024]{1,0:T(4,128)S(1)}, f32[4,1024]{1,0:T(4,128)S(1)}, u32[]{:S(2)}, u32[]{:S(2)}) %collective-permute-start.31) | collective-permute-done | bytes 16416 | tf_op jit(solution)/shard_map/embedding_half/ppermute | solution.py:405
  106.3 0.2 select_bitcast_fusion.5
  106.4 0.7 maximum_multiply_fusion
  (45 shorter events, 0.2 us)
Async XLA Ops:
  0.6 38.0 %collective-permute-start.6 = (bf16[256,2048]{1,0:T(8,128)(2,1)}, bf16[256,2048]{1,0:T(8,128)(2,1)S(1)}, u32[]{:S(2)}, u32[]{:S(2)}) collective-permute-start(bf16[256,2048]{1,0:T(8,128)(2,1)} %bitcast.34), channel_id=1, source_target_pairs={{0,2},{2,0},{4,6},{6,4},{1,3},{3,1},{5,7},{7,5},{8,10},{10,8},{12,... | collective-permute-start | bytes 3145736 | tf_op jit(solution)/shard_map/hidden_core/ppermute | solution.py:405
  1.1 37.4 %collective-permute-start.7 = (bf16[256,2048]{1,0:T(8,128)(2,1)}, bf16[256,2048]{1,0:T(8,128)(2,1)S(1)}, u32[]{:S(2)}, u32[]{:S(2)}) collective-permute-start(bf16[256,2048]{1,0:T(8,128)(2,1)} %bitcast.35), channel_id=1, source_target_pairs={{0,4},{2,6},{4,0},{6,2},{1,5},{3,7},{5,1},{7,3},{8,12},{10,14},{12... | collective-permute-start | bytes 3145736 | tf_op jit(solution)/shard_map/hidden_cross/ppermute | solution.py:405
  7.2 9.7 %collective-permute-start = (bf16[128,768]{1,0:T(8,128)(2,1)}, bf16[128,768]{1,0:T(8,128)(2,1)S(1)}, u32[]{:S(2)}, u32[]{:S(2)}) collective-permute-start(bf16[128,768]{1,0:T(8,128)(2,1)} %get-tuple-element.42), channel_id=1, source_target_pairs={{0,8},{8,16},{16,24},{24,0},{1,9},{9,17},{17,25},{25,1},{2,10},{10... | collective-permute-start | bytes 589832 | tf_op jit(solution)/shard_map/out/ppermute | solution.py:411
  8.8 12.0 %collective-permute-start.3 = (bf16[256,384]{1,0:T(8,128)(2,1)}, bf16[256,384]{1,0:T(8,128)(2,1)S(1)}, u32[]{:S(2)}, u32[]{:S(2)}) collective-permute-start(bf16[256,384]{1,0:T(8,128)(2,1)} %get-tuple-element.43.refs_8_), channel_id=1, source_target_pairs={{0,8},{8,16},{16,24},{24,0},{1,9},{9,17},{17,25},{25,1},{2,10},{10... | collective-permute-start | bytes 589832 | tf_op jit(solution)/shard_map/first/ppermute | solution.py:411
  16.9 8.2 %copy-start.11 = (bf16[128,768]{1,0:T(8,128)(2,1)}, bf16[128,768]{1,0:T(8,128)(2,1)S(1)}, u32[]{:S(2)}) copy-start(bf16[128,768]{1,0:T(8,128)(2,1)S(1)} %collective-permute-done) | copy-start | bytes 589828
  16.9 8.1 %collective-permute-start.1 = (bf16[128,768]{1,0:T(8,128)(2,1)S(1)}, bf16[128,768]{1,0:T(8,128)(2,1)S(1)}, u32[]{:S(2)}, u32[]{:S(2)}) collective-permute-start(bf16[128,768]{1,0:T(8,128)(2,1)S(1)} %collective-permute-done), channel_id=1, source_target_pairs={{0,8},{8,16},{16,24},{24,0},{1,9},{9,17},{17,25},{25,1},{2,10},{10... | collective-permute-start | bytes 589832 | tf_op jit(solution)/shard_map/out/ppermute | solution.py:411
  20.8 9.6 %collective-permute-start.4 = (bf16[256,384]{1,0:T(8,128)(2,1)S(1)}, bf16[256,384]{1,0:T(8,128)(2,1)S(1)}, u32[]{:S(2)}, u32[]{:S(2)}) collective-permute-start(bf16[256,384]{1,0:T(8,128)(2,1)S(1)} %collective-permute-done.3.refs_9_), channel_id=1, source_target_pairs={{0,8},{8,16},{16,24},{24,0},{1,9},{9,17},{17,25},{25,1},{2,10},{10... | collective-permute-start | bytes 589832 | tf_op jit(solution)/shard_map/first/ppermute | solution.py:411
  25.0 13.6 %copy-start.12 = (bf16[128,768]{1,0:T(8,128)(2,1)}, bf16[128,768]{1,0:T(8,128)(2,1)S(1)}, u32[]{:S(2)}) copy-start(bf16[128,768]{1,0:T(8,128)(2,1)S(1)} %collective-permute-done.1) | copy-start | bytes 589828
  25.0 9.3 %collective-permute-start.2 = (bf16[128,768]{1,0:T(8,128)(2,1)S(1)}, bf16[128,768]{1,0:T(8,128)(2,1)S(1)}, u32[]{:S(2)}, u32[]{:S(2)}) collective-permute-start(bf16[128,768]{1,0:T(8,128)(2,1)S(1)} %collective-permute-done.1), channel_id=1, source_target_pairs={{0,8},{8,16},{16,24},{24,0},{1,9},{9,17},{17,25},{25,1},{2,10},{10... | collective-permute-start | bytes 589832 | tf_op jit(solution)/shard_map/out/ppermute | solution.py:411
  30.4 7.5 %collective-permute-start.5 = (bf16[256,384]{1,0:T(8,128)(2,1)S(1)}, bf16[256,384]{1,0:T(8,128)(2,1)S(1)}, u32[]{:S(2)}, u32[]{:S(2)}) collective-permute-start(bf16[256,384]{1,0:T(8,128)(2,1)S(1)} %collective-permute-done.4.refs_10_), channel_id=1, source_target_pairs={{0,8},{8,16},{16,24},{24,0},{1,9},{9,17},{17,25},{25,1},{2,10},{10... | collective-permute-start | bytes 589832 | tf_op jit(solution)/shard_map/first/ppermute | solution.py:411
  34.3 4.3 %copy-start.13 = (bf16[128,768]{1,0:T(8,128)(2,1)}, bf16[128,768]{1,0:T(8,128)(2,1)S(1)}, u32[]{:S(2)}) copy-start(bf16[128,768]{1,0:T(8,128)(2,1)S(1)} %collective-permute-done.2) | copy-start | bytes 589828
  37.9 0.7 copy-start.6
  38.6 23.3 %collective-permute-start.8 = (bf16[256,2048]{1,0:T(8,128)(2,1)S(1)}, bf16[256,2048]{1,0:T(8,128)(2,1)S(1)}, u32[]{:S(2)}, u32[]{:S(2)}) collective-permute-start(bf16[256,2048]{1,0:T(8,128)(2,1)S(1)} %collective-permute-done.7.refs_3_), channel_id=1, source_target_pairs={{0,2},{2,0},{4,6},{6,4},{1,3},{3,1},{5,7},{7,5},{8,10},{10,8},{12,... | collective-permute-start | bytes 3145736 | tf_op jit(solution)/shard_map/hidden_far/ppermute | solution.py:405
  38.8 23.2 %copy-start = (bf16[1,256,2048]{2,1,0:T(8,128)(2,1)S(1)}, bf16[1,256,2048]{2,1,0:T(8,128)(2,1)}, u32[]{:S(2)}) copy-start(bf16[1,256,2048]{2,1,0:T(8,128)(2,1)} %param.6) | copy-start | bytes 3145732
  38.8 23.2 %copy-start.1 = (s32[3]{0:T(128)S(1)}, s32[3]{0:T(128)}, u32[]{:S(2)}) copy-start(s32[3]{0:T(128)} %pad_add_fusion.where.refs_0_) | copy-start | bytes 40
  38.8 23.2 %copy-start.5 = (bf16[256,384]{1,0:T(8,128)(2,1)S(1)}, bf16[256,384]{1,0:T(8,128)(2,1)}, u32[]{:S(2)}) copy-start(bf16[256,384]{1,0:T(8,128)(2,1)} %get-tuple-element.43.refs_8_) | copy-start | bytes 589828
  38.8 23.2 %copy-start.7 = (bf16[256,384]{1,0:T(8,128)(2,1)S(1)}, bf16[256,384]{1,0:T(8,128)(2,1)}, u32[]{:S(2)}) copy-start(bf16[256,384]{1,0:T(8,128)(2,1)} %copy-done.6) | copy-start | bytes 589828
  38.8 23.2 %copy-start.8 = (s32[1,32]{1,0:T(1,128)S(1)}, s32[1,32]{1,0:T(1,128)}, u32[]{:S(2)}) copy-start(s32[1,32]{1,0:T(1,128)} %refs_7_.5) | copy-start | bytes 388
  38.8 23.2 %copy-start.9 = (f32[1024,128]{1,0:T(8,128)S(1)}, f32[1024,128]{1,0:T(8,128)}, u32[]{:S(2)}) copy-start(f32[1024,128]{1,0:T(8,128)} %constant.62.clone.refs_5_) | copy-start | bytes 1572868
  38.8 23.2 %copy-start.10 = (f32[1024,128]{1,0:T(8,128)S(1)}, f32[1024,128]{1,0:T(8,128)}, u32[]{:S(2)}) copy-start(f32[1024,128]{1,0:T(8,128)} %constant.63.clone.refs_6_) | copy-start | bytes 1572868
  40.0 9.8 %collective-permute-start.9 = (bf16[256,384]{1,0:T(8,128)(2,1)}, bf16[256,384]{1,0:T(8,128)(2,1)S(1)}, u32[]{:S(2)}, u32[]{:S(2)}) collective-permute-start(bf16[256,384]{1,0:T(8,128)(2,1)} %get-tuple-element.49.refs_8_), channel_id=1, source_target_pairs={{0,8},{8,16},{16,24},{24,0},{1,9},{9,17},{17,25},{25,1},{2,10},{10... | collective-permute-start | bytes 589832 | tf_op jit(solution)/shard_map/second/ppermute | solution.py:411
  40.1 13.6 %collective-permute-start.11 = (bf16[256,384]{1,0:T(8,128)(2,1)}, bf16[256,384]{1,0:T(8,128)(2,1)S(1)}, u32[]{:S(2)}, u32[]{:S(2)}) collective-permute-start(bf16[256,384]{1,0:T(8,128)(2,1)} %get-tuple-element.50.refs_8_), channel_id=1, source_target_pairs={{0,8},{8,16},{16,24},{24,0},{1,9},{9,17},{17,25},{25,1},{2,10},{10... | collective-permute-start | bytes 589832 | tf_op jit(solution)/shard_map/third/ppermute | solution.py:411
  49.9 8.1 %collective-permute-start.10 = (bf16[256,384]{1,0:T(8,128)(2,1)S(1)}, bf16[256,384]{1,0:T(8,128)(2,1)S(1)}, u32[]{:S(2)}, u32[]{:S(2)}) collective-permute-start(bf16[256,384]{1,0:T(8,128)(2,1)S(1)} %collective-permute-done.9.refs_9_), channel_id=1, source_target_pairs={{0,8},{8,16},{16,24},{24,0},{1,9},{9,17},{17,25},{25,1},{2,10},{10... | collective-permute-start | bytes 589832 | tf_op jit(solution)/shard_map/second/ppermute | solution.py:411
  53.7 8.2 %collective-permute-start.12 = (bf16[256,384]{1,0:T(8,128)(2,1)S(1)}, bf16[256,384]{1,0:T(8,128)(2,1)S(1)}, u32[]{:S(2)}, u32[]{:S(2)}) collective-permute-start(bf16[256,384]{1,0:T(8,128)(2,1)S(1)} %collective-permute-done.11.refs_9_), channel_id=1, source_target_pairs={{0,8},{8,16},{16,24},{24,0},{1,9},{9,17},{17,25},{25,1},{2,10},{10... | collective-permute-start | bytes 589832 | tf_op jit(solution)/shard_map/third/ppermute | solution.py:411
  53.8 13.2 %collective-permute-start.14 = (bf16[2,128,768]{2,1,0:T(8,128)(2,1)S(1)}, bf16[2,128,768]{2,1,0:T(8,128)(2,1)S(1)}, u32[]{:S(2)}, u32[]{:S(2)}) collective-permute-start(bf16[2,128,768]{2,1,0:T(8,128)(2,1)S(1)} %pad_maximum_fusion.2), channel_id=1, source_target_pairs={{0,1},{1,0},{2,3},{3,2},{4,5},{5,4},{6,7},{7,6},{8,9},{9,8},{10,11... | collective-permute-start | bytes 1179656 | tf_op jit(solution)/shard_map/out_group/ppermute | solution.py:405
  55.4 18.1 %copy-start.4 = (bf16[256,384]{1,0:T(8,128)(2,1)S(1)}, bf16[256,384]{1,0:T(8,128)(2,1)}, u32[]{:S(2)}) copy-start(bf16[256,384]{1,0:T(8,128)(2,1)} %get-tuple-element.49.refs_8_) | copy-start | bytes 589828
  55.4 12.1 %collective-permute-start.15 = (bf16[2,128,768]{2,1,0:T(8,128)(2,1)S(1)}, bf16[2,128,768]{2,1,0:T(8,128)(2,1)S(1)}, u32[]{:S(2)}, u32[]{:S(2)}) collective-permute-start(bf16[2,128,768]{2,1,0:T(8,128)(2,1)S(1)} %pad_maximum_fusion.1), channel_id=1, source_target_pairs={{0,4},{2,6},{4,0},{6,2},{1,5},{3,7},{5,1},{7,3},{8,12},{10,14},{12... | collective-permute-start | bytes 1179656 | tf_op jit(solution)/shard_map/out_cross/ppermute | solution.py:405
  57.9 20.2 %collective-permute-start.16 = (bf16[2,128,768]{2,1,0:T(8,128)(2,1)S(1)}, bf16[2,128,768]{2,1,0:T(8,128)(2,1)S(1)}, u32[]{:S(2)}, u32[]{:S(2)}) collective-permute-start(bf16[2,128,768]{2,1,0:T(8,128)(2,1)S(1)} %pad_maximum_fusion.2), channel_id=1, source_target_pairs={{0,5},{1,4},{2,7},{3,6},{4,1},{5,0},{6,3},{7,2},{8,13},{9,12},{10,... | collective-permute-start | bytes 1179656 | tf_op jit(solution)/shard_map/out_across/ppermute | solution.py:435
  61.9 16.2 %collective-permute-start.13 = (bf16[256,384]{1,0:T(8,128)(2,1)S(1)}, bf16[256,384]{1,0:T(8,128)(2,1)S(1)}, u32[]{:S(2)}, u32[]{:S(2)}) collective-permute-start(bf16[256,384]{1,0:T(8,128)(2,1)S(1)} %collective-permute-done.12.refs_10_), channel_id=1, source_target_pairs={{0,8},{8,16},{16,24},{24,0},{1,9},{9,17},{17,25},{25,1},{2,10},{10... | collective-permute-start | bytes 589832 | tf_op jit(solution)/shard_map/third/ppermute | solution.py:411
  61.9 11.5 %collective-permute-start.20 = (bf16[256,384]{1,0:T(8,128)(2,1)S(1)}, bf16[256,384]{1,0:T(8,128)(2,1)S(1)}, u32[]{:S(2)}, u32[]{:S(2)}) collective-permute-start(bf16[256,384]{1,0:T(8,128)(2,1)S(1)} %collective-permute-done.10.refs_10_), channel_id=1, source_target_pairs={{0,8},{8,16},{16,24},{24,0},{1,9},{9,17},{17,25},{25,1},{2,10},{10... | collective-permute-start | bytes 589832 | tf_op jit(solution)/shard_map/second/ppermute | solution.py:411
  67.0 11.1 %collective-permute-start.17 = (bf16[144,128]{1,0:T(8,128)(2,1)S(1)}, bf16[144,128]{1,0:T(8,128)(2,1)S(1)}, u32[]{:S(2)}, u32[]{:S(2)}) collective-permute-start(bf16[144,128]{1,0:T(8,128)(2,1)S(1)} %get-tuple-element.55), channel_id=1, source_target_pairs={{0,2},{2,0},{4,6},{6,4},{1,3},{3,1},{5,7},{7,5},{8,10},{10,8},{12,... | collective-permute-start | bytes 110600 | tf_op jit(solution)/shard_map/context_first/ppermute | solution.py:405
  67.5 10.6 %collective-permute-start.18 = (bf16[144,128]{1,0:T(8,128)(2,1)S(1)}, bf16[144,128]{1,0:T(8,128)(2,1)S(1)}, u32[]{:S(2)}, u32[]{:S(2)}) collective-permute-start(bf16[144,128]{1,0:T(8,128)(2,1)S(1)} %get-tuple-element.56), channel_id=1, source_target_pairs={{0,4},{2,6},{4,0},{6,2},{1,5},{3,7},{5,1},{7,3},{8,12},{10,14},{12... | collective-permute-start | bytes 110600 | tf_op jit(solution)/shard_map/context_first/ppermute | solution.py:405
  73.5 4.7 %collective-permute-start.19 = (bf16[144,128]{1,0:T(8,128)(2,1)S(1)}, bf16[144,128]{1,0:T(8,128)(2,1)S(1)}, u32[]{:S(2)}, u32[]{:S(2)}) collective-permute-start(bf16[144,128]{1,0:T(8,128)(2,1)S(1)} %get-tuple-element.57), channel_id=1, source_target_pairs={{0,6},{2,4},{4,2},{6,0},{1,7},{3,5},{5,3},{7,1},{8,14},{10,12},{12... | collective-permute-start | bytes 110600 | tf_op jit(solution)/shard_map/context_first/ppermute | solution.py:405
  78.2 4.4 %copy-start.3 = (bf16[256,384]{1,0:T(8,128)(2,1)S(1)}, bf16[256,384]{1,0:T(8,128)(2,1)}, u32[]{:S(2)}) copy-start(bf16[256,384]{1,0:T(8,128)(2,1)} %get-tuple-element.50.refs_8_) | copy-start | bytes 589828
  78.4 20.5 %collective-permute-start.30 = (bf16[4,2,128,768]{3,2,1,0:T(8,128)(2,1)S(1)}, bf16[4,2,128,768]{3,2,1,0:T(8,128)(2,1)S(1)}, u32[]{:S(2)}, u32[]{:S(2)}) collective-permute-start(bf16[4,2,128,768]{3,2,1,0:T(8,128)(2,1)S(1)} %pad_maximum_fusion.refs_15_), channel_id=1, source_target_pairs={{0,2},{2,0},{4,6},{6,4},{1,3},{3,1},{5,7},{7,5},{8,10},{10,8},{12,... | collective-permute-start | bytes 4718600 | tf_op jit(solution)/shard_map/out_core/ppermute | solution.py:405
  78.9 20.0 %copy-start.2 = (s32[1,8,1]{1,2,0:T(1,128)S(1)}, s32[1,8,1]{1,2,0:T(1,128)}, u32[]{:S(2)}) copy-start(s32[1,8,1]{1,2,0:T(1,128)} %param.9) | copy-start | bytes 100
  78.9 14.5 %collective-permute-start.21 = (bf16[4,144,128]{2,1,0:T(8,128)(2,1)S(1)}, bf16[4,144,128]{2,1,0:T(8,128)(2,1)S(1)}, u32[]{:S(2)}, u32[]{:S(2)}) collective-permute-start(bf16[4,144,128]{2,1,0:T(8,128)(2,1)S(1)} %pad_maximum_fusion.3), channel_id=1, source_target_pairs={{0,1},{1,0},{2,3},{3,2},{4,5},{5,4},{6,7},{7,6},{8,9},{9,8},{10,11... | collective-permute-start | bytes 442376 | tf_op jit(solution)/shard_map/context_first_group/ppermute | solution.py:405
  80.7 6.5 %collective-permute-start.22 = (bf16[144,128]{1,0:T(8,128)(2,1)S(1)}, bf16[144,128]{1,0:T(8,128)(2,1)S(1)}, u32[]{:S(2)}, u32[]{:S(2)}) collective-permute-start(bf16[144,128]{1,0:T(8,128)(2,1)S(1)} %get-tuple-element.67), channel_id=1, source_target_pairs={{0,2},{2,0},{4,6},{6,4},{1,3},{3,1},{5,7},{7,5},{8,10},{10,8},{12,... | collective-permute-start | bytes 110600 | tf_op jit(solution)/shard_map/context_second/ppermute | solution.py:405
  80.7 6.9 %collective-permute-start.23 = (bf16[144,128]{1,0:T(8,128)(2,1)S(1)}, bf16[144,128]{1,0:T(8,128)(2,1)S(1)}, u32[]{:S(2)}, u32[]{:S(2)}) collective-permute-start(bf16[144,128]{1,0:T(8,128)(2,1)S(1)} %get-tuple-element.68), channel_id=1, source_target_pairs={{0,4},{2,6},{4,0},{6,2},{1,5},{3,7},{5,1},{7,3},{8,12},{10,14},{12... | collective-permute-start | bytes 110600 | tf_op jit(solution)/shard_map/context_second/ppermute | solution.py:405
  82.2 6.9 %collective-permute-start.24 = (bf16[144,128]{1,0:T(8,128)(2,1)S(1)}, bf16[144,128]{1,0:T(8,128)(2,1)S(1)}, u32[]{:S(2)}, u32[]{:S(2)}) collective-permute-start(bf16[144,128]{1,0:T(8,128)(2,1)S(1)} %get-tuple-element.69), channel_id=1, source_target_pairs={{0,6},{2,4},{4,2},{6,0},{1,7},{3,5},{5,3},{7,1},{8,14},{10,12},{12... | collective-permute-start | bytes 110600 | tf_op jit(solution)/shard_map/context_second/ppermute | solution.py:405
  87.3 2.0 %collective-permute-start.26 = (bf16[144,128]{1,0:T(8,128)(2,1)S(1)}, bf16[144,128]{1,0:T(8,128)(2,1)S(1)}, u32[]{:S(2)}, u32[]{:S(2)}) collective-permute-start(bf16[144,128]{1,0:T(8,128)(2,1)S(1)} %get-tuple-element.72), channel_id=1, source_target_pairs={{0,2},{2,0},{4,6},{6,4},{1,3},{3,1},{5,7},{7,5},{8,10},{10,8},{12,... | collective-permute-start | bytes 110600 | tf_op jit(solution)/shard_map/context_third/ppermute | solution.py:405
  87.6 4.0 %collective-permute-start.27 = (bf16[144,128]{1,0:T(8,128)(2,1)S(1)}, bf16[144,128]{1,0:T(8,128)(2,1)S(1)}, u32[]{:S(2)}, u32[]{:S(2)}) collective-permute-start(bf16[144,128]{1,0:T(8,128)(2,1)S(1)} %get-tuple-element.73), channel_id=1, source_target_pairs={{0,4},{2,6},{4,0},{6,2},{1,5},{3,7},{5,1},{7,3},{8,12},{10,14},{12... | collective-permute-start | bytes 110600 | tf_op jit(solution)/shard_map/context_third/ppermute | solution.py:405
  89.1 3.7 %collective-permute-start.28 = (bf16[144,128]{1,0:T(8,128)(2,1)S(1)}, bf16[144,128]{1,0:T(8,128)(2,1)S(1)}, u32[]{:S(2)}, u32[]{:S(2)}) collective-permute-start(bf16[144,128]{1,0:T(8,128)(2,1)S(1)} %get-tuple-element.74), channel_id=1, source_target_pairs={{0,6},{2,4},{4,2},{6,0},{1,7},{3,5},{5,3},{7,1},{8,14},{10,12},{12... | collective-permute-start | bytes 110600 | tf_op jit(solution)/shard_map/context_third/ppermute | solution.py:405
  89.2 6.4 %collective-permute-start.25 = (bf16[4,144,128]{2,1,0:T(8,128)(2,1)S(1)}, bf16[4,144,128]{2,1,0:T(8,128)(2,1)S(1)}, u32[]{:S(2)}, u32[]{:S(2)}) collective-permute-start(bf16[4,144,128]{2,1,0:T(8,128)(2,1)S(1)} %pad_maximum_fusion.4), channel_id=1, source_target_pairs={{0,1},{1,0},{2,3},{3,2},{4,5},{5,4},{6,7},{7,6},{8,9},{9,8},{10,11... | collective-permute-start | bytes 442376 | tf_op jit(solution)/shard_map/context_second_group/ppermute | solution.py:405
  92.8 6.1 %collective-permute-start.29 = (bf16[4,144,128]{2,1,0:T(8,128)(2,1)S(1)}, bf16[4,144,128]{2,1,0:T(8,128)(2,1)S(1)}, u32[]{:S(2)}, u32[]{:S(2)}) collective-permute-start(bf16[4,144,128]{2,1,0:T(8,128)(2,1)S(1)} %pad_maximum_fusion.5), channel_id=1, source_target_pairs={{0,1},{1,0},{2,3},{3,2},{4,5},{5,4},{6,7},{7,6},{8,9},{9,8},{10,11... | collective-permute-start | bytes 442376 | tf_op jit(solution)/shard_map/context_third_group/ppermute | solution.py:405
  102.5 3.7 %collective-permute-start.31 = (f32[4,1024]{1,0:T(4,128)S(1)}, f32[4,1024]{1,0:T(4,128)S(1)}, u32[]{:S(2)}, u32[]{:S(2)}) collective-permute-start(f32[4,1024]{1,0:T(4,128)S(1)} %get-tuple-element.81), channel_id=1, source_target_pairs={{0,1},{1,0},{2,3},{3,2},{4,5},{5,4},{6,7},{7,6},{8,9},{9,8},{10,11... | collective-permute-start | bytes 49160 | tf_op jit(solution)/shard_map/embedding_half/ppermute | solution.py:405

commit v3 on v2

--- a/solution.py
+++ b/solution.py
@@ -12,7 +12,6 @@
 HD = 64
 HALF_WIN = 256
 
-ATTEND = pl.CostEstimate(flops=4 * 10**9, bytes_accessed=1, transcendentals=0)
 SHORT = pl.CostEstimate(flops=1, bytes_accessed=1, transcendentals=0)
 
 
@@ -307,7 +306,7 @@
         out_specs=[vmem] * len(out_shape),
         scratch_shapes=[pltpu.VMEM((total, 128), jnp.bfloat16)] * 4 + [pltpu.VMEM((count, total), jnp.bfloat16)],
         compiler_params=pltpu.CompilerParams(vmem_limit_bytes=24 * 2**20),
-        cost_estimate=ATTEND,
+        cost_estimate=SHORT,
         name="attend_and_pool" if pools else "attend",
     )(where, *blocks, *tables, *pieces)
 
@@ -445,11 +444,11 @@
     h_core = xor_send("hidden_core", h, "seq", 1)
     o0, x0, y0, z0 = pieces(where, proj_weight)
 
-    def rings(names, starts):
+    def rings(names, starts, **before):
         held = [[start] for start in starts]
         for step in range(3):
             for ring, name in zip(held, names):
-                ring.append(ring_send(name, ring[-1]))
+                ring.append(ring_send(name, after(ring[-1], before[name]) if step == 1 and name in before else ring[-1]))
         return held
 
     out_ring, first_ring = rings(("out", "first"), (o0, x0))
@@ -457,8 +456,8 @@
         (out_ring[3], first_ring[3], h_core, h_cross, y0, z0)
     )
 
-    second_ring, third_ring = rings(("second", "third"), (y0, z0))
     h_far = xor_send("hidden_far", h_cross, "seq", 1)
+    second_ring, third_ring = rings(("second", "third"), (y0, z0), third=h_far)
     blocks = [h, h_core, h_cross, h_far]
     four = across(out_ring)
     first_ring[3] = after(first_ring[3], second_ring[2], third_ring[2])

time: 107 us -> 104 us (0.972)
  waiting for transfers between devices: 61.2 us -> 55.1 us
  starting transfers between devices: 19.3 us -> 22.3 us
    ppermute x19, waiting for transfers between devices: 12.2 us -> 8.68 us  [xor_send(): lax.ppermute(value, axis, [(i, i ^ j) for i in range(lax.axis_size(axis))])]
    ppermute x19, starting transfers between devices: 13.6 us -> 16.6 us  [xor_send(): lax.ppermute(value, axis, [(i, i ^ j) for i in range(lax.axis_size(axis))])]
    ppermute x12, waiting for transfers between devices: 49 us -> 46.4 us  [ring_send(): lax.ppermute(value, 'dp', [(i, (i + 1) % count) for i in range(count)])]
  transfers between devices with their start and end apart: 32 -> 32, of which waited for: 17 -> 15; matrix products, arithmetic and copies ran while one was open for 3% -> 3% of each run, Pallas kernels for 16% -> 16%
where the time goes in v3:
time: 104 us
  waiting for transfers between devices  55.1 us (53%)
  starting transfers between devices  22.3 us (21%)
  Pallas kernels  20.8 us (20%)
  other arithmetic  4.05 us (4%)
    ppermute x12, waiting for transfers between devices, ring_send(): lax.ppermute(value, 'dp', [(i, (i + 1) % count) for i in range(count)])  46.4 us
    ppermute x19, starting transfers between devices, xor_send(): lax.ppermute(value, axis, [(i, i ^ j) for i in range(lax.axis_size(axis))])  16.6 us
    pallas_call x3, Pallas kernels, attend(): pl.pallas_call(functools.partial(attend_kernel, pools), out_shape=out_sha...  14.3 us
    ppermute x19, waiting for transfers between devices, xor_send(): lax.ppermute(value, axis, [(i, i ^ j) for i in range(lax.axis_size(axis))])  8.68 us
    ppermute x12, starting transfers between devices, ring_send(): lax.ppermute(value, 'dp', [(i, (i + 1) % count) for i in range(count)])  4.23 us
    pallas_call x1, Pallas kernels, project(): pl.pallas_call(project_kernel, out_shape=[jax.ShapeDtypeStruct((rows, fea...  3.67 us
    pallas_call x1, Pallas kernels, pieces(): pl.pallas_call(pieces_kernel, grid_spec=pltpu.PrefetchScalarGridSpec(num_...  2.86 us
    another operation x3, other arithmetic, across(): send = jnp.stack([jnp.where(mine, two, one) for mine, one, two in pairs])  2.29 us
  transfers between devices with their start and end apart: 32, of which 15 were waited for; matrix products, arithmetic and copies ran while one was open for 3% of the time, Pallas kernels for 16%

profile of v3, /device:TPU:0, one launch (start us, length us, event | category | flops | bytes accessed | tf_op | source)
XLA Modules:
  0.0 104.1 jit_solution(7124757325797097600)
XLA Ops:
  0.6 0.5 collective-permute-start.6
  1.1 2.6 %collective-permute-start.7 = (bf16[256,2048]{1,0:T(8,128)(2,1)}, bf16[256,2048]{1,0:T(8,128)(2,1)S(1)}, u32[]{:S(2)}, u32[]{:S(2)}) collective-permute-start(bf16[256,2048]{1,0:T(8,128)(2,1)} %bitcast.35), channel_id=1, source_target_pairs={{0,4},{2,6},{4,0},{6,2},{1,5},{3,7},{5,1},{7,3},{8,12},{10,14},{12... | collective-permute-start | bytes 3145736 | tf_op jit(solution)/shard_map/hidden_cross/ppermute | solution.py:404
  3.7 0.6 pad_add_fusion.where.refs_0_
  4.3 2.9 %pieces.1 = (bf16[128,768]{1,0:T(8,128)(2,1)}, bf16[256,384]{1,0:T(8,128)(2,1)}, bf16[256,384]{1,0:T(8,128)(2,1)}, bf16[256,384]{1,0:T(8,128)(2,1)}) custom-call(s32[3]{0:T(128)} %pad_add_fusion.where.refs_0_, bf16[4,512,768]{2,1,0:T(8,128)(2,1)} %o_ref.1, bf16[4,512,768]{2,1,0:T(8,128)(2,1)} %o_ref.1, bf16[4,512,768]{2,1,0:T(8,128)(2,1)} %o_ref.1), custom_call_target="tpu_custom_call" | custom-call | flops 1 | bytes 1 | tf_op jit(solution)/shard_map/pieces/pallas_call | solution.py:178
  7.2 1.6 %collective-permute-start = (bf16[128,768]{1,0:T(8,128)(2,1)}, bf16[128,768]{1,0:T(8,128)(2,1)S(1)}, u32[]{:S(2)}, u32[]{:S(2)}) collective-permute-start(bf16[128,768]{1,0:T(8,128)(2,1)} %get-tuple-element.43), channel_id=1, source_target_pairs={{0,8},{8,16},{16,24},{24,0},{1,9},{9,17},{17,25},{25,1},{2,10},{10... | collective-permute-start | bytes 589832 | tf_op jit(solution)/shard_map/out/ppermute | solution.py:410
  8.8 1.6 %collective-permute-start.3 = (bf16[256,384]{1,0:T(8,128)(2,1)}, bf16[256,384]{1,0:T(8,128)(2,1)S(1)}, u32[]{:S(2)}, u32[]{:S(2)}) collective-permute-start(bf16[256,384]{1,0:T(8,128)(2,1)} %get-tuple-element.44.refs_8_), channel_id=1, source_target_pairs={{0,8},{8,16},{16,24},{24,0},{1,9},{9,17},{17,25},{25,1},{2,10},{10... | collective-permute-start | bytes 589832 | tf_op jit(solution)/shard_map/first/ppermute | solution.py:410
  10.3 6.6 %collective-permute-done = bf16[128,768]{1,0:T(8,128)(2,1)S(1)} collective-permute-done((bf16[128,768]{1,0:T(8,128)(2,1)}, bf16[128,768]{1,0:T(8,128)(2,1)S(1)}, u32[]{:S(2)}, u32[]{:S(2)}) %collective-permute-start) | collective-permute-done | bytes 196640 | tf_op jit(solution)/shard_map/out/ppermute | solution.py:410
  16.9 0.0 collective-permute-start.1
  16.9 3.9 %collective-permute-done.3.refs_9_ = bf16[256,384]{1,0:T(8,128)(2,1)S(1)} collective-permute-done((bf16[256,384]{1,0:T(8,128)(2,1)}, bf16[256,384]{1,0:T(8,128)(2,1)S(1)}, u32[]{:S(2)}, u32[]{:S(2)}) %collective-permute-start.3) | collective-permute-done | bytes 196640 | tf_op jit(solution)/shard_map/first/ppermute | solution.py:410
  20.8 0.1 collective-permute-start.4
  20.9 4.1 %collective-permute-done.1 = bf16[128,768]{1,0:T(8,128)(2,1)S(1)} collective-permute-done((bf16[128,768]{1,0:T(8,128)(2,1)S(1)}, bf16[128,768]{1,0:T(8,128)(2,1)S(1)}, u32[]{:S(2)}, u32[]{:S(2)}) %collective-permute-start.1) | collective-permute-done | bytes 196640 | tf_op jit(solution)/shard_map/out/ppermute | solution.py:410
  25.0 0.1 collective-permute-start.2
  25.1 5.3 %collective-permute-done.4.refs_10_ = bf16[256,384]{1,0:T(8,128)(2,1)S(1)} collective-permute-done((bf16[256,384]{1,0:T(8,128)(2,1)S(1)}, bf16[256,384]{1,0:T(8,128)(2,1)S(1)}, u32[]{:S(2)}, u32[]{:S(2)}) %collective-permute-start.4) | collective-permute-done | bytes 196640 | tf_op jit(solution)/shard_map/first/ppermute | solution.py:410
  30.4 3.9 %collective-permute-done.2 = bf16[128,768]{1,0:T(8,128)(2,1)S(1)} collective-permute-done((bf16[128,768]{1,0:T(8,128)(2,1)S(1)}, bf16[128,768]{1,0:T(8,128)(2,1)S(1)}, u32[]{:S(2)}, u32[]{:S(2)}) %collective-permute-start.2) | collective-permute-done | bytes 196640 | tf_op jit(solution)/shard_map/out/ppermute | solution.py:410
  34.3 3.6 %collective-permute-done.5.refs_11_ = bf16[256,384]{1,0:T(8,128)(2,1)S(1)} collective-permute-done((bf16[256,384]{1,0:T(8,128)(2,1)S(1)}, bf16[256,384]{1,0:T(8,128)(2,1)S(1)}, u32[]{:S(2)}, u32[]{:S(2)}) %collective-permute-start.5) | collective-permute-done | bytes 196640 | tf_op jit(solution)/shard_map/first/ppermute | solution.py:410
  37.9 0.7 copy-done.6
  38.6 0.1 collective-permute-start.8
  38.8 0.0 copy-start
  38.8 0.0 copy-start.1
  38.8 0.0 copy-start.2
  38.8 0.0 copy-start.9
  38.8 1.2 %select_bitcast_fusion.1 = (bf16[1,128,768]{2,1,0:T(8,128)(2,1)S(1)}, bf16[1,128,768]{2,1,0:T(8,128)(2,1)S(1)}) fusion(bf16[128,768]{1,0:T(8,128)(2,1)} %copy-done.12, bf16[128,768]{1,0:T(8,128)(2,1)} %get-tuple-element.43, pred[]{:T(512)S(6)} %eq.13), kind=kLoop, calls=%fused_computation.4 | loop fusion | flops 196608 | bytes 786433 | tf_op jit(solution)/shard_map/stack | solution.py:432
  40.0 0.1 collective-permute-start.9
  40.1 0.7 collective-permute-start.11
  40.8 1.1 %select_bitcast_fusion = (bf16[1,128,768]{2,1,0:T(8,128)(2,1)S(1)}, bf16[1,128,768]{2,1,0:T(8,128)(2,1)S(1)}) fusion(bf16[128,768]{1,0:T(8,128)(2,1)} %copy-done.13, bf16[128,768]{1,0:T(8,128)(2,1)} %copy-done.11, pred[]{:T(512)S(6)} %eq.14), kind=kLoop, calls=%fused_computation.3 | loop fusion | flops 196608 | bytes 786433 | tf_op jit(solution)/shard_map/stack | solution.py:432
  41.9 1.6 %collective-permute-start.14 = (bf16[2,128,768]{2,1,0:T(8,128)(2,1)S(1)}, bf16[2,128,768]{2,1,0:T(8,128)(2,1)S(1)}, u32[]{:S(2)}, u32[]{:S(2)}) collective-permute-start(bf16[2,128,768]{2,1,0:T(8,128)(2,1)S(1)} %pad_maximum_fusion.2), channel_id=1, source_target_pairs={{0,1},{1,0},{2,3},{3,2},{4,5},{5,4},{6,7},{7,6},{8,9},{9,8},{10,11... | collective-permute-start | bytes 1179656 | tf_op jit(solution)/shard_map/out_group/ppermute | solution.py:404
  43.6 0.6 collective-permute-start.15
  44.2 5.7 %collective-permute-done.9.refs_9_ = bf16[256,384]{1,0:T(8,128)(2,1)S(1)} collective-permute-done((bf16[256,384]{1,0:T(8,128)(2,1)}, bf16[256,384]{1,0:T(8,128)(2,1)S(1)}, u32[]{:S(2)}, u32[]{:S(2)}) %collective-permute-start.9) | collective-permute-done | bytes 196640 | tf_op jit(solution)/shard_map/second/ppermute | solution.py:410
  49.8 0.0 collective-permute-start.10
  49.8 3.9 %collective-permute-done.11.refs_9_ = bf16[256,384]{1,0:T(8,128)(2,1)S(1)} collective-permute-done((bf16[256,384]{1,0:T(8,128)(2,1)}, bf16[256,384]{1,0:T(8,128)(2,1)S(1)}, u32[]{:S(2)}, u32[]{:S(2)}) %collective-permute-start.11) | collective-permute-done | bytes 196640 | tf_op jit(solution)/shard_map/third/ppermute | solution.py:410
  53.7 1.5 %collective-permute-start.16 = (bf16[2,128,768]{2,1,0:T(8,128)(2,1)S(1)}, bf16[2,128,768]{2,1,0:T(8,128)(2,1)S(1)}, u32[]{:S(2)}, u32[]{:S(2)}) collective-permute-start(bf16[2,128,768]{2,1,0:T(8,128)(2,1)S(1)} %pad_maximum_fusion.2), channel_id=1, source_target_pairs={{0,5},{1,4},{2,7},{3,6},{4,1},{5,0},{6,3},{7,2},{8,13},{9,12},{10,... | collective-permute-start | bytes 1179656 | tf_op jit(solution)/shard_map/out_across/ppermute | solution.py:434
  55.2 2.5 %collective-permute-done.10.refs_10_ = bf16[256,384]{1,0:T(8,128)(2,1)S(1)} collective-permute-done((bf16[256,384]{1,0:T(8,128)(2,1)S(1)}, bf16[256,384]{1,0:T(8,128)(2,1)S(1)}, u32[]{:S(2)}, u32[]{:S(2)}) %collective-permute-start.10) | collective-permute-done | bytes 196640 | tf_op jit(solution)/shard_map/second/ppermute | solution.py:410
  57.7 7.1 %collective-permute-done.12.refs_10_ = bf16[256,384]{1,0:T(8,128)(2,1)S(1)} collective-permute-done((bf16[256,384]{1,0:T(8,128)(2,1)S(1)}, bf16[256,384]{1,0:T(8,128)(2,1)S(1)}, u32[]{:S(2)}, u32[]{:S(2)}) %collective-permute-start.12) | collective-permute-done | bytes 196640 | tf_op jit(solution)/shard_map/third/ppermute | solution.py:410
  64.8 0.0 collective-permute-start.13
  64.9 5.0 %attend_and_pool.1 = (bf16[144,128]{1,0:T(8,128)(2,1)S(1)}, bf16[144,128]{1,0:T(8,128)(2,1)S(1)}, bf16[144,128]{1,0:T(8,128)(2,1)S(1)}, bf16[144,128]{1,0:T(8,128)(2,1)S(1)}, f32[8,1024]{1,0:T(8,128)S(1)}) custom-call(s32[3]{0:T(128)S(1)} %copy-done.8, bf16[256,2048]{1,0:T(8,128)(2,1)S(1)} %bitcast.36, bf16[256,2048]{1,0:T(8,128)(2,1)S(1)} %collective-permute-done.6.refs_2_, ...), custom_call_target="tpu_custom_call" | custom-call | flops 1 | bytes 1 | tf_op jit(solution)/shard_map/attend_and_pool/pallas_call | solution.py:302
  69.9 0.0 collective-permute-done.14
  69.9 0.1 collective-permute-start.17
  70.0 0.0 collective-permute-done.15
  70.0 1.6 %collective-permute-start.18 = (bf16[144,128]{1,0:T(8,128)(2,1)S(1)}, bf16[144,128]{1,0:T(8,128)(2,1)S(1)}, u32[]{:S(2)}, u32[]{:S(2)}) collective-permute-start(bf16[144,128]{1,0:T(8,128)(2,1)S(1)} %get-tuple-element.58), channel_id=1, source_target_pairs={{0,4},{2,6},{4,0},{6,2},{1,5},{3,7},{5,1},{7,3},{8,12},{10,14},{12... | collective-permute-start | bytes 110600 | tf_op jit(solution)/shard_map/context_first/ppermute | solution.py:404
  71.5 0.0 collective-permute-done.20.refs_11_
  71.5 0.3 collective-permute-start.19
  71.8 4.7 %attend.2 = (bf16[144,128]{1,0:T(8,128)(2,1)S(1)}, bf16[144,128]{1,0:T(8,128)(2,1)S(1)}, bf16[144,128]{1,0:T(8,128)(2,1)S(1)}, bf16[144,128]{1,0:T(8,128)(2,1)S(1)}) custom-call(s32[3]{0:T(128)S(1)} %copy-done.8, bf16[256,2048]{1,0:T(8,128)(2,1)S(1)} %bitcast.37, bf16[256,2048]{1,0:T(8,128)(2,1)S(1)} %collective-permute-done.6.refs_2_, ...), custom_call_target="tpu_custom_call" | custom-call | flops 1 | bytes 1 | tf_op jit(solution)/shard_map/attend/pallas_call | solution.py:302
  76.6 0.2 pad_maximum_fusion.refs_15_
  76.8 0.4 collective-permute-start.30
  77.2 0.2 collective-permute-start.22
  77.3 1.5 %collective-permute-start.23 = (bf16[144,128]{1,0:T(8,128)(2,1)S(1)}, bf16[144,128]{1,0:T(8,128)(2,1)S(1)}, u32[]{:S(2)}, u32[]{:S(2)}) collective-permute-start(bf16[144,128]{1,0:T(8,128)(2,1)S(1)} %get-tuple-element.70), channel_id=1, source_target_pairs={{0,4},{2,6},{4,0},{6,2},{1,5},{3,7},{5,1},{7,3},{8,12},{10,14},{12... | collective-permute-start | bytes 110600 | tf_op jit(solution)/shard_map/context_second/ppermute | solution.py:404
  78.8 0.2 collective-permute-start.24
  79.1 0.0 copy-start.10
  79.1 0.4 collective-permute-start.21
  79.5 4.6 %attend.3 = (bf16[144,128]{1,0:T(8,128)(2,1)S(1)}, bf16[144,128]{1,0:T(8,128)(2,1)S(1)}, bf16[144,128]{1,0:T(8,128)(2,1)S(1)}, bf16[144,128]{1,0:T(8,128)(2,1)S(1)}) custom-call(s32[3]{0:T(128)S(1)} %copy-done.8, bf16[256,2048]{1,0:T(8,128)(2,1)S(1)} %bitcast.38, bf16[256,2048]{1,0:T(8,128)(2,1)S(1)} %collective-permute-done.6.refs_2_, ...), custom_call_target="tpu_custom_call" | custom-call | flops 1 | bytes 1 | tf_op jit(solution)/shard_map/attend/pallas_call | solution.py:302
  84.1 0.2 collective-permute-start.26
  84.4 1.7 %collective-permute-start.27 = (bf16[144,128]{1,0:T(8,128)(2,1)S(1)}, bf16[144,128]{1,0:T(8,128)(2,1)S(1)}, u32[]{:S(2)}, u32[]{:S(2)}) collective-permute-start(bf16[144,128]{1,0:T(8,128)(2,1)S(1)} %get-tuple-element.75), channel_id=1, source_target_pairs={{0,4},{2,6},{4,0},{6,2},{1,5},{3,7},{5,1},{7,3},{8,12},{10,14},{12... | collective-permute-start | bytes 110600 | tf_op jit(solution)/shard_map/context_third/ppermute | solution.py:404
  86.1 0.0 collective-permute-start.28
  86.1 1.7 %collective-permute-start.25 = (bf16[4,144,128]{2,1,0:T(8,128)(2,1)S(1)}, bf16[4,144,128]{2,1,0:T(8,128)(2,1)S(1)}, u32[]{:S(2)}, u32[]{:S(2)}) collective-permute-start(bf16[4,144,128]{2,1,0:T(8,128)(2,1)S(1)} %pad_maximum_fusion.4), channel_id=1, source_target_pairs={{0,1},{1,0},{2,3},{3,2},{4,5},{5,4},{6,7},{7,6},{8,9},{9,8},{10,11... | collective-permute-start | bytes 442376 | tf_op jit(solution)/shard_map/context_second_group/ppermute | solution.py:404
  87.9 0.4 collective-permute-done.27.refs_12_
  88.3 1.3 %collective-permute-done.28.refs_13_ = bf16[144,128]{1,0:T(8,128)(2,1)S(1)} collective-permute-done((bf16[144,128]{1,0:T(8,128)(2,1)S(1)}, bf16[144,128]{1,0:T(8,128)(2,1)S(1)}, u32[]{:S(2)}, u32[]{:S(2)}) %collective-permute-start.28) | collective-permute-done | bytes 36896 | tf_op jit(solution)/shard_map/context_third/ppermute | solution.py:404
  89.6 1.6 %collective-permute-start.29 = (bf16[4,144,128]{2,1,0:T(8,128)(2,1)S(1)}, bf16[4,144,128]{2,1,0:T(8,128)(2,1)S(1)}, u32[]{:S(2)}, u32[]{:S(2)}) collective-permute-start(bf16[4,144,128]{2,1,0:T(8,128)(2,1)S(1)} %pad_maximum_fusion.5), channel_id=1, source_target_pairs={{0,1},{1,0},{2,3},{3,2},{4,5},{5,4},{6,7},{7,6},{8,9},{9,8},{10,11... | collective-permute-start | bytes 442376 | tf_op jit(solution)/shard_map/context_third_group/ppermute | solution.py:404
  91.2 1.2 %collective-permute-done.25.refs_9_ = bf16[4,144,128]{2,1,0:T(8,128)(2,1)S(1)} collective-permute-done((bf16[4,144,128]{2,1,0:T(8,128)(2,1)S(1)}, bf16[4,144,128]{2,1,0:T(8,128)(2,1)S(1)}, u32[]{:S(2)}, u32[]{:S(2)}) %collective-permute-start.25) | collective-permute-done | bytes 147488 | tf_op jit(solution)/shard_map/context_second_group/ppermute | solution.py:404
  92.4 3.4 %collective-permute-done.29.refs_14_ = bf16[4,144,128]{2,1,0:T(8,128)(2,1)S(1)} collective-permute-done((bf16[4,144,128]{2,1,0:T(8,128)(2,1)S(1)}, bf16[4,144,128]{2,1,0:T(8,128)(2,1)S(1)}, u32[]{:S(2)}, u32[]{:S(2)}) %collective-permute-start.29) | collective-permute-done | bytes 147488 | tf_op jit(solution)/shard_map/context_third_group/ppermute | solution.py:404
  95.8 3.7 %project.1 = (bf16[256,1024]{1,0:T(8,128)(2,1)}, f32[4,1024]{1,0:T(4,128)S(1)}, f32[4,1024]{1,0:T(4,128)S(1)}) custom-call(s32[3]{0:T(128)S(1)} %copy-done.8, s32[8]{0:T(128)S(1)} %bitcast.52, bf16[256,2048]{1,0:T(8,128)(2,1)S(1)} %bitcast.39, f32[8,1024]{1,0:T(8,128)S(1)} %get-tuple-element.54.pool_ref, bf16[144,128]{1,0:T(8,128)(2,1)S(1)} %get-tuple-element.64.refs_0_, ...), custom_call_target="tpu_custom_call" | custom-call | flops 1 | bytes 1 | tf_op jit(solution)/shard_map/project/pallas_call | solution.py:383
  99.5 1.4 %collective-permute-start.31 = (f32[4,1024]{1,0:T(4,128)S(1)}, f32[4,1024]{1,0:T(4,128)S(1)}, u32[]{:S(2)}, u32[]{:S(2)}) collective-permute-start(f32[4,1024]{1,0:T(4,128)S(1)} %get-tuple-element.83), channel_id=1, source_target_pairs={{0,1},{1,0},{2,3},{3,2},{4,5},{5,4},{6,7},{7,6},{8,9},{9,8},{10,11... | collective-permute-start | bytes 49160 | tf_op jit(solution)/shard_map/embedding_half/ppermute | solution.py:404
  100.9 2.3 %collective-permute-done.31 = f32[4,1024]{1,0:T(4,128)S(1)} collective-permute-done((f32[4,1024]{1,0:T(4,128)S(1)}, f32[4,1024]{1,0:T(4,128)S(1)}, u32[]{:S(2)}, u32[]{:S(2)}) %collective-permute-start.31) | collective-permute-done | bytes 16416 | tf_op jit(solution)/shard_map/embedding_half/ppermute | solution.py:404
  103.2 0.2 select_bitcast_fusion.5
  103.4 0.7 maximum_multiply_fusion
  (45 shorter events, 0.2 us)
Async XLA Ops:
  0.6 38.0 %collective-permute-start.6 = (bf16[256,2048]{1,0:T(8,128)(2,1)}, bf16[256,2048]{1,0:T(8,128)(2,1)S(1)}, u32[]{:S(2)}, u32[]{:S(2)}) collective-permute-start(bf16[256,2048]{1,0:T(8,128)(2,1)} %bitcast.34), channel_id=1, source_target_pairs={{0,2},{2,0},{4,6},{6,4},{1,3},{3,1},{5,7},{7,5},{8,10},{10,8},{12,... | collective-permute-start | bytes 3145736 | tf_op jit(solution)/shard_map/hidden_core/ppermute | solution.py:404
  1.1 37.4 %collective-permute-start.7 = (bf16[256,2048]{1,0:T(8,128)(2,1)}, bf16[256,2048]{1,0:T(8,128)(2,1)S(1)}, u32[]{:S(2)}, u32[]{:S(2)}) collective-permute-start(bf16[256,2048]{1,0:T(8,128)(2,1)} %bitcast.35), channel_id=1, source_target_pairs={{0,4},{2,6},{4,0},{6,2},{1,5},{3,7},{5,1},{7,3},{8,12},{10,14},{12... | collective-permute-start | bytes 3145736 | tf_op jit(solution)/shard_map/hidden_cross/ppermute | solution.py:404
  7.2 9.7 %collective-permute-start = (bf16[128,768]{1,0:T(8,128)(2,1)}, bf16[128,768]{1,0:T(8,128)(2,1)S(1)}, u32[]{:S(2)}, u32[]{:S(2)}) collective-permute-start(bf16[128,768]{1,0:T(8,128)(2,1)} %get-tuple-element.43), channel_id=1, source_target_pairs={{0,8},{8,16},{16,24},{24,0},{1,9},{9,17},{17,25},{25,1},{2,10},{10... | collective-permute-start | bytes 589832 | tf_op jit(solution)/shard_map/out/ppermute | solution.py:410
  8.8 12.0 %collective-permute-start.3 = (bf16[256,384]{1,0:T(8,128)(2,1)}, bf16[256,384]{1,0:T(8,128)(2,1)S(1)}, u32[]{:S(2)}, u32[]{:S(2)}) collective-permute-start(bf16[256,384]{1,0:T(8,128)(2,1)} %get-tuple-element.44.refs_8_), channel_id=1, source_target_pairs={{0,8},{8,16},{16,24},{24,0},{1,9},{9,17},{17,25},{25,1},{2,10},{10... | collective-permute-start | bytes 589832 | tf_op jit(solution)/shard_map/first/ppermute | solution.py:410
  16.9 8.2 %copy-start.11 = (bf16[128,768]{1,0:T(8,128)(2,1)}, bf16[128,768]{1,0:T(8,128)(2,1)S(1)}, u32[]{:S(2)}) copy-start(bf16[128,768]{1,0:T(8,128)(2,1)S(1)} %collective-permute-done) | copy-start | bytes 589828
  16.9 8.1 %collective-permute-start.1 = (bf16[128,768]{1,0:T(8,128)(2,1)S(1)}, bf16[128,768]{1,0:T(8,128)(2,1)S(1)}, u32[]{:S(2)}, u32[]{:S(2)}) collective-permute-start(bf16[128,768]{1,0:T(8,128)(2,1)S(1)} %collective-permute-done), channel_id=1, source_target_pairs={{0,8},{8,16},{16,24},{24,0},{1,9},{9,17},{17,25},{25,1},{2,10},{10... | collective-permute-start | bytes 589832 | tf_op jit(solution)/shard_map/out/ppermute | solution.py:410
  20.8 9.6 %collective-permute-start.4 = (bf16[256,384]{1,0:T(8,128)(2,1)S(1)}, bf16[256,384]{1,0:T(8,128)(2,1)S(1)}, u32[]{:S(2)}, u32[]{:S(2)}) collective-permute-start(bf16[256,384]{1,0:T(8,128)(2,1)S(1)} %collective-permute-done.3.refs_9_), channel_id=1, source_target_pairs={{0,8},{8,16},{16,24},{24,0},{1,9},{9,17},{17,25},{25,1},{2,10},{10... | collective-permute-start | bytes 589832 | tf_op jit(solution)/shard_map/first/ppermute | solution.py:410
  25.0 13.6 %copy-start.12 = (bf16[128,768]{1,0:T(8,128)(2,1)}, bf16[128,768]{1,0:T(8,128)(2,1)S(1)}, u32[]{:S(2)}) copy-start(bf16[128,768]{1,0:T(8,128)(2,1)S(1)} %collective-permute-done.1) | copy-start | bytes 589828
  25.0 9.3 %collective-permute-start.2 = (bf16[128,768]{1,0:T(8,128)(2,1)S(1)}, bf16[128,768]{1,0:T(8,128)(2,1)S(1)}, u32[]{:S(2)}, u32[]{:S(2)}) collective-permute-start(bf16[128,768]{1,0:T(8,128)(2,1)S(1)} %collective-permute-done.1), channel_id=1, source_target_pairs={{0,8},{8,16},{16,24},{24,0},{1,9},{9,17},{17,25},{25,1},{2,10},{10... | collective-permute-start | bytes 589832 | tf_op jit(solution)/shard_map/out/ppermute | solution.py:410
  30.4 7.5 %collective-permute-start.5 = (bf16[256,384]{1,0:T(8,128)(2,1)S(1)}, bf16[256,384]{1,0:T(8,128)(2,1)S(1)}, u32[]{:S(2)}, u32[]{:S(2)}) collective-permute-start(bf16[256,384]{1,0:T(8,128)(2,1)S(1)} %collective-permute-done.4.refs_10_), channel_id=1, source_target_pairs={{0,8},{8,16},{16,24},{24,0},{1,9},{9,17},{17,25},{25,1},{2,10},{10... | collective-permute-start | bytes 589832 | tf_op jit(solution)/shard_map/first/ppermute | solution.py:410
  34.3 4.3 %copy-start.13 = (bf16[128,768]{1,0:T(8,128)(2,1)}, bf16[128,768]{1,0:T(8,128)(2,1)S(1)}, u32[]{:S(2)}) copy-start(bf16[128,768]{1,0:T(8,128)(2,1)S(1)} %collective-permute-done.2) | copy-start | bytes 589828
  37.9 0.7 copy-start.6
  38.6 16.6 %collective-permute-start.8 = (bf16[256,2048]{1,0:T(8,128)(2,1)S(1)}, bf16[256,2048]{1,0:T(8,128)(2,1)S(1)}, u32[]{:S(2)}, u32[]{:S(2)}) collective-permute-start(bf16[256,2048]{1,0:T(8,128)(2,1)S(1)} %collective-permute-done.7.refs_3_), channel_id=1, source_target_pairs={{0,2},{2,0},{4,6},{6,4},{1,3},{3,1},{5,7},{7,5},{8,10},{10,8},{12,... | collective-permute-start | bytes 3145736 | tf_op jit(solution)/shard_map/hidden_far/ppermute | solution.py:404
  38.8 26.1 %copy-start = (bf16[1,256,2048]{2,1,0:T(8,128)(2,1)S(1)}, bf16[1,256,2048]{2,1,0:T(8,128)(2,1)}, u32[]{:S(2)}) copy-start(bf16[1,256,2048]{2,1,0:T(8,128)(2,1)} %param.6) | copy-start | bytes 3145732
  38.8 26.1 %copy-start.1 = (f32[1024,128]{1,0:T(8,128)S(1)}, f32[1024,128]{1,0:T(8,128)}, u32[]{:S(2)}) copy-start(f32[1024,128]{1,0:T(8,128)} %constant.62.clone.refs_5_) | copy-start | bytes 1572868
  38.8 26.1 %copy-start.2 = (f32[1024,128]{1,0:T(8,128)S(1)}, f32[1024,128]{1,0:T(8,128)}, u32[]{:S(2)}) copy-start(f32[1024,128]{1,0:T(8,128)} %constant.63.clone.refs_6_) | copy-start | bytes 1572868
  38.8 26.1 %copy-start.5 = (bf16[256,384]{1,0:T(8,128)(2,1)S(1)}, bf16[256,384]{1,0:T(8,128)(2,1)}, u32[]{:S(2)}) copy-start(bf16[256,384]{1,0:T(8,128)(2,1)} %get-tuple-element.44.refs_8_) | copy-start | bytes 589828
  38.8 26.1 %copy-start.7 = (bf16[256,384]{1,0:T(8,128)(2,1)S(1)}, bf16[256,384]{1,0:T(8,128)(2,1)}, u32[]{:S(2)}) copy-start(bf16[256,384]{1,0:T(8,128)(2,1)} %copy-done.6) | copy-start | bytes 589828
  38.8 26.1 %copy-start.8 = (s32[3]{0:T(128)S(1)}, s32[3]{0:T(128)}, u32[]{:S(2)}) copy-start(s32[3]{0:T(128)} %pad_add_fusion.where.refs_0_) | copy-start | bytes 40
  38.8 26.1 %copy-start.9 = (s32[1,32]{1,0:T(1,128)S(1)}, s32[1,32]{1,0:T(1,128)}, u32[]{:S(2)}) copy-start(s32[1,32]{1,0:T(1,128)} %refs_7_.5) | copy-start | bytes 388
  40.0 9.8 %collective-permute-start.9 = (bf16[256,384]{1,0:T(8,128)(2,1)}, bf16[256,384]{1,0:T(8,128)(2,1)S(1)}, u32[]{:S(2)}, u32[]{:S(2)}) collective-permute-start(bf16[256,384]{1,0:T(8,128)(2,1)} %get-tuple-element.50.refs_8_), channel_id=1, source_target_pairs={{0,8},{8,16},{16,24},{24,0},{1,9},{9,17},{17,25},{25,1},{2,10},{10... | collective-permute-start | bytes 589832 | tf_op jit(solution)/shard_map/second/ppermute | solution.py:410
  40.1 13.6 %collective-permute-start.11 = (bf16[256,384]{1,0:T(8,128)(2,1)}, bf16[256,384]{1,0:T(8,128)(2,1)S(1)}, u32[]{:S(2)}, u32[]{:S(2)}) collective-permute-start(bf16[256,384]{1,0:T(8,128)(2,1)} %get-tuple-element.51.refs_8_), channel_id=1, source_target_pairs={{0,8},{8,16},{16,24},{24,0},{1,9},{9,17},{17,25},{25,1},{2,10},{10... | collective-permute-start | bytes 589832 | tf_op jit(solution)/shard_map/third/ppermute | solution.py:410
  41.9 28.0 %collective-permute-start.14 = (bf16[2,128,768]{2,1,0:T(8,128)(2,1)S(1)}, bf16[2,128,768]{2,1,0:T(8,128)(2,1)S(1)}, u32[]{:S(2)}, u32[]{:S(2)}) collective-permute-start(bf16[2,128,768]{2,1,0:T(8,128)(2,1)S(1)} %pad_maximum_fusion.2), channel_id=1, source_target_pairs={{0,1},{1,0},{2,3},{3,2},{4,5},{5,4},{6,7},{7,6},{8,9},{9,8},{10,11... | collective-permute-start | bytes 1179656 | tf_op jit(solution)/shard_map/out_group/ppermute | solution.py:404
  43.5 28.3 %copy-start.4 = (bf16[256,384]{1,0:T(8,128)(2,1)S(1)}, bf16[256,384]{1,0:T(8,128)(2,1)}, u32[]{:S(2)}) copy-start(bf16[256,384]{1,0:T(8,128)(2,1)} %get-tuple-element.50.refs_8_) | copy-start | bytes 589828
  43.6 26.4 %collective-permute-start.15 = (bf16[2,128,768]{2,1,0:T(8,128)(2,1)S(1)}, bf16[2,128,768]{2,1,0:T(8,128)(2,1)S(1)}, u32[]{:S(2)}, u32[]{:S(2)}) collective-permute-start(bf16[2,128,768]{2,1,0:T(8,128)(2,1)S(1)} %pad_maximum_fusion.1), channel_id=1, source_target_pairs={{0,4},{2,6},{4,0},{6,2},{1,5},{3,7},{5,1},{7,3},{8,12},{10,14},{12... | collective-permute-start | bytes 1179656 | tf_op jit(solution)/shard_map/out_cross/ppermute | solution.py:404
  49.8 7.9 %collective-permute-start.10 = (bf16[256,384]{1,0:T(8,128)(2,1)S(1)}, bf16[256,384]{1,0:T(8,128)(2,1)S(1)}, u32[]{:S(2)}, u32[]{:S(2)}) collective-permute-start(bf16[256,384]{1,0:T(8,128)(2,1)S(1)} %collective-permute-done.9.refs_9_), channel_id=1, source_target_pairs={{0,8},{8,16},{16,24},{24,0},{1,9},{9,17},{17,25},{25,1},{2,10},{10... | collective-permute-start | bytes 589832 | tf_op jit(solution)/shard_map/second/ppermute | solution.py:410
  53.7 22.8 %collective-permute-start.16 = (bf16[2,128,768]{2,1,0:T(8,128)(2,1)S(1)}, bf16[2,128,768]{2,1,0:T(8,128)(2,1)S(1)}, u32[]{:S(2)}, u32[]{:S(2)}) collective-permute-start(bf16[2,128,768]{2,1,0:T(8,128)(2,1)S(1)} %pad_maximum_fusion.2), channel_id=1, source_target_pairs={{0,5},{1,4},{2,7},{3,6},{4,1},{5,0},{6,3},{7,2},{8,13},{9,12},{10,... | collective-permute-start | bytes 1179656 | tf_op jit(solution)/shard_map/out_across/ppermute | solution.py:434
  55.2 9.6 %collective-permute-start.12 = (bf16[256,384]{1,0:T(8,128)(2,1)S(1)}, bf16[256,384]{1,0:T(8,128)(2,1)S(1)}, u32[]{:S(2)}, u32[]{:S(2)}) collective-permute-start(bf16[256,384]{1,0:T(8,128)(2,1)S(1)} %collective-permute-done.11.refs_9_), channel_id=1, source_target_pairs={{0,8},{8,16},{16,24},{24,0},{1,9},{9,17},{17,25},{25,1},{2,10},{10... | collective-permute-start | bytes 589832 | tf_op jit(solution)/shard_map/third/ppermute | solution.py:410
  57.7 13.8 %collective-permute-start.20 = (bf16[256,384]{1,0:T(8,128)(2,1)S(1)}, bf16[256,384]{1,0:T(8,128)(2,1)S(1)}, u32[]{:S(2)}, u32[]{:S(2)}) collective-permute-start(bf16[256,384]{1,0:T(8,128)(2,1)S(1)} %collective-permute-done.10.refs_10_), channel_id=1, source_target_pairs={{0,8},{8,16},{16,24},{24,0},{1,9},{9,17},{17,25},{25,1},{2,10},{10... | collective-permute-start | bytes 589832 | tf_op jit(solution)/shard_map/second/ppermute | solution.py:410
  64.8 11.7 %collective-permute-start.13 = (bf16[256,384]{1,0:T(8,128)(2,1)S(1)}, bf16[256,384]{1,0:T(8,128)(2,1)S(1)}, u32[]{:S(2)}, u32[]{:S(2)}) collective-permute-start(bf16[256,384]{1,0:T(8,128)(2,1)S(1)} %collective-permute-done.12.refs_10_), channel_id=1, source_target_pairs={{0,8},{8,16},{16,24},{24,0},{1,9},{9,17},{17,25},{25,1},{2,10},{10... | collective-permute-start | bytes 589832 | tf_op jit(solution)/shard_map/third/ppermute | solution.py:410
  69.9 6.6 %collective-permute-start.17 = (bf16[144,128]{1,0:T(8,128)(2,1)S(1)}, bf16[144,128]{1,0:T(8,128)(2,1)S(1)}, u32[]{:S(2)}, u32[]{:S(2)}) collective-permute-start(bf16[144,128]{1,0:T(8,128)(2,1)S(1)} %get-tuple-element.57), channel_id=1, source_target_pairs={{0,2},{2,0},{4,6},{6,4},{1,3},{3,1},{5,7},{7,5},{8,10},{10,8},{12,... | collective-permute-start | bytes 110600 | tf_op jit(solution)/shard_map/context_first/ppermute | solution.py:404
  70.0 6.6 %collective-permute-start.18 = (bf16[144,128]{1,0:T(8,128)(2,1)S(1)}, bf16[144,128]{1,0:T(8,128)(2,1)S(1)}, u32[]{:S(2)}, u32[]{:S(2)}) collective-permute-start(bf16[144,128]{1,0:T(8,128)(2,1)S(1)} %get-tuple-element.58), channel_id=1, source_target_pairs={{0,4},{2,6},{4,0},{6,2},{1,5},{3,7},{5,1},{7,3},{8,12},{10,14},{12... | collective-permute-start | bytes 110600 | tf_op jit(solution)/shard_map/context_first/ppermute | solution.py:404
  71.5 5.0 %collective-permute-start.19 = (bf16[144,128]{1,0:T(8,128)(2,1)S(1)}, bf16[144,128]{1,0:T(8,128)(2,1)S(1)}, u32[]{:S(2)}, u32[]{:S(2)}) collective-permute-start(bf16[144,128]{1,0:T(8,128)(2,1)S(1)} %get-tuple-element.59), channel_id=1, source_target_pairs={{0,6},{2,4},{4,2},{6,0},{1,7},{3,5},{5,3},{7,1},{8,14},{10,12},{12... | collective-permute-start | bytes 110600 | tf_op jit(solution)/shard_map/context_first/ppermute | solution.py:404
  76.6 2.9 %copy-start.3 = (bf16[256,384]{1,0:T(8,128)(2,1)S(1)}, bf16[256,384]{1,0:T(8,128)(2,1)}, u32[]{:S(2)}) copy-start(bf16[256,384]{1,0:T(8,128)(2,1)} %get-tuple-element.51.refs_8_) | copy-start | bytes 589828
  76.8 19.0 %collective-permute-start.30 = (bf16[4,2,128,768]{3,2,1,0:T(8,128)(2,1)S(1)}, bf16[4,2,128,768]{3,2,1,0:T(8,128)(2,1)S(1)}, u32[]{:S(2)}, u32[]{:S(2)}) collective-permute-start(bf16[4,2,128,768]{3,2,1,0:T(8,128)(2,1)S(1)} %pad_maximum_fusion.refs_15_), channel_id=1, source_target_pairs={{0,2},{2,0},{4,6},{6,4},{1,3},{3,1},{5,7},{7,5},{8,10},{10,8},{12,... | collective-permute-start | bytes 4718600 | tf_op jit(solution)/shard_map/out_core/ppermute | solution.py:404
  77.2 6.9 %collective-permute-start.22 = (bf16[144,128]{1,0:T(8,128)(2,1)S(1)}, bf16[144,128]{1,0:T(8,128)(2,1)S(1)}, u32[]{:S(2)}, u32[]{:S(2)}) collective-permute-start(bf16[144,128]{1,0:T(8,128)(2,1)S(1)} %get-tuple-element.69), channel_id=1, source_target_pairs={{0,2},{2,0},{4,6},{6,4},{1,3},{3,1},{5,7},{7,5},{8,10},{10,8},{12,... | collective-permute-start | bytes 110600 | tf_op jit(solution)/shard_map/context_second/ppermute | solution.py:404
  77.3 7.0 %collective-permute-start.23 = (bf16[144,128]{1,0:T(8,128)(2,1)S(1)}, bf16[144,128]{1,0:T(8,128)(2,1)S(1)}, u32[]{:S(2)}, u32[]{:S(2)}) collective-permute-start(bf16[144,128]{1,0:T(8,128)(2,1)S(1)} %get-tuple-element.70), channel_id=1, source_target_pairs={{0,4},{2,6},{4,0},{6,2},{1,5},{3,7},{5,1},{7,3},{8,12},{10,14},{12... | collective-permute-start | bytes 110600 | tf_op jit(solution)/shard_map/context_second/ppermute | solution.py:404
  78.8 7.2 %collective-permute-start.24 = (bf16[144,128]{1,0:T(8,128)(2,1)S(1)}, bf16[144,128]{1,0:T(8,128)(2,1)S(1)}, u32[]{:S(2)}, u32[]{:S(2)}) collective-permute-start(bf16[144,128]{1,0:T(8,128)(2,1)S(1)} %get-tuple-element.71), channel_id=1, source_target_pairs={{0,6},{2,4},{4,2},{6,0},{1,7},{3,5},{5,3},{7,1},{8,14},{10,12},{12... | collective-permute-start | bytes 110600 | tf_op jit(solution)/shard_map/context_second/ppermute | solution.py:404
  79.1 16.7 %copy-start.10 = (s32[1,8,1]{1,2,0:T(1,128)S(1)}, s32[1,8,1]{1,2,0:T(1,128)}, u32[]{:S(2)}) copy-start(s32[1,8,1]{1,2,0:T(1,128)} %param.9) | copy-start | bytes 100
  79.1 12.1 %collective-permute-start.21 = (bf16[4,144,128]{2,1,0:T(8,128)(2,1)S(1)}, bf16[4,144,128]{2,1,0:T(8,128)(2,1)S(1)}, u32[]{:S(2)}, u32[]{:S(2)}) collective-permute-start(bf16[4,144,128]{2,1,0:T(8,128)(2,1)S(1)} %pad_maximum_fusion.3), channel_id=1, source_target_pairs={{0,1},{1,0},{2,3},{3,2},{4,5},{5,4},{6,7},{7,6},{8,9},{9,8},{10,11... | collective-permute-start | bytes 442376 | tf_op jit(solution)/shard_map/context_first_group/ppermute | solution.py:404
  84.1 2.0 %collective-permute-start.26 = (bf16[144,128]{1,0:T(8,128)(2,1)S(1)}, bf16[144,128]{1,0:T(8,128)(2,1)S(1)}, u32[]{:S(2)}, u32[]{:S(2)}) collective-permute-start(bf16[144,128]{1,0:T(8,128)(2,1)S(1)} %get-tuple-element.74), channel_id=1, source_target_pairs={{0,2},{2,0},{4,6},{6,4},{1,3},{3,1},{5,7},{7,5},{8,10},{10,8},{12,... | collective-permute-start | bytes 110600 | tf_op jit(solution)/shard_map/context_third/ppermute | solution.py:404
  84.4 4.0 %collective-permute-start.27 = (bf16[144,128]{1,0:T(8,128)(2,1)S(1)}, bf16[144,128]{1,0:T(8,128)(2,1)S(1)}, u32[]{:S(2)}, u32[]{:S(2)}) collective-permute-start(bf16[144,128]{1,0:T(8,128)(2,1)S(1)} %get-tuple-element.75), channel_id=1, source_target_pairs={{0,4},{2,6},{4,0},{6,2},{1,5},{3,7},{5,1},{7,3},{8,12},{10,14},{12... | collective-permute-start | bytes 110600 | tf_op jit(solution)/shard_map/context_third/ppermute | solution.py:404
  86.1 3.5 %collective-permute-start.28 = (bf16[144,128]{1,0:T(8,128)(2,1)S(1)}, bf16[144,128]{1,0:T(8,128)(2,1)S(1)}, u32[]{:S(2)}, u32[]{:S(2)}) collective-permute-start(bf16[144,128]{1,0:T(8,128)(2,1)S(1)} %get-tuple-element.76), channel_id=1, source_target_pairs={{0,6},{2,4},{4,2},{6,0},{1,7},{3,5},{5,3},{7,1},{8,14},{10,12},{12... | collective-permute-start | bytes 110600 | tf_op jit(solution)/shard_map/context_third/ppermute | solution.py:404
  86.1 6.2 %collective-permute-start.25 = (bf16[4,144,128]{2,1,0:T(8,128)(2,1)S(1)}, bf16[4,144,128]{2,1,0:T(8,128)(2,1)S(1)}, u32[]{:S(2)}, u32[]{:S(2)}) collective-permute-start(bf16[4,144,128]{2,1,0:T(8,128)(2,1)S(1)} %pad_maximum_fusion.4), channel_id=1, source_target_pairs={{0,1},{1,0},{2,3},{3,2},{4,5},{5,4},{6,7},{7,6},{8,9},{9,8},{10,11... | collective-permute-start | bytes 442376 | tf_op jit(solution)/shard_map/context_second_group/ppermute | solution.py:404
  89.6 6.2 %collective-permute-start.29 = (bf16[4,144,128]{2,1,0:T(8,128)(2,1)S(1)}, bf16[4,144,128]{2,1,0:T(8,128)(2,1)S(1)}, u32[]{:S(2)}, u32[]{:S(2)}) collective-permute-start(bf16[4,144,128]{2,1,0:T(8,128)(2,1)S(1)} %pad_maximum_fusion.5), channel_id=1, source_target_pairs={{0,1},{1,0},{2,3},{3,2},{4,5},{5,4},{6,7},{7,6},{8,9},{9,8},{10,11... | collective-permute-start | bytes 442376 | tf_op jit(solution)/shard_map/context_third_group/ppermute | solution.py:404
  99.5 3.7 %collective-permute-start.31 = (f32[4,1024]{1,0:T(4,128)S(1)}, f32[4,1024]{1,0:T(4,128)S(1)}, u32[]{:S(2)}, u32[]{:S(2)}) collective-permute-start(f32[4,1024]{1,0:T(4,128)S(1)} %get-tuple-element.83), channel_id=1, source_target_pairs={{0,1},{1,0},{2,3},{3,2},{4,5},{5,4},{6,7},{7,6},{8,9},{9,8},{10,11... | collective-permute-start | bytes 49160 | tf_op jit(solution)/shard_map/embedding_half/ppermute | solution.py:404

commit v4 on v3

--- a/solution.py
+++ b/solution.py
@@ -243,7 +243,7 @@
         v = top[:, 128:] + pltpu.roll(bottom[:, 128:], HD, 1)
         v_s[at, :] = jnp.where(low, v, 1.0).astype(jnp.bfloat16)
 
-    step = 128
+    step = 256
     for r in range(total // step):
         start, end = max(0, r * step - HALF_WIN), min(total, (r + 1) * step + HALF_WIN)
         ahead = lax.broadcasted_iota(jnp.int32, (step, step), 1) - lax.broadcasted_iota(jnp.int32, (step, step), 0)
@@ -311,54 +311,86 @@
     )(where, *blocks, *tables, *pieces)
 
 
-def project_kernel(where, shard_ref, h_ref, pool_ref, *refs):
-    heads = [refs[5 * i : 5 * i + 5] for i in range(3)]
-    w_refs = refs[15:17]
-    layer_ref, keep_ref, send_ref, c_s, o_s = refs[17:]
-    s, d, g = where[0], where[1], where[2]
-    rows = h_ref.shape[0]
-    extra = c_s.shape[0] - rows
-    width = c_s.shape[1] // 2
-    odd = jnp.bitwise_and(s, 1) == 1
-    group_of = (g, 1 - g)
-
-    def place(base, tile, left, right):
-        low = lanes(left.shape) < HD
-        first = jnp.where(low, left, pltpu.roll(right, HD, 1)).astype(jnp.bfloat16)
-        second = jnp.where(low, pltpu.roll(left, HD, 1), right).astype(jnp.bfloat16)
-        at = pl.ds(pl.multiple_of(base + tile * 128, 128), 128)
-        c_s[0 : rows // 2, at] = first[0 : rows // 2]
-        c_s[rows // 2 : rows, at] = second[0 : rows // 2]
-        c_s[rows:, at] = first[rows // 2 :]
-
-    for t in range(2):
-        base = group_of[t] * width
-        parts = [[(r[j][...] if t == 0 else r[4][j]).astype(jnp.float32) for j in range(4)] for r in heads]
-        for j in range(4):
-            place(base, jnp.bitwise_xor(s, j), parts[0][j], parts[1][j])
-        for pair in range(2):
-            one, two = parts[2][2 * pair], parts[2][2 * pair + 1]
-            left, right = jnp.where(odd, two, one), jnp.where(odd, one, two)
-            place(base, 4 + jnp.bitwise_xor(s // 2, pair), left, right)
-
-    feats = w_refs[0].shape[2]
-    per_shard = 4 * feats
+def merge(left, right, rows):
+    left, right = left.astype(jnp.float32), right.astype(jnp.float32)
+    low = lanes(left.shape) < HD
+    first = jnp.where(low, left, pltpu.roll(right, HD, 1)).astype(jnp.bfloat16)
+    second = jnp.where(low, pltpu.roll(left, HD, 1), right).astype(jnp.bfloat16)
+    return first[: rows // 2], second[: rows // 2], first[rows // 2 :]
+
+
+def project_tiles(s, d, c_s, four_ref, near_ref, columns):
+    feats, width = four_ref.shape[2], columns[1] - columns[0]
     for p in range(2):
         in_half = lax.rem(lax.rem(d - p + 4, 4), 2)
         for j in range(4):
-            source = w_refs[j % 2]
-            quarter = jnp.bitwise_xor(s, j)
-            total = jnp.zeros((rows + extra, feats), jnp.float32)
+            source = near_ref if j % 2 else four_ref
+            total = None
             for t in range(2):
-                w = source[2 * (j // 2) + t, p]
-                c = c_s[:, pl.ds(pl.multiple_of(group_of[t] * width, 128), width)]
-                total += lax.dot_general(c, w, (((1,), (1,)), ((), ())), preferred_element_type=jnp.float32)
-            column = pl.multiple_of(in_half * per_shard + quarter * feats, 128)
-            o_s[:, pl.ds(column, feats)] = total[rows:]
-            mine = h_ref[:, pl.ds(pl.multiple_of(g * 2 * per_shard + column, 128), feats)]
-            layer_ref[:, pl.ds(column, feats)] = (mine.astype(jnp.float32) + total[:rows]).astype(jnp.bfloat16)
-
-    half = extra // 2
+                w = source[2 * (j // 2) + t, p, :, columns[0] : columns[1]]
+                c = c_s[:, t * width : (t + 1) * width]
+                product = lax.dot_general(c, w, (((1,), (1,)), ((), ())), preferred_element_type=jnp.float32)
+                total = product if total is None else total + product
+            yield pl.multiple_of((in_half * 4 + jnp.bitwise_xor(s, j)) * feats, 128), total
+
+
+def early_kernel(where, *refs):
+    firsts, seconds, (four_ref, near_ref, out_ref, c_s) = refs[0:5], refs[5:10], refs[10:]
+    s, d = where[0], where[1]
+    rows = 2 * (out_ref.shape[0] - firsts[0].shape[0])
+    for t in range(2):
+        for j in range(4):
+            left, right = [r[j][...] if t == 0 else r[4][j] for r in (firsts, seconds)]
+            top, bottom, sums = merge(left, right, rows)
+            at = pl.ds(pl.multiple_of(t * 512 + jnp.bitwise_xor(s, j) * 128, 128), 128)
+            c_s[0 : rows // 2, at] = top
+            c_s[rows // 2 : rows, at] = bottom
+            c_s[rows:, at] = sums
+    for column, total in project_tiles(s, d, c_s, four_ref, near_ref, (0, 512)):
+        out_ref[:, pl.ds(column, four_ref.shape[2])] = total
+
+
+def project_early(where, first, second, weights):
+    each = first[0].shape[0]
+    feats = 8 * weights[0].shape[2]
+    rows = weights[0].shape[2] * 2
+    vmem = pl.BlockSpec(memory_space=pltpu.VMEM)
+    return pl.pallas_call(
+        early_kernel,
+        out_shape=jax.ShapeDtypeStruct((each + rows // 2, feats), jnp.float32),
+        in_specs=[pl.BlockSpec(memory_space=pltpu.SMEM)] + [vmem] * 12,
+        out_specs=vmem,
+        scratch_shapes=[pltpu.VMEM((each + rows // 2, 1024), jnp.bfloat16)],
+        compiler_params=pltpu.CompilerParams(vmem_limit_bytes=24 * 2**20),
+        cost_estimate=SHORT,
+        name="project_early",
+    )(where, *first, *second, *weights)
+
+
+def late_kernel(where, shard_ref, h_ref, pool_ref, early_ref, *refs):
+    thirds, (four_ref, near_ref, layer_ref, keep_ref, send_ref, c_s, o_s) = refs[0:5], refs[5:]
+    s, d, g = where[0], where[1], where[2]
+    rows = h_ref.shape[0]
+    odd = jnp.bitwise_and(s, 1) == 1
+    for t in range(2):
+        parts = [thirds[j][...] if t == 0 else thirds[4][j] for j in range(4)]
+        for pair in range(2):
+            one, two = parts[2 * pair], parts[2 * pair + 1]
+            top, bottom, sums = merge(jnp.where(odd, two, one), jnp.where(odd, one, two), rows)
+            at = pl.ds(pl.multiple_of(t * 256 + jnp.bitwise_xor(s // 2, pair) * 128, 128), 128)
+            c_s[0 : rows // 2, at] = top
+            c_s[rows // 2 : rows, at] = bottom
+            c_s[rows:, at] = sums
+
+    feats = four_ref.shape[2]
+    for column, total in project_tiles(s, d, c_s, four_ref, near_ref, (512, 768)):
+        at = pl.ds(column, feats)
+        total += early_ref[:, at]
+        o_s[:, at] = total[rows:]
+        mine = h_ref[:, pl.ds(pl.multiple_of(g * 8 * feats + column, 128), feats)]
+        layer_ref[:, at] = (mine.astype(jnp.float32) + total[:rows]).astype(jnp.bfloat16)
+
+    half = pool_ref.shape[0]
     pooled = pool_ref[...] + o_s[0:half] + o_s[half:]
     slots = 2 * keep_ref.shape[0]
     slot = lax.broadcasted_iota(jnp.int32, (slots, half), 0)
@@ -369,34 +401,33 @@
         rank = sum([(ids[e] == ids[c]).astype(jnp.int32) for e in range(c)], jnp.int32(0))
         route = jnp.where((slot == ids[c] * (slots // 2) + rank) & (source == c), 1.0, route)
     routed = jnp.dot(route, pooled, precision=lax.Precision.HIGHEST, preferred_element_type=jnp.float32)
-    cut = routed.shape[0] // 2
+    cut = slots // 2
     keep_ref[...] = jnp.where(g == 0, routed[:cut], routed[cut:])
     send_ref[...] = jnp.where(g == 0, routed[cut:], routed[:cut])
 
 
-def project(where, h, pool, shard_ids, contexts, w_parts):
+def project_late(where, shard_ids, h, pool, early, third, weights):
     rows, d_model = h.shape
     feats = d_model // 2
-    extra = contexts[0].shape[0] - rows // 2
+    slots = shard_ids.shape[0] // 2
     vmem = pl.BlockSpec(memory_space=pltpu.VMEM)
-    slots = shard_ids.shape[0] // 2
     return pl.pallas_call(
-        project_kernel,
+        late_kernel,
         out_shape=[
             jax.ShapeDtypeStruct((rows, feats), jnp.bfloat16),
             jax.ShapeDtypeStruct((slots, feats), jnp.float32),
             jax.ShapeDtypeStruct((slots, feats), jnp.float32),
         ],
-        in_specs=[pl.BlockSpec(memory_space=pltpu.SMEM)] * 2 + [vmem] * 19,
+        in_specs=[pl.BlockSpec(memory_space=pltpu.SMEM)] * 2 + [vmem] * 10,
         out_specs=[vmem] * 3,
         scratch_shapes=[
-            pltpu.VMEM((rows + extra, 2 * w_parts[0].shape[3]), jnp.bfloat16),
-            pltpu.VMEM((extra, feats), jnp.float32),
+            pltpu.VMEM((early.shape[0], 512), jnp.bfloat16),
+            pltpu.VMEM((early.shape[0] - rows, feats), jnp.float32),
         ],
         compiler_params=pltpu.CompilerParams(vmem_limit_bytes=24 * 2**20),
         cost_estimate=SHORT,
-        name="project",
-    )(where, shard_ids, h, pool, *contexts, *w_parts)
+        name="project_late",
+    )(where, shard_ids, h, pool, early, *third, *weights)
 
 
 def xor_send(name, value, axis, j):
@@ -471,11 +502,15 @@
     first_parts = to_other("context_first_group", first_parts)
     second_parts = to_seq("context_second", second)
     third = attend(where, blocks, tables, third_ring, False)
+    first_parts, second_parts, third, near = lax.optimization_barrier((first_parts, second_parts, third, near))
+
     second_parts = to_other("context_second_group", second_parts)
-    third_parts = to_other("context_third_group", to_seq("context_third", third))
-
-    contexts = first_parts + second_parts + third_parts
-    layer, keep, send = project(where, h, first[4], shard_of[0, :, 0], contexts, [four, near])
+    third_parts = to_seq("context_third", third)
+    second_parts[4] = after(second_parts[4], *third_parts)
+    third_parts = to_other("context_third_group", third_parts)
+
+    early = project_early(where, first_parts, second_parts, [four, near])
+    layer, keep, send = project_late(where, shard_of[0, :, 0], h, first[4], early, third_parts, [four, near])
     arrived = xor_send("embedding_half", send, "index", 1)
     feats = keep.shape[1]
     square = (jnp.sum(keep * keep, -1, keepdims=True) + jnp.sum(arrived * arrived, -1, keepdims=True)) / (2 * feats)

time: 104 us -> 101 us (0.971)
  waiting for transfers between devices: 55.1 us -> 53 us
  Pallas kernels: 20.8 us -> 19.1 us
    pallas_call x3, Pallas kernels: 14.3 us -> 11.9 us  [attend(): pl.pallas_call(functools.partial(attend_kernel, pools), out_shape=out_sha...]
    ppermute x19, waiting for transfers between devices: 8.68 us -> 6.53 us  [xor_send(): lax.ppermute(value, axis, [(i, i ^ j) for i in range(lax.axis_size(axis))])]
    pallas_call x1 -> x2, Pallas kernels: 3.67 us -> 4.35 us  [the longest x1 2.21 us: project_late(): pl.pallas_call(late_kernel, out_shape=[jax.ShapeDtypeStruct((rows, feats)...]
  transfers between devices with their start and end apart: 32 -> 32, of which waited for: 15 -> 15; matrix products, arithmetic and copies ran while one was open for 3% -> 3% of each run, Pallas kernels for 16% -> 17%
where the time goes in v4:
time: 101 us; the launch traced here: 100 us
  waiting for transfers between devices  53 us (52%)
  starting transfers between devices  22.5 us (22%)
  Pallas kernels  19.1 us (19%)
  other arithmetic  4.05 us (4%)
  between operations  1.05 us (1%)
    ppermute x12, waiting for transfers between devices, ring_send(): lax.ppermute(value, 'dp', [(i, (i + 1) % count) for i in range(count)])  46.4 us
    ppermute x19, starting transfers between devices, xor_send(): lax.ppermute(value, axis, [(i, i ^ j) for i in range(lax.axis_size(axis))])  16.7 us
    pallas_call x3, Pallas kernels, attend(): pl.pallas_call(functools.partial(attend_kernel, pools), out_shape=out_sha...  11.9 us
    ppermute x19, waiting for transfers between devices, xor_send(): lax.ppermute(value, axis, [(i, i ^ j) for i in range(lax.axis_size(axis))])  6.53 us
    ppermute x12, starting transfers between devices, ring_send(): lax.ppermute(value, 'dp', [(i, (i + 1) % count) for i in range(count)])  4.23 us
    pallas_call x1, Pallas kernels, pieces(): pl.pallas_call(pieces_kernel, grid_spec=pltpu.PrefetchScalarGridSpec(num_...  2.86 us
    another operation x3, other arithmetic, across(): send = jnp.stack([jnp.where(mine, two, one) for mine, one, two in pairs])  2.29 us
    pallas_call x1, Pallas kernels, project_late(): pl.pallas_call(late_kernel, out_shape=[jax.ShapeDtypeStruct((rows, feats)...  2.21 us
  transfers between devices with their start and end apart: 32, of which 15 were waited for; matrix products, arithmetic and copies ran while one was open for 3% of the time, Pallas kernels for 17%

profile of v4, /device:TPU:0, one launch (start us, length us, event | category | flops | bytes accessed | tf_op | source)
XLA Modules:
  0.0 100.4 jit_solution(12976785959360323006)
XLA Ops:
  0.6 0.5 collective-permute-start.6
  1.1 2.6 %collective-permute-start.7 = (bf16[256,2048]{1,0:T(8,128)(2,1)}, bf16[256,2048]{1,0:T(8,128)(2,1)S(1)}, u32[]{:S(2)}, u32[]{:S(2)}) collective-permute-start(bf16[256,2048]{1,0:T(8,128)(2,1)} %bitcast.35), channel_id=1, source_target_pairs={{0,4},{2,6},{4,0},{6,2},{1,5},{3,7},{5,1},{7,3},{8,12},{10,14},{12... | collective-permute-start | bytes 3145736 | tf_op jit(solution)/shard_map/hidden_cross/ppermute | solution.py:435
  3.7 0.6 pad_add_fusion.where.refs_0_
  4.3 2.9 %pieces.1 = (bf16[128,768]{1,0:T(8,128)(2,1)}, bf16[256,384]{1,0:T(8,128)(2,1)}, bf16[256,384]{1,0:T(8,128)(2,1)}, bf16[256,384]{1,0:T(8,128)(2,1)}) custom-call(s32[3]{0:T(128)} %pad_add_fusion.where.refs_0_, bf16[4,512,768]{2,1,0:T(8,128)(2,1)} %o_ref.1, bf16[4,512,768]{2,1,0:T(8,128)(2,1)} %o_ref.1, bf16[4,512,768]{2,1,0:T(8,128)(2,1)} %o_ref.1), custom_call_target="tpu_custom_call" | custom-call | flops 1 | bytes 1 | tf_op jit(solution)/shard_map/pieces/pallas_call | solution.py:178
  7.2 1.6 %collective-permute-start = (bf16[128,768]{1,0:T(8,128)(2,1)}, bf16[128,768]{1,0:T(8,128)(2,1)S(1)}, u32[]{:S(2)}, u32[]{:S(2)}) collective-permute-start(bf16[128,768]{1,0:T(8,128)(2,1)} %get-tuple-element.58), channel_id=1, source_target_pairs={{0,8},{8,16},{16,24},{24,0},{1,9},{9,17},{17,25},{25,1},{2,10},{10... | collective-permute-start | bytes 589832 | tf_op jit(solution)/shard_map/out/ppermute | solution.py:441
  8.8 1.6 %collective-permute-start.3 = (bf16[256,384]{1,0:T(8,128)(2,1)}, bf16[256,384]{1,0:T(8,128)(2,1)S(1)}, u32[]{:S(2)}, u32[]{:S(2)}) collective-permute-start(bf16[256,384]{1,0:T(8,128)(2,1)} %get-tuple-element.59.refs_8_), channel_id=1, source_target_pairs={{0,8},{8,16},{16,24},{24,0},{1,9},{9,17},{17,25},{25,1},{2,10},{10... | collective-permute-start | bytes 589832 | tf_op jit(solution)/shard_map/first/ppermute | solution.py:441
  10.3 6.6 %collective-permute-done = bf16[128,768]{1,0:T(8,128)(2,1)S(1)} collective-permute-done((bf16[128,768]{1,0:T(8,128)(2,1)}, bf16[128,768]{1,0:T(8,128)(2,1)S(1)}, u32[]{:S(2)}, u32[]{:S(2)}) %collective-permute-start) | collective-permute-done | bytes 196640 | tf_op jit(solution)/shard_map/out/ppermute | solution.py:441
  16.9 3.9 %collective-permute-done.3.refs_9_ = bf16[256,384]{1,0:T(8,128)(2,1)S(1)} collective-permute-done((bf16[256,384]{1,0:T(8,128)(2,1)}, bf16[256,384]{1,0:T(8,128)(2,1)S(1)}, u32[]{:S(2)}, u32[]{:S(2)}) %collective-permute-start.3) | collective-permute-done | bytes 196640 | tf_op jit(solution)/shard_map/first/ppermute | solution.py:441
  20.8 0.1 collective-permute-start.4
  20.9 4.1 %collective-permute-done.1 = bf16[128,768]{1,0:T(8,128)(2,1)S(1)} collective-permute-done((bf16[128,768]{1,0:T(8,128)(2,1)S(1)}, bf16[128,768]{1,0:T(8,128)(2,1)S(1)}, u32[]{:S(2)}, u32[]{:S(2)}) %collective-permute-start.1) | collective-permute-done | bytes 196640 | tf_op jit(solution)/shard_map/out/ppermute | solution.py:441
  25.0 0.1 collective-permute-start.2
  25.1 5.3 %collective-permute-done.4.refs_10_ = bf16[256,384]{1,0:T(8,128)(2,1)S(1)} collective-permute-done((bf16[256,384]{1,0:T(8,128)(2,1)S(1)}, bf16[256,384]{1,0:T(8,128)(2,1)S(1)}, u32[]{:S(2)}, u32[]{:S(2)}) %collective-permute-start.4) | collective-permute-done | bytes 196640 | tf_op jit(solution)/shard_map/first/ppermute | solution.py:441
  30.4 0.0 collective-permute-start.5
  30.4 3.9 %collective-permute-done.2 = bf16[128,768]{1,0:T(8,128)(2,1)S(1)} collective-permute-done((bf16[128,768]{1,0:T(8,128)(2,1)S(1)}, bf16[128,768]{1,0:T(8,128)(2,1)S(1)}, u32[]{:S(2)}, u32[]{:S(2)}) %collective-permute-start.2) | collective-permute-done | bytes 196640 | tf_op jit(solution)/shard_map/out/ppermute | solution.py:441
  34.3 3.6 %collective-permute-done.5.refs_11_ = bf16[256,384]{1,0:T(8,128)(2,1)S(1)} collective-permute-done((bf16[256,384]{1,0:T(8,128)(2,1)S(1)}, bf16[256,384]{1,0:T(8,128)(2,1)S(1)}, u32[]{:S(2)}, u32[]{:S(2)}) %collective-permute-start.5) | collective-permute-done | bytes 196640 | tf_op jit(solution)/shard_map/first/ppermute | solution.py:441
  37.9 0.7 copy-done.6
  38.6 0.0 collective-permute-done.6.refs_2_
  38.6 0.0 collective-permute-done.7.refs_3_
  38.6 0.1 collective-permute-start.8
  38.8 0.0 copy-start
  38.8 0.0 copy-start.1
  38.8 0.0 copy-start.2
  38.8 0.0 copy-start.9
  38.8 1.2 %select_bitcast_fusion.1 = (bf16[1,128,768]{2,1,0:T(8,128)(2,1)S(1)}, bf16[1,128,768]{2,1,0:T(8,128)(2,1)S(1)}) fusion(bf16[128,768]{1,0:T(8,128)(2,1)} %copy-done.12, bf16[128,768]{1,0:T(8,128)(2,1)} %get-tuple-element.58, pred[]{:T(512)S(6)} %eq.13), kind=kLoop, calls=%fused_computation.4 | loop fusion | flops 196608 | bytes 786433 | tf_op jit(solution)/shard_map/stack | solution.py:463
  40.0 0.1 collective-permute-start.9
  40.1 0.7 collective-permute-start.11
  40.8 1.1 %select_bitcast_fusion = (bf16[1,128,768]{2,1,0:T(8,128)(2,1)S(1)}, bf16[1,128,768]{2,1,0:T(8,128)(2,1)S(1)}) fusion(bf16[128,768]{1,0:T(8,128)(2,1)} %copy-done.13, bf16[128,768]{1,0:T(8,128)(2,1)} %copy-done.11, pred[]{:T(512)S(6)} %eq.14), kind=kLoop, calls=%fused_computation.3 | loop fusion | flops 196608 | bytes 786433 | tf_op jit(solution)/shard_map/stack | solution.py:463
  41.9 1.6 %collective-permute-start.14 = (bf16[2,128,768]{2,1,0:T(8,128)(2,1)S(1)}, bf16[2,128,768]{2,1,0:T(8,128)(2,1)S(1)}, u32[]{:S(2)}, u32[]{:S(2)}) collective-permute-start(bf16[2,128,768]{2,1,0:T(8,128)(2,1)S(1)} %pad_maximum_fusion.2), channel_id=1, source_target_pairs={{0,1},{1,0},{2,3},{3,2},{4,5},{5,4},{6,7},{7,6},{8,9},{9,8},{10,11... | collective-permute-start | bytes 1179656 | tf_op jit(solution)/shard_map/out_group/ppermute | solution.py:435
  43.6 0.6 collective-permute-start.15
  44.2 5.7 %collective-permute-done.9.refs_9_ = bf16[256,384]{1,0:T(8,128)(2,1)S(1)} collective-permute-done((bf16[256,384]{1,0:T(8,128)(2,1)}, bf16[256,384]{1,0:T(8,128)(2,1)S(1)}, u32[]{:S(2)}, u32[]{:S(2)}) %collective-permute-start.9) | collective-permute-done | bytes 196640 | tf_op jit(solution)/shard_map/second/ppermute | solution.py:441
  49.8 3.9 %collective-permute-done.11.refs_9_ = bf16[256,384]{1,0:T(8,128)(2,1)S(1)} collective-permute-done((bf16[256,384]{1,0:T(8,128)(2,1)}, bf16[256,384]{1,0:T(8,128)(2,1)S(1)}, u32[]{:S(2)}, u32[]{:S(2)}) %collective-permute-start.11) | collective-permute-done | bytes 196640 | tf_op jit(solution)/shard_map/third/ppermute | solution.py:441
  53.7 1.5 %collective-permute-start.16 = (bf16[2,128,768]{2,1,0:T(8,128)(2,1)S(1)}, bf16[2,128,768]{2,1,0:T(8,128)(2,1)S(1)}, u32[]{:S(2)}, u32[]{:S(2)}) collective-permute-start(bf16[2,128,768]{2,1,0:T(8,128)(2,1)S(1)} %pad_maximum_fusion.2), channel_id=1, source_target_pairs={{0,5},{1,4},{2,7},{3,6},{4,1},{5,0},{6,3},{7,2},{8,13},{9,12},{10,... | collective-permute-start | bytes 1179656 | tf_op jit(solution)/shard_map/out_across/ppermute | solution.py:465
  55.2 0.0 collective-permute-done.8.refs_4_
  55.2 0.0 collective-permute-start.12
  55.2 2.5 %collective-permute-done.10.refs_10_ = bf16[256,384]{1,0:T(8,128)(2,1)S(1)} collective-permute-done((bf16[256,384]{1,0:T(8,128)(2,1)S(1)}, bf16[256,384]{1,0:T(8,128)(2,1)S(1)}, u32[]{:S(2)}, u32[]{:S(2)}) %collective-permute-start.10) | collective-permute-done | bytes 196640 | tf_op jit(solution)/shard_map/second/ppermute | solution.py:441
  57.7 7.1 %collective-permute-done.12.refs_10_ = bf16[256,384]{1,0:T(8,128)(2,1)S(1)} collective-permute-done((bf16[256,384]{1,0:T(8,128)(2,1)S(1)}, bf16[256,384]{1,0:T(8,128)(2,1)S(1)}, u32[]{:S(2)}, u32[]{:S(2)}) %collective-permute-start.12) | collective-permute-done | bytes 196640 | tf_op jit(solution)/shard_map/third/ppermute | solution.py:441
  64.8 0.0 collective-permute-start.13
  64.9 4.2 %attend_and_pool.1 = (bf16[144,128]{1,0:T(8,128)(2,1)S(1)}, bf16[144,128]{1,0:T(8,128)(2,1)S(1)}, bf16[144,128]{1,0:T(8,128)(2,1)S(1)}, bf16[144,128]{1,0:T(8,128)(2,1)S(1)}, f32[8,1024]{1,0:T(8,128)S(1)}) custom-call(s32[3]{0:T(128)S(1)} %copy-done.8, bf16[256,2048]{1,0:T(8,128)(2,1)S(1)} %bitcast.36, bf16[256,2048]{1,0:T(8,128)(2,1)S(1)} %collective-permute-done.6.refs_2_, ...), custom_call_target="tpu_custom_call" | custom-call | flops 1 | bytes 1 | tf_op jit(solution)/shard_map/attend_and_pool/pallas_call | solution.py:302
  69.1 0.1 collective-permute-start.17
  69.2 1.6 %collective-permute-start.18 = (bf16[144,128]{1,0:T(8,128)(2,1)S(1)}, bf16[144,128]{1,0:T(8,128)(2,1)S(1)}, u32[]{:S(2)}, u32[]{:S(2)}) collective-permute-start(bf16[144,128]{1,0:T(8,128)(2,1)S(1)} %get-tuple-element.73), channel_id=1, source_target_pairs={{0,4},{2,6},{4,0},{6,2},{1,5},{3,7},{5,1},{7,3},{8,12},{10,14},{12... | collective-permute-start | bytes 110600 | tf_op jit(solution)/shard_map/context_first/ppermute | solution.py:435
  70.7 0.3 collective-permute-start.19
  71.0 3.9 %attend.2 = (bf16[144,128]{1,0:T(8,128)(2,1)S(1)}, bf16[144,128]{1,0:T(8,128)(2,1)S(1)}, bf16[144,128]{1,0:T(8,128)(2,1)S(1)}, bf16[144,128]{1,0:T(8,128)(2,1)S(1)}) custom-call(s32[3]{0:T(128)S(1)} %copy-done.8, bf16[256,2048]{1,0:T(8,128)(2,1)S(1)} %bitcast.37, bf16[256,2048]{1,0:T(8,128)(2,1)S(1)} %collective-permute-done.6.refs_2_, ...), custom_call_target="tpu_custom_call" | custom-call | flops 1 | bytes 1 | tf_op jit(solution)/shard_map/attend/pallas_call | solution.py:302
  75.0 0.2 pad_maximum_fusion.refs_10_.refs_5_
  75.2 0.4 collective-permute-start.25
  75.6 0.2 collective-permute-start.21
  75.8 0.1 collective-permute-start.22
  75.9 1.8 %collective-permute-start.23 = (bf16[144,128]{1,0:T(8,128)(2,1)S(1)}, bf16[144,128]{1,0:T(8,128)(2,1)S(1)}, u32[]{:S(2)}, u32[]{:S(2)}) collective-permute-start(bf16[144,128]{1,0:T(8,128)(2,1)S(1)} %get-tuple-element.85), channel_id=1, source_target_pairs={{0,4},{2,6},{4,0},{6,2},{1,5},{3,7},{5,1},{7,3},{8,12},{10,14},{12... | collective-permute-start | bytes 110600 | tf_op jit(solution)/shard_map/context_second/ppermute | solution.py:435
  77.7 0.1 collective-permute-start.24
  77.8 3.9 %attend.3 = (bf16[144,128]{1,0:T(8,128)(2,1)S(1)}, bf16[144,128]{1,0:T(8,128)(2,1)S(1)}, bf16[144,128]{1,0:T(8,128)(2,1)S(1)}, bf16[144,128]{1,0:T(8,128)(2,1)S(1)}) custom-call(s32[3]{0:T(128)S(1)} %copy-done.8, bf16[256,2048]{1,0:T(8,128)(2,1)S(1)} %bitcast.38, bf16[256,2048]{1,0:T(8,128)(2,1)S(1)} %collective-permute-done.6.refs_2_, ...), custom_call_target="tpu_custom_call" | custom-call | flops 1 | bytes 1 | tf_op jit(solution)/shard_map/attend/pallas_call | solution.py:302
  81.7 0.3 collective-permute-start.27
  82.1 1.7 %collective-permute-start.28 = (bf16[144,128]{1,0:T(8,128)(2,1)S(1)}, bf16[144,128]{1,0:T(8,128)(2,1)S(1)}, u32[]{:S(2)}, u32[]{:S(2)}) collective-permute-start(bf16[144,128]{1,0:T(8,128)(2,1)S(1)} %get-tuple-element.107), channel_id=1, source_target_pairs={{0,4},{2,6},{4,0},{6,2},{1,5},{3,7},{5,1},{7,3},{8,12},{10,14},{12... | collective-permute-start | bytes 110600 | tf_op jit(solution)/shard_map/context_third/ppermute | solution.py:435
  83.8 1.7 %collective-permute-start.26 = (bf16[4,144,128]{2,1,0:T(8,128)(2,1)S(1)}, bf16[4,144,128]{2,1,0:T(8,128)(2,1)S(1)}, u32[]{:S(2)}, u32[]{:S(2)}) collective-permute-start(bf16[4,144,128]{2,1,0:T(8,128)(2,1)S(1)} %pad_maximum_fusion.4), channel_id=1, source_target_pairs={{0,1},{1,0},{2,3},{3,2},{4,5},{5,4},{6,7},{7,6},{8,9},{9,8},{10,11... | collective-permute-start | bytes 442376 | tf_op jit(solution)/shard_map/context_second_group/ppermute | solution.py:435
  85.5 0.5 collective-permute-done.28.refs_2_
  86.0 1.4 %collective-permute-done.29.refs_3_ = bf16[144,128]{1,0:T(8,128)(2,1)S(1)} collective-permute-done((bf16[144,128]{1,0:T(8,128)(2,1)S(1)}, bf16[144,128]{1,0:T(8,128)(2,1)S(1)}, u32[]{:S(2)}, u32[]{:S(2)}) %collective-permute-start.29) | collective-permute-done | bytes 36896 | tf_op jit(solution)/shard_map/context_third/ppermute | solution.py:435
  87.5 0.0 copy-start.10
  87.5 1.6 %collective-permute-start.30 = (bf16[4,144,128]{2,1,0:T(8,128)(2,1)S(1)}, bf16[4,144,128]{2,1,0:T(8,128)(2,1)S(1)}, u32[]{:S(2)}, u32[]{:S(2)}) collective-permute-start(bf16[4,144,128]{2,1,0:T(8,128)(2,1)S(1)} %pad_maximum_fusion.5), channel_id=1, source_target_pairs={{0,1},{1,0},{2,3},{3,2},{4,5},{5,4},{6,7},{7,6},{8,9},{9,8},{10,11... | collective-permute-start | bytes 442376 | tf_op jit(solution)/shard_map/context_third_group/ppermute | solution.py:435
  89.1 1.0 collective-permute-done.26.refs_9_
  90.1 2.1 %project_early.1.early_ref = f32[272,1024]{1,0:T(8,128)S(1)} custom-call(s32[3]{0:T(128)S(1)} %copy-done.8, bf16[144,128]{1,0:T(8,128)(2,1)S(1)} %get-tuple-element.96.refs_0_, bf16[144,128]{1,0:T(8,128)(2,1)S(1)} %collective-permute-done.17.refs_1_, bf16[144,128]{1,0:T(8,128)(2,1)S(1)} %collective-permute-done.18.refs_2_, ...), custom_call_target="tpu_custom_call" | custom-call | flops 1 | bytes 1 | tf_op jit(solution)/shard_map/project_early/pallas_call | solution.py:358
  92.2 1.3 %collective-permute-done.30.refs_4_ = bf16[4,144,128]{2,1,0:T(8,128)(2,1)S(1)} collective-permute-done((bf16[4,144,128]{2,1,0:T(8,128)(2,1)S(1)}, bf16[4,144,128]{2,1,0:T(8,128)(2,1)S(1)}, u32[]{:S(2)}, u32[]{:S(2)}) %collective-permute-start.30) | collective-permute-done | bytes 147488 | tf_op jit(solution)/shard_map/context_third_group/ppermute | solution.py:435
  93.6 2.2 %project_late.1 = (bf16[256,1024]{1,0:T(8,128)(2,1)}, f32[4,1024]{1,0:T(4,128)S(1)}, f32[4,1024]{1,0:T(4,128)S(1)}) custom-call(s32[3]{0:T(128)S(1)} %copy-done.8, s32[8]{0:T(128)S(1)} %bitcast.52, bf16[256,2048]{1,0:T(8,128)(2,1)S(1)} %bitcast.39, f32[8,1024]{1,0:T(8,128)S(1)} %get-tuple-element.69.pool_ref, f32[272,1024]{1,0:T(8,128)S(1)} %project_early.1.early_ref, ...), custom_call_target="tpu_custom_call" | custom-call | flops 1 | bytes 1 | tf_op jit(solution)/shard_map/project_late/pallas_call | solution.py:414
  95.8 1.5 %collective-permute-start.31 = (f32[4,1024]{1,0:T(4,128)S(1)}, f32[4,1024]{1,0:T(4,128)S(1)}, u32[]{:S(2)}, u32[]{:S(2)}) collective-permute-start(f32[4,1024]{1,0:T(4,128)S(1)} %get-tuple-element.113), channel_id=1, source_target_pairs={{0,1},{1,0},{2,3},{3,2},{4,5},{5,4},{6,7},{7,6},{8,9},{9,8},{10,11... | collective-permute-start | bytes 49160 | tf_op jit(solution)/shard_map/embedding_half/ppermute | solution.py:435
  97.3 2.2 %collective-permute-done.31 = f32[4,1024]{1,0:T(4,128)S(1)} collective-permute-done((f32[4,1024]{1,0:T(4,128)S(1)}, f32[4,1024]{1,0:T(4,128)S(1)}, u32[]{:S(2)}, u32[]{:S(2)}) %collective-permute-start.31) | collective-permute-done | bytes 16416 | tf_op jit(solution)/shard_map/embedding_half/ppermute | solution.py:435
  99.5 0.2 select_bitcast_fusion.5
  99.7 0.7 maximum_multiply_fusion
  (46 shorter events, 0.2 us)
Async XLA Ops:
  0.6 38.0 %collective-permute-start.6 = (bf16[256,2048]{1,0:T(8,128)(2,1)}, bf16[256,2048]{1,0:T(8,128)(2,1)S(1)}, u32[]{:S(2)}, u32[]{:S(2)}) collective-permute-start(bf16[256,2048]{1,0:T(8,128)(2,1)} %bitcast.34), channel_id=1, source_target_pairs={{0,2},{2,0},{4,6},{6,4},{1,3},{3,1},{5,7},{7,5},{8,10},{10,8},{12,... | collective-permute-start | bytes 3145736 | tf_op jit(solution)/shard_map/hidden_core/ppermute | solution.py:435
  1.1 37.4 %collective-permute-start.7 = (bf16[256,2048]{1,0:T(8,128)(2,1)}, bf16[256,2048]{1,0:T(8,128)(2,1)S(1)}, u32[]{:S(2)}, u32[]{:S(2)}) collective-permute-start(bf16[256,2048]{1,0:T(8,128)(2,1)} %bitcast.35), channel_id=1, source_target_pairs={{0,4},{2,6},{4,0},{6,2},{1,5},{3,7},{5,1},{7,3},{8,12},{10,14},{12... | collective-permute-start | bytes 3145736 | tf_op jit(solution)/shard_map/hidden_cross/ppermute | solution.py:435
  7.2 9.7 %collective-permute-start = (bf16[128,768]{1,0:T(8,128)(2,1)}, bf16[128,768]{1,0:T(8,128)(2,1)S(1)}, u32[]{:S(2)}, u32[]{:S(2)}) collective-permute-start(bf16[128,768]{1,0:T(8,128)(2,1)} %get-tuple-element.58), channel_id=1, source_target_pairs={{0,8},{8,16},{16,24},{24,0},{1,9},{9,17},{17,25},{25,1},{2,10},{10... | collective-permute-start | bytes 589832 | tf_op jit(solution)/shard_map/out/ppermute | solution.py:441
  8.8 12.0 %collective-permute-start.3 = (bf16[256,384]{1,0:T(8,128)(2,1)}, bf16[256,384]{1,0:T(8,128)(2,1)S(1)}, u32[]{:S(2)}, u32[]{:S(2)}) collective-permute-start(bf16[256,384]{1,0:T(8,128)(2,1)} %get-tuple-element.59.refs_8_), channel_id=1, source_target_pairs={{0,8},{8,16},{16,24},{24,0},{1,9},{9,17},{17,25},{25,1},{2,10},{10... | collective-permute-start | bytes 589832 | tf_op jit(solution)/shard_map/first/ppermute | solution.py:441
  16.9 8.2 %copy-start.11 = (bf16[128,768]{1,0:T(8,128)(2,1)}, bf16[128,768]{1,0:T(8,128)(2,1)S(1)}, u32[]{:S(2)}) copy-start(bf16[128,768]{1,0:T(8,128)(2,1)S(1)} %collective-permute-done) | copy-start | bytes 589828
  16.9 8.1 %collective-permute-start.1 = (bf16[128,768]{1,0:T(8,128)(2,1)S(1)}, bf16[128,768]{1,0:T(8,128)(2,1)S(1)}, u32[]{:S(2)}, u32[]{:S(2)}) collective-permute-start(bf16[128,768]{1,0:T(8,128)(2,1)S(1)} %collective-permute-done), channel_id=1, source_target_pairs={{0,8},{8,16},{16,24},{24,0},{1,9},{9,17},{17,25},{25,1},{2,10},{10... | collective-permute-start | bytes 589832 | tf_op jit(solution)/shard_map/out/ppermute | solution.py:441
  20.8 9.6 %collective-permute-start.4 = (bf16[256,384]{1,0:T(8,128)(2,1)S(1)}, bf16[256,384]{1,0:T(8,128)(2,1)S(1)}, u32[]{:S(2)}, u32[]{:S(2)}) collective-permute-start(bf16[256,384]{1,0:T(8,128)(2,1)S(1)} %collective-permute-done.3.refs_9_), channel_id=1, source_target_pairs={{0,8},{8,16},{16,24},{24,0},{1,9},{9,17},{17,25},{25,1},{2,10},{10... | collective-permute-start | bytes 589832 | tf_op jit(solution)/shard_map/first/ppermute | solution.py:441
  25.0 13.6 %copy-start.12 = (bf16[128,768]{1,0:T(8,128)(2,1)}, bf16[128,768]{1,0:T(8,128)(2,1)S(1)}, u32[]{:S(2)}) copy-start(bf16[128,768]{1,0:T(8,128)(2,1)S(1)} %collective-permute-done.1) | copy-start | bytes 589828
  25.0 9.3 %collective-permute-start.2 = (bf16[128,768]{1,0:T(8,128)(2,1)S(1)}, bf16[128,768]{1,0:T(8,128)(2,1)S(1)}, u32[]{:S(2)}, u32[]{:S(2)}) collective-permute-start(bf16[128,768]{1,0:T(8,128)(2,1)S(1)} %collective-permute-done.1), channel_id=1, source_target_pairs={{0,8},{8,16},{16,24},{24,0},{1,9},{9,17},{17,25},{25,1},{2,10},{10... | collective-permute-start | bytes 589832 | tf_op jit(solution)/shard_map/out/ppermute | solution.py:441
  30.4 7.5 %collective-permute-start.5 = (bf16[256,384]{1,0:T(8,128)(2,1)S(1)}, bf16[256,384]{1,0:T(8,128)(2,1)S(1)}, u32[]{:S(2)}, u32[]{:S(2)}) collective-permute-start(bf16[256,384]{1,0:T(8,128)(2,1)S(1)} %collective-permute-done.4.refs_10_), channel_id=1, source_target_pairs={{0,8},{8,16},{16,24},{24,0},{1,9},{9,17},{17,25},{25,1},{2,10},{10... | collective-permute-start | bytes 589832 | tf_op jit(solution)/shard_map/first/ppermute | solution.py:441
  34.3 4.3 %copy-start.13 = (bf16[128,768]{1,0:T(8,128)(2,1)}, bf16[128,768]{1,0:T(8,128)(2,1)S(1)}, u32[]{:S(2)}) copy-start(bf16[128,768]{1,0:T(8,128)(2,1)S(1)} %collective-permute-done.2) | copy-start | bytes 589828
  37.9 0.7 copy-start.6
  38.6 16.6 %collective-permute-start.8 = (bf16[256,2048]{1,0:T(8,128)(2,1)S(1)}, bf16[256,2048]{1,0:T(8,128)(2,1)S(1)}, u32[]{:S(2)}, u32[]{:S(2)}) collective-permute-start(bf16[256,2048]{1,0:T(8,128)(2,1)S(1)} %collective-permute-done.7.refs_3_), channel_id=1, source_target_pairs={{0,2},{2,0},{4,6},{6,4},{1,3},{3,1},{5,7},{7,5},{8,10},{10,8},{12,... | collective-permute-start | bytes 3145736 | tf_op jit(solution)/shard_map/hidden_far/ppermute | solution.py:435
  38.8 26.1 %copy-start = (bf16[1,256,2048]{2,1,0:T(8,128)(2,1)S(1)}, bf16[1,256,2048]{2,1,0:T(8,128)(2,1)}, u32[]{:S(2)}) copy-start(bf16[1,256,2048]{2,1,0:T(8,128)(2,1)} %param.6) | copy-start | bytes 3145732
  38.8 26.1 %copy-start.1 = (f32[1024,128]{1,0:T(8,128)S(1)}, f32[1024,128]{1,0:T(8,128)}, u32[]{:S(2)}) copy-start(f32[1024,128]{1,0:T(8,128)} %constant.62.clone.refs_5_) | copy-start | bytes 1572868
  38.8 26.1 %copy-start.2 = (f32[1024,128]{1,0:T(8,128)S(1)}, f32[1024,128]{1,0:T(8,128)}, u32[]{:S(2)}) copy-start(f32[1024,128]{1,0:T(8,128)} %constant.63.clone.refs_6_) | copy-start | bytes 1572868
  38.8 26.1 %copy-start.5 = (bf16[256,384]{1,0:T(8,128)(2,1)S(1)}, bf16[256,384]{1,0:T(8,128)(2,1)}, u32[]{:S(2)}) copy-start(bf16[256,384]{1,0:T(8,128)(2,1)} %get-tuple-element.59.refs_8_) | copy-start | bytes 589828
  38.8 26.1 %copy-start.7 = (bf16[256,384]{1,0:T(8,128)(2,1)S(1)}, bf16[256,384]{1,0:T(8,128)(2,1)}, u32[]{:S(2)}) copy-start(bf16[256,384]{1,0:T(8,128)(2,1)} %copy-done.6) | copy-start | bytes 589828
  38.8 26.1 %copy-start.8 = (s32[3]{0:T(128)S(1)}, s32[3]{0:T(128)}, u32[]{:S(2)}) copy-start(s32[3]{0:T(128)} %pad_add_fusion.where.refs_0_) | copy-start | bytes 40
  38.8 26.1 %copy-start.9 = (s32[1,32]{1,0:T(1,128)S(1)}, s32[1,32]{1,0:T(1,128)}, u32[]{:S(2)}) copy-start(s32[1,32]{1,0:T(1,128)} %refs_7_.5) | copy-start | bytes 388
  40.0 9.8 %collective-permute-start.9 = (bf16[256,384]{1,0:T(8,128)(2,1)}, bf16[256,384]{1,0:T(8,128)(2,1)S(1)}, u32[]{:S(2)}, u32[]{:S(2)}) collective-permute-start(bf16[256,384]{1,0:T(8,128)(2,1)} %get-tuple-element.65.refs_8_), channel_id=1, source_target_pairs={{0,8},{8,16},{16,24},{24,0},{1,9},{9,17},{17,25},{25,1},{2,10},{10... | collective-permute-start | bytes 589832 | tf_op jit(solution)/shard_map/second/ppermute | solution.py:441
  40.1 13.6 %collective-permute-start.11 = (bf16[256,384]{1,0:T(8,128)(2,1)}, bf16[256,384]{1,0:T(8,128)(2,1)S(1)}, u32[]{:S(2)}, u32[]{:S(2)}) collective-permute-start(bf16[256,384]{1,0:T(8,128)(2,1)} %get-tuple-element.66.refs_8_), channel_id=1, source_target_pairs={{0,8},{8,16},{16,24},{24,0},{1,9},{9,17},{17,25},{25,1},{2,10},{10... | collective-permute-start | bytes 589832 | tf_op jit(solution)/shard_map/third/ppermute | solution.py:441
  41.9 27.2 %collective-permute-start.14 = (bf16[2,128,768]{2,1,0:T(8,128)(2,1)S(1)}, bf16[2,128,768]{2,1,0:T(8,128)(2,1)S(1)}, u32[]{:S(2)}, u32[]{:S(2)}) collective-permute-start(bf16[2,128,768]{2,1,0:T(8,128)(2,1)S(1)} %pad_maximum_fusion.2), channel_id=1, source_target_pairs={{0,1},{1,0},{2,3},{3,2},{4,5},{5,4},{6,7},{7,6},{8,9},{9,8},{10,11... | collective-permute-start | bytes 1179656 | tf_op jit(solution)/shard_map/out_group/ppermute | solution.py:435
  43.5 27.5 %copy-start.4 = (bf16[256,384]{1,0:T(8,128)(2,1)S(1)}, bf16[256,384]{1,0:T(8,128)(2,1)}, u32[]{:S(2)}) copy-start(bf16[256,384]{1,0:T(8,128)(2,1)} %get-tuple-element.65.refs_8_) | copy-start | bytes 589828
  43.6 25.6 %collective-permute-start.15 = (bf16[2,128,768]{2,1,0:T(8,128)(2,1)S(1)}, bf16[2,128,768]{2,1,0:T(8,128)(2,1)S(1)}, u32[]{:S(2)}, u32[]{:S(2)}) collective-permute-start(bf16[2,128,768]{2,1,0:T(8,128)(2,1)S(1)} %pad_maximum_fusion.1), channel_id=1, source_target_pairs={{0,4},{2,6},{4,0},{6,2},{1,5},{3,7},{5,1},{7,3},{8,12},{10,14},{12... | collective-permute-start | bytes 1179656 | tf_op jit(solution)/shard_map/out_cross/ppermute | solution.py:435
  49.8 7.9 %collective-permute-start.10 = (bf16[256,384]{1,0:T(8,128)(2,1)S(1)}, bf16[256,384]{1,0:T(8,128)(2,1)S(1)}, u32[]{:S(2)}, u32[]{:S(2)}) collective-permute-start(bf16[256,384]{1,0:T(8,128)(2,1)S(1)} %collective-permute-done.9.refs_9_), channel_id=1, source_target_pairs={{0,8},{8,16},{16,24},{24,0},{1,9},{9,17},{17,25},{25,1},{2,10},{10... | collective-permute-start | bytes 589832 | tf_op jit(solution)/shard_map/second/ppermute | solution.py:441
  53.7 21.2 %collective-permute-start.16 = (bf16[2,128,768]{2,1,0:T(8,128)(2,1)S(1)}, bf16[2,128,768]{2,1,0:T(8,128)(2,1)S(1)}, u32[]{:S(2)}, u32[]{:S(2)}) collective-permute-start(bf16[2,128,768]{2,1,0:T(8,128)(2,1)S(1)} %pad_maximum_fusion.2), channel_id=1, source_target_pairs={{0,5},{1,4},{2,7},{3,6},{4,1},{5,0},{6,3},{7,2},{8,13},{9,12},{10,... | collective-permute-start | bytes 1179656 | tf_op jit(solution)/shard_map/out_across/ppermute | solution.py:465
  55.2 9.6 %collective-permute-start.12 = (bf16[256,384]{1,0:T(8,128)(2,1)S(1)}, bf16[256,384]{1,0:T(8,128)(2,1)S(1)}, u32[]{:S(2)}, u32[]{:S(2)}) collective-permute-start(bf16[256,384]{1,0:T(8,128)(2,1)S(1)} %collective-permute-done.11.refs_9_), channel_id=1, source_target_pairs={{0,8},{8,16},{16,24},{24,0},{1,9},{9,17},{17,25},{25,1},{2,10},{10... | collective-permute-start | bytes 589832 | tf_op jit(solution)/shard_map/third/ppermute | solution.py:441
  57.7 13.0 %collective-permute-start.20 = (bf16[256,384]{1,0:T(8,128)(2,1)S(1)}, bf16[256,384]{1,0:T(8,128)(2,1)S(1)}, u32[]{:S(2)}, u32[]{:S(2)}) collective-permute-start(bf16[256,384]{1,0:T(8,128)(2,1)S(1)} %collective-permute-done.10.refs_10_), channel_id=1, source_target_pairs={{0,8},{8,16},{16,24},{24,0},{1,9},{9,17},{17,25},{25,1},{2,10},{10... | collective-permute-start | bytes 589832 | tf_op jit(solution)/shard_map/second/ppermute | solution.py:441
  64.8 10.1 %collective-permute-start.13 = (bf16[256,384]{1,0:T(8,128)(2,1)S(1)}, bf16[256,384]{1,0:T(8,128)(2,1)S(1)}, u32[]{:S(2)}, u32[]{:S(2)}) collective-permute-start(bf16[256,384]{1,0:T(8,128)(2,1)S(1)} %collective-permute-done.12.refs_10_), channel_id=1, source_target_pairs={{0,8},{8,16},{16,24},{24,0},{1,9},{9,17},{17,25},{25,1},{2,10},{10... | collective-permute-start | bytes 589832 | tf_op jit(solution)/shard_map/third/ppermute | solution.py:441
  69.1 5.8 %collective-permute-start.17 = (bf16[144,128]{1,0:T(8,128)(2,1)S(1)}, bf16[144,128]{1,0:T(8,128)(2,1)S(1)}, u32[]{:S(2)}, u32[]{:S(2)}) collective-permute-start(bf16[144,128]{1,0:T(8,128)(2,1)S(1)} %get-tuple-element.72), channel_id=1, source_target_pairs={{0,2},{2,0},{4,6},{6,4},{1,3},{3,1},{5,7},{7,5},{8,10},{10,8},{12,... | collective-permute-start | bytes 110600 | tf_op jit(solution)/shard_map/context_first/ppermute | solution.py:435
  69.2 5.7 %collective-permute-start.18 = (bf16[144,128]{1,0:T(8,128)(2,1)S(1)}, bf16[144,128]{1,0:T(8,128)(2,1)S(1)}, u32[]{:S(2)}, u32[]{:S(2)}) collective-permute-start(bf16[144,128]{1,0:T(8,128)(2,1)S(1)} %get-tuple-element.73), channel_id=1, source_target_pairs={{0,4},{2,6},{4,0},{6,2},{1,5},{3,7},{5,1},{7,3},{8,12},{10,14},{12... | collective-permute-start | bytes 110600 | tf_op jit(solution)/shard_map/context_first/ppermute | solution.py:435
  70.7 4.2 %collective-permute-start.19 = (bf16[144,128]{1,0:T(8,128)(2,1)S(1)}, bf16[144,128]{1,0:T(8,128)(2,1)S(1)}, u32[]{:S(2)}, u32[]{:S(2)}) collective-permute-start(bf16[144,128]{1,0:T(8,128)(2,1)S(1)} %get-tuple-element.74), channel_id=1, source_target_pairs={{0,6},{2,4},{4,2},{6,0},{1,7},{3,5},{5,3},{7,1},{8,14},{10,12},{12... | collective-permute-start | bytes 110600 | tf_op jit(solution)/shard_map/context_first/ppermute | solution.py:435
  75.0 2.9 %copy-start.3 = (bf16[256,384]{1,0:T(8,128)(2,1)S(1)}, bf16[256,384]{1,0:T(8,128)(2,1)}, u32[]{:S(2)}) copy-start(bf16[256,384]{1,0:T(8,128)(2,1)} %get-tuple-element.66.refs_8_) | copy-start | bytes 589828
  75.2 6.6 %collective-permute-start.25 = (bf16[4,2,128,768]{3,2,1,0:T(8,128)(2,1)S(1)}, bf16[4,2,128,768]{3,2,1,0:T(8,128)(2,1)S(1)}, u32[]{:S(2)}, u32[]{:S(2)}) collective-permute-start(bf16[4,2,128,768]{3,2,1,0:T(8,128)(2,1)S(1)} %pad_maximum_fusion.refs_10_.refs_5_), channel_id=1, source_target_pairs={{0,2},{2,0},{4,6},{6,4},{1,3},{3,1},{5,7},{7,5},{8,10},{10,8},{12,... | collective-permute-start | bytes 4718600 | tf_op jit(solution)/shard_map/out_core/ppermute | solution.py:435
  75.6 6.1 %collective-permute-start.21 = (bf16[4,144,128]{2,1,0:T(8,128)(2,1)S(1)}, bf16[4,144,128]{2,1,0:T(8,128)(2,1)S(1)}, u32[]{:S(2)}, u32[]{:S(2)}) collective-permute-start(bf16[4,144,128]{2,1,0:T(8,128)(2,1)S(1)} %pad_maximum_fusion.3), channel_id=1, source_target_pairs={{0,1},{1,0},{2,3},{3,2},{4,5},{5,4},{6,7},{7,6},{8,9},{9,8},{10,11... | collective-permute-start | bytes 442376 | tf_op jit(solution)/shard_map/context_first_group/ppermute | solution.py:435
  75.8 5.9 %collective-permute-start.22 = (bf16[144,128]{1,0:T(8,128)(2,1)S(1)}, bf16[144,128]{1,0:T(8,128)(2,1)S(1)}, u32[]{:S(2)}, u32[]{:S(2)}) collective-permute-start(bf16[144,128]{1,0:T(8,128)(2,1)S(1)} %get-tuple-element.84), channel_id=1, source_target_pairs={{0,2},{2,0},{4,6},{6,4},{1,3},{3,1},{5,7},{7,5},{8,10},{10,8},{12,... | collective-permute-start | bytes 110600 | tf_op jit(solution)/shard_map/context_second/ppermute | solution.py:435
  75.9 5.8 %collective-permute-start.23 = (bf16[144,128]{1,0:T(8,128)(2,1)S(1)}, bf16[144,128]{1,0:T(8,128)(2,1)S(1)}, u32[]{:S(2)}, u32[]{:S(2)}) collective-permute-start(bf16[144,128]{1,0:T(8,128)(2,1)S(1)} %get-tuple-element.85), channel_id=1, source_target_pairs={{0,4},{2,6},{4,0},{6,2},{1,5},{3,7},{5,1},{7,3},{8,12},{10,14},{12... | collective-permute-start | bytes 110600 | tf_op jit(solution)/shard_map/context_second/ppermute | solution.py:435
  77.7 4.0 %collective-permute-start.24 = (bf16[144,128]{1,0:T(8,128)(2,1)S(1)}, bf16[144,128]{1,0:T(8,128)(2,1)S(1)}, u32[]{:S(2)}, u32[]{:S(2)}) collective-permute-start(bf16[144,128]{1,0:T(8,128)(2,1)S(1)} %get-tuple-element.86), channel_id=1, source_target_pairs={{0,6},{2,4},{4,2},{6,0},{1,7},{3,5},{5,3},{7,1},{8,14},{10,12},{12... | collective-permute-start | bytes 110600 | tf_op jit(solution)/shard_map/context_second/ppermute | solution.py:435
  81.7 3.8 %collective-permute-start.27 = (bf16[144,128]{1,0:T(8,128)(2,1)S(1)}, bf16[144,128]{1,0:T(8,128)(2,1)S(1)}, u32[]{:S(2)}, u32[]{:S(2)}) collective-permute-start(bf16[144,128]{1,0:T(8,128)(2,1)S(1)} %get-tuple-element.106), channel_id=1, source_target_pairs={{0,2},{2,0},{4,6},{6,4},{1,3},{3,1},{5,7},{7,5},{8,10},{10,8},{12,... | collective-permute-start | bytes 110600 | tf_op jit(solution)/shard_map/context_third/ppermute | solution.py:435
  82.1 4.0 %collective-permute-start.28 = (bf16[144,128]{1,0:T(8,128)(2,1)S(1)}, bf16[144,128]{1,0:T(8,128)(2,1)S(1)}, u32[]{:S(2)}, u32[]{:S(2)}) collective-permute-start(bf16[144,128]{1,0:T(8,128)(2,1)S(1)} %get-tuple-element.107), channel_id=1, source_target_pairs={{0,4},{2,6},{4,0},{6,2},{1,5},{3,7},{5,1},{7,3},{8,12},{10,14},{12... | collective-permute-start | bytes 110600 | tf_op jit(solution)/shard_map/context_third/ppermute | solution.py:435
  83.8 3.6 %collective-permute-start.29 = (bf16[144,128]{1,0:T(8,128)(2,1)S(1)}, bf16[144,128]{1,0:T(8,128)(2,1)S(1)}, u32[]{:S(2)}, u32[]{:S(2)}) collective-permute-start(bf16[144,128]{1,0:T(8,128)(2,1)S(1)} %get-tuple-element.108), channel_id=1, source_target_pairs={{0,6},{2,4},{4,2},{6,0},{1,7},{3,5},{5,3},{7,1},{8,14},{10,12},{12... | collective-permute-start | bytes 110600 | tf_op jit(solution)/shard_map/context_third/ppermute | solution.py:435
  83.8 6.2 %collective-permute-start.26 = (bf16[4,144,128]{2,1,0:T(8,128)(2,1)S(1)}, bf16[4,144,128]{2,1,0:T(8,128)(2,1)S(1)}, u32[]{:S(2)}, u32[]{:S(2)}) collective-permute-start(bf16[4,144,128]{2,1,0:T(8,128)(2,1)S(1)} %pad_maximum_fusion.4), channel_id=1, source_target_pairs={{0,1},{1,0},{2,3},{3,2},{4,5},{5,4},{6,7},{7,6},{8,9},{9,8},{10,11... | collective-permute-start | bytes 442376 | tf_op jit(solution)/shard_map/context_second_group/ppermute | solution.py:435
  87.5 6.1 %copy-start.10 = (s32[1,8,1]{1,2,0:T(1,128)S(1)}, s32[1,8,1]{1,2,0:T(1,128)}, u32[]{:S(2)}) copy-start(s32[1,8,1]{1,2,0:T(1,128)} %param.9) | copy-start | bytes 100
  87.5 6.1 %collective-permute-start.30 = (bf16[4,144,128]{2,1,0:T(8,128)(2,1)S(1)}, bf16[4,144,128]{2,1,0:T(8,128)(2,1)S(1)}, u32[]{:S(2)}, u32[]{:S(2)}) collective-permute-start(bf16[4,144,128]{2,1,0:T(8,128)(2,1)S(1)} %pad_maximum_fusion.5), channel_id=1, source_target_pairs={{0,1},{1,0},{2,3},{3,2},{4,5},{5,4},{6,7},{7,6},{8,9},{9,8},{10,11... | collective-permute-start | bytes 442376 | tf_op jit(solution)/shard_map/context_third_group/ppermute | solution.py:435
  95.8 3.7 %collective-permute-start.31 = (f32[4,1024]{1,0:T(4,128)S(1)}, f32[4,1024]{1,0:T(4,128)S(1)}, u32[]{:S(2)}, u32[]{:S(2)}) collective-permute-start(f32[4,1024]{1,0:T(4,128)S(1)} %get-tuple-element.113), channel_id=1, source_target_pairs={{0,1},{1,0},{2,3},{3,2},{4,5},{5,4},{6,7},{7,6},{8,9},{9,8},{10,11... | collective-permute-start | bytes 49160 | tf_op jit(solution)/shard_map/embedding_half/ppermute | solution.py:435

commit v5 on v4

--- a/solution.py
+++ b/solution.py
@@ -488,11 +488,14 @@
     )
 
     h_far = xor_send("hidden_far", h_cross, "seq", 1)
-    second_ring, third_ring = rings(("second", "third"), (y0, z0), third=h_far)
+    y1, z1 = ring_send("second", y0), ring_send("third", z0)
+    y2, z2 = ring_send("second", y1), ring_send("third", after(z1, h_far))
     blocks = [h, h_core, h_cross, h_far]
     four = across(out_ring)
-    first_ring[3] = after(first_ring[3], second_ring[2], third_ring[2])
+    first_ring[3] = after(first_ring[3], y1, z1)
     first = attend(where, blocks, tables, first_ring, True)
+    y3, z3 = ring_send("second", after(y2)), ring_send("third", after(z2, first[4]))
+    second_ring, third_ring = [y0, y1, y2, y3], [z0, z1, z2, z3]
     first_parts = to_seq("context_first", first[:4])
     second = attend(where, blocks, tables, second_ring, False)
     third_ring[3], four, first_parts, second = lax.optimization_barrier((third_ring[3], four, first_parts, second))

time: 101 us -> 98 us (0.970)
  starting transfers between devices: 22.5 us -> 19.1 us
    ppermute x19, starting transfers between devices: 16.7 us -> 13.3 us  [xor_send(): lax.ppermute(value, axis, [(i, i ^ j) for i in range(lax.axis_size(axis))])]
    ppermute x19, waiting for transfers between devices: 6.53 us -> 9.63 us  [xor_send(): lax.ppermute(value, axis, [(i, i ^ j) for i in range(lax.axis_size(axis))])]
    ppermute x12, waiting for transfers between devices: 46.4 us -> 44.2 us  [ring_send(): lax.ppermute(value, 'dp', [(i, (i + 1) % count) for i in range(count)])]
  transfers between devices with their start and end apart: 32 -> 32, of which waited for: 15 -> 16; matrix products, arithmetic and copies ran while one was open for 3% -> 3% of each run, Pallas kernels for 17% -> 17%
where the time goes in v5:
time: 98 us; the launch traced here: 97.8 us
  waiting for transfers between devices  53.8 us (55%)
  starting transfers between devices  19.1 us (19%)
  Pallas kernels  19.1 us (19%)
  other arithmetic  4.05 us (4%)
  between operations  1.05 us (1%)
    ppermute x12, waiting for transfers between devices, ring_send(): lax.ppermute(value, 'dp', [(i, (i + 1) % count) for i in range(count)])  44.2 us
    ppermute x19, starting transfers between devices, xor_send(): lax.ppermute(value, axis, [(i, i ^ j) for i in range(lax.axis_size(axis))])  13.3 us
    pallas_call x3, Pallas kernels, attend(): pl.pallas_call(functools.partial(attend_kernel, pools), out_shape=out_sha...  11.9 us
    ppermute x19, waiting for transfers between devices, xor_send(): lax.ppermute(value, axis, [(i, i ^ j) for i in range(lax.axis_size(axis))])  9.63 us
    ppermute x12, starting transfers between devices, ring_send(): lax.ppermute(value, 'dp', [(i, (i + 1) % count) for i in range(count)])  4.23 us
    pallas_call x1, Pallas kernels, pieces(): pl.pallas_call(pieces_kernel, grid_spec=pltpu.PrefetchScalarGridSpec(num_...  2.86 us
    another operation x3, other arithmetic, across(): send = jnp.stack([jnp.where(mine, two, one) for mine, one, two in pairs])  2.29 us
    pallas_call x1, Pallas kernels, project_late(): pl.pallas_call(late_kernel, out_shape=[jax.ShapeDtypeStruct((rows, feats)...  2.21 us
  transfers between devices with their start and end apart: 32, of which 16 were waited for; matrix products, arithmetic and copies ran while one was open for 3% of the time, Pallas kernels for 17%

profile of v5, /device:TPU:0, one launch (start us, length us, event | category | flops | bytes accessed | tf_op | source)
XLA Modules:
  0.0 97.8 jit_solution(7180926495164279424)
XLA Ops:
  0.6 0.5 collective-permute-start.6
  1.1 2.6 %collective-permute-start.7 = (bf16[256,2048]{1,0:T(8,128)(2,1)}, bf16[256,2048]{1,0:T(8,128)(2,1)S(1)}, u32[]{:S(2)}, u32[]{:S(2)}) collective-permute-start(bf16[256,2048]{1,0:T(8,128)(2,1)} %bitcast.35), channel_id=1, source_target_pairs={{0,4},{2,6},{4,0},{6,2},{1,5},{3,7},{5,1},{7,3},{8,12},{10,14},{12... | collective-permute-start | bytes 3145736 | tf_op jit(solution)/shard_map/hidden_cross/ppermute | solution.py:435
  3.7 0.6 pad_add_fusion.where.refs_0_
  4.3 2.9 %pieces.1 = (bf16[128,768]{1,0:T(8,128)(2,1)}, bf16[256,384]{1,0:T(8,128)(2,1)}, bf16[256,384]{1,0:T(8,128)(2,1)}, bf16[256,384]{1,0:T(8,128)(2,1)}) custom-call(s32[3]{0:T(128)} %pad_add_fusion.where.refs_0_, bf16[4,512,768]{2,1,0:T(8,128)(2,1)} %o_ref.1, bf16[4,512,768]{2,1,0:T(8,128)(2,1)} %o_ref.1, bf16[4,512,768]{2,1,0:T(8,128)(2,1)} %o_ref.1), custom_call_target="tpu_custom_call" | custom-call | flops 1 | bytes 1 | tf_op jit(solution)/shard_map/pieces/pallas_call | solution.py:178
  7.2 1.6 %collective-permute-start = (bf16[128,768]{1,0:T(8,128)(2,1)}, bf16[128,768]{1,0:T(8,128)(2,1)S(1)}, u32[]{:S(2)}, u32[]{:S(2)}) collective-permute-start(bf16[128,768]{1,0:T(8,128)(2,1)} %get-tuple-element.59), channel_id=1, source_target_pairs={{0,8},{8,16},{16,24},{24,0},{1,9},{9,17},{17,25},{25,1},{2,10},{10... | collective-permute-start | bytes 589832 | tf_op jit(solution)/shard_map/out/ppermute | solution.py:441
  8.8 1.6 %collective-permute-start.3 = (bf16[256,384]{1,0:T(8,128)(2,1)}, bf16[256,384]{1,0:T(8,128)(2,1)S(1)}, u32[]{:S(2)}, u32[]{:S(2)}) collective-permute-start(bf16[256,384]{1,0:T(8,128)(2,1)} %get-tuple-element.60.refs_8_), channel_id=1, source_target_pairs={{0,8},{8,16},{16,24},{24,0},{1,9},{9,17},{17,25},{25,1},{2,10},{10... | collective-permute-start | bytes 589832 | tf_op jit(solution)/shard_map/first/ppermute | solution.py:441
  10.3 6.6 %collective-permute-done = bf16[128,768]{1,0:T(8,128)(2,1)S(1)} collective-permute-done((bf16[128,768]{1,0:T(8,128)(2,1)}, bf16[128,768]{1,0:T(8,128)(2,1)S(1)}, u32[]{:S(2)}, u32[]{:S(2)}) %collective-permute-start) | collective-permute-done | bytes 196640 | tf_op jit(solution)/shard_map/out/ppermute | solution.py:441
  16.9 3.9 %collective-permute-done.3.refs_9_ = bf16[256,384]{1,0:T(8,128)(2,1)S(1)} collective-permute-done((bf16[256,384]{1,0:T(8,128)(2,1)}, bf16[256,384]{1,0:T(8,128)(2,1)S(1)}, u32[]{:S(2)}, u32[]{:S(2)}) %collective-permute-start.3) | collective-permute-done | bytes 196640 | tf_op jit(solution)/shard_map/first/ppermute | solution.py:441
  20.8 0.1 collective-permute-start.4
  20.9 4.1 %collective-permute-done.1 = bf16[128,768]{1,0:T(8,128)(2,1)S(1)} collective-permute-done((bf16[128,768]{1,0:T(8,128)(2,1)S(1)}, bf16[128,768]{1,0:T(8,128)(2,1)S(1)}, u32[]{:S(2)}, u32[]{:S(2)}) %collective-permute-start.1) | collective-permute-done | bytes 196640 | tf_op jit(solution)/shard_map/out/ppermute | solution.py:441
  25.0 0.1 collective-permute-start.2
  25.1 5.3 %collective-permute-done.4.refs_10_ = bf16[256,384]{1,0:T(8,128)(2,1)S(1)} collective-permute-done((bf16[256,384]{1,0:T(8,128)(2,1)S(1)}, bf16[256,384]{1,0:T(8,128)(2,1)S(1)}, u32[]{:S(2)}, u32[]{:S(2)}) %collective-permute-start.4) | collective-permute-done | bytes 196640 | tf_op jit(solution)/shard_map/first/ppermute | solution.py:441
  30.4 3.9 %collective-permute-done.2 = bf16[128,768]{1,0:T(8,128)(2,1)S(1)} collective-permute-done((bf16[128,768]{1,0:T(8,128)(2,1)S(1)}, bf16[128,768]{1,0:T(8,128)(2,1)S(1)}, u32[]{:S(2)}, u32[]{:S(2)}) %collective-permute-start.2) | collective-permute-done | bytes 196640 | tf_op jit(solution)/shard_map/out/ppermute | solution.py:441
  34.3 3.6 %collective-permute-done.5.refs_11_ = bf16[256,384]{1,0:T(8,128)(2,1)S(1)} collective-permute-done((bf16[256,384]{1,0:T(8,128)(2,1)S(1)}, bf16[256,384]{1,0:T(8,128)(2,1)S(1)}, u32[]{:S(2)}, u32[]{:S(2)}) %collective-permute-start.5) | collective-permute-done | bytes 196640 | tf_op jit(solution)/shard_map/first/ppermute | solution.py:441
  37.9 0.7 copy-done.6
  38.6 0.0 collective-permute-done.6.refs_2_
  38.6 0.0 collective-permute-done.7.refs_3_
  38.6 0.1 collective-permute-start.8
  38.8 0.0 copy-start
  38.8 0.0 copy-start.1
  38.8 0.0 copy-start.2
  38.8 0.0 copy-start.9
  38.8 1.2 %select_bitcast_fusion.1 = (bf16[1,128,768]{2,1,0:T(8,128)(2,1)S(1)}, bf16[1,128,768]{2,1,0:T(8,128)(2,1)S(1)}) fusion(bf16[128,768]{1,0:T(8,128)(2,1)} %copy-done.12, bf16[128,768]{1,0:T(8,128)(2,1)} %get-tuple-element.59, pred[]{:T(512)S(6)} %eq.13), kind=kLoop, calls=%fused_computation.4 | loop fusion | flops 196608 | bytes 786433 | tf_op jit(solution)/shard_map/stack | solution.py:463
  40.0 0.1 collective-permute-start.9
  40.1 0.7 collective-permute-start.10
  40.8 1.1 %select_bitcast_fusion = (bf16[1,128,768]{2,1,0:T(8,128)(2,1)S(1)}, bf16[1,128,768]{2,1,0:T(8,128)(2,1)S(1)}) fusion(bf16[128,768]{1,0:T(8,128)(2,1)} %copy-done.13, bf16[128,768]{1,0:T(8,128)(2,1)} %copy-done.11, pred[]{:T(512)S(6)} %eq.14), kind=kLoop, calls=%fused_computation.3 | loop fusion | flops 196608 | bytes 786433 | tf_op jit(solution)/shard_map/stack | solution.py:463
  41.9 1.6 %collective-permute-start.13 = (bf16[2,128,768]{2,1,0:T(8,128)(2,1)S(1)}, bf16[2,128,768]{2,1,0:T(8,128)(2,1)S(1)}, u32[]{:S(2)}, u32[]{:S(2)}) collective-permute-start(bf16[2,128,768]{2,1,0:T(8,128)(2,1)S(1)} %pad_maximum_fusion.2), channel_id=1, source_target_pairs={{0,1},{1,0},{2,3},{3,2},{4,5},{5,4},{6,7},{7,6},{8,9},{9,8},{10,11... | collective-permute-start | bytes 1179656 | tf_op jit(solution)/shard_map/out_group/ppermute | solution.py:435
  43.6 0.6 collective-permute-start.14
  44.2 5.7 %collective-permute-done.9.refs_9_ = bf16[256,384]{1,0:T(8,128)(2,1)S(1)} collective-permute-done((bf16[256,384]{1,0:T(8,128)(2,1)}, bf16[256,384]{1,0:T(8,128)(2,1)S(1)}, u32[]{:S(2)}, u32[]{:S(2)}) %collective-permute-start.9) | collective-permute-done | bytes 196640 | tf_op jit(solution)/shard_map/second/ppermute | solution.py:441
  49.8 0.0 collective-permute-start.19
  49.8 3.9 %collective-permute-done.10.refs_9_ = bf16[256,384]{1,0:T(8,128)(2,1)S(1)} collective-permute-done((bf16[256,384]{1,0:T(8,128)(2,1)}, bf16[256,384]{1,0:T(8,128)(2,1)S(1)}, u32[]{:S(2)}, u32[]{:S(2)}) %collective-permute-start.10) | collective-permute-done | bytes 196640 | tf_op jit(solution)/shard_map/third/ppermute | solution.py:441
  53.7 0.0 collective-permute-done.8.refs_4_
  53.7 0.0 collective-permute-start.11
  53.7 1.5 %collective-permute-start.15 = (bf16[2,128,768]{2,1,0:T(8,128)(2,1)S(1)}, bf16[2,128,768]{2,1,0:T(8,128)(2,1)S(1)}, u32[]{:S(2)}, u32[]{:S(2)}) collective-permute-start(bf16[2,128,768]{2,1,0:T(8,128)(2,1)S(1)} %pad_maximum_fusion.2), channel_id=1, source_target_pairs={{0,5},{1,4},{2,7},{3,6},{4,1},{5,0},{6,3},{7,2},{8,13},{9,12},{10,... | collective-permute-start | bytes 1179656 | tf_op jit(solution)/shard_map/out_across/ppermute | solution.py:465
  55.2 2.7 %collective-permute-done.19.refs_10_ = bf16[256,384]{1,0:T(8,128)(2,1)S(1)} collective-permute-done((bf16[256,384]{1,0:T(8,128)(2,1)S(1)}, bf16[256,384]{1,0:T(8,128)(2,1)S(1)}, u32[]{:S(2)}, u32[]{:S(2)}) %collective-permute-start.19) | collective-permute-done | bytes 196640 | tf_op jit(solution)/shard_map/second/ppermute | solution.py:441
  57.9 0.0 collective-permute-start.20
  58.0 4.2 %attend_and_pool.1 = (bf16[144,128]{1,0:T(8,128)(2,1)S(1)}, bf16[144,128]{1,0:T(8,128)(2,1)S(1)}, bf16[144,128]{1,0:T(8,128)(2,1)S(1)}, bf16[144,128]{1,0:T(8,128)(2,1)S(1)}, f32[8,1024]{1,0:T(8,128)S(1)}) custom-call(s32[3]{0:T(128)S(1)} %copy-done.8, bf16[256,2048]{1,0:T(8,128)(2,1)S(1)} %bitcast.36, bf16[256,2048]{1,0:T(8,128)(2,1)S(1)} %collective-permute-done.6.refs_2_, ...), custom_call_target="tpu_custom_call" | custom-call | flops 1 | bytes 1 | tf_op jit(solution)/shard_map/attend_and_pool/pallas_call | solution.py:302
  62.1 1.2 %collective-permute-done.11.refs_10_ = bf16[256,384]{1,0:T(8,128)(2,1)S(1)} collective-permute-done((bf16[256,384]{1,0:T(8,128)(2,1)S(1)}, bf16[256,384]{1,0:T(8,128)(2,1)S(1)}, u32[]{:S(2)}, u32[]{:S(2)}) %collective-permute-start.11) | collective-permute-done | bytes 196640 | tf_op jit(solution)/shard_map/third/ppermute | solution.py:441
  63.3 0.0 collective-permute-start.12
  63.4 0.3 collective-permute-start.17
  63.7 3.5 %collective-permute-done.20.refs_11_ = bf16[256,384]{1,0:T(8,128)(2,1)S(1)} collective-permute-done((bf16[256,384]{1,0:T(8,128)(2,1)S(1)}, bf16[256,384]{1,0:T(8,128)(2,1)S(1)}, u32[]{:S(2)}, u32[]{:S(2)}) %collective-permute-start.20) | collective-permute-done | bytes 196640 | tf_op jit(solution)/shard_map/second/ppermute | solution.py:441
  67.2 3.9 %attend.2 = (bf16[144,128]{1,0:T(8,128)(2,1)S(1)}, bf16[144,128]{1,0:T(8,128)(2,1)S(1)}, bf16[144,128]{1,0:T(8,128)(2,1)S(1)}, bf16[144,128]{1,0:T(8,128)(2,1)S(1)}) custom-call(s32[3]{0:T(128)S(1)} %copy-done.8, bf16[256,2048]{1,0:T(8,128)(2,1)S(1)} %bitcast.37, bf16[256,2048]{1,0:T(8,128)(2,1)S(1)} %collective-permute-done.6.refs_2_, ...), custom_call_target="tpu_custom_call" | custom-call | flops 1 | bytes 1 | tf_op jit(solution)/shard_map/attend/pallas_call | solution.py:302
  71.1 0.2 pad_maximum_fusion.refs_10_.refs_5_
  71.3 0.4 collective-permute-start.25
  71.8 1.8 %collective-permute-start.21 = (bf16[4,144,128]{2,1,0:T(8,128)(2,1)S(1)}, bf16[4,144,128]{2,1,0:T(8,128)(2,1)S(1)}, u32[]{:S(2)}, u32[]{:S(2)}) collective-permute-start(bf16[4,144,128]{2,1,0:T(8,128)(2,1)S(1)} %pad_maximum_fusion.3), channel_id=1, source_target_pairs={{0,1},{1,0},{2,3},{3,2},{4,5},{5,4},{6,7},{7,6},{8,9},{9,8},{10,11... | collective-permute-start | bytes 442376 | tf_op jit(solution)/shard_map/context_first_group/ppermute | solution.py:435
  73.7 1.5 %collective-permute-start.23 = (bf16[144,128]{1,0:T(8,128)(2,1)S(1)}, bf16[144,128]{1,0:T(8,128)(2,1)S(1)}, u32[]{:S(2)}, u32[]{:S(2)}) collective-permute-start(bf16[144,128]{1,0:T(8,128)(2,1)S(1)} %get-tuple-element.87), channel_id=1, source_target_pairs={{0,4},{2,6},{4,0},{6,2},{1,5},{3,7},{5,1},{7,3},{8,12},{10,14},{12... | collective-permute-start | bytes 110600 | tf_op jit(solution)/shard_map/context_second/ppermute | solution.py:435
  75.2 0.4 collective-permute-start.24
  75.5 3.8 %attend.3 = (bf16[144,128]{1,0:T(8,128)(2,1)S(1)}, bf16[144,128]{1,0:T(8,128)(2,1)S(1)}, bf16[144,128]{1,0:T(8,128)(2,1)S(1)}, bf16[144,128]{1,0:T(8,128)(2,1)S(1)}) custom-call(s32[3]{0:T(128)S(1)} %copy-done.8, bf16[256,2048]{1,0:T(8,128)(2,1)S(1)} %bitcast.38, bf16[256,2048]{1,0:T(8,128)(2,1)S(1)} %collective-permute-done.6.refs_2_, ...), custom_call_target="tpu_custom_call" | custom-call | flops 1 | bytes 1 | tf_op jit(solution)/shard_map/attend/pallas_call | solution.py:302
  79.4 0.3 collective-permute-start.27
  79.8 1.5 %collective-permute-start.28 = (bf16[144,128]{1,0:T(8,128)(2,1)S(1)}, bf16[144,128]{1,0:T(8,128)(2,1)S(1)}, u32[]{:S(2)}, u32[]{:S(2)}) collective-permute-start(bf16[144,128]{1,0:T(8,128)(2,1)S(1)} %get-tuple-element.109), channel_id=1, source_target_pairs={{0,4},{2,6},{4,0},{6,2},{1,5},{3,7},{5,1},{7,3},{8,12},{10,14},{12... | collective-permute-start | bytes 110600 | tf_op jit(solution)/shard_map/context_third/ppermute | solution.py:435
  81.3 0.1 collective-permute-start.29
  81.4 0.5 collective-permute-start.26
  81.9 1.8 %collective-permute-done.28.refs_2_ = bf16[144,128]{1,0:T(8,128)(2,1)S(1)} collective-permute-done((bf16[144,128]{1,0:T(8,128)(2,1)S(1)}, bf16[144,128]{1,0:T(8,128)(2,1)S(1)}, u32[]{:S(2)}, u32[]{:S(2)}) %collective-permute-start.28) | collective-permute-done | bytes 36896 | tf_op jit(solution)/shard_map/context_third/ppermute | solution.py:435
  83.7 1.2 %collective-permute-done.29.refs_3_ = bf16[144,128]{1,0:T(8,128)(2,1)S(1)} collective-permute-done((bf16[144,128]{1,0:T(8,128)(2,1)S(1)}, bf16[144,128]{1,0:T(8,128)(2,1)S(1)}, u32[]{:S(2)}, u32[]{:S(2)}) %collective-permute-start.29) | collective-permute-done | bytes 36896 | tf_op jit(solution)/shard_map/context_third/ppermute | solution.py:435
  84.9 0.0 copy-start.10
  84.9 0.6 collective-permute-start.30
  85.5 2.2 %collective-permute-done.26.refs_9_ = bf16[4,144,128]{2,1,0:T(8,128)(2,1)S(1)} collective-permute-done((bf16[4,144,128]{2,1,0:T(8,128)(2,1)S(1)}, bf16[4,144,128]{2,1,0:T(8,128)(2,1)S(1)}, u32[]{:S(2)}, u32[]{:S(2)}) %collective-permute-start.26) | collective-permute-done | bytes 147488 | tf_op jit(solution)/shard_map/context_second_group/ppermute | solution.py:435
  87.7 2.1 %project_early.1.early_ref = f32[272,1024]{1,0:T(8,128)S(1)} custom-call(s32[3]{0:T(128)S(1)} %copy-done.8, bf16[144,128]{1,0:T(8,128)(2,1)S(1)} %get-tuple-element.98.refs_0_, bf16[144,128]{1,0:T(8,128)(2,1)S(1)} %collective-permute-done.16.refs_1_, bf16[144,128]{1,0:T(8,128)(2,1)S(1)} %collective-permute-done.17.refs_2_, ...), custom_call_target="tpu_custom_call" | custom-call | flops 1 | bytes 1 | tf_op jit(solution)/shard_map/project_early/pallas_call | solution.py:358
  89.9 1.1 %collective-permute-done.30.refs_4_ = bf16[4,144,128]{2,1,0:T(8,128)(2,1)S(1)} collective-permute-done((bf16[4,144,128]{2,1,0:T(8,128)(2,1)S(1)}, bf16[4,144,128]{2,1,0:T(8,128)(2,1)S(1)}, u32[]{:S(2)}, u32[]{:S(2)}) %collective-permute-start.30) | collective-permute-done | bytes 147488 | tf_op jit(solution)/shard_map/context_third_group/ppermute | solution.py:435
  91.0 2.2 %project_late.1 = (bf16[256,1024]{1,0:T(8,128)(2,1)}, f32[4,1024]{1,0:T(4,128)S(1)}, f32[4,1024]{1,0:T(4,128)S(1)}) custom-call(s32[3]{0:T(128)S(1)} %copy-done.8, s32[8]{0:T(128)S(1)} %bitcast.52, bf16[256,2048]{1,0:T(8,128)(2,1)S(1)} %bitcast.39, f32[8,1024]{1,0:T(8,128)S(1)} %get-tuple-element.69.pool_ref, f32[272,1024]{1,0:T(8,128)S(1)} %project_early.1.early_ref, ...), custom_call_target="tpu_custom_call" | custom-call | flops 1 | bytes 1 | tf_op jit(solution)/shard_map/project_late/pallas_call | solution.py:414
  93.2 0.5 collective-permute-start.31
  93.7 3.2 %collective-permute-done.31 = f32[4,1024]{1,0:T(4,128)S(1)} collective-permute-done((f32[4,1024]{1,0:T(4,128)S(1)}, f32[4,1024]{1,0:T(4,128)S(1)}, u32[]{:S(2)}, u32[]{:S(2)}) %collective-permute-start.31) | collective-permute-done | bytes 16416 | tf_op jit(solution)/shard_map/embedding_half/ppermute | solution.py:435
  97.0 0.2 select_bitcast_fusion.5
  97.1 0.7 maximum_multiply_fusion
  (46 shorter events, 0.2 us)
Async XLA Ops:
  0.6 38.0 %collective-permute-start.6 = (bf16[256,2048]{1,0:T(8,128)(2,1)}, bf16[256,2048]{1,0:T(8,128)(2,1)S(1)}, u32[]{:S(2)}, u32[]{:S(2)}) collective-permute-start(bf16[256,2048]{1,0:T(8,128)(2,1)} %bitcast.34), channel_id=1, source_target_pairs={{0,2},{2,0},{4,6},{6,4},{1,3},{3,1},{5,7},{7,5},{8,10},{10,8},{12,... | collective-permute-start | bytes 3145736 | tf_op jit(solution)/shard_map/hidden_core/ppermute | solution.py:435
  1.1 37.4 %collective-permute-start.7 = (bf16[256,2048]{1,0:T(8,128)(2,1)}, bf16[256,2048]{1,0:T(8,128)(2,1)S(1)}, u32[]{:S(2)}, u32[]{:S(2)}) collective-permute-start(bf16[256,2048]{1,0:T(8,128)(2,1)} %bitcast.35), channel_id=1, source_target_pairs={{0,4},{2,6},{4,0},{6,2},{1,5},{3,7},{5,1},{7,3},{8,12},{10,14},{12... | collective-permute-start | bytes 3145736 | tf_op jit(solution)/shard_map/hidden_cross/ppermute | solution.py:435
  7.2 9.7 %collective-permute-start = (bf16[128,768]{1,0:T(8,128)(2,1)}, bf16[128,768]{1,0:T(8,128)(2,1)S(1)}, u32[]{:S(2)}, u32[]{:S(2)}) collective-permute-start(bf16[128,768]{1,0:T(8,128)(2,1)} %get-tuple-element.59), channel_id=1, source_target_pairs={{0,8},{8,16},{16,24},{24,0},{1,9},{9,17},{17,25},{25,1},{2,10},{10... | collective-permute-start | bytes 589832 | tf_op jit(solution)/shard_map/out/ppermute | solution.py:441
  8.8 12.0 %collective-permute-start.3 = (bf16[256,384]{1,0:T(8,128)(2,1)}, bf16[256,384]{1,0:T(8,128)(2,1)S(1)}, u32[]{:S(2)}, u32[]{:S(2)}) collective-permute-start(bf16[256,384]{1,0:T(8,128)(2,1)} %get-tuple-element.60.refs_8_), channel_id=1, source_target_pairs={{0,8},{8,16},{16,24},{24,0},{1,9},{9,17},{17,25},{25,1},{2,10},{10... | collective-permute-start | bytes 589832 | tf_op jit(solution)/shard_map/first/ppermute | solution.py:441
  16.9 8.2 %copy-start.11 = (bf16[128,768]{1,0:T(8,128)(2,1)}, bf16[128,768]{1,0:T(8,128)(2,1)S(1)}, u32[]{:S(2)}) copy-start(bf16[128,768]{1,0:T(8,128)(2,1)S(1)} %collective-permute-done) | copy-start | bytes 589828
  16.9 8.1 %collective-permute-start.1 = (bf16[128,768]{1,0:T(8,128)(2,1)S(1)}, bf16[128,768]{1,0:T(8,128)(2,1)S(1)}, u32[]{:S(2)}, u32[]{:S(2)}) collective-permute-start(bf16[128,768]{1,0:T(8,128)(2,1)S(1)} %collective-permute-done), channel_id=1, source_target_pairs={{0,8},{8,16},{16,24},{24,0},{1,9},{9,17},{17,25},{25,1},{2,10},{10... | collective-permute-start | bytes 589832 | tf_op jit(solution)/shard_map/out/ppermute | solution.py:441
  20.8 9.6 %collective-permute-start.4 = (bf16[256,384]{1,0:T(8,128)(2,1)S(1)}, bf16[256,384]{1,0:T(8,128)(2,1)S(1)}, u32[]{:S(2)}, u32[]{:S(2)}) collective-permute-start(bf16[256,384]{1,0:T(8,128)(2,1)S(1)} %collective-permute-done.3.refs_9_), channel_id=1, source_target_pairs={{0,8},{8,16},{16,24},{24,0},{1,9},{9,17},{17,25},{25,1},{2,10},{10... | collective-permute-start | bytes 589832 | tf_op jit(solution)/shard_map/first/ppermute | solution.py:441
  25.0 13.6 %copy-start.12 = (bf16[128,768]{1,0:T(8,128)(2,1)}, bf16[128,768]{1,0:T(8,128)(2,1)S(1)}, u32[]{:S(2)}) copy-start(bf16[128,768]{1,0:T(8,128)(2,1)S(1)} %collective-permute-done.1) | copy-start | bytes 589828
  25.0 9.3 %collective-permute-start.2 = (bf16[128,768]{1,0:T(8,128)(2,1)S(1)}, bf16[128,768]{1,0:T(8,128)(2,1)S(1)}, u32[]{:S(2)}, u32[]{:S(2)}) collective-permute-start(bf16[128,768]{1,0:T(8,128)(2,1)S(1)} %collective-permute-done.1), channel_id=1, source_target_pairs={{0,8},{8,16},{16,24},{24,0},{1,9},{9,17},{17,25},{25,1},{2,10},{10... | collective-permute-start | bytes 589832 | tf_op jit(solution)/shard_map/out/ppermute | solution.py:441
  30.4 7.5 %collective-permute-start.5 = (bf16[256,384]{1,0:T(8,128)(2,1)S(1)}, bf16[256,384]{1,0:T(8,128)(2,1)S(1)}, u32[]{:S(2)}, u32[]{:S(2)}) collective-permute-start(bf16[256,384]{1,0:T(8,128)(2,1)S(1)} %collective-permute-done.4.refs_10_), channel_id=1, source_target_pairs={{0,8},{8,16},{16,24},{24,0},{1,9},{9,17},{17,25},{25,1},{2,10},{10... | collective-permute-start | bytes 589832 | tf_op jit(solution)/shard_map/first/ppermute | solution.py:441
  34.3 4.3 %copy-start.13 = (bf16[128,768]{1,0:T(8,128)(2,1)}, bf16[128,768]{1,0:T(8,128)(2,1)S(1)}, u32[]{:S(2)}) copy-start(bf16[128,768]{1,0:T(8,128)(2,1)S(1)} %collective-permute-done.2) | copy-start | bytes 589828
  37.9 0.7 copy-start.6
  38.6 15.1 %collective-permute-start.8 = (bf16[256,2048]{1,0:T(8,128)(2,1)S(1)}, bf16[256,2048]{1,0:T(8,128)(2,1)S(1)}, u32[]{:S(2)}, u32[]{:S(2)}) collective-permute-start(bf16[256,2048]{1,0:T(8,128)(2,1)S(1)} %collective-permute-done.7.refs_3_), channel_id=1, source_target_pairs={{0,2},{2,0},{4,6},{6,4},{1,3},{3,1},{5,7},{7,5},{8,10},{10,8},{12,... | collective-permute-start | bytes 3145736 | tf_op jit(solution)/shard_map/hidden_far/ppermute | solution.py:435
  38.8 19.2 %copy-start = (bf16[1,256,2048]{2,1,0:T(8,128)(2,1)S(1)}, bf16[1,256,2048]{2,1,0:T(8,128)(2,1)}, u32[]{:S(2)}) copy-start(bf16[1,256,2048]{2,1,0:T(8,128)(2,1)} %param.6) | copy-start | bytes 3145732
  38.8 19.2 %copy-start.1 = (f32[1024,128]{1,0:T(8,128)S(1)}, f32[1024,128]{1,0:T(8,128)}, u32[]{:S(2)}) copy-start(f32[1024,128]{1,0:T(8,128)} %constant.62.clone.refs_5_) | copy-start | bytes 1572868
  38.8 19.1 %copy-start.2 = (f32[1024,128]{1,0:T(8,128)S(1)}, f32[1024,128]{1,0:T(8,128)}, u32[]{:S(2)}) copy-start(f32[1024,128]{1,0:T(8,128)} %constant.63.clone.refs_6_) | copy-start | bytes 1572868
  38.8 19.1 %copy-start.5 = (bf16[256,384]{1,0:T(8,128)(2,1)S(1)}, bf16[256,384]{1,0:T(8,128)(2,1)}, u32[]{:S(2)}) copy-start(bf16[256,384]{1,0:T(8,128)(2,1)} %get-tuple-element.60.refs_8_) | copy-start | bytes 589828
  38.8 19.1 %copy-start.7 = (bf16[256,384]{1,0:T(8,128)(2,1)S(1)}, bf16[256,384]{1,0:T(8,128)(2,1)}, u32[]{:S(2)}) copy-start(bf16[256,384]{1,0:T(8,128)(2,1)} %copy-done.6) | copy-start | bytes 589828
  38.8 19.1 %copy-start.8 = (s32[3]{0:T(128)S(1)}, s32[3]{0:T(128)}, u32[]{:S(2)}) copy-start(s32[3]{0:T(128)} %pad_add_fusion.where.refs_0_) | copy-start | bytes 40
  38.8 19.1 %copy-start.9 = (s32[1,32]{1,0:T(1,128)S(1)}, s32[1,32]{1,0:T(1,128)}, u32[]{:S(2)}) copy-start(s32[1,32]{1,0:T(1,128)} %refs_7_.5) | copy-start | bytes 388
  40.0 9.8 %collective-permute-start.9 = (bf16[256,384]{1,0:T(8,128)(2,1)}, bf16[256,384]{1,0:T(8,128)(2,1)S(1)}, u32[]{:S(2)}, u32[]{:S(2)}) collective-permute-start(bf16[256,384]{1,0:T(8,128)(2,1)} %get-tuple-element.66.refs_8_), channel_id=1, source_target_pairs={{0,8},{8,16},{16,24},{24,0},{1,9},{9,17},{17,25},{25,1},{2,10},{10... | collective-permute-start | bytes 589832 | tf_op jit(solution)/shard_map/second/ppermute | solution.py:441
  40.1 13.6 %collective-permute-start.10 = (bf16[256,384]{1,0:T(8,128)(2,1)}, bf16[256,384]{1,0:T(8,128)(2,1)S(1)}, u32[]{:S(2)}, u32[]{:S(2)}) collective-permute-start(bf16[256,384]{1,0:T(8,128)(2,1)} %get-tuple-element.67.refs_8_), channel_id=1, source_target_pairs={{0,8},{8,16},{16,24},{24,0},{1,9},{9,17},{17,25},{25,1},{2,10},{10... | collective-permute-start | bytes 589832 | tf_op jit(solution)/shard_map/third/ppermute | solution.py:441
  41.9 21.4 %collective-permute-start.13 = (bf16[2,128,768]{2,1,0:T(8,128)(2,1)S(1)}, bf16[2,128,768]{2,1,0:T(8,128)(2,1)S(1)}, u32[]{:S(2)}, u32[]{:S(2)}) collective-permute-start(bf16[2,128,768]{2,1,0:T(8,128)(2,1)S(1)} %pad_maximum_fusion.2), channel_id=1, source_target_pairs={{0,1},{1,0},{2,3},{3,2},{4,5},{5,4},{6,7},{7,6},{8,9},{9,8},{10,11... | collective-permute-start | bytes 1179656 | tf_op jit(solution)/shard_map/out_group/ppermute | solution.py:435
  43.5 23.7 %copy-start.4 = (bf16[256,384]{1,0:T(8,128)(2,1)S(1)}, bf16[256,384]{1,0:T(8,128)(2,1)}, u32[]{:S(2)}) copy-start(bf16[256,384]{1,0:T(8,128)(2,1)} %get-tuple-element.66.refs_8_) | copy-start | bytes 589828
  43.6 19.8 %collective-permute-start.14 = (bf16[2,128,768]{2,1,0:T(8,128)(2,1)S(1)}, bf16[2,128,768]{2,1,0:T(8,128)(2,1)S(1)}, u32[]{:S(2)}, u32[]{:S(2)}) collective-permute-start(bf16[2,128,768]{2,1,0:T(8,128)(2,1)S(1)} %pad_maximum_fusion.1), channel_id=1, source_target_pairs={{0,4},{2,6},{4,0},{6,2},{1,5},{3,7},{5,1},{7,3},{8,12},{10,14},{12... | collective-permute-start | bytes 1179656 | tf_op jit(solution)/shard_map/out_cross/ppermute | solution.py:435
  49.8 8.1 %collective-permute-start.19 = (bf16[256,384]{1,0:T(8,128)(2,1)S(1)}, bf16[256,384]{1,0:T(8,128)(2,1)S(1)}, u32[]{:S(2)}, u32[]{:S(2)}) collective-permute-start(bf16[256,384]{1,0:T(8,128)(2,1)S(1)} %collective-permute-done.9.refs_9_), channel_id=1, source_target_pairs={{0,8},{8,16},{16,24},{24,0},{1,9},{9,17},{17,25},{25,1},{2,10},{10... | collective-permute-start | bytes 589832 | tf_op jit(solution)/shard_map/second/ppermute | solution.py:441
  53.7 9.6 %collective-permute-start.11 = (bf16[256,384]{1,0:T(8,128)(2,1)S(1)}, bf16[256,384]{1,0:T(8,128)(2,1)S(1)}, u32[]{:S(2)}, u32[]{:S(2)}) collective-permute-start(bf16[256,384]{1,0:T(8,128)(2,1)S(1)} %collective-permute-done.10.refs_9_), channel_id=1, source_target_pairs={{0,8},{8,16},{16,24},{24,0},{1,9},{9,17},{17,25},{25,1},{2,10},{10... | collective-permute-start | bytes 589832 | tf_op jit(solution)/shard_map/third/ppermute | solution.py:441
  53.7 17.4 %collective-permute-start.15 = (bf16[2,128,768]{2,1,0:T(8,128)(2,1)S(1)}, bf16[2,128,768]{2,1,0:T(8,128)(2,1)S(1)}, u32[]{:S(2)}, u32[]{:S(2)}) collective-permute-start(bf16[2,128,768]{2,1,0:T(8,128)(2,1)S(1)} %pad_maximum_fusion.2), channel_id=1, source_target_pairs={{0,5},{1,4},{2,7},{3,6},{4,1},{5,0},{6,3},{7,2},{8,13},{9,12},{10,... | collective-permute-start | bytes 1179656 | tf_op jit(solution)/shard_map/out_across/ppermute | solution.py:465
  57.9 9.3 %collective-permute-start.20 = (bf16[256,384]{1,0:T(8,128)(2,1)S(1)}, bf16[256,384]{1,0:T(8,128)(2,1)S(1)}, u32[]{:S(2)}, u32[]{:S(2)}) collective-permute-start(bf16[256,384]{1,0:T(8,128)(2,1)S(1)} %collective-permute-done.19.refs_10_), channel_id=1, source_target_pairs={{0,8},{8,16},{16,24},{24,0},{1,9},{9,17},{17,25},{25,1},{2,10},{10... | collective-permute-start | bytes 589832 | tf_op jit(solution)/shard_map/second/ppermute | solution.py:441
  63.3 7.8 %collective-permute-start.12 = (bf16[256,384]{1,0:T(8,128)(2,1)S(1)}, bf16[256,384]{1,0:T(8,128)(2,1)S(1)}, u32[]{:S(2)}, u32[]{:S(2)}) collective-permute-start(bf16[256,384]{1,0:T(8,128)(2,1)S(1)} %collective-permute-done.11.refs_10_), channel_id=1, source_target_pairs={{0,8},{8,16},{16,24},{24,0},{1,9},{9,17},{17,25},{25,1},{2,10},{10... | collective-permute-start | bytes 589832 | tf_op jit(solution)/shard_map/third/ppermute | solution.py:441
  63.4 7.7 %collective-permute-start.16 = (bf16[144,128]{1,0:T(8,128)(2,1)S(1)}, bf16[144,128]{1,0:T(8,128)(2,1)S(1)}, u32[]{:S(2)}, u32[]{:S(2)}) collective-permute-start(bf16[144,128]{1,0:T(8,128)(2,1)S(1)} %get-tuple-element.74), channel_id=1, source_target_pairs={{0,2},{2,0},{4,6},{6,4},{1,3},{3,1},{5,7},{7,5},{8,10},{10,8},{12,... | collective-permute-start | bytes 110600 | tf_op jit(solution)/shard_map/context_first/ppermute | solution.py:435
  63.4 7.7 %collective-permute-start.17 = (bf16[144,128]{1,0:T(8,128)(2,1)S(1)}, bf16[144,128]{1,0:T(8,128)(2,1)S(1)}, u32[]{:S(2)}, u32[]{:S(2)}) collective-permute-start(bf16[144,128]{1,0:T(8,128)(2,1)S(1)} %get-tuple-element.75), channel_id=1, source_target_pairs={{0,4},{2,6},{4,0},{6,2},{1,5},{3,7},{5,1},{7,3},{8,12},{10,14},{12... | collective-permute-start | bytes 110600 | tf_op jit(solution)/shard_map/context_first/ppermute | solution.py:435
  67.2 3.9 %collective-permute-start.18 = (bf16[144,128]{1,0:T(8,128)(2,1)S(1)}, bf16[144,128]{1,0:T(8,128)(2,1)S(1)}, u32[]{:S(2)}, u32[]{:S(2)}) collective-permute-start(bf16[144,128]{1,0:T(8,128)(2,1)S(1)} %get-tuple-element.76), channel_id=1, source_target_pairs={{0,6},{2,4},{4,2},{6,0},{1,7},{3,5},{5,3},{7,1},{8,14},{10,12},{12... | collective-permute-start | bytes 110600 | tf_op jit(solution)/shard_map/context_first/ppermute | solution.py:435
  71.1 4.4 %copy-start.3 = (bf16[256,384]{1,0:T(8,128)(2,1)S(1)}, bf16[256,384]{1,0:T(8,128)(2,1)}, u32[]{:S(2)}) copy-start(bf16[256,384]{1,0:T(8,128)(2,1)} %get-tuple-element.67.refs_8_) | copy-start | bytes 589828
  71.3 8.1 %collective-permute-start.25 = (bf16[4,2,128,768]{3,2,1,0:T(8,128)(2,1)S(1)}, bf16[4,2,128,768]{3,2,1,0:T(8,128)(2,1)S(1)}, u32[]{:S(2)}, u32[]{:S(2)}) collective-permute-start(bf16[4,2,128,768]{3,2,1,0:T(8,128)(2,1)S(1)} %pad_maximum_fusion.refs_10_.refs_5_), channel_id=1, source_target_pairs={{0,2},{2,0},{4,6},{6,4},{1,3},{3,1},{5,7},{7,5},{8,10},{10,8},{12,... | collective-permute-start | bytes 4718600 | tf_op jit(solution)/shard_map/out_core/ppermute | solution.py:435
  71.8 7.6 %collective-permute-start.21 = (bf16[4,144,128]{2,1,0:T(8,128)(2,1)S(1)}, bf16[4,144,128]{2,1,0:T(8,128)(2,1)S(1)}, u32[]{:S(2)}, u32[]{:S(2)}) collective-permute-start(bf16[4,144,128]{2,1,0:T(8,128)(2,1)S(1)} %pad_maximum_fusion.3), channel_id=1, source_target_pairs={{0,1},{1,0},{2,3},{3,2},{4,5},{5,4},{6,7},{7,6},{8,9},{9,8},{10,11... | collective-permute-start | bytes 442376 | tf_op jit(solution)/shard_map/context_first_group/ppermute | solution.py:435
  73.7 5.7 %collective-permute-start.22 = (bf16[144,128]{1,0:T(8,128)(2,1)S(1)}, bf16[144,128]{1,0:T(8,128)(2,1)S(1)}, u32[]{:S(2)}, u32[]{:S(2)}) collective-permute-start(bf16[144,128]{1,0:T(8,128)(2,1)S(1)} %get-tuple-element.86), channel_id=1, source_target_pairs={{0,2},{2,0},{4,6},{6,4},{1,3},{3,1},{5,7},{7,5},{8,10},{10,8},{12,... | collective-permute-start | bytes 110600 | tf_op jit(solution)/shard_map/context_second/ppermute | solution.py:435
  73.7 5.7 %collective-permute-start.23 = (bf16[144,128]{1,0:T(8,128)(2,1)S(1)}, bf16[144,128]{1,0:T(8,128)(2,1)S(1)}, u32[]{:S(2)}, u32[]{:S(2)}) collective-permute-start(bf16[144,128]{1,0:T(8,128)(2,1)S(1)} %get-tuple-element.87), channel_id=1, source_target_pairs={{0,4},{2,6},{4,0},{6,2},{1,5},{3,7},{5,1},{7,3},{8,12},{10,14},{12... | collective-permute-start | bytes 110600 | tf_op jit(solution)/shard_map/context_second/ppermute | solution.py:435
  75.2 4.2 %collective-permute-start.24 = (bf16[144,128]{1,0:T(8,128)(2,1)S(1)}, bf16[144,128]{1,0:T(8,128)(2,1)S(1)}, u32[]{:S(2)}, u32[]{:S(2)}) collective-permute-start(bf16[144,128]{1,0:T(8,128)(2,1)S(1)} %get-tuple-element.88), channel_id=1, source_target_pairs={{0,6},{2,4},{4,2},{6,0},{1,7},{3,5},{5,3},{7,1},{8,14},{10,12},{12... | collective-permute-start | bytes 110600 | tf_op jit(solution)/shard_map/context_second/ppermute | solution.py:435
  79.4 2.5 %collective-permute-start.27 = (bf16[144,128]{1,0:T(8,128)(2,1)S(1)}, bf16[144,128]{1,0:T(8,128)(2,1)S(1)}, u32[]{:S(2)}, u32[]{:S(2)}) collective-permute-start(bf16[144,128]{1,0:T(8,128)(2,1)S(1)} %get-tuple-element.108), channel_id=1, source_target_pairs={{0,2},{2,0},{4,6},{6,4},{1,3},{3,1},{5,7},{7,5},{8,10},{10,8},{12,... | collective-permute-start | bytes 110600 | tf_op jit(solution)/shard_map/context_third/ppermute | solution.py:435
  79.8 4.0 %collective-permute-start.28 = (bf16[144,128]{1,0:T(8,128)(2,1)S(1)}, bf16[144,128]{1,0:T(8,128)(2,1)S(1)}, u32[]{:S(2)}, u32[]{:S(2)}) collective-permute-start(bf16[144,128]{1,0:T(8,128)(2,1)S(1)} %get-tuple-element.109), channel_id=1, source_target_pairs={{0,4},{2,6},{4,0},{6,2},{1,5},{3,7},{5,1},{7,3},{8,12},{10,14},{12... | collective-permute-start | bytes 110600 | tf_op jit(solution)/shard_map/context_third/ppermute | solution.py:435
  81.3 3.6 %collective-permute-start.29 = (bf16[144,128]{1,0:T(8,128)(2,1)S(1)}, bf16[144,128]{1,0:T(8,128)(2,1)S(1)}, u32[]{:S(2)}, u32[]{:S(2)}) collective-permute-start(bf16[144,128]{1,0:T(8,128)(2,1)S(1)} %get-tuple-element.110), channel_id=1, source_target_pairs={{0,6},{2,4},{4,2},{6,0},{1,7},{3,5},{5,3},{7,1},{8,14},{10,12},{12... | collective-permute-start | bytes 110600 | tf_op jit(solution)/shard_map/context_third/ppermute | solution.py:435
  81.4 6.4 %collective-permute-start.26 = (bf16[4,144,128]{2,1,0:T(8,128)(2,1)S(1)}, bf16[4,144,128]{2,1,0:T(8,128)(2,1)S(1)}, u32[]{:S(2)}, u32[]{:S(2)}) collective-permute-start(bf16[4,144,128]{2,1,0:T(8,128)(2,1)S(1)} %pad_maximum_fusion.4), channel_id=1, source_target_pairs={{0,1},{1,0},{2,3},{3,2},{4,5},{5,4},{6,7},{7,6},{8,9},{9,8},{10,11... | collective-permute-start | bytes 442376 | tf_op jit(solution)/shard_map/context_second_group/ppermute | solution.py:435
  84.9 6.1 %copy-start.10 = (s32[1,8,1]{1,2,0:T(1,128)S(1)}, s32[1,8,1]{1,2,0:T(1,128)}, u32[]{:S(2)}) copy-start(s32[1,8,1]{1,2,0:T(1,128)} %param.9) | copy-start | bytes 100
  84.9 6.1 %collective-permute-start.30 = (bf16[4,144,128]{2,1,0:T(8,128)(2,1)S(1)}, bf16[4,144,128]{2,1,0:T(8,128)(2,1)S(1)}, u32[]{:S(2)}, u32[]{:S(2)}) collective-permute-start(bf16[4,144,128]{2,1,0:T(8,128)(2,1)S(1)} %pad_maximum_fusion.5), channel_id=1, source_target_pairs={{0,1},{1,0},{2,3},{3,2},{4,5},{5,4},{6,7},{7,6},{8,9},{9,8},{10,11... | collective-permute-start | bytes 442376 | tf_op jit(solution)/shard_map/context_third_group/ppermute | solution.py:435
  93.2 3.7 %collective-permute-start.31 = (f32[4,1024]{1,0:T(4,128)S(1)}, f32[4,1024]{1,0:T(4,128)S(1)}, u32[]{:S(2)}, u32[]{:S(2)}) collective-permute-start(f32[4,1024]{1,0:T(4,128)S(1)} %get-tuple-element.115), channel_id=1, source_target_pairs={{0,1},{1,0},{2,3},{3,2},{4,5},{5,4},{6,7},{7,6},{8,9},{9,8},{10,11... | collective-permute-start | bytes 49160 | tf_op jit(solution)/shard_map/embedding_half/ppermute | solution.py:435

commit v6 on v5

--- a/solution.py
+++ b/solution.py
@@ -165,11 +165,9 @@
     return jnp.concatenate(parts, 1).astype(columns[0].dtype)
 
 
-def pieces_kernel(where, w_ref, x_ref, o_ref, out_ref, first_ref, second_ref, third_ref):
+def pieces_kernel(where, w_ref, o_ref, out_ref, first_ref):
     out_ref[...] = o_ref[0]
     first_ref[...] = folded([w_ref[j] for j in range(3)], False)
-    second_ref[...] = folded([w_ref[j] for j in range(3)], True)
-    third_ref[...] = folded([x_ref[j] for j in range(3)], lax.rem(where[0], 2) == 1)
 
 
 def pieces(where, proj_weight):
@@ -182,17 +180,45 @@
             grid=(1,),
             in_specs=[
                 pl.BlockSpec((3, shard, 128), lambda i, where: (0, 0, where[0])),
-                pl.BlockSpec((3, shard, 128), lambda i, where: (0, 0, 4 + where[0] // 2)),
                 pl.BlockSpec((1, quarter, width), lambda i, where: (3, where[0], 0)),
             ],
-            out_specs=[pl.BlockSpec((quarter, width), lambda i, where: (0, 0))]
-            + [pl.BlockSpec((shard // 2, 384), lambda i, where: (0, 0))] * 3,
+            out_specs=[
+                pl.BlockSpec((quarter, width), lambda i, where: (0, 0)),
+                pl.BlockSpec((shard // 2, 384), lambda i, where: (0, 0)),
+            ],
         ),
-        out_shape=[jax.ShapeDtypeStruct((quarter, width), proj_weight.dtype)]
-        + [jax.ShapeDtypeStruct((shard // 2, 384), proj_weight.dtype)] * 3,
+        out_shape=[
+            jax.ShapeDtypeStruct((quarter, width), proj_weight.dtype),
+            jax.ShapeDtypeStruct((shard // 2, 384), proj_weight.dtype),
+        ],
         cost_estimate=SHORT,
         name="pieces",
-    )(where, proj_weight, proj_weight, proj_weight)
+    )(where, proj_weight, proj_weight)
+
+
+def others_kernel(where, w_ref, x_ref, token_ref, second_ref, third_ref):
+    second_ref[...] = folded([w_ref[j] for j in range(3)], True)
+    third_ref[...] = folded([x_ref[j] for j in range(3)], lax.rem(where[0], 2) == 1)
+
+
+def other_pieces(where, proj_weight, token):
+    shard = proj_weight.shape[1]
+    return pl.pallas_call(
+        others_kernel,
+        grid_spec=pltpu.PrefetchScalarGridSpec(
+            num_scalar_prefetch=1,
+            grid=(1,),
+            in_specs=[
+                pl.BlockSpec((3, shard, 128), lambda i, where: (0, 0, where[0])),
+                pl.BlockSpec((3, shard, 128), lambda i, where: (0, 0, 4 + where[0] // 2)),
+                pl.BlockSpec(memory_space=pl.ANY),
+            ],
+            out_specs=[pl.BlockSpec((shard // 2, 384), lambda i, where: (0, 0))] * 2,
+        ),
+        out_shape=[jax.ShapeDtypeStruct((shard // 2, 384), proj_weight.dtype)] * 2,
+        cost_estimate=SHORT,
+        name="other_pieces",
+    )(where, proj_weight, proj_weight, token)
 
 
 def after(value, *earlier):
@@ -473,7 +499,7 @@
 
     h_cross = xor_send("hidden_cross", h, "seq", 2)
     h_core = xor_send("hidden_core", h, "seq", 1)
-    o0, x0, y0, z0 = pieces(where, proj_weight)
+    o0, x0 = pieces(where, proj_weight)
 
     def rings(names, starts, **before):
         held = [[start] for start in starts]
@@ -483,6 +509,7 @@
         return held
 
     out_ring, first_ring = rings(("out", "first"), (o0, x0))
+    y0, z0 = other_pieces(where, proj_weight, out_ring[1])
     out_ring[3], first_ring[3], h_core, h_cross, y0, z0 = lax.optimization_barrier(
         (out_ring[3], first_ring[3], h_core, h_cross, y0, z0)
     )

time: 98 us -> 97.7 us (level)
  waiting for transfers between devices: 53.8 us -> 51.1 us
  Pallas kernels: 19.1 us -> 21.5 us
    ppermute x12, waiting for transfers between devices: 44.2 us -> 41.5 us  [ring_send(): lax.ppermute(value, 'dp', [(i, (i + 1) % count) for i in range(count)])]
    pallas_call x0 -> x1, Pallas kernels: none -> 2.72 us  [other_pieces(): pl.pallas_call(others_kernel, grid_spec=pltpu.PrefetchScalarGridSpec(num_...]
  transfers between devices with their start and end apart: 32 -> 32, of which waited for: 16 -> 16; matrix products, arithmetic and copies ran while one was open for 3% -> 3% of each run, Pallas kernels for 17% -> 20%
where the time goes in v6:
time: 97.7 us; the launch traced here: 97.5 us
  waiting for transfers between devices  51.1 us (52%)
  Pallas kernels  21.5 us (22%)
  starting transfers between devices  19.1 us (20%)
  other arithmetic  4.04 us (4%)
  between operations  1.04 us (1%)
    ppermute x12, waiting for transfers between devices, ring_send(): lax.ppermute(value, 'dp', [(i, (i + 1) % count) for i in range(count)])  41.5 us
    ppermute x19, starting transfers between devices, xor_send(): lax.ppermute(value, axis, [(i, i ^ j) for i in range(lax.axis_size(axis))])  13.3 us
    pallas_call x3, Pallas kernels, attend(): pl.pallas_call(functools.partial(attend_kernel, pools), out_shape=out_sha...  11.9 us
    ppermute x19, waiting for transfers between devices, xor_send(): lax.ppermute(value, axis, [(i, i ^ j) for i in range(lax.axis_size(axis))])  9.63 us
    ppermute x12, starting transfers between devices, ring_send(): lax.ppermute(value, 'dp', [(i, (i + 1) % count) for i in range(count)])  4.23 us
    pallas_call x1, Pallas kernels, other_pieces(): pl.pallas_call(others_kernel, grid_spec=pltpu.PrefetchScalarGridSpec(num_...  2.72 us
    pallas_call x1, Pallas kernels, pieces(): pl.pallas_call(pieces_kernel, grid_spec=pltpu.PrefetchScalarGridSpec(num_...  2.53 us
    another operation x3, other arithmetic, across(): send = jnp.stack([jnp.where(mine, two, one) for mine, one, two in pairs])  2.29 us
  transfers between devices with their start and end apart: 32, of which 16 were waited for; matrix products, arithmetic and copies ran while one was open for 3% of the time, Pallas kernels for 20%

profile of v6, /device:TPU:0, one launch (start us, length us, event | category | flops | bytes accessed | tf_op | source)
XLA Modules:
  0.0 97.5 jit_solution(16370984001019760804)
XLA Ops:
  0.6 0.5 collective-permute-start.6
  1.1 2.6 %collective-permute-start.7 = (bf16[256,2048]{1,0:T(8,128)(2,1)}, bf16[256,2048]{1,0:T(8,128)(2,1)S(1)}, u32[]{:S(2)}, u32[]{:S(2)}) collective-permute-start(bf16[256,2048]{1,0:T(8,128)(2,1)} %bitcast.35), channel_id=1, source_target_pairs={{0,4},{2,6},{4,0},{6,2},{1,5},{3,7},{5,1},{7,3},{8,12},{10,14},{12... | collective-permute-start | bytes 3145736 | tf_op jit(solution)/shard_map/hidden_cross/ppermute | solution.py:461
  3.7 0.6 pad_add_fusion.where.refs_0_
  4.3 2.5 %pieces.1 = (bf16[128,768]{1,0:T(8,128)(2,1)}, bf16[256,384]{1,0:T(8,128)(2,1)}) custom-call(s32[3]{0:T(128)} %pad_add_fusion.where.refs_0_, bf16[4,512,768]{2,1,0:T(8,128)(2,1)} %x_ref.1, bf16[4,512,768]{2,1,0:T(8,128)(2,1)} %x_ref.1), custom_call_target="tpu_custom_call" | custom-call | flops 1 | bytes 1 | tf_op jit(solution)/shard_map/pieces/pallas_call | solution.py:176
  6.8 1.6 %collective-permute-start = (bf16[128,768]{1,0:T(8,128)(2,1)}, bf16[128,768]{1,0:T(8,128)(2,1)S(1)}, u32[]{:S(2)}, u32[]{:S(2)}) collective-permute-start(bf16[128,768]{1,0:T(8,128)(2,1)} %get-tuple-element.59), channel_id=1, source_target_pairs={{0,8},{8,16},{16,24},{24,0},{1,9},{9,17},{17,25},{25,1},{2,10},{10... | collective-permute-start | bytes 589832 | tf_op jit(solution)/shard_map/out/ppermute | solution.py:467
  8.4 1.6 %collective-permute-start.3 = (bf16[256,384]{1,0:T(8,128)(2,1)}, bf16[256,384]{1,0:T(8,128)(2,1)S(1)}, u32[]{:S(2)}, u32[]{:S(2)}) collective-permute-start(bf16[256,384]{1,0:T(8,128)(2,1)} %get-tuple-element.60.refs_8_), channel_id=1, source_target_pairs={{0,8},{8,16},{16,24},{24,0},{1,9},{9,17},{17,25},{25,1},{2,10},{10... | collective-permute-start | bytes 589832 | tf_op jit(solution)/shard_map/first/ppermute | solution.py:467
  10.0 6.6 %collective-permute-done.token_ref = bf16[128,768]{1,0:T(8,128)(2,1)S(1)} collective-permute-done((bf16[128,768]{1,0:T(8,128)(2,1)}, bf16[128,768]{1,0:T(8,128)(2,1)S(1)}, u32[]{:S(2)}, u32[]{:S(2)}) %collective-permute-start) | collective-permute-done | bytes 196640 | tf_op jit(solution)/shard_map/out/ppermute | solution.py:467
  16.6 3.9 %collective-permute-done.3.refs_9_ = bf16[256,384]{1,0:T(8,128)(2,1)S(1)} collective-permute-done((bf16[256,384]{1,0:T(8,128)(2,1)}, bf16[256,384]{1,0:T(8,128)(2,1)S(1)}, u32[]{:S(2)}, u32[]{:S(2)}) %collective-permute-start.3) | collective-permute-done | bytes 196640 | tf_op jit(solution)/shard_map/first/ppermute | solution.py:467
  20.4 0.1 collective-permute-start.4
  20.6 4.1 %collective-permute-done.1 = bf16[128,768]{1,0:T(8,128)(2,1)S(1)} collective-permute-done((bf16[128,768]{1,0:T(8,128)(2,1)S(1)}, bf16[128,768]{1,0:T(8,128)(2,1)S(1)}, u32[]{:S(2)}, u32[]{:S(2)}) %collective-permute-start.1) | collective-permute-done | bytes 196640 | tf_op jit(solution)/shard_map/out/ppermute | solution.py:467
  24.6 0.1 collective-permute-start.2
  24.8 5.3 %collective-permute-done.4.refs_10_ = bf16[256,384]{1,0:T(8,128)(2,1)S(1)} collective-permute-done((bf16[256,384]{1,0:T(8,128)(2,1)S(1)}, bf16[256,384]{1,0:T(8,128)(2,1)S(1)}, u32[]{:S(2)}, u32[]{:S(2)}) %collective-permute-start.4) | collective-permute-done | bytes 196640 | tf_op jit(solution)/shard_map/first/ppermute | solution.py:467
  30.1 0.0 collective-permute-start.5
  30.1 2.7 %other_pieces.1 = (bf16[256,384]{1,0:T(8,128)(2,1)}, bf16[256,384]{1,0:T(8,128)(2,1)}) custom-call(s32[3]{0:T(128)} %pad_add_fusion.where.refs_0_, bf16[4,512,768]{2,1,0:T(8,128)(2,1)} %x_ref.1, bf16[4,512,768]{2,1,0:T(8,128)(2,1)} %x_ref.1, bf16[128,768]{1,0:T(8,128)(2,1)} %copy-done.11), custom_call_target="tpu_custom_call" | custom-call | flops 1 | bytes 1 | tf_op jit(solution)/shard_map/other_pieces/pallas_call | solution.py:206
  32.8 1.1 %collective-permute-done.2 = bf16[128,768]{1,0:T(8,128)(2,1)S(1)} collective-permute-done((bf16[128,768]{1,0:T(8,128)(2,1)S(1)}, bf16[128,768]{1,0:T(8,128)(2,1)S(1)}, u32[]{:S(2)}, u32[]{:S(2)}) %collective-permute-start.2) | collective-permute-done | bytes 196640 | tf_op jit(solution)/shard_map/out/ppermute | solution.py:467
  33.9 3.6 %collective-permute-done.5.refs_11_ = bf16[256,384]{1,0:T(8,128)(2,1)S(1)} collective-permute-done((bf16[256,384]{1,0:T(8,128)(2,1)S(1)}, bf16[256,384]{1,0:T(8,128)(2,1)S(1)}, u32[]{:S(2)}, u32[]{:S(2)}) %collective-permute-start.5) | collective-permute-done | bytes 196640 | tf_op jit(solution)/shard_map/first/ppermute | solution.py:467
  37.5 0.7 copy-done.6
  38.2 0.1 collective-permute-start.8
  38.4 0.0 copy-start
  38.4 0.0 copy-start.1
  38.4 0.0 copy-start.2
  38.4 0.0 copy-start.9
  38.5 1.2 %select_bitcast_fusion.1 = (bf16[1,128,768]{2,1,0:T(8,128)(2,1)S(1)}, bf16[1,128,768]{2,1,0:T(8,128)(2,1)S(1)}) fusion(bf16[128,768]{1,0:T(8,128)(2,1)} %copy-done.12, bf16[128,768]{1,0:T(8,128)(2,1)} %get-tuple-element.59, pred[]{:T(512)S(6)} %eq.13), kind=kLoop, calls=%fused_computation.4 | loop fusion | flops 196608 | bytes 786433 | tf_op jit(solution)/shard_map/stack | solution.py:489
  39.7 0.1 collective-permute-start.9
  39.7 0.7 collective-permute-start.10
  40.4 1.1 %select_bitcast_fusion = (bf16[1,128,768]{2,1,0:T(8,128)(2,1)S(1)}, bf16[1,128,768]{2,1,0:T(8,128)(2,1)S(1)}) fusion(bf16[128,768]{1,0:T(8,128)(2,1)} %copy-done.13, bf16[128,768]{1,0:T(8,128)(2,1)} %copy-done.11, pred[]{:T(512)S(6)} %eq.14), kind=kLoop, calls=%fused_computation.3 | loop fusion | flops 196608 | bytes 786433 | tf_op jit(solution)/shard_map/stack | solution.py:489
  41.5 1.6 %collective-permute-start.13 = (bf16[2,128,768]{2,1,0:T(8,128)(2,1)S(1)}, bf16[2,128,768]{2,1,0:T(8,128)(2,1)S(1)}, u32[]{:S(2)}, u32[]{:S(2)}) collective-permute-start(bf16[2,128,768]{2,1,0:T(8,128)(2,1)S(1)} %pad_maximum_fusion.2), channel_id=1, source_target_pairs={{0,1},{1,0},{2,3},{3,2},{4,5},{5,4},{6,7},{7,6},{8,9},{9,8},{10,11... | collective-permute-start | bytes 1179656 | tf_op jit(solution)/shard_map/out_group/ppermute | solution.py:461
  43.2 0.6 collective-permute-start.14
  43.8 5.7 %collective-permute-done.9.refs_9_ = bf16[256,384]{1,0:T(8,128)(2,1)S(1)} collective-permute-done((bf16[256,384]{1,0:T(8,128)(2,1)}, bf16[256,384]{1,0:T(8,128)(2,1)S(1)}, u32[]{:S(2)}, u32[]{:S(2)}) %collective-permute-start.9) | collective-permute-done | bytes 196640 | tf_op jit(solution)/shard_map/second/ppermute | solution.py:467
  49.5 0.0 collective-permute-start.19
  49.5 3.9 %collective-permute-done.10.refs_9_ = bf16[256,384]{1,0:T(8,128)(2,1)S(1)} collective-permute-done((bf16[256,384]{1,0:T(8,128)(2,1)}, bf16[256,384]{1,0:T(8,128)(2,1)S(1)}, u32[]{:S(2)}, u32[]{:S(2)}) %collective-permute-start.10) | collective-permute-done | bytes 196640 | tf_op jit(solution)/shard_map/third/ppermute | solution.py:467
  53.3 0.0 collective-permute-done.8.refs_4_
  53.3 0.0 collective-permute-start.11
  53.3 1.5 %collective-permute-start.15 = (bf16[2,128,768]{2,1,0:T(8,128)(2,1)S(1)}, bf16[2,128,768]{2,1,0:T(8,128)(2,1)S(1)}, u32[]{:S(2)}, u32[]{:S(2)}) collective-permute-start(bf16[2,128,768]{2,1,0:T(8,128)(2,1)S(1)} %pad_maximum_fusion.2), channel_id=1, source_target_pairs={{0,5},{1,4},{2,7},{3,6},{4,1},{5,0},{6,3},{7,2},{8,13},{9,12},{10,... | collective-permute-start | bytes 1179656 | tf_op jit(solution)/shard_map/out_across/ppermute | solution.py:491
  54.8 2.7 %collective-permute-done.19.refs_10_ = bf16[256,384]{1,0:T(8,128)(2,1)S(1)} collective-permute-done((bf16[256,384]{1,0:T(8,128)(2,1)S(1)}, bf16[256,384]{1,0:T(8,128)(2,1)S(1)}, u32[]{:S(2)}, u32[]{:S(2)}) %collective-permute-start.19) | collective-permute-done | bytes 196640 | tf_op jit(solution)/shard_map/second/ppermute | solution.py:467
  57.6 4.2 %attend_and_pool.1 = (bf16[144,128]{1,0:T(8,128)(2,1)S(1)}, bf16[144,128]{1,0:T(8,128)(2,1)S(1)}, bf16[144,128]{1,0:T(8,128)(2,1)S(1)}, bf16[144,128]{1,0:T(8,128)(2,1)S(1)}, f32[8,1024]{1,0:T(8,128)S(1)}) custom-call(s32[3]{0:T(128)S(1)} %copy-done.8, bf16[256,2048]{1,0:T(8,128)(2,1)S(1)} %bitcast.36, bf16[256,2048]{1,0:T(8,128)(2,1)S(1)} %collective-permute-done.6.refs_2_, ...), custom_call_target="tpu_custom_call" | custom-call | flops 1 | bytes 1 | tf_op jit(solution)/shard_map/attend_and_pool/pallas_call | solution.py:328
  61.8 1.2 %collective-permute-done.11.refs_10_ = bf16[256,384]{1,0:T(8,128)(2,1)S(1)} collective-permute-done((bf16[256,384]{1,0:T(8,128)(2,1)S(1)}, bf16[256,384]{1,0:T(8,128)(2,1)S(1)}, u32[]{:S(2)}, u32[]{:S(2)}) %collective-permute-start.11) | collective-permute-done | bytes 196640 | tf_op jit(solution)/shard_map/third/ppermute | solution.py:467
  63.0 0.0 collective-permute-start.12
  63.0 0.0 collective-permute-done.14
  63.0 0.3 collective-permute-start.17
  63.3 3.5 %collective-permute-done.20.refs_11_ = bf16[256,384]{1,0:T(8,128)(2,1)S(1)} collective-permute-done((bf16[256,384]{1,0:T(8,128)(2,1)S(1)}, bf16[256,384]{1,0:T(8,128)(2,1)S(1)}, u32[]{:S(2)}, u32[]{:S(2)}) %collective-permute-start.20) | collective-permute-done | bytes 196640 | tf_op jit(solution)/shard_map/second/ppermute | solution.py:467
  66.8 3.9 %attend.2 = (bf16[144,128]{1,0:T(8,128)(2,1)S(1)}, bf16[144,128]{1,0:T(8,128)(2,1)S(1)}, bf16[144,128]{1,0:T(8,128)(2,1)S(1)}, bf16[144,128]{1,0:T(8,128)(2,1)S(1)}) custom-call(s32[3]{0:T(128)S(1)} %copy-done.8, bf16[256,2048]{1,0:T(8,128)(2,1)S(1)} %bitcast.37, bf16[256,2048]{1,0:T(8,128)(2,1)S(1)} %collective-permute-done.6.refs_2_, ...), custom_call_target="tpu_custom_call" | custom-call | flops 1 | bytes 1 | tf_op jit(solution)/shard_map/attend/pallas_call | solution.py:328
  70.8 0.2 pad_maximum_fusion.refs_10_.refs_5_
  71.0 0.4 collective-permute-start.25
  71.4 1.8 %collective-permute-start.21 = (bf16[4,144,128]{2,1,0:T(8,128)(2,1)S(1)}, bf16[4,144,128]{2,1,0:T(8,128)(2,1)S(1)}, u32[]{:S(2)}, u32[]{:S(2)}) collective-permute-start(bf16[4,144,128]{2,1,0:T(8,128)(2,1)S(1)} %pad_maximum_fusion.3), channel_id=1, source_target_pairs={{0,1},{1,0},{2,3},{3,2},{4,5},{5,4},{6,7},{7,6},{8,9},{9,8},{10,11... | collective-permute-start | bytes 442376 | tf_op jit(solution)/shard_map/context_first_group/ppermute | solution.py:461
  73.3 1.5 %collective-permute-start.23 = (bf16[144,128]{1,0:T(8,128)(2,1)S(1)}, bf16[144,128]{1,0:T(8,128)(2,1)S(1)}, u32[]{:S(2)}, u32[]{:S(2)}) collective-permute-start(bf16[144,128]{1,0:T(8,128)(2,1)S(1)} %get-tuple-element.87), channel_id=1, source_target_pairs={{0,4},{2,6},{4,0},{6,2},{1,5},{3,7},{5,1},{7,3},{8,12},{10,14},{12... | collective-permute-start | bytes 110600 | tf_op jit(solution)/shard_map/context_second/ppermute | solution.py:461
  74.8 0.4 collective-permute-start.24
  75.1 3.8 %attend.3 = (bf16[144,128]{1,0:T(8,128)(2,1)S(1)}, bf16[144,128]{1,0:T(8,128)(2,1)S(1)}, bf16[144,128]{1,0:T(8,128)(2,1)S(1)}, bf16[144,128]{1,0:T(8,128)(2,1)S(1)}) custom-call(s32[3]{0:T(128)S(1)} %copy-done.8, bf16[256,2048]{1,0:T(8,128)(2,1)S(1)} %bitcast.38, bf16[256,2048]{1,0:T(8,128)(2,1)S(1)} %collective-permute-done.6.refs_2_, ...), custom_call_target="tpu_custom_call" | custom-call | flops 1 | bytes 1 | tf_op jit(solution)/shard_map/attend/pallas_call | solution.py:328
  79.0 0.3 collective-permute-start.27
  79.4 1.5 %collective-permute-start.28 = (bf16[144,128]{1,0:T(8,128)(2,1)S(1)}, bf16[144,128]{1,0:T(8,128)(2,1)S(1)}, u32[]{:S(2)}, u32[]{:S(2)}) collective-permute-start(bf16[144,128]{1,0:T(8,128)(2,1)S(1)} %get-tuple-element.109), channel_id=1, source_target_pairs={{0,4},{2,6},{4,0},{6,2},{1,5},{3,7},{5,1},{7,3},{8,12},{10,14},{12... | collective-permute-start | bytes 110600 | tf_op jit(solution)/shard_map/context_third/ppermute | solution.py:461
  80.9 0.1 collective-permute-start.29
  81.0 0.5 collective-permute-start.26
  81.5 1.8 %collective-permute-done.28.refs_2_ = bf16[144,128]{1,0:T(8,128)(2,1)S(1)} collective-permute-done((bf16[144,128]{1,0:T(8,128)(2,1)S(1)}, bf16[144,128]{1,0:T(8,128)(2,1)S(1)}, u32[]{:S(2)}, u32[]{:S(2)}) %collective-permute-start.28) | collective-permute-done | bytes 36896 | tf_op jit(solution)/shard_map/context_third/ppermute | solution.py:461
  83.3 1.2 %collective-permute-done.29.refs_3_ = bf16[144,128]{1,0:T(8,128)(2,1)S(1)} collective-permute-done((bf16[144,128]{1,0:T(8,128)(2,1)S(1)}, bf16[144,128]{1,0:T(8,128)(2,1)S(1)}, u32[]{:S(2)}, u32[]{:S(2)}) %collective-permute-start.29) | collective-permute-done | bytes 36896 | tf_op jit(solution)/shard_map/context_third/ppermute | solution.py:461
  84.5 0.0 copy-start.10
  84.6 0.6 collective-permute-start.30
  85.1 2.2 %collective-permute-done.26.refs_9_ = bf16[4,144,128]{2,1,0:T(8,128)(2,1)S(1)} collective-permute-done((bf16[4,144,128]{2,1,0:T(8,128)(2,1)S(1)}, bf16[4,144,128]{2,1,0:T(8,128)(2,1)S(1)}, u32[]{:S(2)}, u32[]{:S(2)}) %collective-permute-start.26) | collective-permute-done | bytes 147488 | tf_op jit(solution)/shard_map/context_second_group/ppermute | solution.py:461
  87.4 2.1 %project_early.1.early_ref = f32[272,1024]{1,0:T(8,128)S(1)} custom-call(s32[3]{0:T(128)S(1)} %copy-done.8, bf16[144,128]{1,0:T(8,128)(2,1)S(1)} %get-tuple-element.98.refs_0_, bf16[144,128]{1,0:T(8,128)(2,1)S(1)} %collective-permute-done.16.refs_1_, bf16[144,128]{1,0:T(8,128)(2,1)S(1)} %collective-permute-done.17.refs_2_, ...), custom_call_target="tpu_custom_call" | custom-call | flops 1 | bytes 1 | tf_op jit(solution)/shard_map/project_early/pallas_call | solution.py:384
  89.5 1.1 %collective-permute-done.30.refs_4_ = bf16[4,144,128]{2,1,0:T(8,128)(2,1)S(1)} collective-permute-done((bf16[4,144,128]{2,1,0:T(8,128)(2,1)S(1)}, bf16[4,144,128]{2,1,0:T(8,128)(2,1)S(1)}, u32[]{:S(2)}, u32[]{:S(2)}) %collective-permute-start.30) | collective-permute-done | bytes 147488 | tf_op jit(solution)/shard_map/context_third_group/ppermute | solution.py:461
  90.6 2.2 %project_late.1 = (bf16[256,1024]{1,0:T(8,128)(2,1)}, f32[4,1024]{1,0:T(4,128)S(1)}, f32[4,1024]{1,0:T(4,128)S(1)}) custom-call(s32[3]{0:T(128)S(1)} %copy-done.8, s32[8]{0:T(128)S(1)} %bitcast.52, bf16[256,2048]{1,0:T(8,128)(2,1)S(1)} %bitcast.39, f32[8,1024]{1,0:T(8,128)S(1)} %get-tuple-element.69.pool_ref, f32[272,1024]{1,0:T(8,128)S(1)} %project_early.1.early_ref, ...), custom_call_target="tpu_custom_call" | custom-call | flops 1 | bytes 1 | tf_op jit(solution)/shard_map/project_late/pallas_call | solution.py:440
  92.8 0.5 collective-permute-start.31
  93.4 3.2 %collective-permute-done.31 = f32[4,1024]{1,0:T(4,128)S(1)} collective-permute-done((f32[4,1024]{1,0:T(4,128)S(1)}, f32[4,1024]{1,0:T(4,128)S(1)}, u32[]{:S(2)}, u32[]{:S(2)}) %collective-permute-start.31) | collective-permute-done | bytes 16416 | tf_op jit(solution)/shard_map/embedding_half/ppermute | solution.py:461
  96.6 0.2 select_bitcast_fusion.5
  96.8 0.7 maximum_multiply_fusion
  (47 shorter events, 0.2 us)
Async XLA Ops:
  0.6 37.6 %collective-permute-start.6 = (bf16[256,2048]{1,0:T(8,128)(2,1)}, bf16[256,2048]{1,0:T(8,128)(2,1)S(1)}, u32[]{:S(2)}, u32[]{:S(2)}) collective-permute-start(bf16[256,2048]{1,0:T(8,128)(2,1)} %bitcast.34), channel_id=1, source_target_pairs={{0,2},{2,0},{4,6},{6,4},{1,3},{3,1},{5,7},{7,5},{8,10},{10,8},{12,... | collective-permute-start | bytes 3145736 | tf_op jit(solution)/shard_map/hidden_core/ppermute | solution.py:461
  1.1 37.1 %collective-permute-start.7 = (bf16[256,2048]{1,0:T(8,128)(2,1)}, bf16[256,2048]{1,0:T(8,128)(2,1)S(1)}, u32[]{:S(2)}, u32[]{:S(2)}) collective-permute-start(bf16[256,2048]{1,0:T(8,128)(2,1)} %bitcast.35), channel_id=1, source_target_pairs={{0,4},{2,6},{4,0},{6,2},{1,5},{3,7},{5,1},{7,3},{8,12},{10,14},{12... | collective-permute-start | bytes 3145736 | tf_op jit(solution)/shard_map/hidden_cross/ppermute | solution.py:461
  6.8 9.7 %collective-permute-start = (bf16[128,768]{1,0:T(8,128)(2,1)}, bf16[128,768]{1,0:T(8,128)(2,1)S(1)}, u32[]{:S(2)}, u32[]{:S(2)}) collective-permute-start(bf16[128,768]{1,0:T(8,128)(2,1)} %get-tuple-element.59), channel_id=1, source_target_pairs={{0,8},{8,16},{16,24},{24,0},{1,9},{9,17},{17,25},{25,1},{2,10},{10... | collective-permute-start | bytes 589832 | tf_op jit(solution)/shard_map/out/ppermute | solution.py:467
  8.4 12.0 %collective-permute-start.3 = (bf16[256,384]{1,0:T(8,128)(2,1)}, bf16[256,384]{1,0:T(8,128)(2,1)S(1)}, u32[]{:S(2)}, u32[]{:S(2)}) collective-permute-start(bf16[256,384]{1,0:T(8,128)(2,1)} %get-tuple-element.60.refs_8_), channel_id=1, source_target_pairs={{0,8},{8,16},{16,24},{24,0},{1,9},{9,17},{17,25},{25,1},{2,10},{10... | collective-permute-start | bytes 589832 | tf_op jit(solution)/shard_map/first/ppermute | solution.py:467
  16.6 13.5 %copy-start.11 = (bf16[128,768]{1,0:T(8,128)(2,1)}, bf16[128,768]{1,0:T(8,128)(2,1)S(1)}, u32[]{:S(2)}) copy-start(bf16[128,768]{1,0:T(8,128)(2,1)S(1)} %collective-permute-done.token_ref) | copy-start | bytes 589828
  16.6 8.1 %collective-permute-start.1 = (bf16[128,768]{1,0:T(8,128)(2,1)S(1)}, bf16[128,768]{1,0:T(8,128)(2,1)S(1)}, u32[]{:S(2)}, u32[]{:S(2)}) collective-permute-start(bf16[128,768]{1,0:T(8,128)(2,1)S(1)} %collective-permute-done.token_ref), channel_id=1, source_target_pairs={{0,8},{8,16},{16,24},{24,0},{1,9},{9,17},{17,25},{25,1},{2,10},{10... | collective-permute-start | bytes 589832 | tf_op jit(solution)/shard_map/out/ppermute | solution.py:467
  20.4 9.6 %collective-permute-start.4 = (bf16[256,384]{1,0:T(8,128)(2,1)S(1)}, bf16[256,384]{1,0:T(8,128)(2,1)S(1)}, u32[]{:S(2)}, u32[]{:S(2)}) collective-permute-start(bf16[256,384]{1,0:T(8,128)(2,1)S(1)} %collective-permute-done.3.refs_9_), channel_id=1, source_target_pairs={{0,8},{8,16},{16,24},{24,0},{1,9},{9,17},{17,25},{25,1},{2,10},{10... | collective-permute-start | bytes 589832 | tf_op jit(solution)/shard_map/first/ppermute | solution.py:467
  24.6 8.2 %copy-start.12 = (bf16[128,768]{1,0:T(8,128)(2,1)}, bf16[128,768]{1,0:T(8,128)(2,1)S(1)}, u32[]{:S(2)}) copy-start(bf16[128,768]{1,0:T(8,128)(2,1)S(1)} %collective-permute-done.1) | copy-start | bytes 589828
  24.6 9.3 %collective-permute-start.2 = (bf16[128,768]{1,0:T(8,128)(2,1)S(1)}, bf16[128,768]{1,0:T(8,128)(2,1)S(1)}, u32[]{:S(2)}, u32[]{:S(2)}) collective-permute-start(bf16[128,768]{1,0:T(8,128)(2,1)S(1)} %collective-permute-done.1), channel_id=1, source_target_pairs={{0,8},{8,16},{16,24},{24,0},{1,9},{9,17},{17,25},{25,1},{2,10},{10... | collective-permute-start | bytes 589832 | tf_op jit(solution)/shard_map/out/ppermute | solution.py:467
  30.1 7.5 %collective-permute-start.5 = (bf16[256,384]{1,0:T(8,128)(2,1)S(1)}, bf16[256,384]{1,0:T(8,128)(2,1)S(1)}, u32[]{:S(2)}, u32[]{:S(2)}) collective-permute-start(bf16[256,384]{1,0:T(8,128)(2,1)S(1)} %collective-permute-done.4.refs_10_), channel_id=1, source_target_pairs={{0,8},{8,16},{16,24},{24,0},{1,9},{9,17},{17,25},{25,1},{2,10},{10... | collective-permute-start | bytes 589832 | tf_op jit(solution)/shard_map/first/ppermute | solution.py:467
  33.9 4.3 %copy-start.13 = (bf16[128,768]{1,0:T(8,128)(2,1)}, bf16[128,768]{1,0:T(8,128)(2,1)S(1)}, u32[]{:S(2)}) copy-start(bf16[128,768]{1,0:T(8,128)(2,1)S(1)} %collective-permute-done.2) | copy-start | bytes 589828
  37.5 0.7 copy-start.6
  38.2 15.1 %collective-permute-start.8 = (bf16[256,2048]{1,0:T(8,128)(2,1)S(1)}, bf16[256,2048]{1,0:T(8,128)(2,1)S(1)}, u32[]{:S(2)}, u32[]{:S(2)}) collective-permute-start(bf16[256,2048]{1,0:T(8,128)(2,1)S(1)} %collective-permute-done.7.refs_3_), channel_id=1, source_target_pairs={{0,2},{2,0},{4,6},{6,4},{1,3},{3,1},{5,7},{7,5},{8,10},{10,8},{12,... | collective-permute-start | bytes 3145736 | tf_op jit(solution)/shard_map/hidden_far/ppermute | solution.py:461
  38.4 19.2 %copy-start = (bf16[1,256,2048]{2,1,0:T(8,128)(2,1)S(1)}, bf16[1,256,2048]{2,1,0:T(8,128)(2,1)}, u32[]{:S(2)}) copy-start(bf16[1,256,2048]{2,1,0:T(8,128)(2,1)} %param.6) | copy-start | bytes 3145732
  38.4 19.2 %copy-start.1 = (f32[1024,128]{1,0:T(8,128)S(1)}, f32[1024,128]{1,0:T(8,128)}, u32[]{:S(2)}) copy-start(f32[1024,128]{1,0:T(8,128)} %constant.62.clone.refs_5_) | copy-start | bytes 1572868
  38.4 19.1 %copy-start.2 = (f32[1024,128]{1,0:T(8,128)S(1)}, f32[1024,128]{1,0:T(8,128)}, u32[]{:S(2)}) copy-start(f32[1024,128]{1,0:T(8,128)} %constant.63.clone.refs_6_) | copy-start | bytes 1572868
  38.4 19.1 %copy-start.4 = (bf16[256,384]{1,0:T(8,128)(2,1)S(1)}, bf16[256,384]{1,0:T(8,128)(2,1)}, u32[]{:S(2)}) copy-start(bf16[256,384]{1,0:T(8,128)(2,1)} %get-tuple-element.60.refs_8_) | copy-start | bytes 589828
  38.4 19.1 %copy-start.7 = (bf16[256,384]{1,0:T(8,128)(2,1)S(1)}, bf16[256,384]{1,0:T(8,128)(2,1)}, u32[]{:S(2)}) copy-start(bf16[256,384]{1,0:T(8,128)(2,1)} %copy-done.6) | copy-start | bytes 589828
  38.4 19.1 %copy-start.8 = (s32[3]{0:T(128)S(1)}, s32[3]{0:T(128)}, u32[]{:S(2)}) copy-start(s32[3]{0:T(128)} %pad_add_fusion.where.refs_0_) | copy-start | bytes 40
  38.4 19.1 %copy-start.9 = (s32[1,32]{1,0:T(1,128)S(1)}, s32[1,32]{1,0:T(1,128)}, u32[]{:S(2)}) copy-start(s32[1,32]{1,0:T(1,128)} %refs_7_.5) | copy-start | bytes 388
  39.7 9.8 %collective-permute-start.9 = (bf16[256,384]{1,0:T(8,128)(2,1)}, bf16[256,384]{1,0:T(8,128)(2,1)S(1)}, u32[]{:S(2)}, u32[]{:S(2)}) collective-permute-start(bf16[256,384]{1,0:T(8,128)(2,1)} %get-tuple-element.66.refs_8_), channel_id=1, source_target_pairs={{0,8},{8,16},{16,24},{24,0},{1,9},{9,17},{17,25},{25,1},{2,10},{10... | collective-permute-start | bytes 589832 | tf_op jit(solution)/shard_map/second/ppermute | solution.py:467
  39.7 13.6 %collective-permute-start.10 = (bf16[256,384]{1,0:T(8,128)(2,1)}, bf16[256,384]{1,0:T(8,128)(2,1)S(1)}, u32[]{:S(2)}, u32[]{:S(2)}) collective-permute-start(bf16[256,384]{1,0:T(8,128)(2,1)} %get-tuple-element.67.refs_8_), channel_id=1, source_target_pairs={{0,8},{8,16},{16,24},{24,0},{1,9},{9,17},{17,25},{25,1},{2,10},{10... | collective-permute-start | bytes 589832 | tf_op jit(solution)/shard_map/third/ppermute | solution.py:467
  41.5 21.4 %collective-permute-start.13 = (bf16[2,128,768]{2,1,0:T(8,128)(2,1)S(1)}, bf16[2,128,768]{2,1,0:T(8,128)(2,1)S(1)}, u32[]{:S(2)}, u32[]{:S(2)}) collective-permute-start(bf16[2,128,768]{2,1,0:T(8,128)(2,1)S(1)} %pad_maximum_fusion.2), channel_id=1, source_target_pairs={{0,1},{1,0},{2,3},{3,2},{4,5},{5,4},{6,7},{7,6},{8,9},{9,8},{10,11... | collective-permute-start | bytes 1179656 | tf_op jit(solution)/shard_map/out_group/ppermute | solution.py:461
  43.2 23.7 %copy-start.5 = (bf16[256,384]{1,0:T(8,128)(2,1)S(1)}, bf16[256,384]{1,0:T(8,128)(2,1)}, u32[]{:S(2)}) copy-start(bf16[256,384]{1,0:T(8,128)(2,1)} %get-tuple-element.66.refs_8_) | copy-start | bytes 589828
  43.2 19.8 %collective-permute-start.14 = (bf16[2,128,768]{2,1,0:T(8,128)(2,1)S(1)}, bf16[2,128,768]{2,1,0:T(8,128)(2,1)S(1)}, u32[]{:S(2)}, u32[]{:S(2)}) collective-permute-start(bf16[2,128,768]{2,1,0:T(8,128)(2,1)S(1)} %pad_maximum_fusion.1), channel_id=1, source_target_pairs={{0,4},{2,6},{4,0},{6,2},{1,5},{3,7},{5,1},{7,3},{8,12},{10,14},{12... | collective-permute-start | bytes 1179656 | tf_op jit(solution)/shard_map/out_cross/ppermute | solution.py:461
  49.5 8.1 %collective-permute-start.19 = (bf16[256,384]{1,0:T(8,128)(2,1)S(1)}, bf16[256,384]{1,0:T(8,128)(2,1)S(1)}, u32[]{:S(2)}, u32[]{:S(2)}) collective-permute-start(bf16[256,384]{1,0:T(8,128)(2,1)S(1)} %collective-permute-done.9.refs_9_), channel_id=1, source_target_pairs={{0,8},{8,16},{16,24},{24,0},{1,9},{9,17},{17,25},{25,1},{2,10},{10... | collective-permute-start | bytes 589832 | tf_op jit(solution)/shard_map/second/ppermute | solution.py:467
  53.3 9.6 %collective-permute-start.11 = (bf16[256,384]{1,0:T(8,128)(2,1)S(1)}, bf16[256,384]{1,0:T(8,128)(2,1)S(1)}, u32[]{:S(2)}, u32[]{:S(2)}) collective-permute-start(bf16[256,384]{1,0:T(8,128)(2,1)S(1)} %collective-permute-done.10.refs_9_), channel_id=1, source_target_pairs={{0,8},{8,16},{16,24},{24,0},{1,9},{9,17},{17,25},{25,1},{2,10},{10... | collective-permute-start | bytes 589832 | tf_op jit(solution)/shard_map/third/ppermute | solution.py:467
  53.3 17.4 %collective-permute-start.15 = (bf16[2,128,768]{2,1,0:T(8,128)(2,1)S(1)}, bf16[2,128,768]{2,1,0:T(8,128)(2,1)S(1)}, u32[]{:S(2)}, u32[]{:S(2)}) collective-permute-start(bf16[2,128,768]{2,1,0:T(8,128)(2,1)S(1)} %pad_maximum_fusion.2), channel_id=1, source_target_pairs={{0,5},{1,4},{2,7},{3,6},{4,1},{5,0},{6,3},{7,2},{8,13},{9,12},{10,... | collective-permute-start | bytes 1179656 | tf_op jit(solution)/shard_map/out_across/ppermute | solution.py:491
  57.5 9.3 %collective-permute-start.20 = (bf16[256,384]{1,0:T(8,128)(2,1)S(1)}, bf16[256,384]{1,0:T(8,128)(2,1)S(1)}, u32[]{:S(2)}, u32[]{:S(2)}) collective-permute-start(bf16[256,384]{1,0:T(8,128)(2,1)S(1)} %collective-permute-done.19.refs_10_), channel_id=1, source_target_pairs={{0,8},{8,16},{16,24},{24,0},{1,9},{9,17},{17,25},{25,1},{2,10},{10... | collective-permute-start | bytes 589832 | tf_op jit(solution)/shard_map/second/ppermute | solution.py:467
  63.0 7.8 %collective-permute-start.12 = (bf16[256,384]{1,0:T(8,128)(2,1)S(1)}, bf16[256,384]{1,0:T(8,128)(2,1)S(1)}, u32[]{:S(2)}, u32[]{:S(2)}) collective-permute-start(bf16[256,384]{1,0:T(8,128)(2,1)S(1)} %collective-permute-done.11.refs_10_), channel_id=1, source_target_pairs={{0,8},{8,16},{16,24},{24,0},{1,9},{9,17},{17,25},{25,1},{2,10},{10... | collective-permute-start | bytes 589832 | tf_op jit(solution)/shard_map/third/ppermute | solution.py:467
  63.0 7.7 %collective-permute-start.16 = (bf16[144,128]{1,0:T(8,128)(2,1)S(1)}, bf16[144,128]{1,0:T(8,128)(2,1)S(1)}, u32[]{:S(2)}, u32[]{:S(2)}) collective-permute-start(bf16[144,128]{1,0:T(8,128)(2,1)S(1)} %get-tuple-element.74), channel_id=1, source_target_pairs={{0,2},{2,0},{4,6},{6,4},{1,3},{3,1},{5,7},{7,5},{8,10},{10,8},{12,... | collective-permute-start | bytes 110600 | tf_op jit(solution)/shard_map/context_first/ppermute | solution.py:461
  63.0 7.7 %collective-permute-start.17 = (bf16[144,128]{1,0:T(8,128)(2,1)S(1)}, bf16[144,128]{1,0:T(8,128)(2,1)S(1)}, u32[]{:S(2)}, u32[]{:S(2)}) collective-permute-start(bf16[144,128]{1,0:T(8,128)(2,1)S(1)} %get-tuple-element.75), channel_id=1, source_target_pairs={{0,4},{2,6},{4,0},{6,2},{1,5},{3,7},{5,1},{7,3},{8,12},{10,14},{12... | collective-permute-start | bytes 110600 | tf_op jit(solution)/shard_map/context_first/ppermute | solution.py:461
  66.8 3.9 %collective-permute-start.18 = (bf16[144,128]{1,0:T(8,128)(2,1)S(1)}, bf16[144,128]{1,0:T(8,128)(2,1)S(1)}, u32[]{:S(2)}, u32[]{:S(2)}) collective-permute-start(bf16[144,128]{1,0:T(8,128)(2,1)S(1)} %get-tuple-element.76), channel_id=1, source_target_pairs={{0,6},{2,4},{4,2},{6,0},{1,7},{3,5},{5,3},{7,1},{8,14},{10,12},{12... | collective-permute-start | bytes 110600 | tf_op jit(solution)/shard_map/context_first/ppermute | solution.py:461
  70.8 4.4 %copy-start.3 = (bf16[256,384]{1,0:T(8,128)(2,1)S(1)}, bf16[256,384]{1,0:T(8,128)(2,1)}, u32[]{:S(2)}) copy-start(bf16[256,384]{1,0:T(8,128)(2,1)} %get-tuple-element.67.refs_8_) | copy-start | bytes 589828
  71.0 8.1 %collective-permute-start.25 = (bf16[4,2,128,768]{3,2,1,0:T(8,128)(2,1)S(1)}, bf16[4,2,128,768]{3,2,1,0:T(8,128)(2,1)S(1)}, u32[]{:S(2)}, u32[]{:S(2)}) collective-permute-start(bf16[4,2,128,768]{3,2,1,0:T(8,128)(2,1)S(1)} %pad_maximum_fusion.refs_10_.refs_5_), channel_id=1, source_target_pairs={{0,2},{2,0},{4,6},{6,4},{1,3},{3,1},{5,7},{7,5},{8,10},{10,8},{12,... | collective-permute-start | bytes 4718600 | tf_op jit(solution)/shard_map/out_core/ppermute | solution.py:461
  71.4 7.6 %collective-permute-start.21 = (bf16[4,144,128]{2,1,0:T(8,128)(2,1)S(1)}, bf16[4,144,128]{2,1,0:T(8,128)(2,1)S(1)}, u32[]{:S(2)}, u32[]{:S(2)}) collective-permute-start(bf16[4,144,128]{2,1,0:T(8,128)(2,1)S(1)} %pad_maximum_fusion.3), channel_id=1, source_target_pairs={{0,1},{1,0},{2,3},{3,2},{4,5},{5,4},{6,7},{7,6},{8,9},{9,8},{10,11... | collective-permute-start | bytes 442376 | tf_op jit(solution)/shard_map/context_first_group/ppermute | solution.py:461
  73.3 5.7 %collective-permute-start.22 = (bf16[144,128]{1,0:T(8,128)(2,1)S(1)}, bf16[144,128]{1,0:T(8,128)(2,1)S(1)}, u32[]{:S(2)}, u32[]{:S(2)}) collective-permute-start(bf16[144,128]{1,0:T(8,128)(2,1)S(1)} %get-tuple-element.86), channel_id=1, source_target_pairs={{0,2},{2,0},{4,6},{6,4},{1,3},{3,1},{5,7},{7,5},{8,10},{10,8},{12,... | collective-permute-start | bytes 110600 | tf_op jit(solution)/shard_map/context_second/ppermute | solution.py:461
  73.3 5.7 %collective-permute-start.23 = (bf16[144,128]{1,0:T(8,128)(2,1)S(1)}, bf16[144,128]{1,0:T(8,128)(2,1)S(1)}, u32[]{:S(2)}, u32[]{:S(2)}) collective-permute-start(bf16[144,128]{1,0:T(8,128)(2,1)S(1)} %get-tuple-element.87), channel_id=1, source_target_pairs={{0,4},{2,6},{4,0},{6,2},{1,5},{3,7},{5,1},{7,3},{8,12},{10,14},{12... | collective-permute-start | bytes 110600 | tf_op jit(solution)/shard_map/context_second/ppermute | solution.py:461
  74.8 4.2 %collective-permute-start.24 = (bf16[144,128]{1,0:T(8,128)(2,1)S(1)}, bf16[144,128]{1,0:T(8,128)(2,1)S(1)}, u32[]{:S(2)}, u32[]{:S(2)}) collective-permute-start(bf16[144,128]{1,0:T(8,128)(2,1)S(1)} %get-tuple-element.88), channel_id=1, source_target_pairs={{0,6},{2,4},{4,2},{6,0},{1,7},{3,5},{5,3},{7,1},{8,14},{10,12},{12... | collective-permute-start | bytes 110600 | tf_op jit(solution)/shard_map/context_second/ppermute | solution.py:461
  79.0 2.5 %collective-permute-start.27 = (bf16[144,128]{1,0:T(8,128)(2,1)S(1)}, bf16[144,128]{1,0:T(8,128)(2,1)S(1)}, u32[]{:S(2)}, u32[]{:S(2)}) collective-permute-start(bf16[144,128]{1,0:T(8,128)(2,1)S(1)} %get-tuple-element.108), channel_id=1, source_target_pairs={{0,2},{2,0},{4,6},{6,4},{1,3},{3,1},{5,7},{7,5},{8,10},{10,8},{12,... | collective-permute-start | bytes 110600 | tf_op jit(solution)/shard_map/context_third/ppermute | solution.py:461
  79.4 4.0 %collective-permute-start.28 = (bf16[144,128]{1,0:T(8,128)(2,1)S(1)}, bf16[144,128]{1,0:T(8,128)(2,1)S(1)}, u32[]{:S(2)}, u32[]{:S(2)}) collective-permute-start(bf16[144,128]{1,0:T(8,128)(2,1)S(1)} %get-tuple-element.109), channel_id=1, source_target_pairs={{0,4},{2,6},{4,0},{6,2},{1,5},{3,7},{5,1},{7,3},{8,12},{10,14},{12... | collective-permute-start | bytes 110600 | tf_op jit(solution)/shard_map/context_third/ppermute | solution.py:461
  80.9 3.6 %collective-permute-start.29 = (bf16[144,128]{1,0:T(8,128)(2,1)S(1)}, bf16[144,128]{1,0:T(8,128)(2,1)S(1)}, u32[]{:S(2)}, u32[]{:S(2)}) collective-permute-start(bf16[144,128]{1,0:T(8,128)(2,1)S(1)} %get-tuple-element.110), channel_id=1, source_target_pairs={{0,6},{2,4},{4,2},{6,0},{1,7},{3,5},{5,3},{7,1},{8,14},{10,12},{12... | collective-permute-start | bytes 110600 | tf_op jit(solution)/shard_map/context_third/ppermute | solution.py:461
  81.0 6.4 %collective-permute-start.26 = (bf16[4,144,128]{2,1,0:T(8,128)(2,1)S(1)}, bf16[4,144,128]{2,1,0:T(8,128)(2,1)S(1)}, u32[]{:S(2)}, u32[]{:S(2)}) collective-permute-start(bf16[4,144,128]{2,1,0:T(8,128)(2,1)S(1)} %pad_maximum_fusion.4), channel_id=1, source_target_pairs={{0,1},{1,0},{2,3},{3,2},{4,5},{5,4},{6,7},{7,6},{8,9},{9,8},{10,11... | collective-permute-start | bytes 442376 | tf_op jit(solution)/shard_map/context_second_group/ppermute | solution.py:461
  84.5 6.1 %copy-start.10 = (s32[1,8,1]{1,2,0:T(1,128)S(1)}, s32[1,8,1]{1,2,0:T(1,128)}, u32[]{:S(2)}) copy-start(s32[1,8,1]{1,2,0:T(1,128)} %param.9) | copy-start | bytes 100
  84.6 6.1 %collective-permute-start.30 = (bf16[4,144,128]{2,1,0:T(8,128)(2,1)S(1)}, bf16[4,144,128]{2,1,0:T(8,128)(2,1)S(1)}, u32[]{:S(2)}, u32[]{:S(2)}) collective-permute-start(bf16[4,144,128]{2,1,0:T(8,128)(2,1)S(1)} %pad_maximum_fusion.5), channel_id=1, source_target_pairs={{0,1},{1,0},{2,3},{3,2},{4,5},{5,4},{6,7},{7,6},{8,9},{9,8},{10,11... | collective-permute-start | bytes 442376 | tf_op jit(solution)/shard_map/context_third_group/ppermute | solution.py:461
  92.8 3.7 %collective-permute-start.31 = (f32[4,1024]{1,0:T(4,128)S(1)}, f32[4,1024]{1,0:T(4,128)S(1)}, u32[]{:S(2)}, u32[]{:S(2)}) collective-permute-start(f32[4,1024]{1,0:T(4,128)S(1)} %get-tuple-element.115), channel_id=1, source_target_pairs={{0,1},{1,0},{2,3},{3,2},{4,5},{5,4},{6,7},{7,6},{8,9},{9,8},{10,11... | collective-permute-start | bytes 49160 | tf_op jit(solution)/shard_map/embedding_half/ppermute | solution.py:461

commit v7 on v6

--- a/solution.py
+++ b/solution.py
@@ -165,35 +165,48 @@
     return jnp.concatenate(parts, 1).astype(columns[0].dtype)
 
 
-def pieces_kernel(where, w_ref, o_ref, out_ref, first_ref):
+def out_kernel(where, o_ref, out_ref):
     out_ref[...] = o_ref[0]
-    first_ref[...] = folded([w_ref[j] for j in range(3)], False)
-
-
-def pieces(where, proj_weight):
+
+
+def out_piece(where, proj_weight):
     _, shard, width = proj_weight.shape
     quarter = shard // 4
     return pl.pallas_call(
-        pieces_kernel,
+        out_kernel,
+        grid_spec=pltpu.PrefetchScalarGridSpec(
+            num_scalar_prefetch=1,
+            grid=(1,),
+            in_specs=[pl.BlockSpec((1, quarter, width), lambda i, where: (3, where[0], 0))],
+            out_specs=pl.BlockSpec((quarter, width), lambda i, where: (0, 0)),
+        ),
+        out_shape=jax.ShapeDtypeStruct((quarter, width), proj_weight.dtype),
+        cost_estimate=SHORT,
+        name="out_piece",
+    )(where, proj_weight)
+
+
+def first_kernel(where, w_ref, token_ref, first_ref):
+    first_ref[...] = folded([w_ref[j] for j in range(3)], False)
+
+
+def first_piece(where, proj_weight, token):
+    shard = proj_weight.shape[1]
+    return pl.pallas_call(
+        first_kernel,
         grid_spec=pltpu.PrefetchScalarGridSpec(
             num_scalar_prefetch=1,
             grid=(1,),
             in_specs=[
                 pl.BlockSpec((3, shard, 128), lambda i, where: (0, 0, where[0])),
-                pl.BlockSpec((1, quarter, width), lambda i, where: (3, where[0], 0)),
+                pl.BlockSpec(memory_space=pl.ANY),
             ],
-            out_specs=[
-                pl.BlockSpec((quarter, width), lambda i, where: (0, 0)),
-                pl.BlockSpec((shard // 2, 384), lambda i, where: (0, 0)),
-            ],
+            out_specs=pl.BlockSpec((shard // 2, 384), lambda i, where: (0, 0)),
         ),
-        out_shape=[
-            jax.ShapeDtypeStruct((quarter, width), proj_weight.dtype),
-            jax.ShapeDtypeStruct((shard // 2, 384), proj_weight.dtype),
-        ],
+        out_shape=jax.ShapeDtypeStruct((shard // 2, 384), proj_weight.dtype),
         cost_estimate=SHORT,
-        name="pieces",
-    )(where, proj_weight, proj_weight)
+        name="first_piece",
+    )(where, proj_weight, token)
 
 
 def others_kernel(where, w_ref, x_ref, token_ref, second_ref, third_ref):
@@ -499,7 +512,8 @@
 
     h_cross = xor_send("hidden_cross", h, "seq", 2)
     h_core = xor_send("hidden_core", h, "seq", 1)
-    o0, x0 = pieces(where, proj_weight)
+    o0 = out_piece(where, proj_weight)
+    x0 = first_piece(where, proj_weight, o0)
 
     def rings(names, starts, **before):
         held = [[start] for start in starts]

time: 97.7 us -> 97.3 us (level)
  waiting for transfers between devices: 51.1 us -> 48 us
  Pallas kernels: 21.5 us -> 23.7 us
    ppermute x12, waiting for transfers between devices: 41.5 us -> 38.5 us  [ring_send(): lax.ppermute(value, 'dp', [(i, (i + 1) % count) for i in range(count)])]
    pallas_call x1 -> x2, Pallas kernels: 2.53 us -> 4.74 us  [the longest x1 2.46 us: first_piece(): pl.pallas_call(first_kernel, grid_spec=pltpu.PrefetchScalarGridSpec(num_s...]
  transfers between devices with their start and end apart: 32 -> 32, of which waited for: 16 -> 16; matrix products, arithmetic and copies ran while one was open for 3% -> 3% of each run, Pallas kernels for 20% -> 22%
where the time goes in v7:
time: 97.3 us; the launch traced here: 97 us
  waiting for transfers between devices  48 us (49%)
  Pallas kernels  23.7 us (24%)
  starting transfers between devices  19.4 us (20%)
  other arithmetic  4.05 us (4%)
  between operations  1.04 us (1%)
    ppermute x12, waiting for transfers between devices, ring_send(): lax.ppermute(value, 'dp', [(i, (i + 1) % count) for i in range(count)])  38.5 us
    ppermute x19, starting transfers between devices, xor_send(): lax.ppermute(value, axis, [(i, i ^ j) for i in range(lax.axis_size(axis))])  13.6 us
    pallas_call x3, Pallas kernels, attend(): pl.pallas_call(functools.partial(attend_kernel, pools), out_shape=out_sha...  11.9 us
    ppermute x19, waiting for transfers between devices, xor_send(): lax.ppermute(value, axis, [(i, i ^ j) for i in range(lax.axis_size(axis))])  9.59 us
    ppermute x12, starting transfers between devices, ring_send(): lax.ppermute(value, 'dp', [(i, (i + 1) % count) for i in range(count)])  4.31 us
    pallas_call x1, Pallas kernels, other_pieces(): pl.pallas_call(others_kernel, grid_spec=pltpu.PrefetchScalarGridSpec(num_...  2.72 us
    pallas_call x1, Pallas kernels, first_piece(): pl.pallas_call(first_kernel, grid_spec=pltpu.PrefetchScalarGridSpec(num_s...  2.46 us
    another operation x3, other arithmetic, across(): send = jnp.stack([jnp.where(mine, two, one) for mine, one, two in pairs])  2.29 us
  transfers between devices with their start and end apart: 32, of which 16 were waited for; matrix products, arithmetic and copies ran while one was open for 3% of the time, Pallas kernels for 22%

profile of v7, /device:TPU:0, one launch (start us, length us, event | category | flops | bytes accessed | tf_op | source)
XLA Modules:
  0.0 97.0 jit_solution(2040126219697458319)
XLA Ops:
  0.6 0.5 collective-permute-start.6
  1.1 2.6 %collective-permute-start.7 = (bf16[256,2048]{1,0:T(8,128)(2,1)}, bf16[256,2048]{1,0:T(8,128)(2,1)S(1)}, u32[]{:S(2)}, u32[]{:S(2)}) collective-permute-start(bf16[256,2048]{1,0:T(8,128)(2,1)} %bitcast.35), channel_id=1, source_target_pairs={{0,4},{2,6},{4,0},{6,2},{1,5},{3,7},{5,1},{7,3},{8,12},{10,14},{12... | collective-permute-start | bytes 3145736 | tf_op jit(solution)/shard_map/hidden_cross/ppermute | solution.py:474
  3.7 0.6 pad_add_fusion.where.refs_0_
  4.3 2.3 %out_piece.1.token_ref = bf16[128,768]{1,0:T(8,128)(2,1)} custom-call(s32[3]{0:T(128)} %pad_add_fusion.where.refs_0_, bf16[4,512,768]{2,1,0:T(8,128)(2,1)} %x_ref.1), custom_call_target="tpu_custom_call" | custom-call | flops 1 | bytes 1 | tf_op jit(solution)/shard_map/out_piece/pallas_call | solution.py:175
  6.6 1.6 %collective-permute-start = (bf16[128,768]{1,0:T(8,128)(2,1)}, bf16[128,768]{1,0:T(8,128)(2,1)S(1)}, u32[]{:S(2)}, u32[]{:S(2)}) collective-permute-start(bf16[128,768]{1,0:T(8,128)(2,1)} %out_piece.1.token_ref), channel_id=1, source_target_pairs={{0,8},{8,16},{16,24},{24,0},{1,9},{9,17},{17,25},{25,1},{2,10},{10... | collective-permute-start | bytes 589832 | tf_op jit(solution)/shard_map/out/ppermute | solution.py:480
  8.2 2.5 %first_piece.1.refs_8_ = bf16[256,384]{1,0:T(8,128)(2,1)} custom-call(s32[3]{0:T(128)} %pad_add_fusion.where.refs_0_, bf16[4,512,768]{2,1,0:T(8,128)(2,1)} %x_ref.1, bf16[128,768]{1,0:T(8,128)(2,1)} %out_piece.1.token_ref), custom_call_target="tpu_custom_call" | custom-call | flops 1 | bytes 1 | tf_op jit(solution)/shard_map/first_piece/pallas_call | solution.py:195
  10.6 1.6 %collective-permute-start.3 = (bf16[256,384]{1,0:T(8,128)(2,1)}, bf16[256,384]{1,0:T(8,128)(2,1)S(1)}, u32[]{:S(2)}, u32[]{:S(2)}) collective-permute-start(bf16[256,384]{1,0:T(8,128)(2,1)} %first_piece.1.refs_8_), channel_id=1, source_target_pairs={{0,8},{8,16},{16,24},{24,0},{1,9},{9,17},{17,25},{25,1},{2,10},{10... | collective-permute-start | bytes 589832 | tf_op jit(solution)/shard_map/first/ppermute | solution.py:480
  12.2 3.9 %collective-permute-done.token_ref = bf16[128,768]{1,0:T(8,128)(2,1)S(1)} collective-permute-done((bf16[128,768]{1,0:T(8,128)(2,1)}, bf16[128,768]{1,0:T(8,128)(2,1)S(1)}, u32[]{:S(2)}, u32[]{:S(2)}) %collective-permute-start) | collective-permute-done | bytes 196640 | tf_op jit(solution)/shard_map/out/ppermute | solution.py:480
  16.1 0.0 collective-permute-start.1
  16.1 4.1 %collective-permute-done.3.refs_9_ = bf16[256,384]{1,0:T(8,128)(2,1)S(1)} collective-permute-done((bf16[256,384]{1,0:T(8,128)(2,1)}, bf16[256,384]{1,0:T(8,128)(2,1)S(1)}, u32[]{:S(2)}, u32[]{:S(2)}) %collective-permute-start.3) | collective-permute-done | bytes 196640 | tf_op jit(solution)/shard_map/first/ppermute | solution.py:480
  20.2 0.0 collective-permute-start.4
  20.2 4.1 %collective-permute-done.1 = bf16[128,768]{1,0:T(8,128)(2,1)S(1)} collective-permute-done((bf16[128,768]{1,0:T(8,128)(2,1)S(1)}, bf16[128,768]{1,0:T(8,128)(2,1)S(1)}, u32[]{:S(2)}, u32[]{:S(2)}) %collective-permute-start.1) | collective-permute-done | bytes 196640 | tf_op jit(solution)/shard_map/out/ppermute | solution.py:480
  24.3 0.1 collective-permute-start.2
  24.4 5.2 %collective-permute-done.4.refs_10_ = bf16[256,384]{1,0:T(8,128)(2,1)S(1)} collective-permute-done((bf16[256,384]{1,0:T(8,128)(2,1)S(1)}, bf16[256,384]{1,0:T(8,128)(2,1)S(1)}, u32[]{:S(2)}, u32[]{:S(2)}) %collective-permute-start.4) | collective-permute-done | bytes 196640 | tf_op jit(solution)/shard_map/first/ppermute | solution.py:480
  29.6 2.7 %other_pieces.1 = (bf16[256,384]{1,0:T(8,128)(2,1)}, bf16[256,384]{1,0:T(8,128)(2,1)}) custom-call(s32[3]{0:T(128)} %pad_add_fusion.where.refs_0_, bf16[4,512,768]{2,1,0:T(8,128)(2,1)} %x_ref.1, bf16[4,512,768]{2,1,0:T(8,128)(2,1)} %x_ref.1, bf16[128,768]{1,0:T(8,128)(2,1)} %copy-done.11), custom_call_target="tpu_custom_call" | custom-call | flops 1 | bytes 1 | tf_op jit(solution)/shard_map/other_pieces/pallas_call | solution.py:219
  32.3 1.4 %collective-permute-done.2 = bf16[128,768]{1,0:T(8,128)(2,1)S(1)} collective-permute-done((bf16[128,768]{1,0:T(8,128)(2,1)S(1)}, bf16[128,768]{1,0:T(8,128)(2,1)S(1)}, u32[]{:S(2)}, u32[]{:S(2)}) %collective-permute-start.2) | collective-permute-done | bytes 196640 | tf_op jit(solution)/shard_map/out/ppermute | solution.py:480
  33.7 3.4 %collective-permute-done.5.refs_11_ = bf16[256,384]{1,0:T(8,128)(2,1)S(1)} collective-permute-done((bf16[256,384]{1,0:T(8,128)(2,1)S(1)}, bf16[256,384]{1,0:T(8,128)(2,1)S(1)}, u32[]{:S(2)}, u32[]{:S(2)}) %collective-permute-start.5) | collective-permute-done | bytes 196640 | tf_op jit(solution)/shard_map/first/ppermute | solution.py:480
  37.1 0.7 copy-done.6
  37.8 0.0 collective-permute-done.6.refs_2_
  37.8 0.0 collective-permute-done.7.refs_3_
  37.8 0.1 collective-permute-start.8
  37.9 0.0 copy-start
  37.9 0.0 copy-start.1
  37.9 0.0 copy-start.2
  38.0 0.0 copy-start.9
  38.0 1.2 %select_bitcast_fusion.1 = (bf16[1,128,768]{2,1,0:T(8,128)(2,1)S(1)}, bf16[1,128,768]{2,1,0:T(8,128)(2,1)S(1)}) fusion(bf16[128,768]{1,0:T(8,128)(2,1)} %copy-done.12, bf16[128,768]{1,0:T(8,128)(2,1)} %out_piece.1.token_ref, pred[]{:T(512)S(6)} %eq.13), kind=kLoop, calls=%fused_computation.4 | loop fusion | flops 196608 | bytes 786433 | tf_op jit(solution)/shard_map/stack | solution.py:502
  39.2 0.1 collective-permute-start.9
  39.3 0.9 collective-permute-start.10
  40.2 1.1 %select_bitcast_fusion = (bf16[1,128,768]{2,1,0:T(8,128)(2,1)S(1)}, bf16[1,128,768]{2,1,0:T(8,128)(2,1)S(1)}) fusion(bf16[128,768]{1,0:T(8,128)(2,1)} %copy-done.13, bf16[128,768]{1,0:T(8,128)(2,1)} %copy-done.11, pred[]{:T(512)S(6)} %eq.14), kind=kLoop, calls=%fused_computation.3 | loop fusion | flops 196608 | bytes 786433 | tf_op jit(solution)/shard_map/stack | solution.py:502
  41.3 1.6 %collective-permute-start.13 = (bf16[2,128,768]{2,1,0:T(8,128)(2,1)S(1)}, bf16[2,128,768]{2,1,0:T(8,128)(2,1)S(1)}, u32[]{:S(2)}, u32[]{:S(2)}) collective-permute-start(bf16[2,128,768]{2,1,0:T(8,128)(2,1)S(1)} %pad_maximum_fusion.2), channel_id=1, source_target_pairs={{0,1},{1,0},{2,3},{3,2},{4,5},{5,4},{6,7},{7,6},{8,9},{9,8},{10,11... | collective-permute-start | bytes 1179656 | tf_op jit(solution)/shard_map/out_group/ppermute | solution.py:474
  42.9 0.6 collective-permute-start.14
  43.5 5.5 %collective-permute-done.9.refs_9_ = bf16[256,384]{1,0:T(8,128)(2,1)S(1)} collective-permute-done((bf16[256,384]{1,0:T(8,128)(2,1)}, bf16[256,384]{1,0:T(8,128)(2,1)S(1)}, u32[]{:S(2)}, u32[]{:S(2)}) %collective-permute-start.9) | collective-permute-done | bytes 196640 | tf_op jit(solution)/shard_map/second/ppermute | solution.py:480
  49.0 0.0 collective-permute-start.19
  49.0 3.9 %collective-permute-done.10.refs_9_ = bf16[256,384]{1,0:T(8,128)(2,1)S(1)} collective-permute-done((bf16[256,384]{1,0:T(8,128)(2,1)}, bf16[256,384]{1,0:T(8,128)(2,1)S(1)}, u32[]{:S(2)}, u32[]{:S(2)}) %collective-permute-start.10) | collective-permute-done | bytes 196640 | tf_op jit(solution)/shard_map/third/ppermute | solution.py:480
  52.9 1.5 %collective-permute-start.15 = (bf16[2,128,768]{2,1,0:T(8,128)(2,1)S(1)}, bf16[2,128,768]{2,1,0:T(8,128)(2,1)S(1)}, u32[]{:S(2)}, u32[]{:S(2)}) collective-permute-start(bf16[2,128,768]{2,1,0:T(8,128)(2,1)S(1)} %pad_maximum_fusion.2), channel_id=1, source_target_pairs={{0,5},{1,4},{2,7},{3,6},{4,1},{5,0},{6,3},{7,2},{8,13},{9,12},{10,... | collective-permute-start | bytes 1179656 | tf_op jit(solution)/shard_map/out_across/ppermute | solution.py:504
  54.4 2.7 %collective-permute-done.19.refs_10_ = bf16[256,384]{1,0:T(8,128)(2,1)S(1)} collective-permute-done((bf16[256,384]{1,0:T(8,128)(2,1)S(1)}, bf16[256,384]{1,0:T(8,128)(2,1)S(1)}, u32[]{:S(2)}, u32[]{:S(2)}) %collective-permute-start.19) | collective-permute-done | bytes 196640 | tf_op jit(solution)/shard_map/second/ppermute | solution.py:480
  57.1 4.2 %attend_and_pool.1 = (bf16[144,128]{1,0:T(8,128)(2,1)S(1)}, bf16[144,128]{1,0:T(8,128)(2,1)S(1)}, bf16[144,128]{1,0:T(8,128)(2,1)S(1)}, bf16[144,128]{1,0:T(8,128)(2,1)S(1)}, f32[8,1024]{1,0:T(8,128)S(1)}) custom-call(s32[3]{0:T(128)S(1)} %copy-done.8, bf16[256,2048]{1,0:T(8,128)(2,1)S(1)} %bitcast.36, bf16[256,2048]{1,0:T(8,128)(2,1)S(1)} %collective-permute-done.6.refs_2_, ...), custom_call_target="tpu_custom_call" | custom-call | flops 1 | bytes 1 | tf_op jit(solution)/shard_map/attend_and_pool/pallas_call | solution.py:341
  61.3 1.2 %collective-permute-done.11.refs_10_ = bf16[256,384]{1,0:T(8,128)(2,1)S(1)} collective-permute-done((bf16[256,384]{1,0:T(8,128)(2,1)S(1)}, bf16[256,384]{1,0:T(8,128)(2,1)S(1)}, u32[]{:S(2)}, u32[]{:S(2)}) %collective-permute-start.11) | collective-permute-done | bytes 196640 | tf_op jit(solution)/shard_map/third/ppermute | solution.py:480
  62.5 0.0 collective-permute-start.12
  62.5 0.6 collective-permute-start.17
  63.1 3.3 %collective-permute-done.20.refs_11_ = bf16[256,384]{1,0:T(8,128)(2,1)S(1)} collective-permute-done((bf16[256,384]{1,0:T(8,128)(2,1)S(1)}, bf16[256,384]{1,0:T(8,128)(2,1)S(1)}, u32[]{:S(2)}, u32[]{:S(2)}) %collective-permute-start.20) | collective-permute-done | bytes 196640 | tf_op jit(solution)/shard_map/second/ppermute | solution.py:480
  66.4 3.9 %attend.2 = (bf16[144,128]{1,0:T(8,128)(2,1)S(1)}, bf16[144,128]{1,0:T(8,128)(2,1)S(1)}, bf16[144,128]{1,0:T(8,128)(2,1)S(1)}, bf16[144,128]{1,0:T(8,128)(2,1)S(1)}) custom-call(s32[3]{0:T(128)S(1)} %copy-done.8, bf16[256,2048]{1,0:T(8,128)(2,1)S(1)} %bitcast.37, bf16[256,2048]{1,0:T(8,128)(2,1)S(1)} %collective-permute-done.6.refs_2_, ...), custom_call_target="tpu_custom_call" | custom-call | flops 1 | bytes 1 | tf_op jit(solution)/shard_map/attend/pallas_call | solution.py:341
  70.3 0.2 pad_maximum_fusion.refs_10_.refs_5_
  70.5 0.7 collective-permute-start.25
  71.2 1.6 %collective-permute-start.21 = (bf16[4,144,128]{2,1,0:T(8,128)(2,1)S(1)}, bf16[4,144,128]{2,1,0:T(8,128)(2,1)S(1)}, u32[]{:S(2)}, u32[]{:S(2)}) collective-permute-start(bf16[4,144,128]{2,1,0:T(8,128)(2,1)S(1)} %pad_maximum_fusion.3), channel_id=1, source_target_pairs={{0,1},{1,0},{2,3},{3,2},{4,5},{5,4},{6,7},{7,6},{8,9},{9,8},{10,11... | collective-permute-start | bytes 442376 | tf_op jit(solution)/shard_map/context_first_group/ppermute | solution.py:474
  72.8 1.5 %collective-permute-start.23 = (bf16[144,128]{1,0:T(8,128)(2,1)S(1)}, bf16[144,128]{1,0:T(8,128)(2,1)S(1)}, u32[]{:S(2)}, u32[]{:S(2)}) collective-permute-start(bf16[144,128]{1,0:T(8,128)(2,1)S(1)} %get-tuple-element.83), channel_id=1, source_target_pairs={{0,4},{2,6},{4,0},{6,2},{1,5},{3,7},{5,1},{7,3},{8,12},{10,14},{12... | collective-permute-start | bytes 110600 | tf_op jit(solution)/shard_map/context_second/ppermute | solution.py:474
  74.3 0.4 collective-permute-start.24
  74.7 3.8 %attend.3 = (bf16[144,128]{1,0:T(8,128)(2,1)S(1)}, bf16[144,128]{1,0:T(8,128)(2,1)S(1)}, bf16[144,128]{1,0:T(8,128)(2,1)S(1)}, bf16[144,128]{1,0:T(8,128)(2,1)S(1)}) custom-call(s32[3]{0:T(128)S(1)} %copy-done.8, bf16[256,2048]{1,0:T(8,128)(2,1)S(1)} %bitcast.38, bf16[256,2048]{1,0:T(8,128)(2,1)S(1)} %collective-permute-done.6.refs_2_, ...), custom_call_target="tpu_custom_call" | custom-call | flops 1 | bytes 1 | tf_op jit(solution)/shard_map/attend/pallas_call | solution.py:341
  78.6 0.3 collective-permute-start.27
  78.9 1.5 %collective-permute-start.28 = (bf16[144,128]{1,0:T(8,128)(2,1)S(1)}, bf16[144,128]{1,0:T(8,128)(2,1)S(1)}, u32[]{:S(2)}, u32[]{:S(2)}) collective-permute-start(bf16[144,128]{1,0:T(8,128)(2,1)S(1)} %get-tuple-element.105), channel_id=1, source_target_pairs={{0,4},{2,6},{4,0},{6,2},{1,5},{3,7},{5,1},{7,3},{8,12},{10,14},{12... | collective-permute-start | bytes 110600 | tf_op jit(solution)/shard_map/context_third/ppermute | solution.py:474
  80.4 0.1 collective-permute-start.29
  80.6 0.5 collective-permute-start.26
  81.1 1.8 %collective-permute-done.28.refs_2_ = bf16[144,128]{1,0:T(8,128)(2,1)S(1)} collective-permute-done((bf16[144,128]{1,0:T(8,128)(2,1)S(1)}, bf16[144,128]{1,0:T(8,128)(2,1)S(1)}, u32[]{:S(2)}, u32[]{:S(2)}) %collective-permute-start.28) | collective-permute-done | bytes 36896 | tf_op jit(solution)/shard_map/context_third/ppermute | solution.py:474
  82.9 1.2 %collective-permute-done.29.refs_3_ = bf16[144,128]{1,0:T(8,128)(2,1)S(1)} collective-permute-done((bf16[144,128]{1,0:T(8,128)(2,1)S(1)}, bf16[144,128]{1,0:T(8,128)(2,1)S(1)}, u32[]{:S(2)}, u32[]{:S(2)}) %collective-permute-start.29) | collective-permute-done | bytes 36896 | tf_op jit(solution)/shard_map/context_third/ppermute | solution.py:474
  84.1 0.0 copy-start.10
  84.1 0.6 collective-permute-start.30
  84.7 2.2 %collective-permute-done.26.refs_9_ = bf16[4,144,128]{2,1,0:T(8,128)(2,1)S(1)} collective-permute-done((bf16[4,144,128]{2,1,0:T(8,128)(2,1)S(1)}, bf16[4,144,128]{2,1,0:T(8,128)(2,1)S(1)}, u32[]{:S(2)}, u32[]{:S(2)}) %collective-permute-start.26) | collective-permute-done | bytes 147488 | tf_op jit(solution)/shard_map/context_second_group/ppermute | solution.py:474
  86.9 2.1 %project_early.1.early_ref = f32[272,1024]{1,0:T(8,128)S(1)} custom-call(s32[3]{0:T(128)S(1)} %copy-done.8, bf16[144,128]{1,0:T(8,128)(2,1)S(1)} %get-tuple-element.94.refs_0_, bf16[144,128]{1,0:T(8,128)(2,1)S(1)} %collective-permute-done.16.refs_1_, bf16[144,128]{1,0:T(8,128)(2,1)S(1)} %collective-permute-done.17.refs_2_, ...), custom_call_target="tpu_custom_call" | custom-call | flops 1 | bytes 1 | tf_op jit(solution)/shard_map/project_early/pallas_call | solution.py:397
  89.1 1.1 %collective-permute-done.30.refs_4_ = bf16[4,144,128]{2,1,0:T(8,128)(2,1)S(1)} collective-permute-done((bf16[4,144,128]{2,1,0:T(8,128)(2,1)S(1)}, bf16[4,144,128]{2,1,0:T(8,128)(2,1)S(1)}, u32[]{:S(2)}, u32[]{:S(2)}) %collective-permute-start.30) | collective-permute-done | bytes 147488 | tf_op jit(solution)/shard_map/context_third_group/ppermute | solution.py:474
  90.2 2.2 %project_late.1 = (bf16[256,1024]{1,0:T(8,128)(2,1)}, f32[4,1024]{1,0:T(4,128)S(1)}, f32[4,1024]{1,0:T(4,128)S(1)}) custom-call(s32[3]{0:T(128)S(1)} %copy-done.8, s32[8]{0:T(128)S(1)} %bitcast.52, bf16[256,2048]{1,0:T(8,128)(2,1)S(1)} %bitcast.39, f32[8,1024]{1,0:T(8,128)S(1)} %get-tuple-element.65.pool_ref, f32[272,1024]{1,0:T(8,128)S(1)} %project_early.1.early_ref, ...), custom_call_target="tpu_custom_call" | custom-call | flops 1 | bytes 1 | tf_op jit(solution)/shard_map/project_late/pallas_call | solution.py:453
  92.4 0.5 collective-permute-start.31
  92.9 3.2 %collective-permute-done.31 = f32[4,1024]{1,0:T(4,128)S(1)} collective-permute-done((f32[4,1024]{1,0:T(4,128)S(1)}, f32[4,1024]{1,0:T(4,128)S(1)}, u32[]{:S(2)}, u32[]{:S(2)}) %collective-permute-start.31) | collective-permute-done | bytes 16416 | tf_op jit(solution)/shard_map/embedding_half/ppermute | solution.py:474
  96.1 0.2 select_bitcast_fusion.5
  96.3 0.7 maximum_multiply_fusion
  (48 shorter events, 0.2 us)
Async XLA Ops:
  0.6 37.1 %collective-permute-start.6 = (bf16[256,2048]{1,0:T(8,128)(2,1)}, bf16[256,2048]{1,0:T(8,128)(2,1)S(1)}, u32[]{:S(2)}, u32[]{:S(2)}) collective-permute-start(bf16[256,2048]{1,0:T(8,128)(2,1)} %bitcast.34), channel_id=1, source_target_pairs={{0,2},{2,0},{4,6},{6,4},{1,3},{3,1},{5,7},{7,5},{8,10},{10,8},{12,... | collective-permute-start | bytes 3145736 | tf_op jit(solution)/shard_map/hidden_core/ppermute | solution.py:474
  1.1 36.6 %collective-permute-start.7 = (bf16[256,2048]{1,0:T(8,128)(2,1)}, bf16[256,2048]{1,0:T(8,128)(2,1)S(1)}, u32[]{:S(2)}, u32[]{:S(2)}) collective-permute-start(bf16[256,2048]{1,0:T(8,128)(2,1)} %bitcast.35), channel_id=1, source_target_pairs={{0,4},{2,6},{4,0},{6,2},{1,5},{3,7},{5,1},{7,3},{8,12},{10,14},{12... | collective-permute-start | bytes 3145736 | tf_op jit(solution)/shard_map/hidden_cross/ppermute | solution.py:474
  6.6 9.5 %collective-permute-start = (bf16[128,768]{1,0:T(8,128)(2,1)}, bf16[128,768]{1,0:T(8,128)(2,1)S(1)}, u32[]{:S(2)}, u32[]{:S(2)}) collective-permute-start(bf16[128,768]{1,0:T(8,128)(2,1)} %out_piece.1.token_ref), channel_id=1, source_target_pairs={{0,8},{8,16},{16,24},{24,0},{1,9},{9,17},{17,25},{25,1},{2,10},{10... | collective-permute-start | bytes 589832 | tf_op jit(solution)/shard_map/out/ppermute | solution.py:480
  10.6 9.6 %collective-permute-start.3 = (bf16[256,384]{1,0:T(8,128)(2,1)}, bf16[256,384]{1,0:T(8,128)(2,1)S(1)}, u32[]{:S(2)}, u32[]{:S(2)}) collective-permute-start(bf16[256,384]{1,0:T(8,128)(2,1)} %first_piece.1.refs_8_), channel_id=1, source_target_pairs={{0,8},{8,16},{16,24},{24,0},{1,9},{9,17},{17,25},{25,1},{2,10},{10... | collective-permute-start | bytes 589832 | tf_op jit(solution)/shard_map/first/ppermute | solution.py:480
  16.1 13.5 %copy-start.11 = (bf16[128,768]{1,0:T(8,128)(2,1)}, bf16[128,768]{1,0:T(8,128)(2,1)S(1)}, u32[]{:S(2)}) copy-start(bf16[128,768]{1,0:T(8,128)(2,1)S(1)} %collective-permute-done.token_ref) | copy-start | bytes 589828
  16.1 8.2 %collective-permute-start.1 = (bf16[128,768]{1,0:T(8,128)(2,1)S(1)}, bf16[128,768]{1,0:T(8,128)(2,1)S(1)}, u32[]{:S(2)}, u32[]{:S(2)}) collective-permute-start(bf16[128,768]{1,0:T(8,128)(2,1)S(1)} %collective-permute-done.token_ref), channel_id=1, source_target_pairs={{0,8},{8,16},{16,24},{24,0},{1,9},{9,17},{17,25},{25,1},{2,10},{10... | collective-permute-start | bytes 589832 | tf_op jit(solution)/shard_map/out/ppermute | solution.py:480
  20.2 9.4 %collective-permute-start.4 = (bf16[256,384]{1,0:T(8,128)(2,1)S(1)}, bf16[256,384]{1,0:T(8,128)(2,1)S(1)}, u32[]{:S(2)}, u32[]{:S(2)}) collective-permute-start(bf16[256,384]{1,0:T(8,128)(2,1)S(1)} %collective-permute-done.3.refs_9_), channel_id=1, source_target_pairs={{0,8},{8,16},{16,24},{24,0},{1,9},{9,17},{17,25},{25,1},{2,10},{10... | collective-permute-start | bytes 589832 | tf_op jit(solution)/shard_map/first/ppermute | solution.py:480
  24.3 8.1 %copy-start.12 = (bf16[128,768]{1,0:T(8,128)(2,1)}, bf16[128,768]{1,0:T(8,128)(2,1)S(1)}, u32[]{:S(2)}) copy-start(bf16[128,768]{1,0:T(8,128)(2,1)S(1)} %collective-permute-done.1) | copy-start | bytes 589828
  24.3 9.4 %collective-permute-start.2 = (bf16[128,768]{1,0:T(8,128)(2,1)S(1)}, bf16[128,768]{1,0:T(8,128)(2,1)S(1)}, u32[]{:S(2)}, u32[]{:S(2)}) collective-permute-start(bf16[128,768]{1,0:T(8,128)(2,1)S(1)} %collective-permute-done.1), channel_id=1, source_target_pairs={{0,8},{8,16},{16,24},{24,0},{1,9},{9,17},{17,25},{25,1},{2,10},{10... | collective-permute-start | bytes 589832 | tf_op jit(solution)/shard_map/out/ppermute | solution.py:480
  29.6 7.5 %collective-permute-start.5 = (bf16[256,384]{1,0:T(8,128)(2,1)S(1)}, bf16[256,384]{1,0:T(8,128)(2,1)S(1)}, u32[]{:S(2)}, u32[]{:S(2)}) collective-permute-start(bf16[256,384]{1,0:T(8,128)(2,1)S(1)} %collective-permute-done.4.refs_10_), channel_id=1, source_target_pairs={{0,8},{8,16},{16,24},{24,0},{1,9},{9,17},{17,25},{25,1},{2,10},{10... | collective-permute-start | bytes 589832 | tf_op jit(solution)/shard_map/first/ppermute | solution.py:480
  33.7 4.1 %copy-start.13 = (bf16[128,768]{1,0:T(8,128)(2,1)}, bf16[128,768]{1,0:T(8,128)(2,1)S(1)}, u32[]{:S(2)}) copy-start(bf16[128,768]{1,0:T(8,128)(2,1)S(1)} %collective-permute-done.2) | copy-start | bytes 589828
  37.1 0.7 copy-start.6
  37.8 15.1 %collective-permute-start.8 = (bf16[256,2048]{1,0:T(8,128)(2,1)S(1)}, bf16[256,2048]{1,0:T(8,128)(2,1)S(1)}, u32[]{:S(2)}, u32[]{:S(2)}) collective-permute-start(bf16[256,2048]{1,0:T(8,128)(2,1)S(1)} %collective-permute-done.7.refs_3_), channel_id=1, source_target_pairs={{0,2},{2,0},{4,6},{6,4},{1,3},{3,1},{5,7},{7,5},{8,10},{10,8},{12,... | collective-permute-start | bytes 3145736 | tf_op jit(solution)/shard_map/hidden_far/ppermute | solution.py:474
  37.9 19.2 %copy-start = (bf16[1,256,2048]{2,1,0:T(8,128)(2,1)S(1)}, bf16[1,256,2048]{2,1,0:T(8,128)(2,1)}, u32[]{:S(2)}) copy-start(bf16[1,256,2048]{2,1,0:T(8,128)(2,1)} %param.6) | copy-start | bytes 3145732
  37.9 19.2 %copy-start.1 = (f32[1024,128]{1,0:T(8,128)S(1)}, f32[1024,128]{1,0:T(8,128)}, u32[]{:S(2)}) copy-start(f32[1024,128]{1,0:T(8,128)} %constant.62.clone.refs_5_) | copy-start | bytes 1572868
  37.9 19.1 %copy-start.2 = (f32[1024,128]{1,0:T(8,128)S(1)}, f32[1024,128]{1,0:T(8,128)}, u32[]{:S(2)}) copy-start(f32[1024,128]{1,0:T(8,128)} %constant.63.clone.refs_6_) | copy-start | bytes 1572868
  38.0 19.1 %copy-start.3 = (bf16[256,384]{1,0:T(8,128)(2,1)S(1)}, bf16[256,384]{1,0:T(8,128)(2,1)}, u32[]{:S(2)}) copy-start(bf16[256,384]{1,0:T(8,128)(2,1)} %first_piece.1.refs_8_) | copy-start | bytes 589828
  38.0 19.1 %copy-start.7 = (bf16[256,384]{1,0:T(8,128)(2,1)S(1)}, bf16[256,384]{1,0:T(8,128)(2,1)}, u32[]{:S(2)}) copy-start(bf16[256,384]{1,0:T(8,128)(2,1)} %copy-done.6) | copy-start | bytes 589828
  38.0 19.1 %copy-start.8 = (s32[3]{0:T(128)S(1)}, s32[3]{0:T(128)}, u32[]{:S(2)}) copy-start(s32[3]{0:T(128)} %pad_add_fusion.where.refs_0_) | copy-start | bytes 40
  38.0 19.1 %copy-start.9 = (s32[1,32]{1,0:T(1,128)S(1)}, s32[1,32]{1,0:T(1,128)}, u32[]{:S(2)}) copy-start(s32[1,32]{1,0:T(1,128)} %refs_7_.5) | copy-start | bytes 388
  39.2 9.8 %collective-permute-start.9 = (bf16[256,384]{1,0:T(8,128)(2,1)}, bf16[256,384]{1,0:T(8,128)(2,1)S(1)}, u32[]{:S(2)}, u32[]{:S(2)}) collective-permute-start(bf16[256,384]{1,0:T(8,128)(2,1)} %get-tuple-element.62.refs_8_), channel_id=1, source_target_pairs={{0,8},{8,16},{16,24},{24,0},{1,9},{9,17},{17,25},{25,1},{2,10},{10... | collective-permute-start | bytes 589832 | tf_op jit(solution)/shard_map/second/ppermute | solution.py:480
  39.3 13.6 %collective-permute-start.10 = (bf16[256,384]{1,0:T(8,128)(2,1)}, bf16[256,384]{1,0:T(8,128)(2,1)S(1)}, u32[]{:S(2)}, u32[]{:S(2)}) collective-permute-start(bf16[256,384]{1,0:T(8,128)(2,1)} %get-tuple-element.63.refs_8_), channel_id=1, source_target_pairs={{0,8},{8,16},{16,24},{24,0},{1,9},{9,17},{17,25},{25,1},{2,10},{10... | collective-permute-start | bytes 589832 | tf_op jit(solution)/shard_map/third/ppermute | solution.py:480
  41.3 21.2 %collective-permute-start.13 = (bf16[2,128,768]{2,1,0:T(8,128)(2,1)S(1)}, bf16[2,128,768]{2,1,0:T(8,128)(2,1)S(1)}, u32[]{:S(2)}, u32[]{:S(2)}) collective-permute-start(bf16[2,128,768]{2,1,0:T(8,128)(2,1)S(1)} %pad_maximum_fusion.2), channel_id=1, source_target_pairs={{0,1},{1,0},{2,3},{3,2},{4,5},{5,4},{6,7},{7,6},{8,9},{9,8},{10,11... | collective-permute-start | bytes 1179656 | tf_op jit(solution)/shard_map/out_group/ppermute | solution.py:474
  42.9 23.4 %copy-start.5 = (bf16[256,384]{1,0:T(8,128)(2,1)S(1)}, bf16[256,384]{1,0:T(8,128)(2,1)}, u32[]{:S(2)}) copy-start(bf16[256,384]{1,0:T(8,128)(2,1)} %get-tuple-element.62.refs_8_) | copy-start | bytes 589828
  42.9 19.6 %collective-permute-start.14 = (bf16[2,128,768]{2,1,0:T(8,128)(2,1)S(1)}, bf16[2,128,768]{2,1,0:T(8,128)(2,1)S(1)}, u32[]{:S(2)}, u32[]{:S(2)}) collective-permute-start(bf16[2,128,768]{2,1,0:T(8,128)(2,1)S(1)} %pad_maximum_fusion.1), channel_id=1, source_target_pairs={{0,4},{2,6},{4,0},{6,2},{1,5},{3,7},{5,1},{7,3},{8,12},{10,14},{12... | collective-permute-start | bytes 1179656 | tf_op jit(solution)/shard_map/out_cross/ppermute | solution.py:474
  49.0 8.1 %collective-permute-start.19 = (bf16[256,384]{1,0:T(8,128)(2,1)S(1)}, bf16[256,384]{1,0:T(8,128)(2,1)S(1)}, u32[]{:S(2)}, u32[]{:S(2)}) collective-permute-start(bf16[256,384]{1,0:T(8,128)(2,1)S(1)} %collective-permute-done.9.refs_9_), channel_id=1, source_target_pairs={{0,8},{8,16},{16,24},{24,0},{1,9},{9,17},{17,25},{25,1},{2,10},{10... | collective-permute-start | bytes 589832 | tf_op jit(solution)/shard_map/second/ppermute | solution.py:480
  52.9 9.6 %collective-permute-start.11 = (bf16[256,384]{1,0:T(8,128)(2,1)S(1)}, bf16[256,384]{1,0:T(8,128)(2,1)S(1)}, u32[]{:S(2)}, u32[]{:S(2)}) collective-permute-start(bf16[256,384]{1,0:T(8,128)(2,1)S(1)} %collective-permute-done.10.refs_9_), channel_id=1, source_target_pairs={{0,8},{8,16},{16,24},{24,0},{1,9},{9,17},{17,25},{25,1},{2,10},{10... | collective-permute-start | bytes 589832 | tf_op jit(solution)/shard_map/third/ppermute | solution.py:480
  52.9 17.4 %collective-permute-start.15 = (bf16[2,128,768]{2,1,0:T(8,128)(2,1)S(1)}, bf16[2,128,768]{2,1,0:T(8,128)(2,1)S(1)}, u32[]{:S(2)}, u32[]{:S(2)}) collective-permute-start(bf16[2,128,768]{2,1,0:T(8,128)(2,1)S(1)} %pad_maximum_fusion.2), channel_id=1, source_target_pairs={{0,5},{1,4},{2,7},{3,6},{4,1},{5,0},{6,3},{7,2},{8,13},{9,12},{10,... | collective-permute-start | bytes 1179656 | tf_op jit(solution)/shard_map/out_across/ppermute | solution.py:504
  57.1 9.3 %collective-permute-start.20 = (bf16[256,384]{1,0:T(8,128)(2,1)S(1)}, bf16[256,384]{1,0:T(8,128)(2,1)S(1)}, u32[]{:S(2)}, u32[]{:S(2)}) collective-permute-start(bf16[256,384]{1,0:T(8,128)(2,1)S(1)} %collective-permute-done.19.refs_10_), channel_id=1, source_target_pairs={{0,8},{8,16},{16,24},{24,0},{1,9},{9,17},{17,25},{25,1},{2,10},{10... | collective-permute-start | bytes 589832 | tf_op jit(solution)/shard_map/second/ppermute | solution.py:480
  62.5 7.8 %collective-permute-start.12 = (bf16[256,384]{1,0:T(8,128)(2,1)S(1)}, bf16[256,384]{1,0:T(8,128)(2,1)S(1)}, u32[]{:S(2)}, u32[]{:S(2)}) collective-permute-start(bf16[256,384]{1,0:T(8,128)(2,1)S(1)} %collective-permute-done.11.refs_10_), channel_id=1, source_target_pairs={{0,8},{8,16},{16,24},{24,0},{1,9},{9,17},{17,25},{25,1},{2,10},{10... | collective-permute-start | bytes 589832 | tf_op jit(solution)/shard_map/third/ppermute | solution.py:480
  62.5 7.7 %collective-permute-start.16 = (bf16[144,128]{1,0:T(8,128)(2,1)S(1)}, bf16[144,128]{1,0:T(8,128)(2,1)S(1)}, u32[]{:S(2)}, u32[]{:S(2)}) collective-permute-start(bf16[144,128]{1,0:T(8,128)(2,1)S(1)} %get-tuple-element.70), channel_id=1, source_target_pairs={{0,2},{2,0},{4,6},{6,4},{1,3},{3,1},{5,7},{7,5},{8,10},{10,8},{12,... | collective-permute-start | bytes 110600 | tf_op jit(solution)/shard_map/context_first/ppermute | solution.py:474
  62.5 7.7 %collective-permute-start.17 = (bf16[144,128]{1,0:T(8,128)(2,1)S(1)}, bf16[144,128]{1,0:T(8,128)(2,1)S(1)}, u32[]{:S(2)}, u32[]{:S(2)}) collective-permute-start(bf16[144,128]{1,0:T(8,128)(2,1)S(1)} %get-tuple-element.71), channel_id=1, source_target_pairs={{0,4},{2,6},{4,0},{6,2},{1,5},{3,7},{5,1},{7,3},{8,12},{10,14},{12... | collective-permute-start | bytes 110600 | tf_op jit(solution)/shard_map/context_first/ppermute | solution.py:474
  66.4 3.9 %collective-permute-start.18 = (bf16[144,128]{1,0:T(8,128)(2,1)S(1)}, bf16[144,128]{1,0:T(8,128)(2,1)S(1)}, u32[]{:S(2)}, u32[]{:S(2)}) collective-permute-start(bf16[144,128]{1,0:T(8,128)(2,1)S(1)} %get-tuple-element.72), channel_id=1, source_target_pairs={{0,6},{2,4},{4,2},{6,0},{1,7},{3,5},{5,3},{7,1},{8,14},{10,12},{12... | collective-permute-start | bytes 110600 | tf_op jit(solution)/shard_map/context_first/ppermute | solution.py:474
  70.3 4.4 %copy-start.4 = (bf16[256,384]{1,0:T(8,128)(2,1)S(1)}, bf16[256,384]{1,0:T(8,128)(2,1)}, u32[]{:S(2)}) copy-start(bf16[256,384]{1,0:T(8,128)(2,1)} %get-tuple-element.63.refs_8_) | copy-start | bytes 589828
  70.5 8.1 %collective-permute-start.25 = (bf16[4,2,128,768]{3,2,1,0:T(8,128)(2,1)S(1)}, bf16[4,2,128,768]{3,2,1,0:T(8,128)(2,1)S(1)}, u32[]{:S(2)}, u32[]{:S(2)}) collective-permute-start(bf16[4,2,128,768]{3,2,1,0:T(8,128)(2,1)S(1)} %pad_maximum_fusion.refs_10_.refs_5_), channel_id=1, source_target_pairs={{0,2},{2,0},{4,6},{6,4},{1,3},{3,1},{5,7},{7,5},{8,10},{10,8},{12,... | collective-permute-start | bytes 4718600 | tf_op jit(solution)/shard_map/out_core/ppermute | solution.py:474
  71.2 7.4 %collective-permute-start.21 = (bf16[4,144,128]{2,1,0:T(8,128)(2,1)S(1)}, bf16[4,144,128]{2,1,0:T(8,128)(2,1)S(1)}, u32[]{:S(2)}, u32[]{:S(2)}) collective-permute-start(bf16[4,144,128]{2,1,0:T(8,128)(2,1)S(1)} %pad_maximum_fusion.3), channel_id=1, source_target_pairs={{0,1},{1,0},{2,3},{3,2},{4,5},{5,4},{6,7},{7,6},{8,9},{9,8},{10,11... | collective-permute-start | bytes 442376 | tf_op jit(solution)/shard_map/context_first_group/ppermute | solution.py:474
  72.8 5.7 %collective-permute-start.22 = (bf16[144,128]{1,0:T(8,128)(2,1)S(1)}, bf16[144,128]{1,0:T(8,128)(2,1)S(1)}, u32[]{:S(2)}, u32[]{:S(2)}) collective-permute-start(bf16[144,128]{1,0:T(8,128)(2,1)S(1)} %get-tuple-element.82), channel_id=1, source_target_pairs={{0,2},{2,0},{4,6},{6,4},{1,3},{3,1},{5,7},{7,5},{8,10},{10,8},{12,... | collective-permute-start | bytes 110600 | tf_op jit(solution)/shard_map/context_second/ppermute | solution.py:474
  72.8 5.7 %collective-permute-start.23 = (bf16[144,128]{1,0:T(8,128)(2,1)S(1)}, bf16[144,128]{1,0:T(8,128)(2,1)S(1)}, u32[]{:S(2)}, u32[]{:S(2)}) collective-permute-start(bf16[144,128]{1,0:T(8,128)(2,1)S(1)} %get-tuple-element.83), channel_id=1, source_target_pairs={{0,4},{2,6},{4,0},{6,2},{1,5},{3,7},{5,1},{7,3},{8,12},{10,14},{12... | collective-permute-start | bytes 110600 | tf_op jit(solution)/shard_map/context_second/ppermute | solution.py:474
  74.3 4.2 %collective-permute-start.24 = (bf16[144,128]{1,0:T(8,128)(2,1)S(1)}, bf16[144,128]{1,0:T(8,128)(2,1)S(1)}, u32[]{:S(2)}, u32[]{:S(2)}) collective-permute-start(bf16[144,128]{1,0:T(8,128)(2,1)S(1)} %get-tuple-element.84), channel_id=1, source_target_pairs={{0,6},{2,4},{4,2},{6,0},{1,7},{3,5},{5,3},{7,1},{8,14},{10,12},{12... | collective-permute-start | bytes 110600 | tf_op jit(solution)/shard_map/context_second/ppermute | solution.py:474
  78.6 2.5 %collective-permute-start.27 = (bf16[144,128]{1,0:T(8,128)(2,1)S(1)}, bf16[144,128]{1,0:T(8,128)(2,1)S(1)}, u32[]{:S(2)}, u32[]{:S(2)}) collective-permute-start(bf16[144,128]{1,0:T(8,128)(2,1)S(1)} %get-tuple-element.104), channel_id=1, source_target_pairs={{0,2},{2,0},{4,6},{6,4},{1,3},{3,1},{5,7},{7,5},{8,10},{10,8},{12,... | collective-permute-start | bytes 110600 | tf_op jit(solution)/shard_map/context_third/ppermute | solution.py:474
  78.9 4.0 %collective-permute-start.28 = (bf16[144,128]{1,0:T(8,128)(2,1)S(1)}, bf16[144,128]{1,0:T(8,128)(2,1)S(1)}, u32[]{:S(2)}, u32[]{:S(2)}) collective-permute-start(bf16[144,128]{1,0:T(8,128)(2,1)S(1)} %get-tuple-element.105), channel_id=1, source_target_pairs={{0,4},{2,6},{4,0},{6,2},{1,5},{3,7},{5,1},{7,3},{8,12},{10,14},{12... | collective-permute-start | bytes 110600 | tf_op jit(solution)/shard_map/context_third/ppermute | solution.py:474
  80.4 3.6 %collective-permute-start.29 = (bf16[144,128]{1,0:T(8,128)(2,1)S(1)}, bf16[144,128]{1,0:T(8,128)(2,1)S(1)}, u32[]{:S(2)}, u32[]{:S(2)}) collective-permute-start(bf16[144,128]{1,0:T(8,128)(2,1)S(1)} %get-tuple-element.106), channel_id=1, source_target_pairs={{0,6},{2,4},{4,2},{6,0},{1,7},{3,5},{5,3},{7,1},{8,14},{10,12},{12... | collective-permute-start | bytes 110600 | tf_op jit(solution)/shard_map/context_third/ppermute | solution.py:474
  80.6 6.4 %collective-permute-start.26 = (bf16[4,144,128]{2,1,0:T(8,128)(2,1)S(1)}, bf16[4,144,128]{2,1,0:T(8,128)(2,1)S(1)}, u32[]{:S(2)}, u32[]{:S(2)}) collective-permute-start(bf16[4,144,128]{2,1,0:T(8,128)(2,1)S(1)} %pad_maximum_fusion.4), channel_id=1, source_target_pairs={{0,1},{1,0},{2,3},{3,2},{4,5},{5,4},{6,7},{7,6},{8,9},{9,8},{10,11... | collective-permute-start | bytes 442376 | tf_op jit(solution)/shard_map/context_second_group/ppermute | solution.py:474
  84.1 6.1 %copy-start.10 = (s32[1,8,1]{1,2,0:T(1,128)S(1)}, s32[1,8,1]{1,2,0:T(1,128)}, u32[]{:S(2)}) copy-start(s32[1,8,1]{1,2,0:T(1,128)} %param.9) | copy-start | bytes 100
  84.1 6.1 %collective-permute-start.30 = (bf16[4,144,128]{2,1,0:T(8,128)(2,1)S(1)}, bf16[4,144,128]{2,1,0:T(8,128)(2,1)S(1)}, u32[]{:S(2)}, u32[]{:S(2)}) collective-permute-start(bf16[4,144,128]{2,1,0:T(8,128)(2,1)S(1)} %pad_maximum_fusion.5), channel_id=1, source_target_pairs={{0,1},{1,0},{2,3},{3,2},{4,5},{5,4},{6,7},{7,6},{8,9},{9,8},{10,11... | collective-permute-start | bytes 442376 | tf_op jit(solution)/shard_map/context_third_group/ppermute | solution.py:474
  92.4 3.7 %collective-permute-start.31 = (f32[4,1024]{1,0:T(4,128)S(1)}, f32[4,1024]{1,0:T(4,128)S(1)}, u32[]{:S(2)}, u32[]{:S(2)}) collective-permute-start(f32[4,1024]{1,0:T(4,128)S(1)} %get-tuple-element.111), channel_id=1, source_target_pairs={{0,1},{1,0},{2,3},{3,2},{4,5},{5,4},{6,7},{7,6},{8,9},{9,8},{10,11... | collective-permute-start | bytes 49160 | tf_op jit(solution)/shard_map/embedding_half/ppermute | solution.py:474
